TPU v7x, 128 devices: a whole 4x4x4 slice. The times are simulated.
128 devices in a mesh: section: 2 (over x_lo), fsdp: 16 (over z, y), rep: 4 (over x_hi, core).
Axes of the slice: x: 4 (x_hi: 2, x_lo: 2; x = x_hi * 2 + x_lo), y: 4, z: 4, core: 2. Of those that a mesh axis runs over, the one named last changes fastest.
Arguments:
- patch_tokens: bfloat16 [16, 1024, 1024], P('rep', 'fsdp'), may hold values from -6 to 6
- out_grad: bfloat16 [16, 1024, 1024], P('rep', 'fsdp'), may hold values from -6 to 6
- batch_counts: int32 [4, 2], P('rep'), may hold values from 1 to 2, as said below
- norm_gain: bfloat16 [2, 2, 1024], P('section', None, 'fsdp'), may hold values from 0.25 to 1.75
- norm_bias: bfloat16 [2, 2, 1024], P('section', None, 'fsdp'), may hold values from -1.75 to 1.75
- qkv_weight: bfloat16 [2, 1024, 3072], P('section', 'fsdp'), may hold values from -0.1875 to 0.1875
- qv_bias: bfloat16 [2, 2, 1024], P('section', None, 'fsdp'), may hold values from -1.75 to 1.75
- proj_weight: bfloat16 [2, 1024, 1024], P('section', 'fsdp'), may hold values from -3 to 3
- fc1_weight: bfloat16 [2, 1024, 4096], P('section', 'fsdp'), may hold values from -0.1875 to 0.1875
- fc1_bias: bfloat16 [2, 4096], P('section', 'fsdp'), may hold values from -3 to 3
- fc2_weight: bfloat16 [2, 4096, 1024], P('section', 'fsdp'), may hold values from -0.09375 to 0.09375
- out_bias: bfloat16 [2, 2, 1024], P('section', None, 'fsdp'), may hold values from -1.75 to 1.75
- layer_scale: bfloat16 [2, 2, 1024], P('section', None, 'fsdp'), may hold values from 0.29882812 to 1.1953125
Outputs:
- block_out: bfloat16 [2, 16, 1024, 1024], P('section', 'rep', 'fsdp')
- in_grad: bfloat16 [2, 16, 1024, 1024], P('section', 'rep', 'fsdp')
- norm_gain_grad: float32 [2, 2, 1024], P('section', None, 'fsdp')
- norm_bias_grad: float32 [2, 2, 1024], P('section', None, 'fsdp')
- qkv_weight_grad: float32 [2, 1024, 3072], P('section', 'fsdp')
- qv_bias_grad: float32 [2, 2, 1024], P('section', None, 'fsdp')
- proj_weight_grad: float32 [2, 1024, 1024], P('section', 'fsdp')
- fc1_weight_grad: float32 [2, 1024, 4096], P('section', 'fsdp')
- fc1_bias_grad: float32 [2, 4096], P('section', 'fsdp')
- fc2_weight_grad: float32 [2, 4096, 1024], P('section', 'fsdp')
- out_bias_grad: float32 [2, 2, 1024], P('section', None, 'fsdp')
- layer_scale_grad: float32 [2, 2, 1024], P('section', None, 'fsdp')
Inputs may be any that keep to these rules, and one draw needn't show every extreme that they name: Micro-batch m of replica r holds batch_counts[r, m] live images in its first slots; the first micro-batch of every replica is full, and the last micro-batch of one replica holds a single live image.
All inputs are finite; a program needn't handle non-finite values.
Results may differ from a plain program's by a relative error of at most 0.019.
Values may be sent and summed in bfloat16 or wider, within the bound.
No kernel may reach another device: no remote copies, remote signals or barrier semaphores. Data moves between devices by JAX's collectives and lax.ppermute only.
A program may use at most 192 MiB of HBM per device.

v0:
```python
from functools import partial

import jax
import jax.numpy as jnp
from jax import lax
from jax.sharding import PartitionSpec as P

HEAD_DIM = 64
MB = 2
IMG_MB = 2


epsilon = 1e-06


def in_one_piece(arrays, axis, dim, along):
    ends, at = ([], 0)
    for a in arrays[:-1]:
        at += a.shape[along]
        ends.append(at)
    both = jnp.concatenate(arrays, axis=along)
    return tuple(jnp.split(lax.all_gather(both, axis, axis=dim, tiled=True), ends, axis=along))


def side_by_side(arrays, axis, dim, along):
    columns = [a.reshape(*a.shape[:along], -1) for a in arrays]
    both = jnp.concatenate(columns, axis=along)
    filled, at, gathered = (lax.all_gather(both, axis, axis=dim, tiled=True), 0, [])
    for a, column in zip(arrays, columns):
        slab = filled[..., at : at + column.shape[along]]
        gathered.append(slab.reshape(*slab.shape[:along], *a.shape[along:]))
        at += column.shape[along]
    return tuple(gathered)


def shifted(value, axis, by):
    length = lax.axis_size(axis)
    pairs = [(i, i + by) for i in range(length) if 0 <= i + by < length]
    return lax.ppermute(value, axis, pairs)


def in_blocks(value, dim, length):
    before, after = (value.shape[:dim], value.shape[dim + 1 :])
    return jnp.moveaxis(value.reshape(*before, length, -1, *after), dim, 0)


def one_scatter(arrays, axis, dims):
    length = lax.axis_size(axis)
    pieces = [in_blocks(a, dim, length) for a, dim in zip(arrays, dims)]
    lines = jnp.concatenate([b.reshape(length, -1) for b in pieces], axis=1)
    rows = max(16, -(-lines.shape[1] // 1024) * 8)
    lines = jnp.pad(lines, ((0, 0), (0, rows * 128 - lines.shape[1]))).reshape(-1, 128)
    vector, at, gathered = (lax.psum_scatter(lines, axis, tiled=True).reshape(-1), 0, [])
    for b in pieces:
        part = b[0]
        gathered.append(vector[at : at + part.size].reshape(part.shape))
        at += part.size
    return tuple(gathered)


def normalize(values, scale_vec, shift_vec):
    row_mean = jnp.mean(values, axis=-1, keepdims=True)
    centred = values - row_mean
    spread = jnp.mean(centred * centred, axis=-1, keepdims=True)
    return centred * lax.rsqrt(spread + epsilon) * scale_vec + shift_vec


def exact_gelu(values):
    return jax.nn.gelu(values, approximate=False)


def gated(active, function, *operands):

    def skipped(*inner_ops):
        return jax.tree.map(jnp.zeros_like, function(*inner_ops))

    return lax.cond(active, function, skipped, *operands)


def prepare(pieces):
    as_float = lambda array_leaf: array_leaf.astype(jnp.float32)
    (
        norm_gains,
        norm_shifts,
        in_biases,
        out_biases,
        scales,
        qkv_matrix,
        proj_matrix,
        up_matrix,
        hidden_bias,
        down_matrix,
    ) = pieces
    return (
        as_float(norm_gains),
        as_float(norm_shifts),
        as_float(in_biases),
        as_float(out_biases),
        as_float(scales),
        qkv_matrix,
        proj_matrix,
        up_matrix,
        as_float(hidden_bias),
        down_matrix,
    )


def store(buffers, fresh, active, batch_slot):

    def place(stored_all, new_leaf):
        previous = stored_all[batch_slot]
        return stored_all.at[batch_slot].set(jnp.where(active, new_leaf, previous))

    return jax.tree.map(place, buffers, fresh)


def slot_buffers(fresh):
    return jax.tree.map(lambda new_leaf: jnp.zeros((MB,) + new_leaf.shape, new_leaf.dtype), fresh)


def split_heads(values):
    return values.reshape(values.shape[0], values.shape[1], values.shape[2] // HEAD_DIM, HEAD_DIM)


def attend(queries, key_set, value_set, key_pattern):
    factor = HEAD_DIM ** (-0.5)
    scores = (
        jnp.einsum(
            "iqhe," + key_pattern + "->ihqk",
            split_heads(queries),
            split_heads(key_set),
            preferred_element_type=jnp.float32,
        )
        * factor
    )
    top_score = jnp.max(scores, axis=-1, keepdims=True)
    raised = jnp.exp(scores - top_score)
    exp_total = jnp.sum(raised, axis=-1, keepdims=True)
    weighting = (raised / exp_total).astype(jnp.bfloat16)
    log_total = top_score + jnp.log(exp_total)
    attended = jnp.einsum(
        "ihqk," + key_pattern + "->iqhe",
        weighting,
        split_heads(value_set),
        preferred_element_type=jnp.float32,
    )
    return (attended.reshape(queries.shape).astype(jnp.bfloat16), log_total)


def attend_back(grad_attended, queries, key_set, value_set, log_total, key_pattern):
    factor = HEAD_DIM ** (-0.5)
    scores = (
        jnp.einsum(
            "iqhe," + key_pattern + "->ihqk",
            split_heads(queries),
            split_heads(key_set),
            preferred_element_type=jnp.float32,
        )
        * factor
    )
    weighting = jnp.exp(scores - log_total)
    grad_heads = split_heads(grad_attended)
    grad_weighting = jnp.einsum(
        "iqhe," + key_pattern + "->ihqk",
        grad_heads,
        split_heads(value_set),
        preferred_element_type=jnp.float32,
    )
    row_term = jnp.sum(grad_weighting * weighting, axis=-1, keepdims=True)
    grad_scores = (weighting * (grad_weighting - row_term)).astype(jnp.bfloat16)
    grad_queries = (
        jnp.einsum(
            "ihqk," + key_pattern + "->iqhe",
            grad_scores,
            split_heads(key_set),
            preferred_element_type=jnp.float32,
        )
        * factor
    )
    grad_queries = grad_queries.reshape(queries.shape).astype(jnp.bfloat16)
    key_term = (
        jnp.einsum(
            "ihqk,iqhe->" + key_pattern,
            grad_scores,
            split_heads(queries),
            preferred_element_type=jnp.float32,
        )
        * factor
    )
    value_term = jnp.einsum(
        "ihqk,iqhe->" + key_pattern,
        weighting.astype(jnp.bfloat16),
        grad_heads,
        preferred_element_type=jnp.float32,
    )
    return (grad_queries, key_term.reshape(key_set.shape), value_term.reshape(key_set.shape))


def front(inputs, weights, key_layout):
    (
        norm_gains,
        norm_shifts,
        in_biases,
        out_biases,
        scales,
        qkv_matrix,
        proj_matrix,
        up_matrix,
        hidden_bias,
        down_matrix,
    ) = weights
    model_width = proj_matrix.shape[0]
    normed_one = normalize(inputs.astype(jnp.float32), norm_gains[0], norm_shifts[0]).astype(
        jnp.bfloat16
    )
    queries = jnp.einsum(
        "isd,de->ise", normed_one, qkv_matrix[:, :model_width], preferred_element_type=jnp.float32
    )
    queries = (queries + in_biases[0]).astype(jnp.bfloat16)
    key_value = jnp.einsum(
        "isd,de->" + key_layout,
        normed_one,
        qkv_matrix[:, model_width:],
        preferred_element_type=jnp.float32,
    )
    key_part = key_value[..., :model_width].astype(jnp.bfloat16)
    value_part = (key_value[..., model_width:] + in_biases[1]).astype(jnp.bfloat16)
    return (normed_one, queries, key_part, value_part)


def rear(inputs, attended, weights):
    (
        norm_gains,
        norm_shifts,
        in_biases,
        out_biases,
        scales,
        qkv_matrix,
        proj_matrix,
        up_matrix,
        hidden_bias,
        down_matrix,
    ) = weights
    branch = (
        jnp.einsum("isd,de->ise", attended, proj_matrix, preferred_element_type=jnp.float32)
        + out_biases[0]
    )
    middle = inputs.astype(jnp.float32) + scales[0] * branch
    normed_two = normalize(middle, norm_gains[1], norm_shifts[1]).astype(jnp.bfloat16)
    before = (
        jnp.einsum("isd,df->isf", normed_two, up_matrix, preferred_element_type=jnp.float32)
        + hidden_bias
    )
    activated = exact_gelu(before).astype(jnp.bfloat16)
    branch_two = (
        jnp.einsum("isf,fd->isd", activated, down_matrix, preferred_element_type=jnp.float32)
        + out_biases[1]
    )
    result = (middle + scales[1] * branch_two).astype(jnp.bfloat16)
    return (result, (branch, middle, normed_two, before, activated, branch_two))


def mlp_back(grad_out, post, weights):
    (
        norm_gains,
        norm_shifts,
        in_biases,
        out_biases,
        scales,
        qkv_matrix,
        proj_matrix,
        up_matrix,
        hidden_bias,
        down_matrix,
    ) = weights
    attended, branch, middle, normed_two, before, activated, branch_two = post
    grad_branch_two = (scales[1] * grad_out).astype(jnp.bfloat16)
    grad_activated = jnp.einsum(
        "isd,fd->isf", grad_branch_two, down_matrix, preferred_element_type=jnp.float32
    )
    gelu_back = jax.vjp(exact_gelu, before)[1]
    grad_before = gelu_back(grad_activated)[0].astype(jnp.bfloat16)
    grad_normed_two = jnp.einsum(
        "isf,df->isd", grad_before, up_matrix, preferred_element_type=jnp.float32
    )
    norm_back = jax.vjp(normalize, middle, norm_gains[1], norm_shifts[1])[1]
    grad_middle, gain_two, shift_two = norm_back(grad_normed_two)
    grad_middle = grad_middle + grad_out
    grad_branch = (scales[0] * grad_middle).astype(jnp.bfloat16)
    grad_attended = jnp.einsum(
        "ise,de->isd", grad_branch, proj_matrix, preferred_element_type=jnp.float32
    ).astype(jnp.bfloat16)
    vectors = (
        gain_two,
        shift_two,
        jnp.sum(grad_middle * branch, axis=(0, 1)),
        jnp.sum(grad_out * branch_two, axis=(0, 1)),
        jnp.sum(grad_branch.astype(jnp.float32), axis=(0, 1)),
        jnp.sum(grad_branch_two.astype(jnp.float32), axis=(0, 1)),
        jnp.sum(grad_before.astype(jnp.float32), axis=(0, 1)),
    )
    return (grad_attended, grad_middle, grad_branch, grad_before, grad_branch_two, vectors)


def front_back(grad_middle, grad_queries, grad_keys, grad_values, inputs, weights, key_layout):
    (
        norm_gains,
        norm_shifts,
        in_biases,
        out_biases,
        scales,
        qkv_matrix,
        proj_matrix,
        up_matrix,
        hidden_bias,
        down_matrix,
    ) = weights
    model_width = proj_matrix.shape[0]
    grad_normed = jnp.einsum(
        "ise,de->isd", grad_queries, qkv_matrix[:, :model_width], preferred_element_type=jnp.float32
    )
    kv_grads = jnp.concatenate([grad_keys, grad_values], axis=-1)
    grad_normed = grad_normed + jnp.einsum(
        key_layout + ",de->isd",
        kv_grads,
        qkv_matrix[:, model_width:],
        preferred_element_type=jnp.float32,
    )
    norm_back = jax.vjp(normalize, inputs.astype(jnp.float32), norm_gains[0], norm_shifts[0])[1]
    grad_inputs, gain_one, shift_one = norm_back(grad_normed)
    grad_inputs = (grad_inputs + grad_middle).astype(jnp.bfloat16)
    vectors = (
        gain_one,
        shift_one,
        jnp.sum(grad_queries.astype(jnp.float32), axis=(0, 1)),
        jnp.sum(grad_values.astype(jnp.float32), axis=(0, 1)),
    )
    return (grad_inputs, vectors)


def assemble(rear_vectors, front_vectors):
    gain_two, shift_two, scale_one, scale_two, bias_one, bias_two, hidden_grad = rear_vectors
    gain_one, shift_one, query_bias, value_bias = front_vectors
    return (
        jnp.stack([gain_one, gain_two]),
        jnp.stack([shift_one, shift_two]),
        jnp.stack([query_bias, value_bias]),
        jnp.stack([bias_one, bias_two]),
        jnp.stack([scale_one, scale_two]),
        hidden_grad,
    )


def matrix_grads(
    normed_one,
    grad_queries,
    grad_keys,
    grad_values,
    attended,
    grad_branch,
    normed_two,
    grad_before,
    activated,
    grad_branch_two,
    key_layout,
):
    key_form = "misd,m" + key_layout + "->de"
    qkv_grad = jnp.concatenate(
        [
            jnp.einsum(
                "misd,mise->de", normed_one, grad_queries, preferred_element_type=jnp.float32
            ),
            jnp.einsum(key_form, normed_one, grad_keys, preferred_element_type=jnp.float32),
            jnp.einsum(key_form, normed_one, grad_values, preferred_element_type=jnp.float32),
        ],
        axis=1,
    )
    proj_grad = jnp.einsum(
        "misd,mise->de", attended, grad_branch, preferred_element_type=jnp.float32
    )
    up_grad = jnp.einsum(
        "misd,misf->df", normed_two, grad_before, preferred_element_type=jnp.float32
    )
    down_grad = jnp.einsum(
        "misf,misd->fd", activated, grad_branch_two, preferred_element_type=jnp.float32
    )
    return (qkv_grad, proj_grad, up_grad, down_grad)


def per_device(
    patch_tokens,
    out_grad,
    batch_counts,
    norm_gain,
    norm_bias,
    qkv_weight,
    qv_bias,
    proj_weight,
    fc1_weight,
    fc1_bias,
    fc2_weight,
    out_bias,
    layer_scale,
):
    section_index = lax.axis_index("section")
    per_slot = IMG_MB
    image_rows = patch_tokens.shape[1]
    model_width = patch_tokens.shape[2]
    key_layout = "ise"
    weights = prepare(
        (
            *in_one_piece(
                (norm_gain[0], norm_bias[0], qv_bias[0], out_bias[0], layer_scale[0]), "fsdp", 1, 0
            ),
            *in_one_piece((qkv_weight[0], proj_weight[0], fc1_weight[0]), "fsdp", 0, 1),
            *side_by_side((fc1_bias[0], fc2_weight[0]), "fsdp", 0, 1),
        )
    )
    zero_block = jnp.zeros((per_slot, image_rows, model_width), jnp.bfloat16)
    received = zero_block
    out_buffer = jnp.zeros((MB, per_slot, image_rows, model_width), jnp.bfloat16)
    buffers = None
    for moment in range(MB + 1):
        batch_index = moment - section_index
        active = (batch_index >= 0) & (batch_index < MB)
        batch_slot = jnp.clip(batch_index, 0, MB - 1)
        own_block = lax.dynamic_slice_in_dim(patch_tokens, batch_slot * per_slot, per_slot, 0)
        inputs = jnp.where(section_index == 0, own_block, received)
        normed_one, queries, key_part, value_part = gated(
            active, partial(front, key_layout=key_layout), inputs, weights
        )
        head_query, head_key, head_value = (
            lax.all_to_all(queries, "fsdp", split_axis=2, concat_axis=1, tiled=True),
            lax.all_to_all(key_part, "fsdp", split_axis=2, concat_axis=1, tiled=True),
            lax.all_to_all(value_part, "fsdp", split_axis=2, concat_axis=1, tiled=True),
        )
        head_out, log_total = gated(
            active, partial(attend, key_pattern="ikhe"), head_query, head_key, head_value
        )
        attended = lax.all_to_all(head_out, "fsdp", split_axis=1, concat_axis=2, tiled=True)
        attn_kept = (head_query, head_key, head_value, log_total)
        result, kept = gated(active, rear, inputs, attended, weights)
        fresh = (inputs, normed_one) + attn_kept + (attended,) + kept
        if moment == 0:
            buffers = slot_buffers(fresh)
        buffers = store(buffers, fresh, active, batch_slot)
        out_buffer = store(out_buffer, result, active, batch_slot)
        if moment < MB:
            received = shifted(result, "section", 1)
    live_mask = (
        jnp.arange(MB * per_slot) % per_slot < jnp.repeat(batch_counts[0], per_slot)
    ).astype(jnp.float32)
    received_grad = zero_block
    in_buffer = jnp.zeros((MB, per_slot, image_rows, model_width), jnp.bfloat16)
    grad_store = None
    vector_sums = None
    shard_sums = None
    for moment in range(MB + 1):
        batch_index = moment - 1 + section_index
        active = (batch_index >= 0) & (batch_index < MB)
        batch_slot = jnp.clip(batch_index, 0, MB - 1)
        own_grad = lax.dynamic_slice_in_dim(out_grad, batch_slot * per_slot, per_slot, 0).astype(
            jnp.float32
        )
        own_live = lax.dynamic_slice_in_dim(live_mask, batch_slot * per_slot, per_slot, 0)
        grad_out = jnp.where(
            section_index == 1,
            own_grad * own_live[:, None, None],
            received_grad.astype(jnp.float32),
        )
        saved = jax.tree.map(lambda stored_all: stored_all[batch_slot], buffers)
        inputs, normed_one = (saved[0], saved[1])
        first_kept, second_kept, third_kept, log_total = saved[2:6]
        outcome = gated(active, mlp_back, grad_out, saved[6:], weights)
        grad_attended, grad_middle, grad_branch, grad_before, grad_branch_two, rear_vectors = (
            outcome
        )
        head_grad = lax.all_to_all(grad_attended, "fsdp", split_axis=2, concat_axis=1, tiled=True)
        head_terms = gated(
            active,
            partial(attend_back, key_pattern="ikhe"),
            head_grad,
            first_kept,
            second_kept,
            third_kept,
            log_total,
        )
        grad_queries, grad_keys, grad_values = (
            lax.all_to_all(head_terms[0], "fsdp", split_axis=1, concat_axis=2, tiled=True),
            lax.all_to_all(
                head_terms[1].astype(jnp.bfloat16), "fsdp", split_axis=1, concat_axis=2, tiled=True
            ),
            lax.all_to_all(
                head_terms[2].astype(jnp.bfloat16), "fsdp", split_axis=1, concat_axis=2, tiled=True
            ),
        )
        grad_inputs, front_vectors = gated(
            active,
            partial(front_back, key_layout=key_layout),
            grad_middle,
            grad_queries,
            grad_keys,
            grad_values,
            inputs,
            weights,
        )
        in_buffer = store(in_buffer, grad_inputs, active, batch_slot)
        if moment < MB:
            received_grad = shifted(grad_inputs, "section", -1)
        vectors = assemble(rear_vectors, front_vectors)
        new_grads = (
            grad_queries,
            grad_keys,
            grad_values,
            grad_branch,
            grad_before,
            grad_branch_two,
        )
        if moment == 0:
            grad_store = slot_buffers(new_grads)
        grad_store = store(grad_store, new_grads, active, batch_slot)
        vector_sums = (
            vectors if vector_sums is None else jax.tree.map(jnp.add, vector_sums, vectors)
        )
    matrices = matrix_grads(
        buffers[1],
        grad_store[0],
        grad_store[1],
        grad_store[2],
        buffers[6],
        grad_store[3],
        buffers[9],
        grad_store[4],
        buffers[11],
        grad_store[5],
        key_layout=key_layout,
    )
    full = vector_sums[:5] + (matrices[0], matrices[1], matrices[2], vector_sums[5], matrices[3])
    shard_sums = tuple(
        (
            part.astype(jnp.float32)
            for part in one_scatter(
                (
                    full[0].astype(jnp.bfloat16),
                    full[1].astype(jnp.bfloat16),
                    full[2].astype(jnp.bfloat16),
                    full[3].astype(jnp.bfloat16),
                    full[4].astype(jnp.bfloat16),
                    full[5].astype(jnp.bfloat16),
                    full[6].astype(jnp.bfloat16),
                    full[7].astype(jnp.bfloat16),
                    full[8].astype(jnp.bfloat16),
                    full[9].astype(jnp.bfloat16),
                ),
                "fsdp",
                (1, 1, 1, 1, 1, 0, 0, 0, 0, 0),
            )
        )
    )
    totals = (
        lax.psum(shard_sums[0].astype(jnp.bfloat16), "rep").astype(jnp.float32),
        lax.psum(shard_sums[1].astype(jnp.bfloat16), "rep").astype(jnp.float32),
        lax.psum(shard_sums[2].astype(jnp.bfloat16), "rep").astype(jnp.float32),
        lax.psum(shard_sums[3].astype(jnp.bfloat16), "rep").astype(jnp.float32),
        lax.psum(shard_sums[4].astype(jnp.bfloat16), "rep").astype(jnp.float32),
        lax.psum(shard_sums[5].astype(jnp.bfloat16), "rep").astype(jnp.float32),
        lax.psum(shard_sums[6].astype(jnp.bfloat16), "rep").astype(jnp.float32),
        lax.psum(shard_sums[7].astype(jnp.bfloat16), "rep").astype(jnp.float32),
        lax.psum(shard_sums[8].astype(jnp.bfloat16), "rep").astype(jnp.float32),
        lax.psum(shard_sums[9].astype(jnp.bfloat16), "rep").astype(jnp.float32),
    )
    block_out = out_buffer.reshape(MB * per_slot, image_rows, model_width)[None]
    in_grad = in_buffer.reshape(MB * per_slot, image_rows, model_width)[None]
    return (
        block_out,
        in_grad,
        totals[0][None],
        totals[1][None],
        totals[5][None],
        totals[2][None],
        totals[6][None],
        totals[7][None],
        totals[8][None],
        totals[9][None],
        totals[3][None],
        totals[4][None],
    )


def solution(mesh):
    return jax.shard_map(
        per_device,
        mesh=mesh,
        in_specs=(
            P("rep", "fsdp", None),
            P("rep", "fsdp", None),
            P("rep", None),
            P("section", None, "fsdp"),
            P("section", None, "fsdp"),
            P("section", "fsdp", None),
            P("section", None, "fsdp"),
            P("section", "fsdp", None),
            P("section", "fsdp", None),
            P("section", "fsdp"),
            P("section", "fsdp", None),
            P("section", None, "fsdp"),
            P("section", None, "fsdp"),
        ),
        out_specs=(
            P("section", "rep", "fsdp", None),
            P("section", "rep", "fsdp", None),
            P("section", None, "fsdp"),
            P("section", None, "fsdp"),
            P("section", "fsdp", None),
            P("section", None, "fsdp"),
            P("section", "fsdp", None),
            P("section", "fsdp", None),
            P("section", "fsdp"),
            P("section", "fsdp", None),
            P("section", None, "fsdp"),
            P("section", None, "fsdp"),
        ),
        check_vma=False,
    )
```

profile of v0, /device:TPU:1, one launch (start us, length us, event | category | flops | bytes accessed | tf_op | source)
XLA Modules:
  0.0 1700.0 jit_solution(13465544554573797625)
XLA Ops:
  11.1 21.4 %all-gather = bf16[16,64,10]{1,2,0:T(8,128)(2,1)S(1)} all-gather(bf16[1,64,10]{1,2,0:T(8,128)(2,1)S(1)} %bitcast.1527), channel_id=1, replica_groups=mesh['section'=2,'fsdp'=16,'rep'=4] {'fsdp'}, dimensions={0}, use_global_device_ids=true | all-gather | bytes 21760 | tf_op jit(solution)/shard_map/all_gather | solution.py:22
  39.3 86.4 %all-gather.4.cloned.1.call-done = bf16[1024,8192]{1,0:T(8,128)(2,1)} async-done(((bf16[64,8192]{1,0:T(8,128)(2,1)}), bf16[1024,8192]{1,0:T(8,128)(2,1)}) %all-gather.4.cloned.1.call-update) | async-done | bytes 16777232 | tf_op jit(solution)/shard_map/all_gather | solution.py:22
  147.9 7.7 all-to-all-done
  160.4 46.7 %all-gather.6.cloned.1.call-done = bf16[4096,1025]{1,0:T(8,128)(2,1)} async-done(((bf16[256,1025]{1,0:T(8,128)(2,1)}), bf16[4096,1025]{1,0:T(8,128)(2,1)}) %all-gather.6.cloned.1.call-update) | async-done | bytes 8396816 | tf_op jit(solution)/shard_map/all_gather | solution.py:28
  207.1 12.2 slice.1805
  224.1 7.7 split.39
  252.3 15.8 conditional.19
  292.1 17.8 %conditional.20 = (bf16[2,64,1024]{2,1,0:T(8,128)(2,1)}, f32[2,64,1024]{2,1,0:T(8,128)S(1)}, f32[2,64,1024]{2,1,0:T(8,128)}, bf16[2,64,1024]{2,1,0:T(8,128)(2,1)...) conditional(s32[]{:T(128)} %convert_element_type.500, () %tuple.494, ...), branch_computations={%region_9.10_spmd, %region_10.13_spmd} | conditional | flops 2452750336 | bytes 55931552 | solution.py:77
  297.2 9.2 fusion.32
  331.4 8.6 conditional.21
  409.5 20.2 %conditional.22 = (bf16[2,1024,64]{1,2,0:T(8,128)(2,1)}, f32[2,1,1024,1]{2,0,3,1:T(2,128)S(1)}) conditional(s32[]{:T(128)} %convert_element_type.508, () %tuple.501, (bf16[2,16,64,64]{3,1,2,0:T(8,128)(2,1)}, bf16[2,16,64,64]{3,1,2,0:T(8,128)(2,1)}, bf16[2,16,64,64]{3,1,2,0:T(8,128)(2,1)}) %tuple.741), branch_computations={%region_18.19_spmd, %region_19.22_spmd} | conditional | flops 555874304 | bytes 30474284 | solution.py:77
  461.8 23.4 %conditional.23 = (bf16[2,64,1024]{2,1,0:T(8,128)(2,1)}, f32[2,64,1024]{2,1,0:T(8,128)}, f32[2,64,1024]{2,1,0:T(8,128)}, bf16[2,64,1024]{2,1,0:T(8,128)(2,1)}, f...) conditional(s32[]{:T(128)} %convert_element_type.508, () %tuple.500, ...), branch_computations={%region_22.23_spmd, %region_23.26_spmd} | conditional | flops 2452750336 | bytes 53834344 | solution.py:77
  472.3 9.2 fusion.80
  626.7 8.1 conditional.27
  732.2 106.4 %collective-permute-done.2 = bf16[2,64,1024]{2,1,0:T(8,128)(2,1)} collective-permute-done((bf16[2,64,1024]{2,1,0:T(8,128)(2,1)}, bf16[2,64,1024]{2,1,0:T(8,128)(2,1)}, u32[]{:S(2)}, u32[]{:S(2)}) %collective-permute-start.2) | collective-permute-done | bytes 262176 | tf_op jit(solution)/shard_map/ppermute | solution.py:39
  839.5 35.8 %conditional.30 = (bf16[2,64,1024]{2,1,0:T(8,128)(2,1)}, f32[2,64,1024]{2,1,0:T(8,128)}, bf16[2,64,1024]{2,1,0:T(8,128)(2,1)}, bf16[2,64,4096]{2,1,0:T(8,128)(2,...) conditional(s32[]{:T(128)} %convert_element_type.515, ...), branch_computations={%region_70.71_spmd, %region_71.83_spmd} | conditional | flops 2460080896 | bytes 57686212 | solution.py:77
  843.1 11.3 convert_reduce_fusion.9
  905.0 26.4 %conditional.31 = (bf16[2,1024,64]{1,2,0:T(8,128)(2,1)}, bf16[2,1024,64]{1,2,0:T(8,128)(2,1)}, bf16[2,1024,64]{1,2,0:T(8,128)(2,1)}) conditional(s32[]{:T(128)} %convert_element_type.515, () %tuple.519, (bf16[2,2,1024,64]{2,3,1,0:T(8,128)(2,1)}, s32[]{:T(128)}, bf16[2,2,1024,64]{2,3,1,0:T(8,128)(2,1)}, f32[2,2,1,1024,1]{3,1,4,2,0:T(2,128)S(1)}, ...), branch_computations={%region_83.84_spmd, %region_84.86_spmd} | conditional | flops 1367865344 | bytes 91843176 | solution.py:77
  994.3 28.7 %conditional.32 = (bf16[2,64,1024]{2,1,0:T(8,128)(2,1)}, f32[1,16,64]{2,1,0:T(8,128)S(1)}, f32[1,16,64]{2,1,0:T(8,128)S(1)}, f32[1,16,64]{2,1,0:T(8,128)S(1)}, f32[1,16,64]{2,1,0:T(8,128)S(1)}) conditional(s32[]{:T(128)} %convert_element_type.515, () %tuple.518, (bf16[2,64,16,64]{1,2,3,0:T(8,128)(2,1)}, bf16[1024,3072]{1,0:T(8,128)(2,1)}, ...), branch_computations={%region_86.87_spmd, %region_87.0_spmd} | conditional | flops 811070080 | bytes 15303816 | solution.py:77
  1039.9 24.2 %conditional.33 = (bf16[2,64,1024]{2,1,0:T(8,128)(2,1)S(1)}, f32[2,64,1024]{2,1,0:T(8,128)}, bf16[2,64,1024]{2,1,0:T(8,128)(2,1)}, bf16[2,64,4096]{2,1,0:T(8,128...) conditional(s32[]{:T(128)} %convert_element_type.520, ...), branch_computations={%region_97.98_spmd, %region_98.110_spmd} | conditional | flops 2460080896 | bytes 57686212 | solution.py:77
  1043.0 10.7 convert_reduce_fusion.15
  1090.3 21.1 %conditional.34 = (bf16[2,1024,64]{1,2,0:T(8,128)(2,1)S(1)}, bf16[2,1024,64]{1,2,0:T(8,128)(2,1)S(1)}, bf16[2,1024,64]{1,2,0:T(8,128)(2,1)S(1)}) conditional(s32[]{:T(128)} %convert_element_type.520, () %tuple.525, (bf16[2,2,1024,64]{2,3,1,0:T(8,128)(2,1)}, s32[]{:T(128)}, bf16[2,2,1024,64]{2,3,1,0:T(8,128)(2,1)}, ...), branch_computations={%region_110.111_spmd, %region_111.113_spmd} | conditional | flops 1367865344 | bytes 91810376 | solution.py:77
  1147.4 8.0 reshape_reshape.11
  1156.2 7.9 reshape_reshape.12
  1172.5 17.7 %conditional.35 = (bf16[2,64,1024]{2,1,0:T(8,128)(2,1)S(1)}, f32[1,16,64]{2,1,0:T(8,128)S(1)}, f32[1,16,64]{2,1,0:T(8,128)S(1)}, f32[1,16,64]{2,1,0:T(8,128)S(1)}, f32[1,16,64]{2,1,0:T(8,128)S(1)}) conditional(s32[]{:T(128)} %convert_element_type.520, () %tuple.524, (bf16[2,64,16,64]{1,2,3,0:T(8,128)(2,1)}, bf16[1024,3072]{1,0:T(8,128)(2,1)}, ...), branch_computations={%region_113.114_spmd, %region_114.123_spmd} | conditional | flops 811070080 | bytes 15268404 | solution.py:77
  1216.4 8.6 copy.297
  1241.8 8.3 constant_dynamic-update-slice_fusion.12
  1254.3 20.6 %pad.130 = bf16[16,787456]{1,0:T(8,128)(2,1)} pad(bf16[16,787328]{1,0:T(8,128)(2,1)} %constant_dynamic-update-slice_fusion.10, bf16[]{:T(256)} %constant.2191.clone.1), padding=0_0x0_128 | pad | bytes 50393088 | tf_op jit(solution)/shard_map/jit(_pad)/pad | solution.py:52
  1274.8 29.6 %reshape.3348 = bf16[98432,128]{1,0:T(8,128)(2,1)} reshape(bf16[16,787456]{1,0:T(8,128)(2,1)} %pad.130) | data formatting | bytes 50397184 | tf_op jit(solution)/shard_map/reshape | solution.py:52
  1306.3 320.6 %all-reduce.7.cloned.1.call-done = bf16[98432,128]{1,0:T(8,128)(2,1)} async-done(((bf16[98432,128]{1,0:T(8,128)(2,1)}), bf16[98432,128]{1,0:T(8,128)(2,1)}) %all-reduce.7.cloned.1.call-update) | async-done | bytes 25198608
  1640.1 7.2 all-reduce.2
  1650.7 35.8 %all-reduce.9.cloned.1.call-done = (bf16[1,64,3072]{2,1,0:T(8,128)(2,1)}, bf16[1,64,1024]{2,1,0:T(8,128)(2,1)}, bf16[1,64,4096]{2,1,0:T(8,128)(2,1)}, bf16[1,256,1024]{2,1,0:T(8,128)(2,1)}) async-done(((bf16[1,64,3072]{2,1,0:T(8,128)(2,1)}, bf16[1,64,1024]{2,1,0:T(8,128)(2,1)}, bf16[1,64,4096]{2,1,0:T(8,128)(2,1)}, bf16[1,256,1024]{2,1,0:T(8,128)(2,1)}), (bf16[1,64,3072]{2,1,0:T(8,128)(2,1)}, ...) | async-done | bytes 1572880 | tf_op jit(solution)/shard_map/psum | solution.py:566
  (803 shorter events, 926.3 us)
Async XLA Ops:
  7.2 118.5 %all-gather.4.cloned.1.call-start = ((), (), s32[]{:S(2)}) async-start(), calls=%async_computation.24 | async-start | bytes 17825792 | tf_op jit(solution)/shard_map/all_gather | solution.py:22
  9.7 197.3 %all-gather.6.cloned.1.call-start = ((), (), s32[]{:S(2)}) async-start(), calls=%async_computation.25 | async-start | bytes 10027008 | tf_op jit(solution)/shard_map/all_gather | solution.py:28
  139.6 16.0 all-to-all-start
  155.6 76.2 %all-to-all-start.1 = ((bf16[16,2,4096]{2,1,0:T(2,128)(2,1)}), bf16[16,2,4096]{2,1,0:T(2,128)(2,1)S(1)}, u32[]{:S(2)}, u32[]{:S(2)}) async-start(bf16[16,2,4096]{2,1,0:T(2,128)(2,1)} %reshape.3438), calls=%async_computation.1 | async-start | bytes 524288 | tf_op jit(solution)/shard_map/all_to_all | solution.py:434
  231.8 12.0 all-to-all-start.2
  270.6 18.2 %all-to-all-start.3 = ((bf16[16,2,4096]{2,1,0:T(2,128)(2,1)}), bf16[16,2,4096]{2,1,0:T(2,128)(2,1)}, u32[]{:S(2)}, u32[]{:S(2)}) async-start(bf16[16,2,4096]{2,1,0:T(2,128)(2,1)} %reshape.3442), calls=%async_computation.3 | async-start | bytes 524288 | tf_op jit(solution)/shard_map/all_to_all | solution.py:440
  310.0 19.9 %collective-permute-start = (bf16[2,64,1024]{2,1,0:T(8,128)(2,1)}, bf16[2,64,1024]{2,1,0:T(8,128)(2,1)S(1)}, u32[]{:S(2)}, u32[]{:S(2)}) collective-permute-start(bf16[2,64,1024]{2,1,0:T(8,128)(2,1)} %get-tuple-element.1798), channel_id=1, source_target_pairs={{0,64},{1,65},{2,66},{3,67},{4,68},{5,69},{6,70},{7,71},{8,72},{9,... | collective-permute-start | bytes 786440 | tf_op jit(solution)/shard_map/ppermute | solution.py:39
  344.1 20.8 %all-to-all-start.4 = ((bf16[16,2,4096]{2,1,0:T(2,128)(2,1)}), bf16[16,2,4096]{2,1,0:T(2,128)(2,1)}, u32[]{:S(2)}, u32[]{:S(2)}) async-start(bf16[16,2,4096]{2,1,0:T(2,128)(2,1)} %reshape.3444), calls=%async_computation.4 | async-start | bytes 524288 | tf_op jit(solution)/shard_map/all_to_all | solution.py:433
  364.8 14.5 all-to-all-start.5
  379.3 25.9 %all-to-all-start.6 = ((bf16[16,2,4096]{2,1,0:T(2,128)(2,1)}), bf16[16,2,4096]{2,1,0:T(2,128)(2,1)}, u32[]{:S(2)}, u32[]{:S(2)}) async-start(bf16[16,2,4096]{2,1,0:T(2,128)(2,1)} %reshape.3448), calls=%async_computation.6 | async-start | bytes 524288 | tf_op jit(solution)/shard_map/all_to_all | solution.py:435
  433.8 23.7 %all-to-all-start.7 = ((bf16[16,2,4096]{2,1,0:T(2,128)(2,1)}), bf16[16,2,4096]{2,1,0:T(2,128)(2,1)}, u32[]{:S(2)}, u32[]{:S(2)}) async-start(bf16[16,2,4096]{2,1,0:T(2,128)(2,1)} %reshape.3450), calls=%async_computation.7 | async-start | bytes 524288 | tf_op jit(solution)/shard_map/all_to_all | solution.py:440
  485.2 24.3 %collective-permute-start.1 = (bf16[2,64,1024]{2,1,0:T(8,128)(2,1)}, bf16[2,64,1024]{2,1,0:T(8,128)(2,1)}, u32[]{:S(2)}, u32[]{:S(2)}) collective-permute-start(bf16[2,64,1024]{2,1,0:T(8,128)(2,1)} %get-tuple-element.1803), channel_id=1, source_target_pairs={{0,64},{1,65},{2,66},{3,67},{4,68},{5,69},{6,70},{7,71},{8,72},{9,... | collective-permute-start | bytes 786440 | tf_op jit(solution)/shard_map/ppermute | solution.py:39
  519.4 16.4 all-to-all-start.8
  535.8 14.3 all-to-all-start.9
  550.1 23.0 %all-to-all-start.10 = ((bf16[16,2,4096]{2,1,0:T(2,128)(2,1)}), bf16[16,2,4096]{2,1,0:T(2,128)(2,1)}, u32[]{:S(2)}, u32[]{:S(2)}) async-start(bf16[16,2,4096]{2,1,0:T(2,128)(2,1)} %reshape.3456), calls=%async_computation.10 | async-start | bytes 524288 | tf_op jit(solution)/shard_map/all_to_all | solution.py:435
  582.3 23.0 %all-to-all-start.11 = ((bf16[16,2,4096]{2,1,0:T(2,128)(2,1)}), bf16[16,2,4096]{2,1,0:T(2,128)(2,1)}, u32[]{:S(2)}, u32[]{:S(2)}) async-start(bf16[16,2,4096]{2,1,0:T(2,128)(2,1)} %reshape.3458), calls=%async_computation.11 | async-start | bytes 524288 | tf_op jit(solution)/shard_map/all_to_all | solution.py:440
  638.0 14.2 all-to-all-start.12
  662.0 18.8 %all-to-all-start.13 = ((bf16[16,2,4096]{2,1,0:T(2,128)(2,1)}), bf16[16,2,4096]{2,1,0:T(2,128)(2,1)S(1)}, u32[]{:S(2)}, u32[]{:S(2)}) async-start(bf16[16,2,4096]{2,1,0:T(2,128)(2,1)} %reshape.3462), calls=%async_computation.13 | async-start | bytes 524288 | tf_op jit(solution)/shard_map/all_to_all | solution.py:489
  680.8 14.7 all-to-all-start.14
  695.5 18.5 %all-to-all-start.15 = ((bf16[16,2,4096]{2,1,0:T(2,128)(2,1)}), bf16[16,2,4096]{2,1,0:T(2,128)(2,1)}, u32[]{:S(2)}, u32[]{:S(2)}) async-start(bf16[16,2,4096]{2,1,0:T(2,128)(2,1)} %reshape.3466), calls=%async_computation.15 | async-start | bytes 524288 | tf_op jit(solution)/shard_map/all_to_all | solution.py:493
  721.6 117.0 %collective-permute-start.2 = (bf16[2,64,1024]{2,1,0:T(8,128)(2,1)}, bf16[2,64,1024]{2,1,0:T(8,128)(2,1)}, u32[]{:S(2)}, u32[]{:S(2)}) collective-permute-start(bf16[2,64,1024]{2,1,0:T(8,128)(2,1)} %get-tuple-element.1829), channel_id=1, source_target_pairs={{64,0},{65,1},{66,2},{67,3},{68,4},{69,5},{70,6},{71,7},{72,8},{73... | collective-permute-start | bytes 786440 | tf_op jit(solution)/shard_map/ppermute | solution.py:39
  879.4 21.3 %all-to-all-start.16 = ((bf16[16,2,4096]{2,1,0:T(2,128)(2,1)}), bf16[16,2,4096]{2,1,0:T(2,128)(2,1)}, u32[]{:S(2)}, u32[]{:S(2)}) async-start(bf16[16,2,4096]{2,1,0:T(2,128)(2,1)} %reshape.3468), calls=%async_computation.16 | async-start | bytes 524288 | tf_op jit(solution)/shard_map/all_to_all | solution.py:478
  935.5 14.4 all-to-all-start.18
  949.9 15.7 all-to-all-start.19
  965.6 24.5 %all-to-all-start.17 = ((bf16[16,2,4096]{2,1,0:T(2,128)(2,1)}), bf16[16,2,4096]{2,1,0:T(2,128)(2,1)}, u32[]{:S(2)}, u32[]{:S(2)}) async-start(bf16[16,2,4096]{2,1,0:T(2,128)(2,1)} %reshape.3470), calls=%async_computation.17 | async-start | bytes 524288 | tf_op jit(solution)/shard_map/all_to_all | solution.py:489
  1023.1 15.9 collective-permute-start.3
  1065.7 23.7 %all-to-all-start.20 = ((bf16[16,2,4096]{2,1,0:T(2,128)(2,1)}), bf16[16,2,4096]{2,1,0:T(2,128)(2,1)S(1)}, u32[]{:S(2)}, u32[]{:S(2)}) async-start(bf16[16,2,4096]{2,1,0:T(2,128)(2,1)} %reshape.3476), calls=%async_computation.20 | async-start | bytes 524288 | tf_op jit(solution)/shard_map/all_to_all | solution.py:478
  1112.9 14.2 all-to-all-start.22
  1127.1 11.3 all-to-all-start.23
  1138.4 30.4 %all-to-all-start.21 = ((bf16[16,2,4096]{2,1,0:T(2,128)(2,1)}), bf16[16,2,4096]{2,1,0:T(2,128)(2,1)}, u32[]{:S(2)}, u32[]{:S(2)}) async-start(bf16[16,2,4096]{2,1,0:T(2,128)(2,1)} %reshape.3478), calls=%async_computation.21 | async-start | bytes 524288 | tf_op jit(solution)/shard_map/all_to_all | solution.py:489
  1142.6 484.3 %all-reduce.7.cloned.1.call-start = ((), (), s32[]{:S(2)}) async-start(), calls=%async_computation.26 | async-start | bytes 50397184
  1304.4 382.1 %all-reduce.9.cloned.1.call-start = ((), (), s32[]{:S(2)}) async-start(), calls=%async_computation.27 | async-start | bytes 3145728 | tf_op jit(solution)/shard_map/psum | solution.py:566
  (98 other events, 843.1 us)
Sparse Core Ops, SparseCore 0:
  10.8 114.8 all-gather.3
  128.4 78.6 all-gather.5
  1304.6 322.2 all-reduce.6
  1634.2 52.2 all-reduce.8
where the time goes:
time: 1720 us; the launch traced here: 1700 us
  waiting for transfers between devices  611 us (36%)
  local copies, waits for them, and re-layouts  530 us (31%)
  other arithmetic  198 us (12%)
  matrix products  158 us (9%)
  starting transfers between devices  155 us (9%)
  blocking collectives  28.6 us (2%)
    unnamed x5, waiting for transfers between devices  321 us
    scatter x53, other arithmetic, place(): return stored_all.at[batch_slot].set(jnp.where(active, new_leaf, previous))  112 us
    unnamed x217, local copies, waits for them, and re-layouts  108 us
    ppermute x4, waiting for transfers between devices, shifted(): return lax.ppermute(value, axis, pairs)  106 us
    all_gather x1, waiting for transfers between devices, in_one_piece(): lax.all_gather(both, axis, axis=dim, tiled=True)  86.4 us
    another operation x76, local copies, waits for them, and re-layouts  81.8 us
    all_gather x1, waiting for transfers between devices, side_by_side(): lax.all_gather(both, axis, axis=dim, tiled=True)  46.7 us
    dynamic_slice x28, local copies, waits for them, and re-layouts, place(): previous = stored_all[batch_slot]  37.5 us
  transfers between devices with their start and end apart: 32, of which 10 were waited for; matrix products, arithmetic and copies ran while one was open for 21% of the time, Pallas kernels for 0%

commit v1 on v0

v1 whole, which is shorter than its diff:
```python
import jax
import jax.numpy as jnp
from jax import lax
from jax.experimental import pallas as pl
from jax.experimental.pallas import tpu as pltpu
from jax.sharding import Mesh, PartitionSpec as P

HEAD_DIM = 64
IMG_MB = 2
PAIR = 2 * HEAD_DIM
EPSILON = 1e-06

FSDP = ("z", "yh", "yl")
REP = ("xhi", "core")
bf16 = jnp.bfloat16
f32 = jnp.float32


def dot(a, b, dims):
    return lax.dot_general(a, b, (dims, ((), ())), preferred_element_type=f32)


def mm(a, b):
    return dot(a, b, ((1,), (0,)))


def mm_t(a, b):
    return dot(a, b, ((1,), (1,)))


def t_mm(a, b):
    return dot(a, b, ((0,), (0,)))


def swap(value, axis):
    return lax.ppermute(value, axis, [(0, 1), (1, 0)])


def attend_kernel(q_ref, own_ref, mate_ref, near_ref, far_ref, out_ref, log_ref):
    rows = q_ref.shape[0]
    both = [r[...] for r in (own_ref, mate_ref, near_ref, far_ref)]
    keys = jnp.concatenate([b[:, :PAIR] for b in both], axis=0)
    values = jnp.concatenate([b[:, PAIR:] for b in both], axis=0)
    queries = q_ref[...] * jnp.asarray(HEAD_DIM**-0.5, bf16)
    lane = lax.broadcasted_iota(jnp.int32, (rows, PAIR), 1)
    outs = []
    for head in range(2):
        mine = (lane >= head * HEAD_DIM) & (lane < (head + 1) * HEAD_DIM)
        picked = jnp.where(mine, queries, jnp.zeros_like(queries))
        scores = mm_t(keys, picked)
        top = jnp.max(scores, axis=0, keepdims=True)
        raised = jnp.exp(scores - top)
        total = jnp.sum(raised, axis=0, keepdims=True)
        out = t_mm(values, raised.astype(bf16))
        outs.append(out * (1.0 / total))
        log_ref[0, head : head + 1, :] = top + jnp.log(total)
    row = lax.broadcasted_iota(jnp.int32, (PAIR, rows), 0)
    joined = jnp.where(row < HEAD_DIM, outs[0], outs[1])
    out_ref[...] = joined.T.astype(bf16)


def attend_back_kernel(
    q_ref, own_ref, mate_ref, near_ref, far_ref, grad_ref, log_ref, dq_ref, *dkv_refs
):
    rows = q_ref.shape[0]
    both = [r[...] for r in (own_ref, mate_ref, near_ref, far_ref)]
    keys = jnp.concatenate([b[:, :PAIR] for b in both], axis=0)
    values = jnp.concatenate([b[:, PAIR:] for b in both], axis=0)
    queries = q_ref[...] * jnp.asarray(HEAD_DIM**-0.5, bf16)
    grads = grad_ref[...]
    lane = lax.broadcasted_iota(jnp.int32, (rows, PAIR), 1)
    dqs, dk, dv = [], None, None
    for head in range(2):
        mine = (lane >= head * HEAD_DIM) & (lane < (head + 1) * HEAD_DIM)
        picked = jnp.where(mine, queries, jnp.zeros_like(queries))
        grad = jnp.where(mine, grads, jnp.zeros_like(grads))
        scores = mm_t(keys, picked)
        weighting = jnp.exp(scores - log_ref[0, head : head + 1, :])
        grad_weighting = mm_t(values, grad)
        row_term = jnp.sum(grad_weighting * weighting, axis=0, keepdims=True)
        grad_scores = (weighting * (grad_weighting - row_term)).astype(bf16)
        dqs.append(t_mm(keys, grad_scores))
        k_part = mm(grad_scores, picked)
        v_part = mm(weighting.astype(bf16), grad)
        dk = k_part if dk is None else dk + k_part
        dv = v_part if dv is None else dv + v_part
    row = lax.broadcasted_iota(jnp.int32, (PAIR, rows), 0)
    joined = jnp.where(row < HEAD_DIM, dqs[0], dqs[1]) * (HEAD_DIM**-0.5)
    dq_ref[...] = joined.T.astype(bf16)
    for i, ref in enumerate(dkv_refs):
        ref[:, :PAIR] = dk[i * rows : (i + 1) * rows].astype(bf16)
        ref[:, PAIR:] = dv[i * rows : (i + 1) * rows].astype(bf16)


def pair_specs(rows, pairs):
    half = pairs // 2
    q_spec = pl.BlockSpec((rows, PAIR), lambda i: (0, i))
    kv_spec = pl.BlockSpec((rows, 2 * PAIR), lambda i: (0, i))
    kv_swapped = pl.BlockSpec((rows, 2 * PAIR), lambda i: (0, (i + half) % pairs))
    log_spec = pl.BlockSpec((1, 2, rows), lambda i: (i, 0, 0))
    return q_spec, [kv_spec, kv_swapped, kv_spec, kv_swapped], log_spec


def attend(queries, blocks):
    rows, width = queries.shape
    pairs = width // PAIR
    q_spec, kv_specs, log_spec = pair_specs(rows, pairs)
    return pl.pallas_call(
        attend_kernel,
        grid=(pairs,),
        in_specs=[q_spec] + kv_specs,
        out_specs=[q_spec, log_spec],
        out_shape=[
            jax.ShapeDtypeStruct((rows, width), bf16),
            jax.ShapeDtypeStruct((pairs, 2, rows), f32),
        ],
        compiler_params=pltpu.CompilerParams(vmem_limit_bytes=40 * 2**20),
        name="attend",
    )(queries, *blocks)


def attend_back(queries, blocks, grad, log_total):
    rows, width = queries.shape
    pairs = width // PAIR
    q_spec, kv_specs, log_spec = pair_specs(rows, pairs)
    return pl.pallas_call(
        attend_back_kernel,
        grid=(pairs,),
        in_specs=[q_spec] + kv_specs + [q_spec, log_spec],
        out_specs=[q_spec] + kv_specs,
        out_shape=[jax.ShapeDtypeStruct((rows, width), bf16)]
        + [jax.ShapeDtypeStruct((rows, 2 * width), bf16)] * 4,
        compiler_params=pltpu.CompilerParams(vmem_limit_bytes=40 * 2**20),
        name="attend_back",
    )(queries, *blocks, grad, log_total)


def to_images(tokens):
    count, rows, width = tokens.shape
    mixed = lax.all_to_all(tokens, "z", split_axis=0, concat_axis=0, tiled=True)
    mixed = mixed.reshape(count * rows, width)
    return lax.ppermute(mixed, ("yh", "core"), [(0, 0), (1, 2), (2, 1), (3, 3)])


def from_images(tokens, count):
    rows, width = tokens.shape
    mixed = lax.ppermute(tokens, ("yh", "core"), [(0, 0), (1, 2), (2, 1), (3, 3)])
    mixed = mixed.reshape(count, rows // count, width)
    return lax.all_to_all(mixed, "z", split_axis=0, concat_axis=0, tiled=True)


def group_blocks(key_value):
    mate = swap(key_value, "core")
    near = swap(key_value, "yl")
    far = swap(near, "core")
    return (key_value, mate, near, far)


def group_sum(own, mate, near, far):
    mate, far = swap(mate, "core"), swap(far, "core")
    sent = (near.astype(f32) + far.astype(f32)).astype(bf16)
    kept = own.astype(f32) + mate.astype(f32)
    return (kept + swap(sent, "yl").astype(f32)).astype(bf16)


def normal_part(values):
    mean = jnp.mean(values, axis=-1, keepdims=True)
    centred = values - mean
    factor = lax.rsqrt(jnp.mean(centred * centred, axis=-1, keepdims=True) + EPSILON)
    return centred * factor, factor


def norm_back(grad, normal, factor, gain):
    e = grad * gain
    inner = jnp.mean(e * normal, axis=-1, keepdims=True)
    return factor * (e - jnp.mean(e, axis=-1, keepdims=True) - normal * inner)


def forward(tokens, w):
    inputs = tokens.astype(f32)
    normed_one = (normal_part(inputs)[0] * w["gain"][0] + w["shift"][0]).astype(bf16)
    width = tokens.shape[1]
    half = width // 2
    joined = [
        (mm(normed_one, part) + bias).astype(bf16) for part, bias in zip(w["qkv"], w["qkv_bias"])
    ]
    queries = jnp.concatenate([j[:, :half] for j in joined], axis=1)
    blocks = group_blocks(jnp.concatenate([j[:, half:] for j in joined], axis=1))
    attended, log_total = attend(queries, blocks)
    branch = mm(attended, w["proj"]) + w["out_bias"][0]
    middle = inputs + w["scale"][0] * branch
    normed_two = (normal_part(middle)[0] * w["gain"][1] + w["shift"][1]).astype(bf16)
    activated, slope, branch_two = [], [], w["out_bias"][1]
    for up, bias, down in zip(w["fc1"], w["fc1_bias"], w["fc2"]):
        before = mm(normed_two, up) + bias
        phi = 0.5 * (1.0 + lax.erf(before * (0.5**0.5)))
        density = jnp.exp(-0.5 * before * before) * 0.3989422804014327
        active = (before * phi).astype(bf16)
        activated.append(active)
        slope.append((phi + before * density).astype(bf16))
        branch_two = branch_two + mm(active, down)
    result = (middle + w["scale"][1] * branch_two).astype(bf16)
    kept = dict(
        inputs=inputs,
        normed_one=normed_one,
        queries=queries,
        blocks=blocks,
        attended=attended,
        log_total=log_total,
        branch=branch,
        middle=middle,
        normed_two=normed_two,
        activated=activated,
        slope=slope,
        branch_two=branch_two,
    )
    return result, kept


def backward(grad_out, kept, w):
    grad_branch_two = (w["scale"][1] * grad_out).astype(bf16)
    grad_before = []
    grad_normed_two = 0.0
    for up, down, slope in zip(w["fc1"], w["fc2"], kept["slope"]):
        part = (mm_t(grad_branch_two, down) * slope.astype(f32)).astype(bf16)
        grad_before.append(part)
        grad_normed_two = grad_normed_two + mm_t(part, up)
    normal_two, factor_two = normal_part(kept["middle"])
    grad_middle = grad_out + norm_back(grad_normed_two, normal_two, factor_two, w["gain"][1])
    grad_branch = (w["scale"][0] * grad_middle).astype(bf16)
    grad_attended = mm_t(grad_branch, w["proj"]).astype(bf16)
    parts = attend_back(kept["queries"], kept["blocks"], grad_attended, kept["log_total"])
    grad_queries = parts[0]
    grad_key_value = group_sum(*parts[1:])
    width = grad_queries.shape[1]
    half = width // 2
    grad_joined = [
        jnp.concatenate(
            [
                grad_queries[:, i * half : (i + 1) * half],
                grad_key_value[:, i * width : (i + 1) * width],
            ],
            axis=1,
        )
        for i in range(2)
    ]
    grad_normed_one = sum(mm_t(g, part) for g, part in zip(grad_joined, w["qkv"]))
    normal_one, factor_one = normal_part(kept["inputs"])
    grad_inputs = grad_middle + norm_back(grad_normed_one, normal_one, factor_one, w["gain"][0])
    total = lambda a: jnp.sum(a.astype(f32), axis=0)
    joined_sums = [total(g) for g in grad_joined]
    vectors = dict(
        gain=(total(grad_normed_one * normal_one), total(grad_normed_two * normal_two)),
        shift=(total(grad_normed_one), total(grad_normed_two)),
        out_bias=(total(grad_branch), total(grad_branch_two)),
        scale=(total(grad_middle * kept["branch"]), total(grad_out * kept["branch_two"])),
        joined=joined_sums,
        fc1_bias=[total(g) for g in grad_before],
    )
    outer = dict(
        qkv=(kept["normed_one"], grad_joined),
        proj=(kept["attended"], grad_branch),
        fc1=(kept["normed_two"], grad_before),
        fc2=(kept["activated"], grad_branch_two),
    )
    return grad_inputs.astype(bf16), vectors, outer


def ordered(core, mine, other):
    return jnp.where(core == 0, mine, other), jnp.where(core == 0, other, mine)


def per_device(
    patch_tokens,
    out_grad,
    batch_counts,
    norm_gain,
    norm_bias,
    qkv_weight,
    qv_bias,
    proj_weight,
    fc1_weight,
    fc1_bias,
    fc2_weight,
    out_bias,
    layer_scale,
):
    section = lax.axis_index("section")
    core = lax.axis_index("core")
    shards = lax.axis_size(FSDP)
    images, rows, width = patch_tokens.shape
    half = width // 2
    own = width // shards
    hidden = fc2_weight.shape[1]
    mid = hidden // 2
    groups = half // PAIR
    pick = lambda a, i, axis: lax.dynamic_index_in_dim(a, i, axis, keepdims=False)
    gather = lambda a: lax.all_gather(a, FSDP, axis=0, tiled=True)

    q, k, v = (qkv_weight[0][:, i * width : (i + 1) * width] for i in range(3))
    q_mine = pick(q.reshape(own, 2, half), core, 1)
    kv = jnp.stack([k.reshape(own, 2, groups, PAIR), v.reshape(own, 2, groups, PAIR)], axis=3)
    kv_mine = pick(kv, core, 1).reshape(own, width)
    vectors = jnp.concatenate(
        [a[0] for a in (norm_gain, norm_bias, qv_bias, out_bias, layer_scale)]
        + [fc1_bias[0].reshape(own, hidden // own).T],
        axis=0,
    ).T
    count = vectors.shape[1]
    vectors = jnp.pad(vectors, ((0, 0), (0, 128 - count)))
    first = gather(jnp.concatenate([q_mine, kv_mine, vectors], axis=1))
    qkv_mine = first[:, : half + width]
    vectors = first[:, half + width : half + width + count].T.astype(f32)
    fc1_b = vectors[10:].T.reshape(shards, 2, mid // 1)
    fc1_mine = pick(fc1_weight[0].reshape(own, shards, 2, mid), core, 2).reshape(own, shards * mid)
    fc2_mine = pick(fc2_weight[0].reshape(2, mid, width), core, 0)
    proj_mine = pick(proj_weight[0].reshape(2, own // 2, width), core, 0)
    proj_half = gather(proj_mine)
    fc1_half = gather(fc1_mine)
    fc2_half = gather(fc2_mine)
    lower, upper = ordered(core, proj_half, swap(proj_half, "core"))
    proj = jnp.stack(
        [lower.reshape(shards, own // 2, width), upper.reshape(shards, own // 2, width)], axis=1
    ).reshape(2, half, width)
    proj = jnp.concatenate([pick(proj, core, 0), pick(proj, 1 - core, 0)], axis=0)

    def halves(vector):
        pair = vector.reshape(2, half)
        return pick(pair, core, 0), pick(pair, 1 - core, 0)

    def qkv_bias(q_half, v_half):
        v_part = v_half.reshape(groups, 1, PAIR)
        kv_part = jnp.concatenate([jnp.zeros_like(v_part), v_part], axis=1).reshape(width)
        return jnp.concatenate([q_half, kv_part])

    w = dict(
        gain=vectors[0:2],
        shift=vectors[2:4],
        out_bias=vectors[6:8],
        scale=vectors[8:10],
        qkv=(qkv_mine, swap(qkv_mine, "core")),
        qkv_bias=[qkv_bias(a, b) for a, b in zip(halves(vectors[4]), halves(vectors[5]))],
        proj=proj,
        fc1=(fc1_half, swap(fc1_half, "core")),
        fc1_bias=(pick(fc1_b, core, 1).reshape(-1), pick(fc1_b, 1 - core, 1).reshape(-1)),
        fc2=(fc2_half, swap(fc2_half, "core")),
    )

    live = (
        jnp.arange(images) % IMG_MB < jnp.repeat(batch_counts[0], IMG_MB)
    ).astype(bf16)
    first_tokens = to_images(patch_tokens)
    last_grad = to_images(out_grad * live[:, None, None])

    sent, _ = forward(first_tokens, w)
    passed = lax.ppermute(sent, "section", [(0, 1)])
    tokens = jnp.where(section == 0, first_tokens, passed)
    result, kept = forward(tokens, w)
    block_out = from_images(result, images)

    sent, _, _ = backward(last_grad.astype(f32), kept, w)
    passed = lax.ppermute(sent, "section", [(1, 0)])
    grad_out = jnp.where(section == 1, last_grad, passed).astype(f32)
    grad_inputs, sums, outer = backward(grad_out, kept, w)
    in_grad = from_images(grad_inputs, images)

    def core_sum(mine, other):
        return (mine + swap(other.astype(bf16), "core").astype(f32)).astype(bf16)

    def scatter(a):
        return lax.psum_scatter(a, FSDP, scatter_dimension=0, tiled=True)

    def natural(pair):
        return jnp.concatenate(ordered(core, *pair))

    joined = sums["joined"]
    v_sum = lambda a: a[half:].reshape(groups, 2, PAIR)[:, 1].reshape(half)
    fc1_sum = jnp.stack(
        ordered(core, *(s.reshape(shards, mid) for s in sums["fc1_bias"])), axis=1
    ).reshape(width, hidden // own)
    vector_grads = jnp.concatenate(
        [
            jnp.stack(
                [
                    *sums["gain"],
                    *sums["shift"],
                    natural([j[:half] for j in joined]),
                    natural([v_sum(j) for j in joined]),
                    *sums["out_bias"],
                    *sums["scale"],
                ],
                axis=1,
            ),
            fc1_sum,
        ],
        axis=1,
    )
    vector_grads = jnp.pad(vector_grads, ((0, 0), (0, 128 - count)))

    a2, du = outer["fc1"]
    z, e2 = outer["fc2"]
    fc2_grad = scatter(core_sum(t_mm(z[0], e2), t_mm(z[1], e2)))
    fc1_grad = scatter(core_sum(t_mm(a2, du[0]), t_mm(a2, du[1])))
    o, e1 = outer["proj"]
    proj_full = t_mm(o, e1).astype(bf16).reshape(2, half, width)
    proj_full = jnp.concatenate(ordered(core, proj_full[0], proj_full[1]))
    proj_full = proj_full.reshape(shards, 2, own // 2, width)
    proj_grad = scatter(
        core_sum(pick(proj_full, core, 1).astype(f32), pick(proj_full, 1 - core, 1)).reshape(
            half, width
        )
    )
    a1, dj = outer["qkv"]
    vec = [vector_grads, vector_grads]
    qkv_grad = scatter(
        core_sum(*(jnp.concatenate([t_mm(a1, d), g], axis=1) for d, g in zip(dj, vec)))
    )

    parts = [qkv_grad, fc1_grad, proj_grad, fc2_grad]
    parts = [
        (a.astype(f32) + swap(a, "xhi").astype(f32)).astype(bf16) for a in parts
    ]
    others = [swap(a, "core") for a in parts]
    qkv_pair, fc1_pair, proj_pair, fc2_pair = (
        ordered(core, a.astype(f32), b.astype(f32)) for a, b in zip(parts, others)
    )
    vec_grad = parts[0][:, half + width : half + width + count].T.astype(f32)
    q_grad = jnp.concatenate([p[:, :half] for p in qkv_pair], axis=1)
    kv_grads = [p[:, half : half + width].reshape(own, groups, 2, PAIR) for p in qkv_pair]
    k_grad, v_grad = (
        jnp.concatenate([p[:, :, i].reshape(own, half) for p in kv_grads], axis=1)
        for i in range(2)
    )
    qkv_out = jnp.concatenate([q_grad, k_grad, v_grad], axis=1)
    fc1_out = jnp.stack([p.reshape(own, shards, mid) for p in fc1_pair], axis=2).reshape(
        own, 2 * shards * mid
    )
    fc2_out = jnp.concatenate(fc2_pair, axis=0)
    proj_out = jnp.concatenate(proj_pair, axis=0)
    return (
        block_out[None],
        in_grad[None],
        vec_grad[0:2][None],
        vec_grad[2:4][None],
        qkv_out[None],
        vec_grad[4:6][None],
        proj_out[None],
        fc1_out[None],
        vec_grad[10:].T.reshape(1, hidden),
        fc2_out[None],
        vec_grad[6:8][None],
        vec_grad[8:10][None],
    )


def solution(mesh):
    sections, fsdp, rep = mesh.devices.shape
    inner = Mesh(
        mesh.devices.reshape(sections, fsdp // 4, 2, 2, rep // 2, 2),
        ("section",) + FSDP + REP,
    )
    weight = P("section", FSDP, None)
    vector = P("section", None, FSDP)
    tokens = P(REP, FSDP, None)
    both = P("section", REP, FSDP, None)
    return jax.shard_map(
        per_device,
        mesh=inner,
        in_specs=(
            tokens,
            tokens,
            P(REP, None),
            vector,
            vector,
            weight,
            vector,
            weight,
            weight,
            P("section", FSDP),
            weight,
            vector,
            vector,
        ),
        out_specs=(
            both,
            both,
            vector,
            vector,
            weight,
            vector,
            weight,
            weight,
            P("section", FSDP),
            weight,
            vector,
            vector,
        ),
        check_vma=False,
    )
```

time: 1720 us -> 893 us (0.52)
  local copies, waits for them, and re-layouts: 530 us -> 60 us
  other arithmetic: 198 us -> 31.5 us
  waiting for transfers between devices: 611 us -> 515 us
  starting transfers between devices: 155 us -> 61.3 us
  Pallas kernels: 0 us -> 68.8 us
  matrix products: 158 us -> 96.4 us
    unnamed x5 -> x8, waiting for transfers between devices: 321 us -> 0.13 us
    reduce_scatter x0 -> x4, waiting for transfers between devices: none -> 225 us  [scatter(): return lax.psum_scatter(a, FSDP, scatter_dimension=0, tiled=True)]
    all_to_all x24 -> x1, starting transfers between devices: 148 us -> 3.47 us  [from_images(): return lax.all_to_all(mixed, 'z', split_axis=0, concat_axis=0, tiled=True)]
    all_to_all x68 -> x0, local copies, waits for them, and re-layouts: 116 us -> none  [the longest x9 19.4 us: per_device(): lax.all_to_all(value_part, 'fsdp', split_axis=2, concat_axis=1, tiled=True)]
    scatter x53 -> x0, other arithmetic: 112 us -> none  [place(): return stored_all.at[batch_slot].set(jnp.where(active, new_leaf, previous))]
    another operation x106 -> x20, local copies, waits for them, and re-layouts: 112 us -> 11.6 us  [the longest x10 7.95 us: per_device(): jnp.stack([*sums['gain'], *sums['shift'], natural([j[:half] for j in join...]
    unnamed x217 -> x145, local copies, waits for them, and re-layouts: 108 us -> 16.7 us
    pallas_call x0 -> x4, Pallas kernels: none -> 68.8 us  [the longest x2 38.1 us: attend_back(): pl.pallas_call(attend_back_kernel, grid=(pairs,), in_specs=[q_spec] + kv_...]
  transfers between devices with their start and end apart: 32 -> 43, of which waited for: 10 -> 25; matrix products, arithmetic and copies ran while one was open for 21% -> 10% of each run, Pallas kernels for 0% -> 3%
where the time goes in v1:
time: 893 us; the launch traced here: 883 us
  waiting for transfers between devices  515 us (58%)
  matrix products  96.4 us (11%)
  Pallas kernels  68.8 us (8%)
  starting transfers between devices  61.3 us (7%)
  local copies, waits for them, and re-layouts  60 us (7%)
  blocking collectives  34.6 us (4%)
  other arithmetic  31.5 us (4%)
  between operations  16.1 us (2%)
    reduce_scatter x4, waiting for transfers between devices, scatter(): return lax.psum_scatter(a, FSDP, scatter_dimension=0, tiled=True)  225 us
    all_gather x4, waiting for transfers between devices, per_device(): gather = lambda a: lax.all_gather(a, FSDP, axis=0, tiled=True)  158 us
    ppermute x28, waiting for transfers between devices, swap(): return lax.ppermute(value, axis, [(0, 1), (1, 0)])  97.5 us
    dot_general x31, matrix products, dot(): return lax.dot_general(a, b, (dims, ((), ())), preferred_element_type=f32)  96.4 us
    pallas_call x2, Pallas kernels, attend_back(): pl.pallas_call(attend_back_kernel, grid=(pairs,), in_specs=[q_spec] + kv_...  38.1 us
    ppermute x28, starting transfers between devices, swap(): return lax.ppermute(value, axis, [(0, 1), (1, 0)])  37.5 us
    pallas_call x2, Pallas kernels, attend(): pl.pallas_call(attend_kernel, grid=(pairs,), in_specs=[q_spec] + kv_specs...  30.6 us
    all_to_all x2, blocking collectives, to_images(): mixed = lax.all_to_all(tokens, 'z', split_axis=0, concat_axis=0, tiled=True)  25.1 us
  transfers between devices with their start and end apart: 43, of which 25 were waited for; matrix products, arithmetic and copies ran while one was open for 10% of the time, Pallas kernels for 3%

profile of v1, /device:TPU:1, one launch (start us, length us, event | category | flops | bytes accessed | tf_op | source)
XLA Modules:
  0.0 883.3 jit_solution(4302905751975613787)
XLA Ops:
  18.7 48.4 %all-gather.7.cloned.1.call-done = bf16[1024,1664]{1,0:T(8,128)(2,1)} async-done(((bf16[64,1664]{1,0:T(8,128)(2,1)}), bf16[1024,1664]{1,0:T(8,128)(2,1)}) %all-gather.7.cloned.1.call-update) | async-done | bytes 3407888 | tf_op jit(solution)/shard_map/all_gather | solution.py:298
  71.9 12.6 %all_to_all.20 = bf16[4,64,1024]{2,1,0:T(8,128)(2,1)S(1)} all-to-all(bf16[4,64,1024]{2,1,0:T(8,128)(2,1)S(1)} %copy-done.57), channel_id=1, replica_groups=mesh['section'=2,'z'=4,'yh'=2,'yl'=2,'xhi'=2,'core'=2] {'z'}, dimensions={0} | all-to-all | bytes 1048576 | tf_op jit(solution)/shard_map/all_to_all | solution.py:140
  89.2 8.1 collective-permute-done
  105.4 18.7 %all-gather.13.cloned.1.call-done = bf16[1,2048,1024]{2,1,0:T(8,128)(2,1)} async-done(((bf16[1,128,1024]{2,1,0:T(8,128)(2,1)}), bf16[1,2048,1024]{2,1,0:T(8,128)(2,1)}) %all-gather.13.cloned.1.call-update) | async-done | bytes 4194320 | tf_op jit(solution)/shard_map/all_gather | solution.py:298
  124.7 53.3 %all-gather.9.cloned.1.call-done = bf16[1024,2048]{1,0:T(8,128)(2,1)} async-done(((bf16[64,2048]{1,0:T(8,128)(2,1)}), bf16[1024,2048]{1,0:T(8,128)(2,1)}) %all-gather.9.cloned.1.call-update) | async-done | bytes 4194320 | tf_op jit(solution)/shard_map/all_gather | solution.py:298
  183.8 37.9 %all-gather.11.cloned.1.call-done = bf16[1,512,1024]{2,1,0:T(8,128)(2,1)} async-done(((bf16[1,32,1024]{2,1,0:T(8,128)(2,1)}), bf16[1,512,1024]{2,1,0:T(8,128)(2,1)}) %all-gather.11.cloned.1.call-update) | async-done | bytes 1048592 | tf_op jit(solution)/shard_map/all_gather | solution.py:298
  234.9 15.6 %attend.2 = (bf16[256,1024]{1,0:T(8,128)(2,1)S(1)}, f32[8,2,256]{2,1,0:T(2,128)}) custom-call(bf16[256,1024]{1,0:T(8,128)(2,1)S(1)} %pad_maximum_fusion.9.q_ref, bf16[256,2048]{1,0:T(8,128)(2,1)S(1)} %pad_maximum_fusion.4.own_ref, bf16[256,2048]{1,0:T(8,128)(2,1)S(1)} %collective-permute-done.2.mate_ref, ...), custom_call_target="tpu_custom_call" | custom-call | tf_op jit(solution)/shard_map/attend/pallas_call | solution.py:108
  251.6 6.1 convolution_add_fusion.15
  257.7 6.2 fusion.24
  267.0 10.9 %collective-permute-done.8 = bf16[256,1024]{1,0:T(8,128)(2,1)S(1)} collective-permute-done((bf16[256,1024]{1,0:T(8,128)(2,1)S(1)}, bf16[256,1024]{1,0:T(8,128)(2,1)S(1)}, u32[]{:S(2)}, u32[]{:S(2)}) %collective-permute-start.8) | collective-permute-done | bytes 524320 | tf_op jit(solution)/shard_map/ppermute | solution.py:356
  286.3 21.1 %collective-permute-done.10.near_ref = bf16[256,2048]{1,0:T(8,128)(2,1)S(1)} collective-permute-done((bf16[256,2048]{1,0:T(8,128)(2,1)S(1)}, bf16[256,2048]{1,0:T(8,128)(2,1)S(1)}, u32[]{:S(2)}, u32[]{:S(2)}) %collective-permute-start.10) | collective-permute-done | bytes 1048608 | tf_op jit(solution)/shard_map/ppermute | solution.py:36
  310.9 12.5 %all_to_all.21 = bf16[4,64,1024]{2,1,0:T(8,128)(2,1)S(1)} all-to-all(bf16[4,64,1024]{2,1,0:T(8,128)(2,1)S(1)} %broadcast_multiply_fusion), channel_id=1, replica_groups=mesh['section'=2,'z'=4,'yh'=2,'yl'=2,'xhi'=2,'core'=2] {'z'}, dimensions={0} | all-to-all | bytes 1048576 | tf_op jit(solution)/shard_map/all_to_all | solution.py:140
  328.1 15.1 %attend.3 = (bf16[256,1024]{1,0:T(8,128)(2,1)S(1)}, f32[8,2,256]{2,1,0:T(2,128)S(1)}) custom-call(bf16[256,1024]{1,0:T(8,128)(2,1)S(1)} %pad_maximum_fusion.10.q_ref, bf16[256,2048]{1,0:T(8,128)(2,1)S(1)} %pad_maximum_fusion.5.own_ref, bf16[256,2048]{1,0:T(8,128)(2,1)S(1)} %collective-permute-done.9.mate_ref, ...), custom_call_target="tpu_custom_call" | custom-call | tf_op jit(solution)/shard_map/attend/pallas_call | solution.py:108
  349.9 5.3 multiply_convert_fusion
  355.1 7.9 fusion.66
  363.0 8.4 fusion.130
  374.8 19.0 %attend_back.2 = (bf16[256,1024]{1,0:T(8,128)(2,1)S(1)}, bf16[256,2048]{1,0:T(8,128)(2,1)S(1)}, bf16[256,2048]{1,0:T(8,128)(2,1)S(1)}, bf16[256,2048]{1,0:T(8,128)(2,1)S(1)}, bf16[256,2048]{1,0:T(8,128)(2,1)S(1)}) custom-call(bf16[256,1024]{1,0:T(8,128)(2,1)S(1)} %copy-done.3, bf16[256,2048]{1,0:T(8,128)(2,1)S(1)} %pad_maximum_fusion.5.own_ref, ...), custom_call_target="tpu_custom_call" | custom-call | tf_op jit(solution)/shard_map/attend_back/pallas_call | solution.py:126
  398.1 23.6 %collective-permute-done.16 = bf16[256,2048]{1,0:T(8,128)(2,1)S(1)} collective-permute-done((bf16[256,2048]{1,0:T(8,128)(2,1)S(1)}, bf16[256,2048]{1,0:T(8,128)(2,1)S(1)}, u32[]{:S(2)}, u32[]{:S(2)}) %collective-permute-start.16) | collective-permute-done | bytes 1048608 | tf_op jit(solution)/shard_map/ppermute | solution.py:36
  434.9 9.4 %collective-permute-done.17 = bf16[256,1024]{1,0:T(8,128)(2,1)} collective-permute-done((bf16[256,1024]{1,0:T(8,128)(2,1)}, bf16[256,1024]{1,0:T(8,128)(2,1)}, u32[]{:S(2)}, u32[]{:S(2)}) %collective-permute-start.17) | collective-permute-done | bytes 524320 | tf_op jit(solution)/shard_map/ppermute | solution.py:362
  444.3 4.8 fusion.55
  464.4 19.1 %attend_back.3 = (bf16[256,1024]{1,0:T(8,128)(2,1)S(1)}, bf16[256,2048]{1,0:T(8,128)(2,1)S(1)}, bf16[256,2048]{1,0:T(8,128)(2,1)}, bf16[256,2048]{1,0:T(8,128)(2,1)S(1)}, bf16[256,2048]{1,0:T(8,128)(2,1)S(1)}) custom-call(bf16[256,1024]{1,0:T(8,128)(2,1)S(1)} %copy-done.4, bf16[256,2048]{1,0:T(8,128)(2,1)S(1)} %pad_maximum_fusion.5.own_ref, ...), custom_call_target="tpu_custom_call" | custom-call | tf_op jit(solution)/shard_map/attend_back/pallas_call | solution.py:126
  495.4 18.9 %collective-permute-done.20 = bf16[256,2048]{1,0:T(8,128)(2,1)} collective-permute-done((bf16[256,2048]{1,0:T(8,128)(2,1)}, bf16[256,2048]{1,0:T(8,128)(2,1)}, u32[]{:S(2)}, u32[]{:S(2)}) %collective-permute-start.20) | collective-permute-done | bytes 1048608 | tf_op jit(solution)/shard_map/ppermute | solution.py:36
  540.1 5.9 collective-permute-done.25
  548.6 4.8 fusion
  556.9 6.8 collective-permute-done.28
  570.0 6.8 collective-permute-done.31
  588.6 4.9 collective-permute-done.12
  593.5 9.5 %all_to_all.22 = bf16[4,64,1024]{2,1,0:T(8,128)(2,1)S(1)} all-to-all(bf16[4,64,1024]{2,1,0:T(8,128)(2,1)S(1)} %bitcast.178), channel_id=1, replica_groups=mesh['section'=2,'z'=4,'yh'=2,'yl'=2,'xhi'=2,'core'=2] {'z'}, dimensions={0} | all-to-all | bytes 1048576 | tf_op jit(solution)/shard_map/all_to_all | solution.py:149
  606.5 12.0 %reduce-scatter.7.cloned.1.call-done = bf16[32,1024]{1,0:T(8,128)(2,1)} async-done(((bf16[512,1024]{1,0:T(8,128)(2,1)}), bf16[32,1024]{1,0:T(8,128)(2,1)}) %reduce-scatter.7.cloned.1.call-update) | async-done | bytes 65552 | tf_op jit(solution)/shard_map/reduce_scatter | solution.py:371
  627.8 69.9 %reduce-scatter.5.cloned.1.call-done = bf16[64,1664]{1,0:T(8,128)(2,1)} async-done(((bf16[1024,1664]{1,0:T(8,128)(2,1)}), bf16[64,1664]{1,0:T(8,128)(2,1)}) %reduce-scatter.5.cloned.1.call-update) | async-done | bytes 213008 | tf_op jit(solution)/shard_map/reduce_scatter | solution.py:371
  712.7 65.8 %reduce-scatter.9.cloned.1.call-done = bf16[64,2048]{1,0:T(8,128)(2,1)} async-done(((bf16[1024,2048]{1,0:T(8,128)(2,1)}), bf16[64,2048]{1,0:T(8,128)(2,1)}) %reduce-scatter.9.cloned.1.call-update) | async-done | bytes 262160 | tf_op jit(solution)/shard_map/reduce_scatter | solution.py:371
  781.2 77.7 %reduce-scatter.11.cloned.1.call-done = bf16[128,1024]{1,0:T(8,128)(2,1)} async-done(((bf16[2048,1024]{1,0:T(8,128)(2,1)}), bf16[128,1024]{1,0:T(8,128)(2,1)}) %reduce-scatter.11.cloned.1.call-update) | async-done | bytes 262160 | tf_op jit(solution)/shard_map/reduce_scatter | solution.py:371
  (396 shorter events, 220.3 us)
Async XLA Ops:
  7.2 59.9 %all-gather.7.cloned.1.call-start = ((), (), s32[]{:S(2)}) async-start(), calls=%async_computation.8 | async-start | bytes 3620864 | tf_op jit(solution)/shard_map/all_gather | solution.py:298
  15.1 109.0 %all-gather.13.cloned.1.call-start = ((), (), s32[]{:S(2)}) async-start(), calls=%async_computation.15 | async-start | bytes 4456448 | tf_op jit(solution)/shard_map/all_gather | solution.py:298
  15.9 162.1 %all-gather.9.cloned.1.call-start = ((), (), s32[]{:S(2)}) async-start(), calls=%async_computation.9 | async-start | bytes 4456448 | tf_op jit(solution)/shard_map/all_gather | solution.py:298
  18.7 203.0 %all-gather.11.cloned.1.call-start = ((), (), s32[]{:S(2)}) async-start(), calls=%async_computation.14 | async-start | bytes 1114112 | tf_op jit(solution)/shard_map/all_gather | solution.py:298
  70.9 107.8 %collective-permute-start.1 = (bf16[1024,1536]{1,0:T(8,128)(2,1)}, bf16[1024,1536]{1,0:T(8,128)(2,1)}, u32[]{:S(2)}, u32[]{:S(2)}) collective-permute-start(bf16[1024,1536]{1,0:T(8,128)(2,1)} %slice.279), channel_id=1, source_target_pairs={{0,1},{1,0},{2,3},{3,2},{4,5},{5,4},{6,7},{7,6},{8,9},{9,8},{10,11... | collective-permute-start | bytes 9437192 | tf_op jit(solution)/shard_map/ppermute | solution.py:36
  84.5 12.7 %collective-permute-start = (bf16[256,1024]{1,0:T(8,128)(2,1)S(1)}, bf16[256,1024]{1,0:T(8,128)(2,1)S(1)}, u32[]{:S(2)}, u32[]{:S(2)}) collective-permute-start(bf16[256,1024]{1,0:T(8,128)(2,1)S(1)} %bitcast.177), channel_id=1, source_target_pairs={{0,0},{1,8},{8,1},{9,9},{2,2},{3,10},{10,3},{11,11},{4,4},{5,12},{... | collective-permute-start | bytes 1572872 | tf_op jit(solution)/shard_map/ppermute | solution.py:142
  89.1 529.4 %reduce-scatter.7.cloned.1.call-start = ((), (), s32[]{:S(2)}) async-start(), calls=%async_computation.11 | async-start | bytes 1114112 | tf_op jit(solution)/shard_map/reduce_scatter | solution.py:371
  124.1 133.7 %collective-permute-start.7 = (bf16[2048,1024]{1,0:T(8,128)(2,1)}, bf16[2048,1024]{1,0:T(8,128)(2,1)}, u32[]{:S(2)}, u32[]{:S(2)}) collective-permute-start(bf16[2048,1024]{1,0:T(8,128)(2,1)} %bitcast.222), channel_id=1, source_target_pairs={{0,1},{1,0},{2,3},{3,2},{4,5},{5,4},{6,7},{7,6},{8,9},{9,8},{10,11... | collective-permute-start | bytes 12582920 | tf_op jit(solution)/shard_map/ppermute | solution.py:36
  178.0 79.7 %collective-permute-start.6 = (bf16[1024,2048]{1,0:T(8,128)(2,1)}, bf16[1024,2048]{1,0:T(8,128)(2,1)}, u32[]{:S(2)}, u32[]{:S(2)}) collective-permute-start(bf16[1024,2048]{1,0:T(8,128)(2,1)} %all-gather.9.cloned.1.call-done), channel_id=1, source_target_pairs={{0,1},{1,0},{2,3},{3,2},{4,5},{5,4},{6,7},{7,6},{8,9},{9,8},{10,11... | collective-permute-start | bytes 12582920 | tf_op jit(solution)/shard_map/ppermute | solution.py:36
  182.6 41.3 %collective-permute-start.3 = (bf16[256,2048]{1,0:T(8,128)(2,1)S(1)}, bf16[256,2048]{1,0:T(8,128)(2,1)S(1)}, u32[]{:S(2)}, u32[]{:S(2)}) collective-permute-start(bf16[256,2048]{1,0:T(8,128)(2,1)S(1)} %pad_maximum_fusion.4.own_ref), channel_id=1, source_target_pairs={{0,4},{4,0},{1,5},{5,1},{2,6},{6,2},{3,7},{7,3},{8,12},{12,8},{9,1... | collective-permute-start | bytes 3145736 | tf_op jit(solution)/shard_map/ppermute | solution.py:36
  223.9 11.0 %collective-permute-start.2 = (bf16[256,2048]{1,0:T(8,128)(2,1)S(1)}, bf16[256,2048]{1,0:T(8,128)(2,1)S(1)}, u32[]{:S(2)}, u32[]{:S(2)}) collective-permute-start(bf16[256,2048]{1,0:T(8,128)(2,1)S(1)} %pad_maximum_fusion.4.own_ref), channel_id=1, source_target_pairs={{0,1},{1,0},{2,3},{3,2},{4,5},{5,4},{6,7},{7,6},{8,9},{9,8},{10,11... | collective-permute-start | bytes 3145736 | tf_op jit(solution)/shard_map/ppermute | solution.py:36
  223.9 11.0 %collective-permute-start.4 = (bf16[256,2048]{1,0:T(8,128)(2,1)S(1)}, bf16[256,2048]{1,0:T(8,128)(2,1)}, u32[]{:S(2)}, u32[]{:S(2)}) collective-permute-start(bf16[256,2048]{1,0:T(8,128)(2,1)S(1)} %collective-permute-done.3.near_ref), channel_id=1, source_target_pairs={{0,1},{1,0},{2,3},{3,2},{4,5},{5,4},{6,7},{7,6},{8,9},{9,8},{10,11... | collective-permute-start | bytes 3145736 | tf_op jit(solution)/shard_map/ppermute | solution.py:36
  263.9 14.0 %collective-permute-start.8 = (bf16[256,1024]{1,0:T(8,128)(2,1)S(1)}, bf16[256,1024]{1,0:T(8,128)(2,1)S(1)}, u32[]{:S(2)}, u32[]{:S(2)}) collective-permute-start(bf16[256,1024]{1,0:T(8,128)(2,1)S(1)} %fusion.24), channel_id=1, source_target_pairs={{0,64},{1,65},{2,66},{3,67},{4,68},{5,69},{6,70},{7,71},{8,72},{9,... | collective-permute-start | bytes 1572872 | tf_op jit(solution)/shard_map/ppermute | solution.py:356
  283.9 23.5 %collective-permute-start.10 = (bf16[256,2048]{1,0:T(8,128)(2,1)S(1)}, bf16[256,2048]{1,0:T(8,128)(2,1)S(1)}, u32[]{:S(2)}, u32[]{:S(2)}) collective-permute-start(bf16[256,2048]{1,0:T(8,128)(2,1)S(1)} %pad_maximum_fusion.5.own_ref), channel_id=1, source_target_pairs={{0,4},{4,0},{1,5},{5,1},{2,6},{6,2},{3,7},{7,3},{8,12},{12,8},{9,1... | collective-permute-start | bytes 3145736 | tf_op jit(solution)/shard_map/ppermute | solution.py:36
  284.8 43.2 %collective-permute-start.9 = (bf16[256,2048]{1,0:T(8,128)(2,1)S(1)}, bf16[256,2048]{1,0:T(8,128)(2,1)S(1)}, u32[]{:S(2)}, u32[]{:S(2)}) collective-permute-start(bf16[256,2048]{1,0:T(8,128)(2,1)S(1)} %pad_maximum_fusion.5.own_ref), channel_id=1, source_target_pairs={{0,1},{1,0},{2,3},{3,2},{4,5},{5,4},{6,7},{7,6},{8,9},{9,8},{10,11... | collective-permute-start | bytes 3145736 | tf_op jit(solution)/shard_map/ppermute | solution.py:36
  307.4 20.7 %collective-permute-start.11 = (bf16[256,2048]{1,0:T(8,128)(2,1)S(1)}, bf16[256,2048]{1,0:T(8,128)(2,1)}, u32[]{:S(2)}, u32[]{:S(2)}) collective-permute-start(bf16[256,2048]{1,0:T(8,128)(2,1)S(1)} %collective-permute-done.10.near_ref), channel_id=1, source_target_pairs={{0,1},{1,0},{2,3},{3,2},{4,5},{5,4},{6,7},{7,6},{8,9},{9,8},{10,11... | collective-permute-start | bytes 3145736 | tf_op jit(solution)/shard_map/ppermute | solution.py:36
  323.4 31.8 %collective-permute-start.13 = (bf16[256,1024]{1,0:T(8,128)(2,1)S(1)}, bf16[256,1024]{1,0:T(8,128)(2,1)}, u32[]{:S(2)}, u32[]{:S(2)}) collective-permute-start(bf16[256,1024]{1,0:T(8,128)(2,1)S(1)} %bitcast.176), channel_id=1, source_target_pairs={{0,0},{1,8},{8,1},{9,9},{2,2},{3,10},{10,3},{11,11},{4,4},{5,12},{... | collective-permute-start | bytes 1572872 | tf_op jit(solution)/shard_map/ppermute | solution.py:142
  397.0 24.7 %collective-permute-start.16 = (bf16[256,2048]{1,0:T(8,128)(2,1)S(1)}, bf16[256,2048]{1,0:T(8,128)(2,1)S(1)}, u32[]{:S(2)}, u32[]{:S(2)}) collective-permute-start(bf16[256,2048]{1,0:T(8,128)(2,1)S(1)} %add_convert_fusion.5), channel_id=1, source_target_pairs={{0,4},{4,0},{1,5},{5,1},{2,6},{6,2},{3,7},{7,3},{8,12},{12,8},{9,1... | collective-permute-start | bytes 3145736 | tf_op jit(solution)/shard_map/ppermute | solution.py:36
  429.4 14.9 %collective-permute-start.17 = (bf16[256,1024]{1,0:T(8,128)(2,1)}, bf16[256,1024]{1,0:T(8,128)(2,1)}, u32[]{:S(2)}, u32[]{:S(2)}) collective-permute-start(bf16[256,1024]{1,0:T(8,128)(2,1)} %fusion.41), channel_id=1, source_target_pairs={{64,0},{65,1},{66,2},{67,3},{68,4},{69,5},{70,6},{71,7},{72,8},{73... | collective-permute-start | bytes 1572872 | tf_op jit(solution)/shard_map/ppermute | solution.py:362
  485.2 10.2 %collective-permute-start.18 = (bf16[256,2048]{1,0:T(8,128)(2,1)}, bf16[256,2048]{1,0:T(8,128)(2,1)}, u32[]{:S(2)}, u32[]{:S(2)}) collective-permute-start(bf16[256,2048]{1,0:T(8,128)(2,1)} %get-tuple-element.35), channel_id=1, source_target_pairs={{0,1},{1,0},{2,3},{3,2},{4,5},{5,4},{6,7},{7,6},{8,9},{9,8},{10,11... | collective-permute-start | bytes 3145736 | tf_op jit(solution)/shard_map/ppermute | solution.py:36
  489.5 24.9 %collective-permute-start.20 = (bf16[256,2048]{1,0:T(8,128)(2,1)}, bf16[256,2048]{1,0:T(8,128)(2,1)}, u32[]{:S(2)}, u32[]{:S(2)}) collective-permute-start(bf16[256,2048]{1,0:T(8,128)(2,1)} %add_convert_fusion.3), channel_id=1, source_target_pairs={{0,4},{4,0},{1,5},{5,1},{2,6},{6,2},{3,7},{7,3},{8,12},{12,8},{9,1... | collective-permute-start | bytes 3145736 | tf_op jit(solution)/shard_map/ppermute | solution.py:36
  537.6 11.0 %collective-permute-start.22 = (bf16[1024,1664]{1,0:T(8,128)(2,1)}, bf16[1024,1664]{1,0:T(8,128)(2,1)}, u32[]{:S(2)}, u32[]{:S(2)}) collective-permute-start(bf16[1024,1664]{1,0:T(8,128)(2,1)} %pad_maximum_fusion), channel_id=1, source_target_pairs={{0,1},{1,0},{2,3},{3,2},{4,5},{5,4},{6,7},{7,6},{8,9},{9,8},{10,11... | collective-permute-start | bytes 10223624 | tf_op jit(solution)/shard_map/ppermute | solution.py:36
  547.4 150.3 %reduce-scatter.5.cloned.1.call-start = ((), (), s32[]{:S(2)}) async-start(), calls=%async_computation.10 | async-start | bytes 3620864 | tf_op jit(solution)/shard_map/reduce_scatter | solution.py:371
  553.5 224.9 %reduce-scatter.9.cloned.1.call-start = ((), (), s32[]{:S(2)}) async-start(), calls=%async_computation.12 | async-start | bytes 4456448 | tf_op jit(solution)/shard_map/reduce_scatter | solution.py:371
  566.9 291.9 %reduce-scatter.11.cloned.1.call-start = ((), (), s32[]{:S(2)}) async-start(), calls=%async_computation.13 | async-start | bytes 4456448 | tf_op jit(solution)/shard_map/reduce_scatter | solution.py:371
  581.1 12.4 %collective-permute-start.12 = (bf16[256,1024]{1,0:T(8,128)(2,1)S(1)}, bf16[256,1024]{1,0:T(8,128)(2,1)S(1)}, u32[]{:S(2)}, u32[]{:S(2)}) collective-permute-start(bf16[256,1024]{1,0:T(8,128)(2,1)S(1)} %copy-done.64), channel_id=1, source_target_pairs={{0,0},{1,8},{8,1},{9,9},{2,2},{3,10},{10,3},{11,11},{4,4},{5,12},{... | collective-permute-start | bytes 1572872 | tf_op jit(solution)/shard_map/ppermute | solution.py:147
  584.0 19.0 %collective-permute-start.21 = (bf16[256,1024]{1,0:T(8,128)(2,1)S(1)}, bf16[256,1024]{1,0:T(8,128)(2,1)}, u32[]{:S(2)}, u32[]{:S(2)}) collective-permute-start(bf16[256,1024]{1,0:T(8,128)(2,1)S(1)} %fusion.46), channel_id=1, source_target_pairs={{0,0},{1,8},{8,1},{9,9},{2,2},{3,10},{10,3},{11,11},{4,4},{5,12},{... | collective-permute-start | bytes 1572872 | tf_op jit(solution)/shard_map/ppermute | solution.py:147
  603.0 24.8 %all-to-all-start.3 = ((bf16[4,64,1024]{2,1,0:T(8,128)(2,1)}), bf16[4,64,1024]{2,1,0:T(8,128)(2,1)S(1)}, u32[]{:S(2)}, u32[]{:S(2)}) async-start(bf16[4,64,1024]{2,1,0:T(8,128)(2,1)} %bitcast.34), calls=%async_computation.3 | async-start | bytes 1048576 | tf_op jit(solution)/shard_map/all_to_all | solution.py:149
  624.2 76.2 %collective-permute-start.27 = (bf16[32,1024]{1,0:T(8,128)(2,1)S(1)}, bf16[32,1024]{1,0:T(8,128)(2,1)S(1)}, u32[]{:S(2)}, u32[]{:S(2)}) collective-permute-start(bf16[32,1024]{1,0:T(8,128)(2,1)S(1)} %add_convert_fusion.16), channel_id=1, source_target_pairs={{0,1},{1,0},{2,3},{3,2},{4,5},{5,4},{6,7},{7,6},{8,9},{9,8},{10,11... | collective-permute-start | bytes 196616 | tf_op jit(solution)/shard_map/ppermute | solution.py:36
  705.1 156.4 %collective-permute-start.24 = (bf16[64,1664]{1,0:T(8,128)(2,1)S(1)}, bf16[64,1664]{1,0:T(8,128)(2,1)S(1)}, u32[]{:S(2)}, u32[]{:S(2)}) collective-permute-start(bf16[64,1664]{1,0:T(8,128)(2,1)S(1)} %add_convert_fusion.15), channel_id=1, source_target_pairs={{0,1},{1,0},{2,3},{3,2},{4,5},{5,4},{6,7},{7,6},{8,9},{9,8},{10,11... | collective-permute-start | bytes 638984 | tf_op jit(solution)/shard_map/ppermute | solution.py:36
  778.5 87.9 %collective-permute-start.29 = (bf16[64,2048]{1,0:T(8,128)(2,1)}, bf16[64,2048]{1,0:T(8,128)(2,1)S(1)}, u32[]{:S(2)}, u32[]{:S(2)}) collective-permute-start(bf16[64,2048]{1,0:T(8,128)(2,1)} %reduce-scatter.9.cloned.1.call-done), channel_id=1, source_target_pairs={{0,2},{2,0},{1,3},{3,1},{4,6},{6,4},{5,7},{7,5},{8,10},{10,8},{9,1... | collective-permute-start | bytes 786440 | tf_op jit(solution)/shard_map/ppermute | solution.py:36
  858.8 10.9 %collective-permute-start.32 = (bf16[128,1024]{1,0:T(8,128)(2,1)}, bf16[128,1024]{1,0:T(8,128)(2,1)S(1)}, u32[]{:S(2)}, u32[]{:S(2)}) collective-permute-start(bf16[128,1024]{1,0:T(8,128)(2,1)} %reduce-scatter.11.cloned.1.call-done), channel_id=1, source_target_pairs={{0,2},{2,0},{1,3},{3,1},{4,6},{6,4},{5,7},{7,5},{8,10},{10,8},{9,1... | collective-permute-start | bytes 786440 | tf_op jit(solution)/shard_map/ppermute | solution.py:36
  (81 other events, 738.4 us)
Sparse Core Ops, SparseCore 0:
  15.2 51.8 all-gather.6
  69.8 54.2 all-gather.12
  126.8 51.2 all-gather.8
  180.6 41.0 all-gather.10
  547.5 71.0 reduce-scatter.6
  622.1 75.5 reduce-scatter.4
  701.4 77.0 reduce-scatter.8
  781.8 76.9 reduce-scatter.10

commit v2 on v1

--- a/solution.py
+++ b/solution.py
@@ -135,18 +135,80 @@
     )(queries, *blocks, grad, log_total)
 
 
-def to_images(tokens):
-    count, rows, width = tokens.shape
-    mixed = lax.all_to_all(tokens, "z", split_axis=0, concat_axis=0, tiled=True)
-    mixed = mixed.reshape(count * rows, width)
-    return lax.ppermute(mixed, ("yh", "core"), [(0, 0), (1, 2), (2, 1), (3, 3)])
-
-
-def from_images(tokens, count):
-    rows, width = tokens.shape
-    mixed = lax.ppermute(tokens, ("yh", "core"), [(0, 0), (1, 2), (2, 1), (3, 3)])
-    mixed = mixed.reshape(count, rows // count, width)
-    return lax.all_to_all(mixed, "z", split_axis=0, concat_axis=0, tiled=True)
+FLIP = [(0, 0), (1, 2), (2, 1), (3, 3)]
+
+
+def to_images(arrays):
+    count, rows, width = arrays[0].shape
+    mixed = jnp.stack(arrays, axis=1)
+    mixed = lax.all_to_all(mixed, "z", split_axis=0, concat_axis=0, tiled=True)
+    mixed = [mixed[:, i].reshape(count * rows, width) for i in range(len(arrays))]
+    return [lax.ppermute(m, ("yh", "core"), FLIP) for m in mixed]
+
+
+def from_images(arrays, count):
+    rows, width = arrays[0].shape
+    mixed = [lax.ppermute(a, ("yh", "core"), FLIP) for a in arrays]
+    mixed = jnp.stack([m.reshape(count, rows // count, width) for m in mixed], axis=1)
+    mixed = lax.all_to_all(mixed, "z", split_axis=0, concat_axis=0, tiled=True)
+    return [mixed[:, i] for i in range(len(arrays))]
+
+
+RING_Z, RING_Y = "z", ("yh", "yl")
+AHEAD = [(i, (i + 1) % 4) for i in range(4)]
+BACK = [(i, (i - 1) % 4) for i in range(4)]
+
+
+def ring_place(value, axis, out_shapes, views):
+    half = value.shape[0] // 2
+    ahead = lax.ppermute(value, axis, AHEAD)
+    back = lax.ppermute(value, axis, BACK)
+    far_a = lax.ppermute(ahead[:half], axis, AHEAD)
+    far_b = lax.ppermute(back[half:], axis, BACK)
+    pieces = [(value, 0, 0), (ahead, 3, 0), (back, 1, 0), (far_a, 2, 0), (far_b, 2, half)]
+    n_outs = len(out_shapes)
+
+    def kernel(index_ref, *refs):
+        sources, outs, sems = refs[:5], refs[5 : 5 + n_outs], refs[5 + n_outs]
+        copies = []
+        for source, (_, step, start) in zip(sources, pieces):
+            place = lax.rem(index_ref[0] + step, 4)
+            for src, dst in views(outs, source, place, start):
+                copies.append(pltpu.make_async_copy(src, dst, sems.at[len(copies)]))
+        for copy in copies:
+            copy.start()
+        for copy in copies:
+            copy.wait()
+
+    size = 2 * sum(2 * value.size * 4 for _ in range(1))
+    return pl.pallas_call(
+        kernel,
+        in_specs=[pl.BlockSpec(memory_space=pltpu.SMEM)] + [pl.BlockSpec(memory_space=pl.ANY)] * 5,
+        out_specs=[pl.BlockSpec(memory_space=pl.ANY)] * n_outs,
+        out_shape=[jax.ShapeDtypeStruct(shape, value.dtype) for shape in out_shapes],
+        scratch_shapes=[pltpu.SemaphoreType.DMA((5 * max(n_outs, 1),))],
+        cost_estimate=pl.CostEstimate(flops=0, bytes_accessed=size, transcendentals=0),
+        name="ring_place",
+    )(lax.axis_index(axis).reshape(1), *(p[0] for p in pieces))
+
+
+def in_order(outs, piece, place, start):
+    return [(piece, outs[0].at[place, pl.ds(start, piece.shape[0])])]
+
+
+def ring_sum(blocks, axis):
+    index = lax.axis_index(axis)
+    block = lambda k: lax.dynamic_index_in_dim(blocks, (index + k) % 4, 0, keepdims=False)
+    add = lambda *parts: sum(p.astype(f32) for p in parts).astype(bf16)
+    far, after, before = block(2), block(1), block(3)
+    half = far.shape[0] // 2
+    low = lax.ppermute(far[:half], axis, AHEAD)
+    high = lax.ppermute(far[half:], axis, BACK)
+    after = jnp.concatenate([add(after[:half], low), after[half:]])
+    before = jnp.concatenate([before[:half], add(before[half:], high)])
+    after = lax.ppermute(after, axis, AHEAD)
+    before = lax.ppermute(before, axis, BACK)
+    return add(block(0), after, before)
 
 
 def group_blocks(key_value):
@@ -176,18 +238,28 @@
     return factor * (e - jnp.mean(e, axis=-1, keepdims=True) - normal * inner)
 
 
+def flip_halves(core, value):
+    half = value.shape[-1] // 2
+    turned = jnp.concatenate([value[..., half:], value[..., :half]], axis=-1)
+    return jnp.where(core == 0, value, turned)
+
+
 def forward(tokens, w):
     inputs = tokens.astype(f32)
     normed_one = (normal_part(inputs)[0] * w["gain"][0] + w["shift"][0]).astype(bf16)
-    width = tokens.shape[1]
-    half = width // 2
-    joined = [
-        (mm(normed_one, part) + bias).astype(bf16) for part, bias in zip(w["qkv"], w["qkv_bias"])
-    ]
-    queries = jnp.concatenate([j[:, :half] for j in joined], axis=1)
-    blocks = group_blocks(jnp.concatenate([j[:, half:] for j in joined], axis=1))
+    project = lambda name: jnp.concatenate(
+        [
+            (mm(normed_one, part) + bias).astype(bf16)
+            for part, bias in zip(w[name], w[name + "_bias"])
+        ],
+        axis=1,
+    )
+    blocks = group_blocks(project("kv"))
+    queries = project("q")
     attended, log_total = attend(queries, blocks)
-    branch = mm(attended, w["proj"]) + w["out_bias"][0]
+    attended = flip_halves(w["core"], attended)
+    branch = flip_halves(w["core"], jnp.concatenate([mm(attended, p) for p in w["proj"]], axis=1))
+    branch = branch + w["out_bias"][0]
     middle = inputs + w["scale"][0] * branch
     normed_two = (normal_part(middle)[0] * w["gain"][1] + w["shift"][1]).astype(bf16)
     activated, slope, branch_two = [], [], w["out_bias"][1]
@@ -198,7 +270,9 @@
         active = (before * phi).astype(bf16)
         activated.append(active)
         slope.append((phi + before * density).astype(bf16))
-        branch_two = branch_two + mm(active, down)
+        for i, part in enumerate(down):
+            rows = part.shape[0]
+            branch_two = branch_two + mm(active[:, i * rows : (i + 1) * rows], part)
     result = (middle + w["scale"][1] * branch_two).astype(bf16)
     kept = dict(
         inputs=inputs,
@@ -222,44 +296,43 @@
     grad_before = []
     grad_normed_two = 0.0
     for up, down, slope in zip(w["fc1"], w["fc2"], kept["slope"]):
-        part = (mm_t(grad_branch_two, down) * slope.astype(f32)).astype(bf16)
+        part = jnp.concatenate([mm_t(grad_branch_two, d) for d in down], axis=1)
+        part = (part * slope.astype(f32)).astype(bf16)
         grad_before.append(part)
         grad_normed_two = grad_normed_two + mm_t(part, up)
     normal_two, factor_two = normal_part(kept["middle"])
     grad_middle = grad_out + norm_back(grad_normed_two, normal_two, factor_two, w["gain"][1])
     grad_branch = (w["scale"][0] * grad_middle).astype(bf16)
-    grad_attended = mm_t(grad_branch, w["proj"]).astype(bf16)
+    width = grad_branch.shape[1]
+    half = width // 2
+    grad_halves = flip_halves(w["core"], grad_branch)
+    grad_halves = [grad_halves[:, :half], grad_halves[:, half:]]
+    grad_attended = sum(mm_t(g, p) for g, p in zip(grad_halves, w["proj"])).astype(bf16)
+    grad_attended = flip_halves(w["core"], grad_attended)
     parts = attend_back(kept["queries"], kept["blocks"], grad_attended, kept["log_total"])
     grad_queries = parts[0]
     grad_key_value = group_sum(*parts[1:])
-    width = grad_queries.shape[1]
-    half = width // 2
-    grad_joined = [
-        jnp.concatenate(
-            [
-                grad_queries[:, i * half : (i + 1) * half],
-                grad_key_value[:, i * width : (i + 1) * width],
-            ],
-            axis=1,
-        )
-        for i in range(2)
-    ]
-    grad_normed_one = sum(mm_t(g, part) for g, part in zip(grad_joined, w["qkv"]))
+    grad_q = [grad_queries[:, i * half : (i + 1) * half] for i in range(2)]
+    grad_kv = [grad_key_value[:, i * width : (i + 1) * width] for i in range(2)]
+    grad_normed_one = sum(
+        mm_t(g, part) for g, part in zip(grad_q + grad_kv, w["q"] + w["kv"])
+    )
     normal_one, factor_one = normal_part(kept["inputs"])
     grad_inputs = grad_middle + norm_back(grad_normed_one, normal_one, factor_one, w["gain"][0])
     total = lambda a: jnp.sum(a.astype(f32), axis=0)
-    joined_sums = [total(g) for g in grad_joined]
     vectors = dict(
         gain=(total(grad_normed_one * normal_one), total(grad_normed_two * normal_two)),
         shift=(total(grad_normed_one), total(grad_normed_two)),
         out_bias=(total(grad_branch), total(grad_branch_two)),
         scale=(total(grad_middle * kept["branch"]), total(grad_out * kept["branch_two"])),
-        joined=joined_sums,
+        q=[total(g) for g in grad_q],
+        kv=[total(g) for g in grad_kv],
         fc1_bias=[total(g) for g in grad_before],
     )
     outer = dict(
-        qkv=(kept["normed_one"], grad_joined),
-        proj=(kept["attended"], grad_branch),
+        q=(kept["normed_one"], grad_q),
+        kv=(kept["normed_one"], grad_kv),
+        proj=(kept["attended"], grad_halves),
         fc1=(kept["normed_two"], grad_before),
         fc2=(kept["activated"], grad_branch_two),
     )
@@ -295,12 +368,13 @@
     mid = hidden // 2
     groups = half // PAIR
     pick = lambda a, i, axis: lax.dynamic_index_in_dim(a, i, axis, keepdims=False)
-    gather = lambda a: lax.all_gather(a, FSDP, axis=0, tiled=True)
-
+
+    part = mid // 2
     q, k, v = (qkv_weight[0][:, i * width : (i + 1) * width] for i in range(3))
     q_mine = pick(q.reshape(own, 2, half), core, 1)
     kv = jnp.stack([k.reshape(own, 2, groups, PAIR), v.reshape(own, 2, groups, PAIR)], axis=3)
     kv_mine = pick(kv, core, 1).reshape(own, width)
+    proj_mine = pick(proj_weight[0].reshape(own, 2, half), core, 1)
     vectors = jnp.concatenate(
         [a[0] for a in (norm_gain, norm_bias, qv_bias, out_bias, layer_scale)]
         + [fc1_bias[0].reshape(own, hidden // own).T],
@@ -308,75 +382,92 @@
     ).T
     count = vectors.shape[1]
     vectors = jnp.pad(vectors, ((0, 0), (0, 128 - count)))
-    first = gather(jnp.concatenate([q_mine, kv_mine, vectors], axis=1))
-    qkv_mine = first[:, : half + width]
-    vectors = first[:, half + width : half + width + count].T.astype(f32)
-    fc1_b = vectors[10:].T.reshape(shards, 2, mid // 1)
-    fc1_mine = pick(fc1_weight[0].reshape(own, shards, 2, mid), core, 2).reshape(own, shards * mid)
-    fc2_mine = pick(fc2_weight[0].reshape(2, mid, width), core, 0)
-    proj_mine = pick(proj_weight[0].reshape(2, own // 2, width), core, 0)
-    proj_half = gather(proj_mine)
-    fc1_half = gather(fc1_mine)
-    fc2_half = gather(fc2_mine)
-    lower, upper = ordered(core, proj_half, swap(proj_half, "core"))
-    proj = jnp.stack(
-        [lower.reshape(shards, own // 2, width), upper.reshape(shards, own // 2, width)], axis=1
-    ).reshape(2, half, width)
-    proj = jnp.concatenate([pick(proj, core, 0), pick(proj, 1 - core, 0)], axis=0)
+    fc1_mine = pick(fc1_weight[0].reshape(own, shards, 2, 2, part), core, 2)
+    fc1_mine = jnp.swapaxes(fc1_mine, 1, 2).reshape(own, shards * mid)
+    fc2_mine = pick(fc2_weight[0].reshape(2, 2, part, width), core, 0)
+    fc_mine = jnp.concatenate([fc1_mine, fc2_mine[0], fc2_mine[1]], axis=1)
+    fc_half = lax.all_gather(fc_mine, FSDP, axis=0, tiled=True)
+
+    a_mine = jnp.concatenate([q_mine, proj_mine, vectors], axis=1)
+    a_row = ring_place(a_mine, RING_Y, [(4, own, a_mine.shape[1])], in_order)[0]
+    a_row = a_row.reshape(4 * own, a_mine.shape[1])
+    b_row = ring_place(kv_mine, RING_Z, [(4, own, width)], in_order)[0]
+
+    def a_views(outs, piece, place, start):
+        rows = pl.ds(start, piece.shape[0])
+        columns = [pl.ds(0, half), pl.ds(half, half), pl.ds(width, 128)]
+        return [(piece.at[:, c], out.at[place, rows]) for c, out in zip(columns, outs)]
+
+    def b_views(outs, piece, place, start):
+        return [(piece, outs[0].at[pl.ds(start, piece.shape[0]), place])]
+
+    q_half, proj_half, vectors = (
+        o.reshape(width, -1)
+        for o in ring_place(
+            a_row, RING_Z, [(4, 4 * own, half), (4, 4 * own, half), (4, 4 * own, 128)], a_views
+        )
+    )
+    kv_half = ring_place(b_row, RING_Y, [(4, 4, own, width)], b_views)[0].reshape(width, width)
+    vectors = vectors[:, :count].T.astype(f32)
+    fc1_b = vectors[10:].T.reshape(shards, 2, 2, part)
 
     def halves(vector):
         pair = vector.reshape(2, half)
         return pick(pair, core, 0), pick(pair, 1 - core, 0)
 
-    def qkv_bias(q_half, v_half):
+    def kv_bias(v_half):
         v_part = v_half.reshape(groups, 1, PAIR)
-        kv_part = jnp.concatenate([jnp.zeros_like(v_part), v_part], axis=1).reshape(width)
-        return jnp.concatenate([q_half, kv_part])
-
+        return jnp.concatenate([jnp.zeros_like(v_part), v_part], axis=1).reshape(width)
+
+    wide = shards * mid
+    fc_pair = (fc_half, swap(fc_half, "core"))
     w = dict(
+        core=core,
         gain=vectors[0:2],
         shift=vectors[2:4],
         out_bias=vectors[6:8],
         scale=vectors[8:10],
-        qkv=(qkv_mine, swap(qkv_mine, "core")),
-        qkv_bias=[qkv_bias(a, b) for a, b in zip(halves(vectors[4]), halves(vectors[5]))],
-        proj=proj,
-        fc1=(fc1_half, swap(fc1_half, "core")),
-        fc1_bias=(pick(fc1_b, core, 1).reshape(-1), pick(fc1_b, 1 - core, 1).reshape(-1)),
-        fc2=(fc2_half, swap(fc2_half, "core")),
+        q=[q_half, swap(q_half, "core")],
+        q_bias=halves(vectors[4]),
+        kv=[kv_half, swap(kv_half, "core")],
+        kv_bias=[kv_bias(b) for b in halves(vectors[5])],
+        proj=(proj_half, swap(proj_half, "core")),
+        fc1=[f[:, :wide] for f in fc_pair],
+        fc1_bias=[
+            jnp.swapaxes(pick(fc1_b, c, 1), 0, 1).reshape(-1) for c in (core, 1 - core)
+        ],
+        fc2=[(f[:, wide : wide + width], f[:, wide + width :]) for f in fc_pair],
     )
 
     live = (
         jnp.arange(images) % IMG_MB < jnp.repeat(batch_counts[0], IMG_MB)
     ).astype(bf16)
-    first_tokens = to_images(patch_tokens)
-    last_grad = to_images(out_grad * live[:, None, None])
+    first_tokens, last_grad = to_images([patch_tokens, out_grad * live[:, None, None]])
 
     sent, _ = forward(first_tokens, w)
     passed = lax.ppermute(sent, "section", [(0, 1)])
     tokens = jnp.where(section == 0, first_tokens, passed)
     result, kept = forward(tokens, w)
-    block_out = from_images(result, images)
 
     sent, _, _ = backward(last_grad.astype(f32), kept, w)
     passed = lax.ppermute(sent, "section", [(1, 0)])
     grad_out = jnp.where(section == 1, last_grad, passed).astype(f32)
     grad_inputs, sums, outer = backward(grad_out, kept, w)
-    in_grad = from_images(grad_inputs, images)
+    result, grad_inputs = lax.optimization_barrier((result, grad_inputs))
+    block_out, in_grad = from_images([result, grad_inputs], images)
 
     def core_sum(mine, other):
         return (mine + swap(other.astype(bf16), "core").astype(f32)).astype(bf16)
 
-    def scatter(a):
-        return lax.psum_scatter(a, FSDP, scatter_dimension=0, tiled=True)
-
     def natural(pair):
         return jnp.concatenate(ordered(core, *pair))
 
-    joined = sums["joined"]
-    v_sum = lambda a: a[half:].reshape(groups, 2, PAIR)[:, 1].reshape(half)
+    v_sum = lambda a: a.reshape(groups, 2, PAIR)[:, 1].reshape(half)
     fc1_sum = jnp.stack(
-        ordered(core, *(s.reshape(shards, mid) for s in sums["fc1_bias"])), axis=1
+        ordered(
+            core, *(jnp.swapaxes(s.reshape(2, shards, part), 0, 1) for s in sums["fc1_bias"])
+        ),
+        axis=1,
     ).reshape(width, hidden // own)
     vector_grads = jnp.concatenate(
         [
@@ -384,8 +475,8 @@
                 [
                     *sums["gain"],
                     *sums["shift"],
-                    natural([j[:half] for j in joined]),
-                    natural([v_sum(j) for j in joined]),
+                    natural(sums["q"]),
+                    natural([v_sum(g) for g in sums["kv"]]),
                     *sums["out_bias"],
                     *sums["scale"],
                 ],
@@ -399,44 +490,45 @@
 
     a2, du = outer["fc1"]
     z, e2 = outer["fc2"]
-    fc2_grad = scatter(core_sum(t_mm(z[0], e2), t_mm(z[1], e2)))
-    fc1_grad = scatter(core_sum(t_mm(a2, du[0]), t_mm(a2, du[1])))
+    fc_parts = [
+        jnp.concatenate([t_mm(a2, du[i]), t_mm(z[i][:, :width], e2), t_mm(z[i][:, width:], e2)], 1)
+        for i in range(2)
+    ]
+    fc_grad = lax.psum_scatter(core_sum(*fc_parts), FSDP, scatter_dimension=0, tiled=True)
+    a1, dq = outer["q"]
+    dkv = outer["kv"][1]
     o, e1 = outer["proj"]
-    proj_full = t_mm(o, e1).astype(bf16).reshape(2, half, width)
-    proj_full = jnp.concatenate(ordered(core, proj_full[0], proj_full[1]))
-    proj_full = proj_full.reshape(shards, 2, own // 2, width)
-    proj_grad = scatter(
-        core_sum(pick(proj_full, core, 1).astype(f32), pick(proj_full, 1 - core, 1)).reshape(
-            half, width
-        )
-    )
-    a1, dj = outer["qkv"]
-    vec = [vector_grads, vector_grads]
-    qkv_grad = scatter(
-        core_sum(*(jnp.concatenate([t_mm(a1, d), g], axis=1) for d, g in zip(dj, vec)))
-    )
-
-    parts = [qkv_grad, fc1_grad, proj_grad, fc2_grad]
-    parts = [
-        (a.astype(f32) + swap(a, "xhi").astype(f32)).astype(bf16) for a in parts
+    a_parts = [
+        jnp.concatenate([t_mm(a1, dq[i]), t_mm(o, e1[i]), vector_grads], axis=1) for i in range(2)
     ]
+    b_parts = [t_mm(a1, dkv[i]) for i in range(2)]
+    b_sum = ring_sum(core_sum(*b_parts).reshape(4, 4, own, width), RING_Z)
+    b_grad = ring_sum(b_sum, RING_Y)
+    a_blocks = core_sum(*a_parts).reshape(4, 4, own, width + 128)
+    a_sum = ring_sum(jnp.swapaxes(a_blocks, 0, 1), RING_Y)
+    a_grad = ring_sum(a_sum, RING_Z)
+
+    parts = [a_grad, b_grad, fc_grad]
+    parts = [(a.astype(f32) + swap(a, "xhi").astype(f32)).astype(bf16) for a in parts]
+    vec_grad = parts[0][:, width : width + count].T.astype(f32)
     others = [swap(a, "core") for a in parts]
-    qkv_pair, fc1_pair, proj_pair, fc2_pair = (
+    a_pair, b_pair, fc_pair = (
         ordered(core, a.astype(f32), b.astype(f32)) for a, b in zip(parts, others)
     )
-    vec_grad = parts[0][:, half + width : half + width + count].T.astype(f32)
-    q_grad = jnp.concatenate([p[:, :half] for p in qkv_pair], axis=1)
-    kv_grads = [p[:, half : half + width].reshape(own, groups, 2, PAIR) for p in qkv_pair]
+    q_grad = jnp.concatenate([p[:, :half] for p in a_pair], axis=1)
+    proj_out = jnp.concatenate([p[:, half:width] for p in a_pair], axis=1)
+    kv_grads = [p.reshape(own, groups, 2, PAIR) for p in b_pair]
     k_grad, v_grad = (
         jnp.concatenate([p[:, :, i].reshape(own, half) for p in kv_grads], axis=1)
         for i in range(2)
     )
     qkv_out = jnp.concatenate([q_grad, k_grad, v_grad], axis=1)
-    fc1_out = jnp.stack([p.reshape(own, shards, mid) for p in fc1_pair], axis=2).reshape(
-        own, 2 * shards * mid
-    )
-    fc2_out = jnp.concatenate(fc2_pair, axis=0)
-    proj_out = jnp.concatenate(proj_pair, axis=0)
+    fc1_out = jnp.stack(
+        [jnp.swapaxes(p[:, :wide].reshape(own, 2, shards, part), 1, 2) for p in fc_pair], axis=2
+    ).reshape(own, 2 * wide)
+    fc2_out = jnp.concatenate(
+        [p[:, wide + i * width : wide + (i + 1) * width] for p in fc_pair for i in range(2)], axis=0
+    )
     return (
         block_out[None],
         in_grad[None],

time: 893 us -> 801 us (0.90)
  waiting for transfers between devices: 515 us -> 214 us
  Pallas kernels: 68.8 us -> 240 us
  starting transfers between devices: 61.3 us -> 108 us
  blocking collectives: 34.6 us -> 0 us
  other arithmetic: 31.5 us -> 51.4 us
  matrix products: 96.4 us -> 116 us
  local copies, waits for them, and re-layouts: 60 us -> 43.7 us
    reduce_scatter x4 -> x1, waiting for transfers between devices: 225 us -> 0.02 us  [per_device(): lax.psum_scatter(core_sum(*fc_parts), FSDP, scatter_dimension=0, tiled=True)]
    pallas_call x0 -> x4, Pallas kernels: none -> 173 us  [ring_place(): pl.pallas_call(kernel, in_specs=[pl.BlockSpec(memory_space=pltpu.SMEM)] +...]
    all_gather x4 -> x1, waiting for transfers between devices: 158 us -> 46.8 us  [per_device(): fc_half = lax.all_gather(fc_mine, FSDP, axis=0, tiled=True)]
    ppermute x4 -> x36, starting transfers between devices: 15.5 us -> 60.1 us  [the longest x4 10.3 us: ring_place(): far_b = lax.ppermute(back[half:], axis, BACK)]
    ppermute x4 -> x36, waiting for transfers between devices: 13 us -> 56.4 us  [the longest x2 20.1 us: from_images(): mixed = [lax.ppermute(a, ('yh', 'core'), FLIP) for a in arrays]]
    all_to_all x3 -> x0, blocking collectives: 34.6 us -> none  [the longest x2 25.1 us: to_images(): mixed = lax.all_to_all(tokens, 'z', split_axis=0, concat_axis=0, tiled=True)]
    dot_general x31 -> x60, matrix products: 96.4 us -> 116 us  [dot(): return lax.dot_general(a, b, (dims, ((), ())), preferred_element_type=f32)]
    ppermute x28 -> x25, waiting for transfers between devices: 97.5 us -> 93.5 us  [swap(): return lax.ppermute(value, axis, [(0, 1), (1, 0)])]
  transfers between devices with their start and end apart: 43 -> 67, of which waited for: 25 -> 28; matrix products, arithmetic and copies ran while one was open for 10% -> 17% of each run, Pallas kernels for 3% -> 26%
where the time goes in v2:
time: 801 us; the launch traced here: 790 us
  Pallas kernels  240 us (30%)
  waiting for transfers between devices  214 us (27%)
  matrix products  116 us (14%)
  starting transfers between devices  108 us (13%)
  other arithmetic  51.4 us (6%)
  local copies, waits for them, and re-layouts  43.7 us (5%)
  between operations  17 us (2%)
    pallas_call x4, Pallas kernels, ring_place(): pl.pallas_call(kernel, in_specs=[pl.BlockSpec(memory_space=pltpu.SMEM)] +...  173 us
    dot_general x60, matrix products, dot(): return lax.dot_general(a, b, (dims, ((), ())), preferred_element_type=f32)  116 us
    ppermute x25, waiting for transfers between devices, swap(): return lax.ppermute(value, axis, [(0, 1), (1, 0)])  93.5 us
    all_gather x1, waiting for transfers between devices, per_device(): fc_half = lax.all_gather(fc_mine, FSDP, axis=0, tiled=True)  46.8 us
    pallas_call x2, Pallas kernels, attend_back(): pl.pallas_call(attend_back_kernel, grid=(pairs,), in_specs=[q_spec] + kv_...  37.2 us
    ppermute x25, starting transfers between devices, swap(): return lax.ppermute(value, axis, [(0, 1), (1, 0)])  35.7 us
    pallas_call x2, Pallas kernels, attend(): pl.pallas_call(attend_kernel, grid=(pairs,), in_specs=[q_spec] + kv_specs...  29.8 us
    ppermute x2, waiting for transfers between devices, from_images(): mixed = [lax.ppermute(a, ('yh', 'core'), FLIP) for a in arrays]  20.1 us
  transfers between devices with their start and end apart: 67, of which 28 were waited for; matrix products, arithmetic and copies ran while one was open for 17% of the time, Pallas kernels for 26%

profile of v2, /device:TPU:1, one launch (start us, length us, event | category | flops | bytes accessed | tf_op | source)
XLA Modules:
  0.0 790.4 jit_solution(1387994826467815115)
XLA Ops:
  27.3 17.0 %ring_place.6.refs_0_ = bf16[4,64,1024]{2,1,0:T(8,128)(2,1)} custom-call(s32[1]{0:T(128)} %bitcast.4.index_ref, bf16[64,1024]{1,0:T(8,128)(2,1)} %copy-done.70, bf16[64,1024]{1,0:T(8,128)(2,1)} %copy-done.76, bf16[64,1024]{1,0:T(8,128)(2,1)} %copy-done.77, bf16[32,1024]{1,0:T(8,128)(2,1)} %copy-done.84, bf16[32,1024]{1,0:T(8,128)(2,1)} %copy-done.85), custom_call_target="tpu_custom_call" | custom-call | bytes 1048576 | tf_op jit(solution)/shard_map/ring_place/pallas_call | solution.py:184
  47.1 46.8 %all-gather.2.cloned.1.call-done = bf16[1024,4096]{1,0:T(8,128)(2,1)} async-done(((bf16[64,4096]{1,0:T(8,128)(2,1)}), bf16[1024,4096]{1,0:T(8,128)(2,1)}) %all-gather.2.cloned.1.call-update) | async-done | bytes 8388624 | tf_op jit(solution)/shard_map/all_gather | solution.py:389
  95.5 4.0 all-to-all-start
  104.7 19.0 %ring_place.4 = bf16[4,64,1152]{2,1,0:T(8,128)(2,1)} custom-call(s32[1]{0:T(128)} %bitcast.5.index_ref, bf16[64,1152]{1,0:T(8,128)(2,1)} %copy-done.65, bf16[64,1152]{1,0:T(8,128)(2,1)} %copy-done.72, bf16[64,1152]{1,0:T(8,128)(2,1)} %copy-done.73, bf16[32,1152]{1,0:T(8,128)(2,1)} %copy-done.82, bf16[32,1152]{1,0:T(8,128)(2,1)} %copy-done.83), custom_call_target="tpu_custom_call" | custom-call | bytes 1179648 | tf_op jit(solution)/shard_map/ring_place/pallas_call | solution.py:184
  135.7 64.7 %ring_place.7 = bf16[4,4,64,1024]{3,2,1,0:T(8,128)(2,1)} custom-call(s32[1]{0:T(128)} %bitcast.5.index_ref, bf16[4,64,1024]{2,1,0:T(8,128)(2,1)} %ring_place.6.refs_0_, bf16[4,64,1024]{2,1,0:T(8,128)(2,1)} %copy-done.56, bf16[4,64,1024]{2,1,0:T(8,128)(2,1)} %collective-permute-done.15.refs_2_, bf16[2,64,1024]{2,1,0:T(8,128)(2,1)} %copy-done.78, ...), custom_call_target="tpu_custom_call" | custom-call | bytes 4194304 | tf_op jit(solution)/shard_map/ring_place/pallas_call | solution.py:184
  208.9 5.4 collective-permute-start
  215.7 72.7 %ring_place.5 = (bf16[4,256,512]{2,1,0:T(8,128)(2,1)}, bf16[4,256,512]{2,1,0:T(8,128)(2,1)}, bf16[4,256,128]{2,1,0:T(8,128)(2,1)}) custom-call(s32[1]{0:T(128)} %bitcast.4.index_ref, bf16[256,1152]{1,0:T(8,128)(2,1)} %bitcast.276, bf16[256,1152]{1,0:T(8,128)(2,1)} %copy-done.54, bf16[256,1152]{1,0:T(8,128)(2,1)} %copy-done.55, bf16[128,1152]{1,0:T(8,128)(2,1)} %copy-done.74, ...), custom_call_target="tpu_custom_call" | custom-call | bytes 4718592 | tf_op jit(solution)/shard_map/ring_place/pallas_call | solution.py:184
  298.7 21.5 %collective-permute-done.20.near_ref = bf16[256,2048]{1,0:T(8,128)(2,1)S(1)} collective-permute-done((bf16[256,2048]{1,0:T(8,128)(2,1)S(1)}, bf16[256,2048]{1,0:T(8,128)(2,1)S(1)}, u32[]{:S(2)}, u32[]{:S(2)}) %collective-permute-start.20) | collective-permute-done | bytes 1048608 | tf_op jit(solution)/shard_map/ppermute | solution.py:36
  328.9 15.6 %attend.2 = (bf16[256,1024]{1,0:T(8,128)(2,1)S(1)}, f32[8,2,256]{2,1,0:T(2,128)}) custom-call(bf16[256,1024]{1,0:T(8,128)(2,1)S(1)} %pad_maximum_fusion.9.q_ref, bf16[256,2048]{1,0:T(8,128)(2,1)S(1)} %pad_maximum_fusion.4.own_ref, bf16[256,2048]{1,0:T(8,128)(2,1)S(1)} %collective-permute-done.19.mate_ref, ...), custom_call_target="tpu_custom_call" | custom-call | tf_op jit(solution)/shard_map/attend/pallas_call | solution.py:108
  364.4 4.7 collective-permute-start.28
  369.2 6.9 collective-permute-done.24
  385.8 18.4 %collective-permute-done.26.near_ref = bf16[256,2048]{1,0:T(8,128)(2,1)S(1)} collective-permute-done((bf16[256,2048]{1,0:T(8,128)(2,1)S(1)}, bf16[256,2048]{1,0:T(8,128)(2,1)S(1)}, u32[]{:S(2)}, u32[]{:S(2)}) %collective-permute-start.26) | collective-permute-done | bytes 1048608 | tf_op jit(solution)/shard_map/ppermute | solution.py:36
  414.1 14.2 %attend.3 = (bf16[256,1024]{1,0:T(8,128)(2,1)S(1)}, f32[8,2,256]{2,1,0:T(2,128)S(1)}) custom-call(bf16[256,1024]{1,0:T(8,128)(2,1)S(1)} %pad_maximum_fusion.11.q_ref, bf16[256,2048]{1,0:T(8,128)(2,1)S(1)} %pad_maximum_fusion.5.own_ref, bf16[256,2048]{1,0:T(8,128)(2,1)S(1)} %collective-permute-done.25.mate_ref, ...), custom_call_target="tpu_custom_call" | custom-call | tf_op jit(solution)/shard_map/attend/pallas_call | solution.py:108
  436.5 5.6 fusion.43
  443.4 3.8 fusion.236
  452.5 18.6 %attend_back.2 = (bf16[256,1024]{1,0:T(8,128)(2,1)S(1)}, bf16[256,2048]{1,0:T(8,128)(2,1)S(1)}, bf16[256,2048]{1,0:T(8,128)(2,1)}, bf16[256,2048]{1,0:T(8,128)(2,1)S(1)}, bf16[256,2048]{1,0:T(8,128)(2,1)S(1)}) custom-call(bf16[256,1024]{1,0:T(8,128)(2,1)S(1)} %pad_maximum_fusion.11.q_ref, bf16[256,2048]{1,0:T(8,128)(2,1)S(1)} %pad_maximum_fusion.5.own_ref, ...), custom_call_target="tpu_custom_call" | custom-call | tf_op jit(solution)/shard_map/attend_back/pallas_call | solution.py:126
  480.5 19.6 %collective-permute-done.31 = bf16[256,2048]{1,0:T(8,128)(2,1)} collective-permute-done((bf16[256,2048]{1,0:T(8,128)(2,1)}, bf16[256,2048]{1,0:T(8,128)(2,1)}, u32[]{:S(2)}, u32[]{:S(2)}) %collective-permute-start.31) | collective-permute-done | bytes 1048608 | tf_op jit(solution)/shard_map/ppermute | solution.py:36
  512.7 10.0 %collective-permute-done.32 = bf16[256,1024]{1,0:T(8,128)(2,1)S(1)} collective-permute-done((bf16[256,1024]{1,0:T(8,128)(2,1)S(1)}, bf16[256,1024]{1,0:T(8,128)(2,1)S(1)}, u32[]{:S(2)}, u32[]{:S(2)}) %collective-permute-start.32) | collective-permute-done | bytes 524320 | tf_op jit(solution)/shard_map/ppermute | solution.py:453
  535.0 3.8 pad_maximum_fusion
  555.0 18.6 %attend_back.3 = (bf16[256,1024]{1,0:T(8,128)(2,1)S(1)}, bf16[256,2048]{1,0:T(8,128)(2,1)S(1)}, bf16[256,2048]{1,0:T(8,128)(2,1)}, bf16[256,2048]{1,0:T(8,128)(2,1)S(1)}, bf16[256,2048]{1,0:T(8,128)(2,1)}) custom-call(bf16[256,1024]{1,0:T(8,128)(2,1)S(1)} %copy-done.3, bf16[256,2048]{1,0:T(8,128)(2,1)S(1)} %pad_maximum_fusion.5.own_ref, ...), custom_call_target="tpu_custom_call" | custom-call | tf_op jit(solution)/shard_map/attend_back/pallas_call | solution.py:126
  585.5 7.8 fusion
  599.4 13.8 %collective-permute-done.35 = bf16[256,2048]{1,0:T(8,128)(2,1)} collective-permute-done((bf16[256,2048]{1,0:T(8,128)(2,1)}, bf16[256,2048]{1,0:T(8,128)(2,1)}, u32[]{:S(2)}, u32[]{:S(2)}) %collective-permute-start.35) | collective-permute-done | bytes 1048608 | tf_op jit(solution)/shard_map/ppermute | solution.py:36
  630.7 5.1 collective-permute-start.37
  641.7 11.1 %collective-permute-done.37 = bf16[256,1024]{1,0:T(8,128)(2,1)S(1)} collective-permute-done((bf16[256,1024]{1,0:T(8,128)(2,1)S(1)}, bf16[256,1024]{1,0:T(8,128)(2,1)S(1)}, u32[]{:S(2)}, u32[]{:S(2)}) %collective-permute-start.37) | collective-permute-done | bytes 524320 | tf_op jit(solution)/shard_map/ppermute | solution.py:151
  652.7 9.1 %collective-permute-done.36 = bf16[256,1024]{1,0:T(8,128)(2,1)S(1)} collective-permute-done((bf16[256,1024]{1,0:T(8,128)(2,1)S(1)}, bf16[256,1024]{1,0:T(8,128)(2,1)S(1)}, u32[]{:S(2)}, u32[]{:S(2)}) %collective-permute-start.36) | collective-permute-done | bytes 524320 | tf_op jit(solution)/shard_map/ppermute | solution.py:151
  672.8 4.1 fusion.1
  693.8 5.6 collective-permute-done.53
  706.7 3.9 collective-permute-done.56
  716.1 6.9 collective-permute-done.55
  729.5 4.3 collective-permute-start.59
  745.0 7.5 collective-permute-start.48
  758.9 13.1 %collective-permute-done.61 = bf16[64,4096]{1,0:T(8,128)(2,1)S(1)} collective-permute-done((bf16[64,4096]{1,0:T(8,128)(2,1)}, bf16[64,4096]{1,0:T(8,128)(2,1)S(1)}, u32[]{:S(2)}, u32[]{:S(2)}) %collective-permute-start.61) | collective-permute-done | bytes 524320 | tf_op jit(solution)/shard_map/ppermute | solution.py:36
  (567 shorter events, 290.3 us)
Async XLA Ops:
  7.2 86.7 %all-gather.2.cloned.1.call-start = ((), (), s32[]{:S(2)}) async-start(), calls=%async_computation.3 | async-start | bytes 8912896 | tf_op jit(solution)/shard_map/all_gather | solution.py:389
  19.2 80.4 %collective-permute-start.1 = (bf16[64,1152]{1,0:T(8,128)(2,1)S(1)}, bf16[64,1152]{1,0:T(8,128)(2,1)S(1)}, u32[]{:S(2)}, u32[]{:S(2)}) collective-permute-start(bf16[64,1152]{1,0:T(8,128)(2,1)S(1)} %fusion.200.refs_0_), channel_id=1, source_target_pairs={{0,4},{4,8},{8,12},{12,0},{1,5},{5,9},{9,13},{13,1},{2,6},{6,10},{... | collective-permute-start | bytes 442376 | tf_op jit(solution)/shard_map/ppermute | solution.py:164
  20.5 79.2 %collective-permute-start.2 = (bf16[64,1152]{1,0:T(8,128)(2,1)S(1)}, bf16[64,1152]{1,0:T(8,128)(2,1)S(1)}, u32[]{:S(2)}, u32[]{:S(2)}) collective-permute-start(bf16[64,1152]{1,0:T(8,128)(2,1)S(1)} %fusion.200.refs_0_), channel_id=1, source_target_pairs={{0,12},{4,0},{8,4},{12,8},{1,13},{5,1},{9,5},{13,9},{2,14},{6,2},{... | collective-permute-start | bytes 442376 | tf_op jit(solution)/shard_map/ppermute | solution.py:165
  44.3 82.5 %collective-permute-start.14 = (bf16[4,64,1024]{2,1,0:T(8,128)(2,1)}, bf16[4,64,1024]{2,1,0:T(8,128)(2,1)S(1)}, u32[]{:S(2)}, u32[]{:S(2)}) collective-permute-start(bf16[4,64,1024]{2,1,0:T(8,128)(2,1)} %ring_place.6.refs_0_), channel_id=1, source_target_pairs={{0,4},{4,8},{8,12},{12,0},{1,5},{5,9},{9,13},{13,1},{2,6},{6,10},{... | collective-permute-start | bytes 1572872 | tf_op jit(solution)/shard_map/ppermute | solution.py:164
  44.4 83.5 %collective-permute-start.15 = (bf16[4,64,1024]{2,1,0:T(8,128)(2,1)}, bf16[4,64,1024]{2,1,0:T(8,128)(2,1)}, u32[]{:S(2)}, u32[]{:S(2)}) collective-permute-start(bf16[4,64,1024]{2,1,0:T(8,128)(2,1)} %ring_place.6.refs_0_), channel_id=1, source_target_pairs={{0,12},{4,0},{8,4},{12,8},{1,13},{5,1},{9,5},{13,9},{2,14},{6,2},{... | collective-permute-start | bytes 1572872 | tf_op jit(solution)/shard_map/ppermute | solution.py:165
  93.9 257.8 %collective-permute-start.23 = (bf16[1024,4096]{1,0:T(8,128)(2,1)}, bf16[1024,4096]{1,0:T(8,128)(2,1)}, u32[]{:S(2)}, u32[]{:S(2)}) collective-permute-start(bf16[1024,4096]{1,0:T(8,128)(2,1)} %all-gather.2.cloned.1.call-done), channel_id=1, source_target_pairs={{0,1},{1,0},{2,3},{3,2},{4,5},{5,4},{6,7},{7,6},{8,9},{9,8},{10,11... | collective-permute-start | bytes 25165832 | tf_op jit(solution)/shard_map/ppermute | solution.py:36
  95.5 112.3 %all-to-all-start = ((bf16[4,2,64,1024]{3,2,1,0:T(8,128)(2,1)}), bf16[4,2,64,1024]{3,2,1,0:T(8,128)(2,1)S(1)}, u32[]{:S(2)}, u32[]{:S(2)}) async-start(bf16[4,2,64,1024]{3,2,1,0:T(8,128)(2,1)} %pad_maximum_fusion.3), calls=%async_computation | async-start | bytes 2097152 | tf_op jit(solution)/shard_map/all_to_all | solution.py:144
  99.5 657.1 %reduce-scatter.2.cloned.1.call-start = ((), (), s32[]{:S(2)}) async-start(), calls=%async_computation.4 | async-start | bytes 8912896 | tf_op jit(solution)/shard_map/reduce_scatter | solution.py:497
  123.8 79.4 %collective-permute-start.5 = (bf16[256,1152]{1,0:T(8,128)(2,1)}, bf16[256,1152]{1,0:T(8,128)(2,1)S(1)}, u32[]{:S(2)}, u32[]{:S(2)}) collective-permute-start(bf16[256,1152]{1,0:T(8,128)(2,1)} %bitcast.274), channel_id=1, source_target_pairs={{0,16},{16,32},{32,48},{48,0},{1,17},{17,33},{33,49},{49,1},{2,18}... | collective-permute-start | bytes 1769480 | tf_op jit(solution)/shard_map/ppermute | solution.py:164
  125.3 78.8 %collective-permute-start.6 = (bf16[256,1152]{1,0:T(8,128)(2,1)}, bf16[256,1152]{1,0:T(8,128)(2,1)S(1)}, u32[]{:S(2)}, u32[]{:S(2)}) collective-permute-start(bf16[256,1152]{1,0:T(8,128)(2,1)} %bitcast.275), channel_id=1, source_target_pairs={{0,48},{16,0},{32,16},{48,32},{1,49},{17,1},{33,17},{49,33},{2,50}... | collective-permute-start | bytes 1769480 | tf_op jit(solution)/shard_map/ppermute | solution.py:165
  200.4 93.0 %collective-permute-start.18 = (bf16[1024,1024]{1,0:T(8,128)(2,1)}, bf16[1024,1024]{1,0:T(8,128)(2,1)}, u32[]{:S(2)}, u32[]{:S(2)}) collective-permute-start(bf16[1024,1024]{1,0:T(8,128)(2,1)} %bitcast.265), channel_id=1, source_target_pairs={{0,1},{1,0},{2,3},{3,2},{4,5},{5,4},{6,7},{7,6},{8,9},{9,8},{10,11... | collective-permute-start | bytes 6291464 | tf_op jit(solution)/shard_map/ppermute | solution.py:36
  208.9 83.3 %collective-permute-start = (bf16[256,1024]{1,0:T(8,128)(2,1)}, bf16[256,1024]{1,0:T(8,128)(2,1)S(1)}, u32[]{:S(2)}, u32[]{:S(2)}) collective-permute-start(bf16[256,1024]{1,0:T(8,128)(2,1)} %bitcast.3), channel_id=1, source_target_pairs={{0,0},{1,8},{8,1},{9,9},{2,2},{3,10},{10,3},{11,11},{4,4},{5,12},{... | collective-permute-start | bytes 1572872 | tf_op jit(solution)/shard_map/ppermute | solution.py:146
  295.9 24.3 %collective-permute-start.20 = (bf16[256,2048]{1,0:T(8,128)(2,1)S(1)}, bf16[256,2048]{1,0:T(8,128)(2,1)S(1)}, u32[]{:S(2)}, u32[]{:S(2)}) collective-permute-start(bf16[256,2048]{1,0:T(8,128)(2,1)S(1)} %pad_maximum_fusion.4.own_ref), channel_id=1, source_target_pairs={{0,4},{4,0},{1,5},{5,1},{2,6},{6,2},{3,7},{7,3},{8,12},{12,8},{9,1... | collective-permute-start | bytes 3145736 | tf_op jit(solution)/shard_map/ppermute | solution.py:36
  297.0 30.0 %collective-permute-start.9 = (bf16[1024,512]{1,0:T(8,128)(2,1)}, bf16[1024,512]{1,0:T(8,128)(2,1)}, u32[]{:S(2)}, u32[]{:S(2)}) collective-permute-start(bf16[1024,512]{1,0:T(8,128)(2,1)} %bitcast.19), channel_id=1, source_target_pairs={{0,1},{1,0},{2,3},{3,2},{4,5},{5,4},{6,7},{7,6},{8,9},{9,8},{10,11... | collective-permute-start | bytes 3145736 | tf_op jit(solution)/shard_map/ppermute | solution.py:36
  298.2 48.2 %collective-permute-start.22 = (bf16[1024,512]{1,0:T(8,128)(2,1)}, bf16[1024,512]{1,0:T(8,128)(2,1)}, u32[]{:S(2)}, u32[]{:S(2)}) collective-permute-start(bf16[1024,512]{1,0:T(8,128)(2,1)} %bitcast.27), channel_id=1, source_target_pairs={{0,1},{1,0},{2,3},{3,2},{4,5},{5,4},{6,7},{7,6},{8,9},{9,8},{10,11... | collective-permute-start | bytes 3145736 | tf_op jit(solution)/shard_map/ppermute | solution.py:36
  298.2 30.7 %collective-permute-start.19 = (bf16[256,2048]{1,0:T(8,128)(2,1)S(1)}, bf16[256,2048]{1,0:T(8,128)(2,1)S(1)}, u32[]{:S(2)}, u32[]{:S(2)}) collective-permute-start(bf16[256,2048]{1,0:T(8,128)(2,1)S(1)} %pad_maximum_fusion.4.own_ref), channel_id=1, source_target_pairs={{0,1},{1,0},{2,3},{3,2},{4,5},{5,4},{6,7},{7,6},{8,9},{9,8},{10,11... | collective-permute-start | bytes 3145736 | tf_op jit(solution)/shard_map/ppermute | solution.py:36
  361.1 14.9 %collective-permute-start.24 = (bf16[256,1024]{1,0:T(8,128)(2,1)}, bf16[256,1024]{1,0:T(8,128)(2,1)S(1)}, u32[]{:S(2)}, u32[]{:S(2)}) collective-permute-start(bf16[256,1024]{1,0:T(8,128)(2,1)} %fusion.92), channel_id=1, source_target_pairs={{0,64},{1,65},{2,66},{3,67},{4,68},{5,69},{6,70},{7,71},{8,72},{9,... | collective-permute-start | bytes 1572872 | tf_op jit(solution)/shard_map/ppermute | solution.py:448
  364.4 16.9 %collective-permute-start.28 = (bf16[256,1024]{1,0:T(8,128)(2,1)}, bf16[256,1024]{1,0:T(8,128)(2,1)S(1)}, u32[]{:S(2)}, u32[]{:S(2)}) collective-permute-start(bf16[256,1024]{1,0:T(8,128)(2,1)} %bitcast.292), channel_id=1, source_target_pairs={{0,0},{1,8},{8,1},{9,9},{2,2},{3,10},{10,3},{11,11},{4,4},{5,12},{... | collective-permute-start | bytes 1572872 | tf_op jit(solution)/shard_map/ppermute | solution.py:146
  380.2 24.0 %collective-permute-start.26 = (bf16[256,2048]{1,0:T(8,128)(2,1)S(1)}, bf16[256,2048]{1,0:T(8,128)(2,1)S(1)}, u32[]{:S(2)}, u32[]{:S(2)}) collective-permute-start(bf16[256,2048]{1,0:T(8,128)(2,1)S(1)} %pad_maximum_fusion.5.own_ref), channel_id=1, source_target_pairs={{0,4},{4,0},{1,5},{5,1},{2,6},{6,2},{3,7},{7,3},{8,12},{12,8},{9,1... | collective-permute-start | bytes 3145736 | tf_op jit(solution)/shard_map/ppermute | solution.py:36
  384.7 29.4 %collective-permute-start.25 = (bf16[256,2048]{1,0:T(8,128)(2,1)S(1)}, bf16[256,2048]{1,0:T(8,128)(2,1)S(1)}, u32[]{:S(2)}, u32[]{:S(2)}) collective-permute-start(bf16[256,2048]{1,0:T(8,128)(2,1)S(1)} %pad_maximum_fusion.5.own_ref), channel_id=1, source_target_pairs={{0,1},{1,0},{2,3},{3,2},{4,5},{5,4},{6,7},{7,6},{8,9},{9,8},{10,11... | collective-permute-start | bytes 3145736 | tf_op jit(solution)/shard_map/ppermute | solution.py:36
  475.2 24.9 %collective-permute-start.31 = (bf16[256,2048]{1,0:T(8,128)(2,1)}, bf16[256,2048]{1,0:T(8,128)(2,1)}, u32[]{:S(2)}, u32[]{:S(2)}) collective-permute-start(bf16[256,2048]{1,0:T(8,128)(2,1)} %add_convert_fusion.4), channel_id=1, source_target_pairs={{0,4},{4,0},{1,5},{5,1},{2,6},{6,2},{3,7},{7,3},{8,12},{12,8},{9,1... | collective-permute-start | bytes 3145736 | tf_op jit(solution)/shard_map/ppermute | solution.py:36
  538.8 46.7 %collective-permute-start.60 = (bf16[1024,4096]{1,0:T(8,128)(2,1)}, bf16[1024,4096]{1,0:T(8,128)(2,1)}, u32[]{:S(2)}, u32[]{:S(2)}) collective-permute-start(bf16[1024,4096]{1,0:T(8,128)(2,1)} %pad_maximum_fusion), channel_id=1, source_target_pairs={{0,1},{1,0},{2,3},{3,2},{4,5},{5,4},{6,7},{7,6},{8,9},{9,8},{10,11... | collective-permute-start | bytes 25165832 | tf_op jit(solution)/shard_map/ppermute | solution.py:36
  576.3 23.0 %collective-permute-start.33 = (bf16[256,2048]{1,0:T(8,128)(2,1)}, bf16[256,2048]{1,0:T(8,128)(2,1)}, u32[]{:S(2)}, u32[]{:S(2)}) collective-permute-start(bf16[256,2048]{1,0:T(8,128)(2,1)} %get-tuple-element.43), channel_id=1, source_target_pairs={{0,1},{1,0},{2,3},{3,2},{4,5},{5,4},{6,7},{7,6},{8,9},{9,8},{10,11... | collective-permute-start | bytes 3145736 | tf_op jit(solution)/shard_map/ppermute | solution.py:36
  584.3 28.8 %collective-permute-start.35 = (bf16[256,2048]{1,0:T(8,128)(2,1)}, bf16[256,2048]{1,0:T(8,128)(2,1)}, u32[]{:S(2)}, u32[]{:S(2)}) collective-permute-start(bf16[256,2048]{1,0:T(8,128)(2,1)} %add_convert_fusion.2), channel_id=1, source_target_pairs={{0,4},{4,0},{1,5},{5,1},{2,6},{6,2},{3,7},{7,3},{8,12},{12,8},{9,1... | collective-permute-start | bytes 3145736 | tf_op jit(solution)/shard_map/ppermute | solution.py:36
  617.5 48.9 %collective-permute-start.49 = (bf16[1024,1024]{1,0:T(8,128)(2,1)}, bf16[1024,1024]{1,0:T(8,128)(2,1)}, u32[]{:S(2)}, u32[]{:S(2)}) collective-permute-start(bf16[1024,1024]{1,0:T(8,128)(2,1)} %convolution_convert_fusion.3), channel_id=1, source_target_pairs={{0,1},{1,0},{2,3},{3,2},{4,5},{5,4},{6,7},{7,6},{8,9},{9,8},{10,11... | collective-permute-start | bytes 6291464 | tf_op jit(solution)/shard_map/ppermute | solution.py:36
  629.0 43.7 %collective-permute-start.38 = (bf16[1024,1152]{0,1:T(8,128)(2,1)}, bf16[1024,1152]{0,1:T(8,128)(2,1)}, u32[]{:S(2)}, u32[]{:S(2)}) collective-permute-start(bf16[1024,1152]{0,1:T(8,128)(2,1)} %pad_maximum_fusion.1), channel_id=1, source_target_pairs={{0,1},{1,0},{2,3},{3,2},{4,5},{5,4},{6,7},{7,6},{8,9},{9,8},{10,11... | collective-permute-start | bytes 7077896 | tf_op jit(solution)/shard_map/ppermute | solution.py:36
  630.7 22.0 %collective-permute-start.37 = (bf16[256,1024]{1,0:T(8,128)(2,1)S(1)}, bf16[256,1024]{1,0:T(8,128)(2,1)S(1)}, u32[]{:S(2)}, u32[]{:S(2)}) collective-permute-start(bf16[256,1024]{1,0:T(8,128)(2,1)S(1)} %fusion.128), channel_id=1, source_target_pairs={{0,0},{1,8},{8,1},{9,9},{2,2},{3,10},{10,3},{11,11},{4,4},{5,12},{... | collective-permute-start | bytes 1572872 | tf_op jit(solution)/shard_map/ppermute | solution.py:151
  635.8 26.0 %collective-permute-start.36 = (bf16[256,1024]{1,0:T(8,128)(2,1)S(1)}, bf16[256,1024]{1,0:T(8,128)(2,1)S(1)}, u32[]{:S(2)}, u32[]{:S(2)}) collective-permute-start(bf16[256,1024]{1,0:T(8,128)(2,1)S(1)} %copy-done.93), channel_id=1, source_target_pairs={{0,0},{1,8},{8,1},{9,9},{2,2},{3,10},{10,3},{11,11},{4,4},{5,12},{... | collective-permute-start | bytes 1572872 | tf_op jit(solution)/shard_map/ppermute | solution.py:151
  662.9 50.6 %all-to-all-start.1 = ((bf16[4,2,64,1024]{3,2,1,0:T(8,128)(2,1)}), bf16[4,2,64,1024]{3,2,1,0:T(8,128)(2,1)S(1)}, u32[]{:S(2)}, u32[]{:S(2)}) async-start(bf16[4,2,64,1024]{3,2,1,0:T(8,128)(2,1)} %pad_maximum_fusion.6), calls=%async_computation.1 | async-start | bytes 2097152 | tf_op jit(solution)/shard_map/all_to_all | solution.py:153
  691.7 32.4 %collective-permute-start.42 = (bf16[4,64,1152]{2,1,0:T(8,128)(2,1)}, bf16[4,64,1152]{2,1,0:T(8,128)(2,1)}, u32[]{:S(2)}, u32[]{:S(2)}) collective-permute-start(bf16[4,64,1152]{2,1,0:T(8,128)(2,1)} %pad_maximum_fusion.8), channel_id=1, source_target_pairs={{0,12},{4,0},{8,4},{12,8},{1,13},{5,1},{9,5},{13,9},{2,14},{6,2},{... | collective-permute-start | bytes 1769480 | tf_op jit(solution)/shard_map/ppermute | solution.py:210
  705.9 18.2 %collective-permute-start.40 = (bf16[4,64,1152]{2,1,0:T(8,128)(2,1)}, bf16[4,64,1152]{2,1,0:T(8,128)(2,1)}, u32[]{:S(2)}, u32[]{:S(2)}) collective-permute-start(bf16[4,64,1152]{2,1,0:T(8,128)(2,1)} %pad_maximum_fusion.7), channel_id=1, source_target_pairs={{0,4},{4,8},{8,12},{12,0},{1,5},{5,9},{9,13},{13,1},{2,6},{6,10},{... | collective-permute-start | bytes 1769480 | tf_op jit(solution)/shard_map/ppermute | solution.py:209
  756.6 15.3 %collective-permute-start.61 = (bf16[64,4096]{1,0:T(8,128)(2,1)}, bf16[64,4096]{1,0:T(8,128)(2,1)S(1)}, u32[]{:S(2)}, u32[]{:S(2)}) collective-permute-start(bf16[64,4096]{1,0:T(8,128)(2,1)} %reduce-scatter.2.cloned.1.call-done), channel_id=1, source_target_pairs={{0,2},{2,0},{1,3},{3,1},{4,6},{6,4},{5,7},{7,5},{8,10},{10,8},{9,1... | collective-permute-start | bytes 1572872 | tf_op jit(solution)/shard_map/ppermute | solution.py:36
  (136 other events, 1192.0 us)
Sparse Core Ops, SparseCore 0:
  12.1 81.7 all-gather.1
  593.5 99.0 reduce-scatter.1

commit v3 on v2

--- a/solution.py
+++ b/solution.py
@@ -135,6 +135,61 @@
     )(queries, *blocks, grad, log_total)
 
 
+def fc_outer(normed, grad_before, activated, grad_branch, add=None):
+    rows, width = normed.shape
+    wide = grad_before.shape[1]
+    step = min(512, width)
+    first = wide // step
+    per = width // step
+    blocks = first + (wide // width) * per
+    second = lambda i: jnp.maximum(i - first, 0)
+
+    def kernel(n_ref, b_ref, a_ref, g_ref, *rest):
+        out_ref = rest[-1]
+        i = pl.program_id(0)
+        more = rest[0][...].astype(f32) if add is not None else 0.0
+
+        @pl.when(i < first)
+        def _():
+            out_ref[...] = (mm(n_ref[...], b_ref[...]) + more).astype(bf16)
+
+        @pl.when(i >= first)
+        def _():
+            out_ref[...] = (mm(a_ref[...], g_ref[...]) + more).astype(bf16)
+
+    out_spec = pl.BlockSpec((width, step), lambda i: (0, i))
+    in_specs = [
+        pl.BlockSpec((width, rows), lambda i: (0, 0)),
+        pl.BlockSpec((rows, step), lambda i: (0, jnp.minimum(i, first - 1))),
+        pl.BlockSpec((width, rows), lambda i: (second(i) // per, 0)),
+        pl.BlockSpec((rows, step), lambda i: (0, second(i) % per)),
+    ]
+    operands = [normed.T, grad_before, activated.T, grad_branch]
+    if add is not None:
+        in_specs.append(out_spec)
+        operands.append(add)
+    return pl.pallas_call(
+        kernel,
+        grid=(blocks,),
+        in_specs=in_specs,
+        out_specs=out_spec,
+        out_shape=jax.ShapeDtypeStruct((width, blocks * step), bf16),
+        compiler_params=pltpu.CompilerParams(vmem_limit_bytes=40 * 2**20),
+        cost_estimate=pl.CostEstimate(
+            flops=2 * rows * width * blocks * step,
+            bytes_accessed=2 * width * blocks * step * (1 if add is None else 2),
+            transcendentals=0,
+        ),
+        name="fc_outer",
+    )(*operands)
+
+
+def fc_sum(normed, grad_before, activated, grad_branch):
+    parts = list(zip(grad_before, activated))
+    sent = swap(fc_outer(normed, *parts[1], grad_branch), "core")
+    return fc_outer(normed, *parts[0], grad_branch, add=sent)
+
+
 FLIP = [(0, 0), (1, 2), (2, 1), (3, 3)]
 
 
@@ -169,31 +224,27 @@
     n_outs = len(out_shapes)
 
     def kernel(index_ref, *refs):
-        sources, outs, sems = refs[:5], refs[5 : 5 + n_outs], refs[5 + n_outs]
-        copies = []
+        sources, outs = refs[:5], refs[5:]
         for source, (_, step, start) in zip(sources, pieces):
             place = lax.rem(index_ref[0] + step, 4)
-            for src, dst in views(outs, source, place, start):
-                copies.append(pltpu.make_async_copy(src, dst, sems.at[len(copies)]))
-        for copy in copies:
-            copy.start()
-        for copy in copies:
-            copy.wait()
-
-    size = 2 * sum(2 * value.size * 4 for _ in range(1))
+            views(outs, source, place, start)
+
+    vmem = pl.BlockSpec(memory_space=pltpu.VMEM)
     return pl.pallas_call(
         kernel,
-        in_specs=[pl.BlockSpec(memory_space=pltpu.SMEM)] + [pl.BlockSpec(memory_space=pl.ANY)] * 5,
-        out_specs=[pl.BlockSpec(memory_space=pl.ANY)] * n_outs,
+        in_specs=[pl.BlockSpec(memory_space=pltpu.SMEM)] + [vmem] * 5,
+        out_specs=[vmem] * n_outs,
         out_shape=[jax.ShapeDtypeStruct(shape, value.dtype) for shape in out_shapes],
-        scratch_shapes=[pltpu.SemaphoreType.DMA((5 * max(n_outs, 1),))],
-        cost_estimate=pl.CostEstimate(flops=0, bytes_accessed=size, transcendentals=0),
+        compiler_params=pltpu.CompilerParams(vmem_limit_bytes=24 * 2**20),
+        cost_estimate=pl.CostEstimate(
+            flops=0, bytes_accessed=16 * value.size, transcendentals=0
+        ),
         name="ring_place",
     )(lax.axis_index(axis).reshape(1), *(p[0] for p in pieces))
 
 
 def in_order(outs, piece, place, start):
-    return [(piece, outs[0].at[place, pl.ds(start, piece.shape[0])])]
+    outs[0][place, pl.ds(start, piece.shape[0])] = piece[...]
 
 
 def ring_sum(blocks, axis):
@@ -244,19 +295,36 @@
     return jnp.where(core == 0, value, turned)
 
 
-def forward(tokens, w):
+CHUNKS = 2
+
+
+def chunked(halves):
+    size = halves[0].shape[1] // CHUNKS
+    cut = lambda h, i: h[:, i * size : (i + 1) * size]
+    return [jnp.concatenate([cut(h, i) for h in halves], axis=1) for i in range(CHUNKS)]
+
+
+def unchunked(chunks):
+    size = chunks[0].shape[1] // 2
+    return [
+        jnp.concatenate([c[:, i * size : (i + 1) * size] for c in chunks], axis=1)
+        for i in range(2)
+    ]
+
+
+def forward(tokens, w, late=None):
     inputs = tokens.astype(f32)
     normed_one = (normal_part(inputs)[0] * w["gain"][0] + w["shift"][0]).astype(bf16)
-    project = lambda name: jnp.concatenate(
-        [
-            (mm(normed_one, part) + bias).astype(bf16)
-            for part, bias in zip(w[name], w[name + "_bias"])
-        ],
-        axis=1,
-    )
-    blocks = group_blocks(project("kv"))
-    queries = project("q")
-    attended, log_total = attend(queries, blocks)
+    project = lambda name: [
+        (mm(normed_one, part) + bias).astype(bf16) for part, bias in zip(w[name], w[name + "_bias"])
+    ]
+    blocks = [group_blocks(c) for c in chunked(project("kv"))]
+    queries = chunked(project("q"))
+    if late is not None:
+        blocks[0], gathered = lax.optimization_barrier((blocks[0], late[0]))
+        w.update(late[1](gathered))
+    attended, log_total = zip(*(attend(q, b) for q, b in zip(queries, blocks)))
+    attended = jnp.concatenate(unchunked(attended), axis=1)
     attended = flip_halves(w["core"], attended)
     branch = flip_halves(w["core"], jnp.concatenate([mm(attended, p) for p in w["proj"]], axis=1))
     branch = branch + w["out_bias"][0]
@@ -291,7 +359,7 @@
     return result, kept
 
 
-def backward(grad_out, kept, w):
+def backward(grad_out, kept, w, fc_sum=None):
     grad_branch_two = (w["scale"][1] * grad_out).astype(bf16)
     grad_before = []
     grad_normed_two = 0.0
@@ -309,11 +377,19 @@
     grad_halves = [grad_halves[:, :half], grad_halves[:, half:]]
     grad_attended = sum(mm_t(g, p) for g, p in zip(grad_halves, w["proj"])).astype(bf16)
     grad_attended = flip_halves(w["core"], grad_attended)
-    parts = attend_back(kept["queries"], kept["blocks"], grad_attended, kept["log_total"])
-    grad_queries = parts[0]
-    grad_key_value = group_sum(*parts[1:])
-    grad_q = [grad_queries[:, i * half : (i + 1) * half] for i in range(2)]
-    grad_kv = [grad_key_value[:, i * width : (i + 1) * width] for i in range(2)]
+    fc_grad = None
+    if fc_sum is not None:
+        fc_grad = fc_sum(
+            kept["normed_two"], grad_before, kept["activated"], grad_branch_two
+        )
+        fc_grad, grad_attended = lax.optimization_barrier((fc_grad, grad_attended))
+    grad_chunks = chunked([grad_attended[:, :half], grad_attended[:, half:]])
+    q_chunks, kv_chunks = [], []
+    for q, b, g, t in zip(kept["queries"], kept["blocks"], grad_chunks, kept["log_total"]):
+        parts = attend_back(q, b, g, t)
+        q_chunks.append(parts[0])
+        kv_chunks.append(group_sum(*parts[1:]))
+    grad_q, grad_kv = unchunked(q_chunks), unchunked(kv_chunks)
     grad_normed_one = sum(
         mm_t(g, part) for g, part in zip(grad_q + grad_kv, w["q"] + w["kv"])
     )
@@ -333,8 +409,7 @@
         q=(kept["normed_one"], grad_q),
         kv=(kept["normed_one"], grad_kv),
         proj=(kept["attended"], grad_halves),
-        fc1=(kept["normed_two"], grad_before),
-        fc2=(kept["activated"], grad_branch_two),
+        fc=fc_grad,
     )
     return grad_inputs.astype(bf16), vectors, outer
 
@@ -394,12 +469,15 @@
     b_row = ring_place(kv_mine, RING_Z, [(4, own, width)], in_order)[0]
 
     def a_views(outs, piece, place, start):
-        rows = pl.ds(start, piece.shape[0])
-        columns = [pl.ds(0, half), pl.ds(half, half), pl.ds(width, 128)]
-        return [(piece.at[:, c], out.at[place, rows]) for c, out in zip(columns, outs)]
+        at = 0
+        for out in outs:
+            size = out.shape[-1]
+            out[place, pl.ds(start, piece.shape[0])] = piece[:, pl.ds(at, size)]
+            at += size
 
     def b_views(outs, piece, place, start):
-        return [(piece, outs[0].at[pl.ds(start, piece.shape[0]), place])]
+        for i in range(piece.shape[0]):
+            outs[0][start + i, place] = piece[i]
 
     q_half, proj_half, vectors = (
         o.reshape(width, -1)
@@ -420,7 +498,6 @@
         return jnp.concatenate([jnp.zeros_like(v_part), v_part], axis=1).reshape(width)
 
     wide = shards * mid
-    fc_pair = (fc_half, swap(fc_half, "core"))
     w = dict(
         core=core,
         gain=vectors[0:2],
@@ -432,19 +509,25 @@
         kv=[kv_half, swap(kv_half, "core")],
         kv_bias=[kv_bias(b) for b in halves(vectors[5])],
         proj=(proj_half, swap(proj_half, "core")),
-        fc1=[f[:, :wide] for f in fc_pair],
         fc1_bias=[
             jnp.swapaxes(pick(fc1_b, c, 1), 0, 1).reshape(-1) for c in (core, 1 - core)
         ],
-        fc2=[(f[:, wide : wide + width], f[:, wide + width :]) for f in fc_pair],
-    )
+    )
+
+    def fc_weights(gathered):
+        pair = (gathered, swap(gathered, "core"))
+        return dict(
+            fc1=[f[:, :wide] for f in pair],
+            fc2=[(f[:, wide : wide + width], f[:, wide + width :]) for f in pair],
+        )
+
 
     live = (
         jnp.arange(images) % IMG_MB < jnp.repeat(batch_counts[0], IMG_MB)
     ).astype(bf16)
     first_tokens, last_grad = to_images([patch_tokens, out_grad * live[:, None, None]])
 
-    sent, _ = forward(first_tokens, w)
+    sent, _ = forward(first_tokens, w, late=(fc_half, fc_weights))
     passed = lax.ppermute(sent, "section", [(0, 1)])
     tokens = jnp.where(section == 0, first_tokens, passed)
     result, kept = forward(tokens, w)
@@ -452,7 +535,7 @@
     sent, _, _ = backward(last_grad.astype(f32), kept, w)
     passed = lax.ppermute(sent, "section", [(1, 0)])
     grad_out = jnp.where(section == 1, last_grad, passed).astype(f32)
-    grad_inputs, sums, outer = backward(grad_out, kept, w)
+    grad_inputs, sums, outer = backward(grad_out, kept, w, fc_sum)
     result, grad_inputs = lax.optimization_barrier((result, grad_inputs))
     block_out, in_grad = from_images([result, grad_inputs], images)
 
@@ -488,13 +571,7 @@
     )
     vector_grads = jnp.pad(vector_grads, ((0, 0), (0, 128 - count)))
 
-    a2, du = outer["fc1"]
-    z, e2 = outer["fc2"]
-    fc_parts = [
-        jnp.concatenate([t_mm(a2, du[i]), t_mm(z[i][:, :width], e2), t_mm(z[i][:, width:], e2)], 1)
-        for i in range(2)
-    ]
-    fc_grad = lax.psum_scatter(core_sum(*fc_parts), FSDP, scatter_dimension=0, tiled=True)
+    fc_grad = lax.psum_scatter(outer["fc"], FSDP, scatter_dimension=0, tiled=True)
     a1, dq = outer["q"]
     dkv = outer["kv"][1]
     o, e1 = outer["proj"]

time: 801 us -> 689 us (0.86)
  Pallas kernels: 240 us -> 85.1 us
  local copies, waits for them, and re-layouts: 43.7 us -> 88.6 us
  waiting for transfers between devices: 214 us -> 198 us
  starting transfers between devices: 108 us -> 118 us
    pallas_call x4, Pallas kernels: 173 us -> 2.42 us  [ring_place(): pl.pallas_call(kernel, in_specs=[pl.BlockSpec(memory_space=pltpu.SMEM)] +...]
    all_gather x1, waiting for transfers between devices: 46.8 us -> 0.01 us  [per_device(): fc_half = lax.all_gather(fc_mine, FSDP, axis=0, tiled=True)]
    unnamed x207 -> x325, local copies, waits for them, and re-layouts: 10.8 us -> 30.7 us
    ppermute x25 -> x37, waiting for transfers between devices: 93.5 us -> 113 us  [swap(): return lax.ppermute(value, axis, [(0, 1), (1, 0)])]
    ppermute x4, waiting for transfers between devices: 0.01 us -> 18.7 us  [ring_place(): back = lax.ppermute(value, axis, BACK)]
    ppermute x2, waiting for transfers between devices: 20.1 us -> 4.69 us  [from_images(): mixed = [lax.ppermute(a, ('yh', 'core'), FLIP) for a in arrays]]
    pallas_call x0 -> x2, Pallas kernels: none -> 14.9 us  [fc_outer(): pl.pallas_call(kernel, grid=(blocks,), in_specs=in_specs, out_specs=out_s...]
    ppermute x25 -> x37, starting transfers between devices: 35.7 us -> 48.5 us  [swap(): return lax.ppermute(value, axis, [(0, 1), (1, 0)])]
  transfers between devices with their start and end apart: 67 -> 79, of which waited for: 28 -> 29; matrix products, arithmetic and copies ran while one was open for 17% -> 22% of each run, Pallas kernels for 26% -> 7%
where the time goes in v3:
time: 689 us; the launch traced here: 676 us
  waiting for transfers between devices  198 us (29%)
  starting transfers between devices  118 us (17%)
  matrix products  110 us (16%)
  local copies, waits for them, and re-layouts  88.6 us (13%)
  Pallas kernels  85.1 us (12%)
  other arithmetic  58.9 us (9%)
  between operations  17.5 us (3%)
    ppermute x37, waiting for transfers between devices, swap(): return lax.ppermute(value, axis, [(0, 1), (1, 0)])  113 us
    dot_general x54, matrix products, dot(): return lax.dot_general(a, b, (dims, ((), ())), preferred_element_type=f32)  110 us
    ppermute x37, starting transfers between devices, swap(): return lax.ppermute(value, axis, [(0, 1), (1, 0)])  48.5 us
    pallas_call x4, Pallas kernels, attend_back(): pl.pallas_call(attend_back_kernel, grid=(pairs,), in_specs=[q_spec] + kv_...  37.3 us
    unnamed x325, local copies, waits for them, and re-layouts  30.7 us
    pallas_call x4, Pallas kernels, attend(): pl.pallas_call(attend_kernel, grid=(pairs,), in_specs=[q_spec] + kv_specs...  30.5 us
    ppermute x4, waiting for transfers between devices, ring_place(): back = lax.ppermute(value, axis, BACK)  18.7 us
    pallas_call x2, Pallas kernels, fc_outer(): pl.pallas_call(kernel, grid=(blocks,), in_specs=in_specs, out_specs=out_s...  14.9 us
  transfers between devices with their start and end apart: 79, of which 29 were waited for; matrix products, arithmetic and copies ran while one was open for 22% of the time, Pallas kernels for 7%

profile of v3, /device:TPU:1, one launch (start us, length us, event | category | flops | bytes accessed | tf_op | source)
XLA Modules:
  0.0 676.5 jit_solution(3594398117838056663)
XLA Ops:
  13.1 4.7 collective-permute-start.11
  41.7 6.5 collective-permute-done.4.refs_4_
  55.8 18.7 %collective-permute-done.6.refs_2_ = bf16[256,1152]{1,0:T(8,128)(2,1)S(1)} collective-permute-done((bf16[256,1152]{1,0:T(8,128)(2,1)S(1)}, bf16[256,1152]{1,0:T(8,128)(2,1)S(1)}, u32[]{:S(2)}, u32[]{:S(2)}) %collective-permute-start.6) | collective-permute-done | bytes 589856 | tf_op jit(solution)/shard_map/ppermute | solution.py:220
  81.8 5.2 collective-permute-start.18
  118.7 6.7 collective-permute-done.20.near_ref
  148.2 8.4 %collective-permute-done.23.near_ref = bf16[256,1024]{1,0:T(8,128)(2,1)} collective-permute-done((bf16[256,1024]{1,0:T(8,128)(2,1)}, bf16[256,1024]{1,0:T(8,128)(2,1)}, u32[]{:S(2)}, u32[]{:S(2)}) %collective-permute-start.23) | collective-permute-done | bytes 524320 | tf_op jit(solution)/shard_map/ppermute | solution.py:36
  159.4 8.8 %attend.5 = (bf16[256,512]{1,0:T(8,128)(2,1)S(1)}, f32[4,2,256]{2,1,0:T(2,128)}) custom-call(bf16[256,512]{1,0:T(8,128)(2,1)S(1)} %pad_maximum_fusion.16.q_ref, bf16[256,1024]{1,0:T(8,128)(2,1)} %pad_maximum_fusion.8.own_ref, bf16[256,1024]{1,0:T(8,128)(2,1)S(1)} %collective-permute-done.22.mate_ref, bf16[256,1024]{1,0:T(8,128)(2,1)} %collective-permute-done.23.near_ref, ...), custom_call_target="tpu_custom_call" | custom-call | tf_op jit(solution)/shard_map/attend/pallas_call | solution.py:108
  168.3 7.6 %attend.4 = (bf16[256,512]{1,0:T(8,128)(2,1)S(1)}, f32[4,2,256]{2,1,0:T(2,128)}) custom-call(bf16[256,512]{1,0:T(8,128)(2,1)S(1)} %pad_maximum_fusion.15.q_ref, bf16[256,1024]{1,0:T(8,128)(2,1)S(1)} %copy-done.35, bf16[256,1024]{1,0:T(8,128)(2,1)S(1)} %copy-done.45, bf16[256,1024]{1,0:T(8,128)(2,1)S(1)} %copy-done.43, bf16[256,1024]{1,0:T(8,128)(2,1)S(1)} %copy-done.47), custom_call_target="tpu_custom_call" | custom-call | tf_op jit(solution)/shard_map/attend/pallas_call | solution.py:108
  221.1 7.3 %collective-permute-done.32.near_ref = bf16[256,1024]{1,0:T(8,128)(2,1)S(1)} collective-permute-done((bf16[256,1024]{1,0:T(8,128)(2,1)S(1)}, bf16[256,1024]{1,0:T(8,128)(2,1)S(1)}, u32[]{:S(2)}, u32[]{:S(2)}) %collective-permute-start.32) | collective-permute-done | bytes 524320 | tf_op jit(solution)/shard_map/ppermute | solution.py:36
  231.3 8.3 %collective-permute-done.29.near_ref = bf16[256,1024]{1,0:T(8,128)(2,1)S(1)} collective-permute-done((bf16[256,1024]{1,0:T(8,128)(2,1)S(1)}, bf16[256,1024]{1,0:T(8,128)(2,1)S(1)}, u32[]{:S(2)}, u32[]{:S(2)}) %collective-permute-start.29) | collective-permute-done | bytes 524320 | tf_op jit(solution)/shard_map/ppermute | solution.py:36
  241.4 7.0 %attend.7 = (bf16[256,512]{1,0:T(8,128)(2,1)S(1)}, f32[4,2,256]{2,1,0:T(2,128)S(1)}) custom-call(bf16[256,512]{1,0:T(8,128)(2,1)S(1)} %pad_maximum_fusion.18.q_ref, bf16[256,1024]{1,0:T(8,128)(2,1)S(1)} %pad_maximum_fusion.10.own_ref, bf16[256,1024]{1,0:T(8,128)(2,1)S(1)} %collective-permute-done.31.mate_ref, ...), custom_call_target="tpu_custom_call" | custom-call | tf_op jit(solution)/shard_map/attend/pallas_call | solution.py:108
  248.5 7.0 %attend.6 = (bf16[256,512]{1,0:T(8,128)(2,1)S(1)}, f32[4,2,256]{2,1,0:T(2,128)S(1)}) custom-call(bf16[256,512]{1,0:T(8,128)(2,1)S(1)} %pad_maximum_fusion.17.q_ref, bf16[256,1024]{1,0:T(8,128)(2,1)S(1)} %pad_maximum_fusion.9.own_ref, bf16[256,1024]{1,0:T(8,128)(2,1)S(1)} %collective-permute-done.28.mate_ref, ...), custom_call_target="tpu_custom_call" | custom-call | tf_op jit(solution)/shard_map/attend/pallas_call | solution.py:108
  261.9 6.3 fusion.42
  280.8 9.6 %attend_back.5 = (bf16[256,512]{1,0:T(8,128)(2,1)S(1)}, bf16[256,1024]{1,0:T(8,128)(2,1)S(1)}, bf16[256,1024]{1,0:T(8,128)(2,1)}, bf16[256,1024]{1,0:T(8,128)(2,1)S(1)}, bf16[256,1024]{1,0:T(8,128)(2,1)S(1)}) custom-call(bf16[256,512]{1,0:T(8,128)(2,1)S(1)} %pad_maximum_fusion.18.q_ref, bf16[256,1024]{1,0:T(8,128)(2,1)S(1)} %pad_maximum_fusion.10.own_ref, ...), custom_call_target="tpu_custom_call" | custom-call | tf_op jit(solution)/shard_map/attend_back/pallas_call | solution.py:126
  291.2 9.8 %attend_back.4 = (bf16[256,512]{1,0:T(8,128)(2,1)S(1)}, bf16[256,1024]{1,0:T(8,128)(2,1)S(1)}, bf16[256,1024]{1,0:T(8,128)(2,1)}, bf16[256,1024]{1,0:T(8,128)(2,1)S(1)}, bf16[256,1024]{1,0:T(8,128)(2,1)S(1)}) custom-call(bf16[256,512]{1,0:T(8,128)(2,1)S(1)} %pad_maximum_fusion.17.q_ref, bf16[256,1024]{1,0:T(8,128)(2,1)S(1)} %pad_maximum_fusion.9.own_ref, ...), custom_call_target="tpu_custom_call" | custom-call | tf_op jit(solution)/shard_map/attend_back/pallas_call | solution.py:126
  313.7 6.6 collective-permute-done.40
  322.1 9.5 %collective-permute-done.37 = bf16[256,1024]{1,0:T(8,128)(2,1)} collective-permute-done((bf16[256,1024]{1,0:T(8,128)(2,1)}, bf16[256,1024]{1,0:T(8,128)(2,1)}, u32[]{:S(2)}, u32[]{:S(2)}) %collective-permute-start.37) | collective-permute-done | bytes 524320 | tf_op jit(solution)/shard_map/ppermute | solution.py:36
  341.3 11.8 %collective-permute-done.41 = bf16[256,1024]{1,0:T(8,128)(2,1)S(1)} collective-permute-done((bf16[256,1024]{1,0:T(8,128)(2,1)S(1)}, bf16[256,1024]{1,0:T(8,128)(2,1)S(1)}, u32[]{:S(2)}, u32[]{:S(2)}) %collective-permute-start.41) | collective-permute-done | bytes 524320 | tf_op jit(solution)/shard_map/ppermute | solution.py:536
  371.0 6.7 fc_outer.2
  398.2 4.5 multiply_reduce_fusion.1
  409.7 8.3 %fc_outer.3 = bf16[1024,4096]{1,0:T(8,128)(2,1)S(1)} custom-call(bf16[1024,256]{1,0:T(8,128)(2,1)S(1)} %copy-done.2, bf16[256,2048]{1,0:T(8,128)(2,1)S(1)} %copy-done.22, bf16[2048,256]{1,0:T(8,128)(2,1)S(1)} %copy-done.19, bf16[256,1024]{1,0:T(8,128)(2,1)S(1)} %copy-done.6, bf16[1024,4096]{1,0:T(8,128)(2,1)} %collective-permute-done.42.rest_0_), custom_call_target="tpu_custom_call" | custom-call | flops 2147483648 | bytes 16777216 | tf_op jit(solution)/shard_map/fc_outer/pallas_call | solution.py:171
  427.2 9.0 %attend_back.6 = (bf16[256,512]{1,0:T(8,128)(2,1)S(1)}, bf16[256,1024]{1,0:T(8,128)(2,1)S(1)}, bf16[256,1024]{1,0:T(8,128)(2,1)S(1)}, bf16[256,1024]{1,0:T(8,128)(2,1)S(1)}, bf16[256,1024]{1,0:T(8,128)(2,1)S(1)}) custom-call(bf16[256,512]{1,0:T(8,128)(2,1)S(1)} %copy-done.21, bf16[256,1024]{1,0:T(8,128)(2,1)S(1)} %pad_maximum_fusion.9.own_ref, ...), custom_call_target="tpu_custom_call" | custom-call | tf_op jit(solution)/shard_map/attend_back/pallas_call | solution.py:126
  443.5 9.0 %attend_back.7 = (bf16[256,512]{1,0:T(8,128)(2,1)S(1)}, bf16[256,1024]{1,0:T(8,128)(2,1)S(1)}, bf16[256,1024]{1,0:T(8,128)(2,1)S(1)}, bf16[256,1024]{1,0:T(8,128)(2,1)S(1)}, bf16[256,1024]{1,0:T(8,128)(2,1)S(1)}) custom-call(bf16[256,512]{1,0:T(8,128)(2,1)S(1)} %pad_maximum_fusion.18.q_ref, bf16[256,1024]{1,0:T(8,128)(2,1)S(1)} %pad_maximum_fusion.10.own_ref, ...), custom_call_target="tpu_custom_call" | custom-call | tf_op jit(solution)/shard_map/attend_back/pallas_call | solution.py:126
  460.7 22.4 %collective-permute-done.48 = bf16[256,1024]{1,0:T(8,128)(2,1)S(1)} collective-permute-done((bf16[256,1024]{1,0:T(8,128)(2,1)S(1)}, bf16[256,1024]{1,0:T(8,128)(2,1)S(1)}, u32[]{:S(2)}, u32[]{:S(2)}) %collective-permute-start.48) | collective-permute-done | bytes 524320 | tf_op jit(solution)/shard_map/ppermute | solution.py:36
  483.5 22.1 %collective-permute-done.45 = bf16[256,1024]{1,0:T(8,128)(2,1)S(1)} collective-permute-done((bf16[256,1024]{1,0:T(8,128)(2,1)S(1)}, bf16[256,1024]{1,0:T(8,128)(2,1)S(1)}, u32[]{:S(2)}, u32[]{:S(2)}) %collective-permute-start.45) | collective-permute-done | bytes 524320 | tf_op jit(solution)/shard_map/ppermute | solution.py:36
  524.8 5.1 collective-permute-start.50
  538.9 4.7 collective-permute-done.50
  555.3 4.6 fusion
  568.6 6.8 collective-permute-done.54
  585.9 7.8 %collective-permute-done.69 = bf16[32,1024]{1,0:T(8,128)(2,1)S(1)} collective-permute-done((bf16[32,1024]{1,0:T(8,128)(2,1)S(1)}, bf16[32,1024]{1,0:T(8,128)(2,1)S(1)}, u32[]{:S(2)}, u32[]{:S(2)}) %collective-permute-start.69) | collective-permute-done | bytes 65568 | tf_op jit(solution)/shard_map/ppermute | solution.py:257
  625.8 6.1 collective-permute-start.61
  636.5 14.9 %collective-permute-done.73 = bf16[64,4096]{1,0:T(8,128)(2,1)S(1)} collective-permute-done((bf16[64,4096]{1,0:T(8,128)(2,1)}, bf16[64,4096]{1,0:T(8,128)(2,1)S(1)}, u32[]{:S(2)}, u32[]{:S(2)}) %collective-permute-start.73) | collective-permute-done | bytes 524320 | tf_op jit(solution)/shard_map/ppermute | solution.py:36
  (744 shorter events, 377.3 us)
Async XLA Ops:
  7.2 124.4 %all-gather.2.cloned.1.call-start = ((), (), s32[]{:S(2)}) async-start(), calls=%async_computation.3 | async-start | bytes 8912896 | tf_op jit(solution)/shard_map/all_gather | solution.py:464
  19.1 19.7 %collective-permute-start.2 = (bf16[64,1152]{1,0:T(8,128)(2,1)S(1)}, bf16[64,1152]{1,0:T(8,128)(2,1)S(1)}, u32[]{:S(2)}, u32[]{:S(2)}) collective-permute-start(bf16[64,1152]{1,0:T(8,128)(2,1)S(1)} %fusion.200.refs_0_), channel_id=1, source_target_pairs={{0,12},{4,0},{8,4},{12,8},{1,13},{5,1},{9,5},{13,9},{2,14},{6,2},{... | collective-permute-start | bytes 442376 | tf_op jit(solution)/shard_map/ppermute | solution.py:220
  21.9 19.7 %collective-permute-start.1 = (bf16[64,1152]{1,0:T(8,128)(2,1)S(1)}, bf16[64,1152]{1,0:T(8,128)(2,1)S(1)}, u32[]{:S(2)}, u32[]{:S(2)}) collective-permute-start(bf16[64,1152]{1,0:T(8,128)(2,1)S(1)} %fusion.200.refs_0_), channel_id=1, source_target_pairs={{0,4},{4,8},{8,12},{12,0},{1,5},{5,9},{9,13},{13,1},{2,6},{6,10},{... | collective-permute-start | bytes 442376 | tf_op jit(solution)/shard_map/ppermute | solution.py:219
  29.3 23.9 %collective-permute-start.15 = (bf16[4,64,1024]{2,1,0:T(8,128)(2,1)S(1)}, bf16[4,64,1024]{2,1,0:T(8,128)(2,1)S(1)}, u32[]{:S(2)}, u32[]{:S(2)}) collective-permute-start(bf16[4,64,1024]{2,1,0:T(8,128)(2,1)S(1)} %ring_place.6.refs_0_), channel_id=1, source_target_pairs={{0,12},{4,0},{8,4},{12,8},{1,13},{5,1},{9,5},{13,9},{2,14},{6,2},{... | collective-permute-start | bytes 1572872 | tf_op jit(solution)/shard_map/ppermute | solution.py:220
  32.4 21.0 %collective-permute-start.14 = (bf16[4,64,1024]{2,1,0:T(8,128)(2,1)S(1)}, bf16[4,64,1024]{2,1,0:T(8,128)(2,1)}, u32[]{:S(2)}, u32[]{:S(2)}) collective-permute-start(bf16[4,64,1024]{2,1,0:T(8,128)(2,1)S(1)} %ring_place.6.refs_0_), channel_id=1, source_target_pairs={{0,4},{4,8},{8,12},{12,0},{1,5},{5,9},{9,13},{13,1},{2,6},{6,10},{... | collective-permute-start | bytes 1572872 | tf_op jit(solution)/shard_map/ppermute | solution.py:219
  34.5 52.4 %all-to-all-start = ((bf16[4,2,64,1024]{3,2,1,0:T(8,128)(2,1)}), bf16[4,2,64,1024]{3,2,1,0:T(8,128)(2,1)}, u32[]{:S(2)}, u32[]{:S(2)}) async-start(bf16[4,2,64,1024]{3,2,1,0:T(8,128)(2,1)} %pad_maximum_fusion.2), calls=%async_computation | async-start | bytes 2097152 | tf_op jit(solution)/shard_map/all_to_all | solution.py:199
  38.8 597.3 %reduce-scatter.2.cloned.1.call-start = ((), (), s32[]{:S(2)}) async-start(), calls=%async_computation.4 | async-start | bytes 8912896 | tf_op jit(solution)/shard_map/reduce_scatter | solution.py:574
  51.6 22.9 %collective-permute-start.6 = (bf16[256,1152]{1,0:T(8,128)(2,1)S(1)}, bf16[256,1152]{1,0:T(8,128)(2,1)S(1)}, u32[]{:S(2)}, u32[]{:S(2)}) collective-permute-start(bf16[256,1152]{1,0:T(8,128)(2,1)S(1)} %bitcast.303), channel_id=1, source_target_pairs={{0,48},{16,0},{32,16},{48,32},{1,49},{17,1},{33,17},{49,33},{2,50}... | collective-permute-start | bytes 1769480 | tf_op jit(solution)/shard_map/ppermute | solution.py:220
  52.4 26.4 %collective-permute-start.5 = (bf16[256,1152]{1,0:T(8,128)(2,1)S(1)}, bf16[256,1152]{1,0:T(8,128)(2,1)S(1)}, u32[]{:S(2)}, u32[]{:S(2)}) collective-permute-start(bf16[256,1152]{1,0:T(8,128)(2,1)S(1)} %bitcast.304), channel_id=1, source_target_pairs={{0,16},{16,32},{32,48},{48,0},{1,17},{17,33},{33,49},{49,1},{2,18}... | collective-permute-start | bytes 1769480 | tf_op jit(solution)/shard_map/ppermute | solution.py:219
  53.2 27.4 %collective-permute-start.17 = (bf16[2,64,1024]{2,1,0:T(8,128)(2,1)S(1)}, bf16[2,64,1024]{2,1,0:T(8,128)(2,1)S(1)}, u32[]{:S(2)}, u32[]{:S(2)}) collective-permute-start(bf16[2,64,1024]{2,1,0:T(8,128)(2,1)S(1)} %slice.732), channel_id=1, source_target_pairs={{0,12},{4,0},{8,4},{12,8},{1,13},{5,1},{9,5},{13,9},{2,14},{6,2},{... | collective-permute-start | bytes 786440 | tf_op jit(solution)/shard_map/ppermute | solution.py:222
  54.5 26.1 %collective-permute-start.16 = (bf16[2,64,1024]{2,1,0:T(8,128)(2,1)S(1)}, bf16[2,64,1024]{2,1,0:T(8,128)(2,1)S(1)}, u32[]{:S(2)}, u32[]{:S(2)}) collective-permute-start(bf16[2,64,1024]{2,1,0:T(8,128)(2,1)S(1)} %slice.731), channel_id=1, source_target_pairs={{0,4},{4,8},{8,12},{12,0},{1,5},{5,9},{9,13},{13,1},{2,6},{6,10},{... | collective-permute-start | bytes 786440 | tf_op jit(solution)/shard_map/ppermute | solution.py:221
  81.8 29.7 %collective-permute-start.18 = (bf16[1024,1024]{1,0:T(8,128)(2,1)S(1)}, bf16[1024,1024]{1,0:T(8,128)(2,1)}, u32[]{:S(2)}, u32[]{:S(2)}) collective-permute-start(bf16[1024,1024]{1,0:T(8,128)(2,1)S(1)} %bitcast.288), channel_id=1, source_target_pairs={{0,1},{1,0},{2,3},{3,2},{4,5},{5,4},{6,7},{7,6},{8,9},{9,8},{10,11... | collective-permute-start | bytes 6291464 | tf_op jit(solution)/shard_map/ppermute | solution.py:36
  131.6 55.6 %collective-permute-start.26 = (bf16[1024,4096]{1,0:T(8,128)(2,1)}, bf16[1024,4096]{1,0:T(8,128)(2,1)}, u32[]{:S(2)}, u32[]{:S(2)}) collective-permute-start(bf16[1024,4096]{1,0:T(8,128)(2,1)} %all-gather.2.cloned.1.call-done), channel_id=1, source_target_pairs={{0,1},{1,0},{2,3},{3,2},{4,5},{5,4},{6,7},{7,6},{8,9},{9,8},{10,11... | collective-permute-start | bytes 25165832 | tf_op jit(solution)/shard_map/ppermute | solution.py:36
  131.9 51.0 %collective-permute-start.34 = (bf16[256,1024]{1,0:T(8,128)(2,1)}, bf16[256,1024]{1,0:T(8,128)(2,1)}, u32[]{:S(2)}, u32[]{:S(2)}) collective-permute-start(bf16[256,1024]{1,0:T(8,128)(2,1)} %bitcast.323), channel_id=1, source_target_pairs={{0,0},{1,8},{8,1},{9,9},{2,2},{3,10},{10,3},{11,11},{4,4},{5,12},{... | collective-permute-start | bytes 1572872 | tf_op jit(solution)/shard_map/ppermute | solution.py:201
  142.8 33.5 %collective-permute-start.25 = (bf16[1024,512]{1,0:T(8,128)(2,1)}, bf16[1024,512]{1,0:T(8,128)(2,1)S(1)}, u32[]{:S(2)}, u32[]{:S(2)}) collective-permute-start(bf16[1024,512]{1,0:T(8,128)(2,1)} %bitcast.298), channel_id=1, source_target_pairs={{0,1},{1,0},{2,3},{3,2},{4,5},{5,4},{6,7},{7,6},{8,9},{9,8},{10,11... | collective-permute-start | bytes 3145736 | tf_op jit(solution)/shard_map/ppermute | solution.py:36
  215.8 23.8 %collective-permute-start.29 = (bf16[256,1024]{1,0:T(8,128)(2,1)S(1)}, bf16[256,1024]{1,0:T(8,128)(2,1)S(1)}, u32[]{:S(2)}, u32[]{:S(2)}) collective-permute-start(bf16[256,1024]{1,0:T(8,128)(2,1)S(1)} %pad_maximum_fusion.9.own_ref), channel_id=1, source_target_pairs={{0,4},{4,0},{1,5},{5,1},{2,6},{6,2},{3,7},{7,3},{8,12},{12,8},{9,1... | collective-permute-start | bytes 1572872 | tf_op jit(solution)/shard_map/ppermute | solution.py:36
  217.8 23.6 %collective-permute-start.31 = (bf16[256,1024]{1,0:T(8,128)(2,1)S(1)}, bf16[256,1024]{1,0:T(8,128)(2,1)S(1)}, u32[]{:S(2)}, u32[]{:S(2)}) collective-permute-start(bf16[256,1024]{1,0:T(8,128)(2,1)S(1)} %pad_maximum_fusion.10.own_ref), channel_id=1, source_target_pairs={{0,1},{1,0},{2,3},{3,2},{4,5},{5,4},{6,7},{7,6},{8,9},{9,8},{10,11... | collective-permute-start | bytes 1572872 | tf_op jit(solution)/shard_map/ppermute | solution.py:36
  219.2 29.3 %collective-permute-start.28 = (bf16[256,1024]{1,0:T(8,128)(2,1)S(1)}, bf16[256,1024]{1,0:T(8,128)(2,1)S(1)}, u32[]{:S(2)}, u32[]{:S(2)}) collective-permute-start(bf16[256,1024]{1,0:T(8,128)(2,1)S(1)} %pad_maximum_fusion.9.own_ref), channel_id=1, source_target_pairs={{0,1},{1,0},{2,3},{3,2},{4,5},{5,4},{6,7},{7,6},{8,9},{9,8},{10,11... | collective-permute-start | bytes 1572872 | tf_op jit(solution)/shard_map/ppermute | solution.py:36
  290.4 23.3 %collective-permute-start.38 = (bf16[256,1024]{1,0:T(8,128)(2,1)}, bf16[256,1024]{1,0:T(8,128)(2,1)}, u32[]{:S(2)}, u32[]{:S(2)}) collective-permute-start(bf16[256,1024]{1,0:T(8,128)(2,1)} %get-tuple-element.71), channel_id=1, source_target_pairs={{0,1},{1,0},{2,3},{3,2},{4,5},{5,4},{6,7},{7,6},{8,9},{9,8},{10,11... | collective-permute-start | bytes 1572872 | tf_op jit(solution)/shard_map/ppermute | solution.py:36
  301.0 21.0 %collective-permute-start.35 = (bf16[256,1024]{1,0:T(8,128)(2,1)}, bf16[256,1024]{1,0:T(8,128)(2,1)}, u32[]{:S(2)}, u32[]{:S(2)}) collective-permute-start(bf16[256,1024]{1,0:T(8,128)(2,1)} %get-tuple-element.67), channel_id=1, source_target_pairs={{0,1},{1,0},{2,3},{3,2},{4,5},{5,4},{6,7},{7,6},{8,9},{9,8},{10,11... | collective-permute-start | bytes 1572872 | tf_op jit(solution)/shard_map/ppermute | solution.py:36
  307.5 24.1 %collective-permute-start.37 = (bf16[256,1024]{1,0:T(8,128)(2,1)}, bf16[256,1024]{1,0:T(8,128)(2,1)}, u32[]{:S(2)}, u32[]{:S(2)}) collective-permute-start(bf16[256,1024]{1,0:T(8,128)(2,1)} %add_convert_fusion.9), channel_id=1, source_target_pairs={{0,4},{4,0},{1,5},{5,1},{2,6},{6,2},{3,7},{7,3},{8,12},{12,8},{9,1... | collective-permute-start | bytes 1572872 | tf_op jit(solution)/shard_map/ppermute | solution.py:36
  377.7 31.2 %collective-permute-start.42 = (bf16[1024,4096]{1,0:T(8,128)(2,1)}, bf16[1024,4096]{1,0:T(8,128)(2,1)}, u32[]{:S(2)}, u32[]{:S(2)}) collective-permute-start(bf16[1024,4096]{1,0:T(8,128)(2,1)} %fc_outer.2), channel_id=1, source_target_pairs={{0,1},{1,0},{2,3},{3,2},{4,5},{5,4},{6,7},{7,6},{8,9},{9,8},{10,11... | collective-permute-start | bytes 25165832 | tf_op jit(solution)/shard_map/ppermute | solution.py:36
  453.1 30.3 %collective-permute-start.43 = (bf16[256,1024]{1,0:T(8,128)(2,1)S(1)}, bf16[256,1024]{1,0:T(8,128)(2,1)S(1)}, u32[]{:S(2)}, u32[]{:S(2)}) collective-permute-start(bf16[256,1024]{1,0:T(8,128)(2,1)S(1)} %copy-done.54), channel_id=1, source_target_pairs={{0,1},{1,0},{2,3},{3,2},{4,5},{5,4},{6,7},{7,6},{8,9},{9,8},{10,11... | collective-permute-start | bytes 1572872 | tf_op jit(solution)/shard_map/ppermute | solution.py:36
  458.2 24.9 %collective-permute-start.48 = (bf16[256,1024]{1,0:T(8,128)(2,1)S(1)}, bf16[256,1024]{1,0:T(8,128)(2,1)S(1)}, u32[]{:S(2)}, u32[]{:S(2)}) collective-permute-start(bf16[256,1024]{1,0:T(8,128)(2,1)S(1)} %add_convert_fusion.3), channel_id=1, source_target_pairs={{0,4},{4,0},{1,5},{5,1},{2,6},{6,2},{3,7},{7,3},{8,12},{12,8},{9,1... | collective-permute-start | bytes 1572872 | tf_op jit(solution)/shard_map/ppermute | solution.py:36
  458.6 47.0 %collective-permute-start.45 = (bf16[256,1024]{1,0:T(8,128)(2,1)S(1)}, bf16[256,1024]{1,0:T(8,128)(2,1)S(1)}, u32[]{:S(2)}, u32[]{:S(2)}) collective-permute-start(bf16[256,1024]{1,0:T(8,128)(2,1)S(1)} %add_convert_fusion.5), channel_id=1, source_target_pairs={{0,4},{4,0},{1,5},{5,1},{2,6},{6,2},{3,7},{7,3},{8,12},{12,8},{9,1... | collective-permute-start | bytes 1572872 | tf_op jit(solution)/shard_map/ppermute | solution.py:36
  508.1 21.8 %collective-permute-start.62 = (bf16[1024,1024]{1,0:T(8,128)(2,1)}, bf16[1024,1024]{1,0:T(8,128)(2,1)}, u32[]{:S(2)}, u32[]{:S(2)}) collective-permute-start(bf16[1024,1024]{1,0:T(8,128)(2,1)} %convolution_convert_fusion), channel_id=1, source_target_pairs={{0,1},{1,0},{2,3},{3,2},{4,5},{5,4},{6,7},{7,6},{8,9},{9,8},{10,11... | collective-permute-start | bytes 6291464 | tf_op jit(solution)/shard_map/ppermute | solution.py:36
  519.8 35.4 %collective-permute-start.51 = (bf16[1024,1152]{0,1:T(8,128)(2,1)}, bf16[1024,1152]{0,1:T(8,128)(2,1)}, u32[]{:S(2)}, u32[]{:S(2)}) collective-permute-start(bf16[1024,1152]{0,1:T(8,128)(2,1)} %pad_maximum_fusion), channel_id=1, source_target_pairs={{0,1},{1,0},{2,3},{3,2},{4,5},{5,4},{6,7},{7,6},{8,9},{9,8},{10,11... | collective-permute-start | bytes 7077896 | tf_op jit(solution)/shard_map/ppermute | solution.py:36
  544.7 52.6 %all-to-all-start.1 = ((bf16[4,2,64,1024]{3,2,1,0:T(8,128)(2,1)}), bf16[4,2,64,1024]{3,2,1,0:T(8,128)(2,1)S(1)}, u32[]{:S(2)}, u32[]{:S(2)}) async-start(bf16[4,2,64,1024]{3,2,1,0:T(8,128)(2,1)} %pad_maximum_fusion.3), calls=%async_computation.1 | async-start | bytes 2097152 | tf_op jit(solution)/shard_map/all_to_all | solution.py:208
  551.6 28.2 %collective-permute-start.66 = (bf16[4,64,1024]{2,1,0:T(8,128)(2,1)}, bf16[4,64,1024]{2,1,0:T(8,128)(2,1)}, u32[]{:S(2)}, u32[]{:S(2)}) collective-permute-start(bf16[4,64,1024]{2,1,0:T(8,128)(2,1)} %pad_maximum_fusion.14), channel_id=1, source_target_pairs={{0,48},{16,0},{32,16},{48,32},{1,49},{17,1},{33,17},{49,33},{2,50}... | collective-permute-start | bytes 1572872 | tf_op jit(solution)/shard_map/ppermute | solution.py:261
  555.0 24.8 %collective-permute-start.64 = (bf16[4,64,1024]{2,1,0:T(8,128)(2,1)}, bf16[4,64,1024]{2,1,0:T(8,128)(2,1)}, u32[]{:S(2)}, u32[]{:S(2)}) collective-permute-start(bf16[4,64,1024]{2,1,0:T(8,128)(2,1)} %pad_maximum_fusion.13), channel_id=1, source_target_pairs={{0,16},{16,32},{32,48},{48,0},{1,17},{17,33},{33,49},{49,1},{2,18}... | collective-permute-start | bytes 1572872 | tf_op jit(solution)/shard_map/ppermute | solution.py:260
  576.3 29.9 %collective-permute-start.55 = (bf16[4,64,1152]{2,1,0:T(8,128)(2,1)}, bf16[4,64,1152]{2,1,0:T(8,128)(2,1)S(1)}, u32[]{:S(2)}, u32[]{:S(2)}) collective-permute-start(bf16[4,64,1152]{2,1,0:T(8,128)(2,1)} %pad_maximum_fusion.5), channel_id=1, source_target_pairs={{0,12},{4,0},{8,4},{12,8},{1,13},{5,1},{9,5},{13,9},{2,14},{6,2},{... | collective-permute-start | bytes 1769480 | tf_op jit(solution)/shard_map/ppermute | solution.py:261
  585.1 21.1 %collective-permute-start.53 = (bf16[4,64,1152]{2,1,0:T(8,128)(2,1)}, bf16[4,64,1152]{2,1,0:T(8,128)(2,1)S(1)}, u32[]{:S(2)}, u32[]{:S(2)}) collective-permute-start(bf16[4,64,1152]{2,1,0:T(8,128)(2,1)} %pad_maximum_fusion.4), channel_id=1, source_target_pairs={{0,4},{4,8},{8,12},{12,0},{1,5},{5,9},{9,13},{13,1},{2,6},{6,10},{... | collective-permute-start | bytes 1769480 | tf_op jit(solution)/shard_map/ppermute | solution.py:260
  (207 other events, 2658.4 us)
Sparse Core Ops, SparseCore 0:
  12.1 97.2 all-gather.1
  440.3 93.8 reduce-scatter.1

commit v4 on v3

--- a/solution.py
+++ b/solution.py
@@ -101,6 +101,16 @@
     return q_spec, [kv_spec, kv_swapped, kv_spec, kv_swapped], log_spec
 
 
+def attend_cost(queries, blocks, products):
+    rows, width = queries.shape
+    scores = rows * rows * len(blocks) * width // HEAD_DIM
+    return pl.CostEstimate(
+        flops=products * scores * 2 * 256,
+        bytes_accessed=2 * 2 * len(blocks) * rows * width * 2,
+        transcendentals=scores,
+    )
+
+
 def attend(queries, blocks):
     rows, width = queries.shape
     pairs = width // PAIR
@@ -115,6 +125,7 @@
             jax.ShapeDtypeStruct((pairs, 2, rows), f32),
         ],
         compiler_params=pltpu.CompilerParams(vmem_limit_bytes=40 * 2**20),
+        cost_estimate=attend_cost(queries, blocks, 2),
         name="attend",
     )(queries, *blocks)
 
@@ -131,74 +142,89 @@
         out_shape=[jax.ShapeDtypeStruct((rows, width), bf16)]
         + [jax.ShapeDtypeStruct((rows, 2 * width), bf16)] * 4,
         compiler_params=pltpu.CompilerParams(vmem_limit_bytes=40 * 2**20),
+        cost_estimate=attend_cost(queries, blocks, 5),
         name="attend_back",
     )(queries, *blocks, grad, log_total)
 
 
-def fc_outer(normed, grad_before, activated, grad_branch, add=None):
-    rows, width = normed.shape
-    wide = grad_before.shape[1]
-    step = min(512, width)
-    first = wide // step
-    per = width // step
-    blocks = first + (wide // width) * per
-    second = lambda i: jnp.maximum(i - first, 0)
-
-    def kernel(n_ref, b_ref, a_ref, g_ref, *rest):
-        out_ref = rest[-1]
+def outer(segments, step, add=None, tail=None):
+    rows = segments[0][1].shape[0]
+    width = segments[0][2]
+    counts = [right.shape[1] // step for _, right, _ in segments]
+    starts = [sum(counts[:k]) for k in range(len(counts))]
+    total = sum(counts)
+    grid = total + (tail is not None)
+    n = len(segments)
+
+    def kernel(*refs):
+        out_ref = refs[-1]
         i = pl.program_id(0)
-        more = rest[0][...].astype(f32) if add is not None else 0.0
-
-        @pl.when(i < first)
-        def _():
-            out_ref[...] = (mm(n_ref[...], b_ref[...]) + more).astype(bf16)
-
-        @pl.when(i >= first)
-        def _():
-            out_ref[...] = (mm(a_ref[...], g_ref[...]) + more).astype(bf16)
-
-    out_spec = pl.BlockSpec((width, step), lambda i: (0, i))
-    in_specs = [
-        pl.BlockSpec((width, rows), lambda i: (0, 0)),
-        pl.BlockSpec((rows, step), lambda i: (0, jnp.minimum(i, first - 1))),
-        pl.BlockSpec((width, rows), lambda i: (second(i) // per, 0)),
-        pl.BlockSpec((rows, step), lambda i: (0, second(i) % per)),
-    ]
-    operands = [normed.T, grad_before, activated.T, grad_branch]
+        for k in range(n):
+
+            @pl.when((i >= starts[k]) & (i < starts[k] + counts[k]))
+            def _(k=k):
+                value = t_mm(refs[2 * k][...], refs[2 * k + 1][...])
+                if add is not None:
+                    value = value + refs[2 * n][...].astype(f32)
+                out_ref[...] = value.astype(bf16)
+
+        if tail is not None:
+
+            @pl.when(i == total)
+            def _():
+                out_ref[...] = refs[2 * n + (add is not None)][...]
+
+    in_specs, operands = [], []
+    for (left, right, _), start, count in zip(segments, starts, counts):
+        array, which = left
+        in_specs.append(pl.BlockSpec((rows, width), lambda i, w=which: (0, w)))
+        in_specs.append(
+            pl.BlockSpec((rows, step), lambda i, s=start, c=count: (0, jnp.clip(i - s, 0, c - 1)))
+        )
+        operands += [array, right]
     if add is not None:
-        in_specs.append(out_spec)
+        in_specs.append(pl.BlockSpec((width, step), lambda i: (0, jnp.minimum(i, total - 1))))
         operands.append(add)
+    if tail is not None:
+        in_specs.append(pl.BlockSpec((width, step), lambda i: (0, 0)))
+        operands.append(tail)
     return pl.pallas_call(
         kernel,
-        grid=(blocks,),
+        grid=(grid,),
         in_specs=in_specs,
-        out_specs=out_spec,
-        out_shape=jax.ShapeDtypeStruct((width, blocks * step), bf16),
+        out_specs=pl.BlockSpec((width, step), lambda i: (0, i)),
+        out_shape=jax.ShapeDtypeStruct((width, grid * step), bf16),
         compiler_params=pltpu.CompilerParams(vmem_limit_bytes=40 * 2**20),
         cost_estimate=pl.CostEstimate(
-            flops=2 * rows * width * blocks * step,
-            bytes_accessed=2 * width * blocks * step * (1 if add is None else 2),
+            flops=2 * rows * width * total * step,
+            bytes_accessed=2 * width * grid * step * (1 if add is None else 2),
             transcendentals=0,
         ),
-        name="fc_outer",
+        name="outer",
     )(*operands)
 
 
-def fc_sum(normed, grad_before, activated, grad_branch):
-    parts = list(zip(grad_before, activated))
-    sent = swap(fc_outer(normed, *parts[1], grad_branch), "core")
-    return fc_outer(normed, *parts[0], grad_branch, add=sent)
+def fc1_sum(normed, grad_before):
+    width = normed.shape[1]
+    make = lambda g, add=None: outer([((normed, 0), g, width)], 512, add=add)
+    return make(grad_before[0], swap(make(grad_before[1]), "core"))
+
+
+def fc2_sum(activated, grad_branch):
+    width = grad_branch.shape[1]
+    make = lambda z, add=None: outer(
+        [((z, i), grad_branch, width) for i in range(z.shape[1] // width)], 512, add=add
+    )
+    return make(activated[0], swap(make(activated[1]), "core"))
 
 
 FLIP = [(0, 0), (1, 2), (2, 1), (3, 3)]
 
 
-def to_images(arrays):
-    count, rows, width = arrays[0].shape
-    mixed = jnp.stack(arrays, axis=1)
-    mixed = lax.all_to_all(mixed, "z", split_axis=0, concat_axis=0, tiled=True)
-    mixed = [mixed[:, i].reshape(count * rows, width) for i in range(len(arrays))]
-    return [lax.ppermute(m, ("yh", "core"), FLIP) for m in mixed]
+def to_images(tokens):
+    count, rows, width = tokens.shape
+    mixed = lax.all_to_all(tokens, "z", split_axis=0, concat_axis=0, tiled=True)
+    return lax.ppermute(mixed.reshape(count * rows, width), ("yh", "core"), FLIP)
 
 
 def from_images(arrays, count):
@@ -214,17 +240,23 @@
 BACK = [(i, (i - 1) % 4) for i in range(4)]
 
 
-def ring_place(value, axis, out_shapes, views):
+ACROSS = [(i, (i + 2) % 4) for i in range(4)]
+
+
+def ring_place(value, axis, out_shapes, views, direct=False):
     half = value.shape[0] // 2
     ahead = lax.ppermute(value, axis, AHEAD)
     back = lax.ppermute(value, axis, BACK)
-    far_a = lax.ppermute(ahead[:half], axis, AHEAD)
-    far_b = lax.ppermute(back[half:], axis, BACK)
-    pieces = [(value, 0, 0), (ahead, 3, 0), (back, 1, 0), (far_a, 2, 0), (far_b, 2, half)]
+    pieces = [(value, 0, 0), (ahead, 3, 0), (back, 1, 0)]
+    if direct:
+        pieces.append((lax.ppermute(value, axis, ACROSS), 2, 0))
+    else:
+        pieces.append((lax.ppermute(ahead[:half], axis, AHEAD), 2, 0))
+        pieces.append((lax.ppermute(back[half:], axis, BACK), 2, half))
     n_outs = len(out_shapes)
 
     def kernel(index_ref, *refs):
-        sources, outs = refs[:5], refs[5:]
+        sources, outs = refs[: len(pieces)], refs[len(pieces) :]
         for source, (_, step, start) in zip(sources, pieces):
             place = lax.rem(index_ref[0] + step, 4)
             views(outs, source, place, start)
@@ -232,7 +264,7 @@
     vmem = pl.BlockSpec(memory_space=pltpu.VMEM)
     return pl.pallas_call(
         kernel,
-        in_specs=[pl.BlockSpec(memory_space=pltpu.SMEM)] + [vmem] * 5,
+        in_specs=[pl.BlockSpec(memory_space=pltpu.SMEM)] + [vmem] * len(pieces),
         out_specs=[vmem] * n_outs,
         out_shape=[jax.ShapeDtypeStruct(shape, value.dtype) for shape in out_shapes],
         compiler_params=pltpu.CompilerParams(vmem_limit_bytes=24 * 2**20),
@@ -247,10 +279,13 @@
     outs[0][place, pl.ds(start, piece.shape[0])] = piece[...]
 
 
-def ring_sum(blocks, axis):
+def ring_sum(blocks, axis, dim, direct=False):
     index = lax.axis_index(axis)
-    block = lambda k: lax.dynamic_index_in_dim(blocks, (index + k) % 4, 0, keepdims=False)
+    block = lambda k: lax.dynamic_index_in_dim(blocks, (index + k) % 4, dim, keepdims=False)
     add = lambda *parts: sum(p.astype(f32) for p in parts).astype(bf16)
+    if direct:
+        ways = [(1, AHEAD), (3, BACK), (2, ACROSS)]
+        return add(block(0), *(lax.ppermute(block(k), axis, way) for k, way in ways))
     far, after, before = block(2), block(1), block(3)
     half = far.shape[0] // 2
     low = lax.ppermute(far[:half], axis, AHEAD)
@@ -269,10 +304,13 @@
     return (key_value, mate, near, far)
 
 
-def group_sum(own, mate, near, far):
+def group_parts(own, mate, near, far):
     mate, far = swap(mate, "core"), swap(far, "core")
     sent = (near.astype(f32) + far.astype(f32)).astype(bf16)
-    kept = own.astype(f32) + mate.astype(f32)
+    return own.astype(f32) + mate.astype(f32), sent
+
+
+def group_add(kept, sent):
     return (kept + swap(sent, "yl").astype(f32)).astype(bf16)
 
 
@@ -318,11 +356,16 @@
     project = lambda name: [
         (mm(normed_one, part) + bias).astype(bf16) for part, bias in zip(w[name], w[name + "_bias"])
     ]
-    blocks = [group_blocks(c) for c in chunked(project("kv"))]
+    key_value = chunked(project("kv"))
+    if late is not None:
+        key_value, gathered = lax.optimization_barrier((key_value, late[0]))
+        w.update(late[1](gathered))
+    blocks = [group_blocks(key_value[0])]
+    for c in key_value[1:]:
+        c, near = lax.optimization_barrier((c, blocks[-1][2]))
+        blocks[-1] = (*blocks[-1][:2], near, blocks[-1][3])
+        blocks.append(group_blocks(c))
     queries = chunked(project("q"))
-    if late is not None:
-        blocks[0], gathered = lax.optimization_barrier((blocks[0], late[0]))
-        w.update(late[1](gathered))
     attended, log_total = zip(*(attend(q, b) for q, b in zip(queries, blocks)))
     attended = jnp.concatenate(unchunked(attended), axis=1)
     attended = flip_halves(w["core"], attended)
@@ -359,10 +402,12 @@
     return result, kept
 
 
-def backward(grad_out, kept, w, fc_sum=None):
+def backward(grad_out, kept, w, last=False):
     grad_branch_two = (w["scale"][1] * grad_out).astype(bf16)
     grad_before = []
     grad_normed_two = 0.0
+    if last:
+        fc2 = fc2_sum(kept["activated"], grad_branch_two)
     for up, down, slope in zip(w["fc1"], w["fc2"], kept["slope"]):
         part = jnp.concatenate([mm_t(grad_branch_two, d) for d in down], axis=1)
         part = (part * slope.astype(f32)).astype(bf16)
@@ -378,17 +423,20 @@
     grad_attended = sum(mm_t(g, p) for g, p in zip(grad_halves, w["proj"])).astype(bf16)
     grad_attended = flip_halves(w["core"], grad_attended)
     fc_grad = None
-    if fc_sum is not None:
-        fc_grad = fc_sum(
-            kept["normed_two"], grad_before, kept["activated"], grad_branch_two
-        )
+    if last:
+        fc_grad = [fc1_sum(kept["normed_two"], grad_before), fc2]
         fc_grad, grad_attended = lax.optimization_barrier((fc_grad, grad_attended))
     grad_chunks = chunked([grad_attended[:, :half], grad_attended[:, half:]])
     q_chunks, kv_chunks = [], []
+    ready = None
     for q, b, g, t in zip(kept["queries"], kept["blocks"], grad_chunks, kept["log_total"]):
+        if ready is not None:
+            sent, g = lax.optimization_barrier((ready[1], g))
+            kv_chunks.append(group_add(ready[0], sent))
         parts = attend_back(q, b, g, t)
         q_chunks.append(parts[0])
-        kv_chunks.append(group_sum(*parts[1:]))
+        ready = group_parts(*parts[1:])
+    kv_chunks.append(group_add(*ready))
     grad_q, grad_kv = unchunked(q_chunks), unchunked(kv_chunks)
     grad_normed_one = sum(
         mm_t(g, part) for g, part in zip(grad_q + grad_kv, w["q"] + w["kv"])
@@ -405,13 +453,13 @@
         kv=[total(g) for g in grad_kv],
         fc1_bias=[total(g) for g in grad_before],
     )
-    outer = dict(
+    products = dict(
         q=(kept["normed_one"], grad_q),
         kv=(kept["normed_one"], grad_kv),
         proj=(kept["attended"], grad_halves),
         fc=fc_grad,
     )
-    return grad_inputs.astype(bf16), vectors, outer
+    return grad_inputs.astype(bf16), vectors, products
 
 
 def ordered(core, mine, other):
@@ -461,12 +509,14 @@
     fc1_mine = jnp.swapaxes(fc1_mine, 1, 2).reshape(own, shards * mid)
     fc2_mine = pick(fc2_weight[0].reshape(2, 2, part, width), core, 0)
     fc_mine = jnp.concatenate([fc1_mine, fc2_mine[0], fc2_mine[1]], axis=1)
+
+    a_mine = jnp.concatenate([q_mine, proj_mine, vectors], axis=1)
+    first_tokens = to_images(patch_tokens)
+    a_row = ring_place(a_mine, RING_Y, [(4, own, a_mine.shape[1])], in_order, direct=True)[0]
+    b_row = ring_place(kv_mine, RING_Z, [(4, own, width)], in_order, direct=True)[0]
+    a_row, b_row, fc_mine = lax.optimization_barrier((a_row, b_row, fc_mine))
     fc_half = lax.all_gather(fc_mine, FSDP, axis=0, tiled=True)
-
-    a_mine = jnp.concatenate([q_mine, proj_mine, vectors], axis=1)
-    a_row = ring_place(a_mine, RING_Y, [(4, own, a_mine.shape[1])], in_order)[0]
     a_row = a_row.reshape(4 * own, a_mine.shape[1])
-    b_row = ring_place(kv_mine, RING_Z, [(4, own, width)], in_order)[0]
 
     def a_views(outs, piece, place, start):
         at = 0
@@ -525,28 +575,27 @@
     live = (
         jnp.arange(images) % IMG_MB < jnp.repeat(batch_counts[0], IMG_MB)
     ).astype(bf16)
-    first_tokens, last_grad = to_images([patch_tokens, out_grad * live[:, None, None]])
 
     sent, _ = forward(first_tokens, w, late=(fc_half, fc_weights))
+    live_grad = out_grad * live[:, None, None]
+    sent, live_grad = lax.optimization_barrier((sent, live_grad))
     passed = lax.ppermute(sent, "section", [(0, 1)])
+    last_grad = to_images(live_grad)
     tokens = jnp.where(section == 0, first_tokens, passed)
     result, kept = forward(tokens, w)
 
     sent, _, _ = backward(last_grad.astype(f32), kept, w)
     passed = lax.ppermute(sent, "section", [(1, 0)])
     grad_out = jnp.where(section == 1, last_grad, passed).astype(f32)
-    grad_inputs, sums, outer = backward(grad_out, kept, w, fc_sum)
+    grad_inputs, sums, outer_parts = backward(grad_out, kept, w, last=True)
     result, grad_inputs = lax.optimization_barrier((result, grad_inputs))
     block_out, in_grad = from_images([result, grad_inputs], images)
 
-    def core_sum(mine, other):
-        return (mine + swap(other.astype(bf16), "core").astype(f32)).astype(bf16)
-
     def natural(pair):
         return jnp.concatenate(ordered(core, *pair))
 
     v_sum = lambda a: a.reshape(groups, 2, PAIR)[:, 1].reshape(half)
-    fc1_sum = jnp.stack(
+    fc1_bias_sum = jnp.stack(
         ordered(
             core, *(jnp.swapaxes(s.reshape(2, shards, part), 0, 1) for s in sums["fc1_bias"])
         ),
@@ -565,36 +614,39 @@
                 ],
                 axis=1,
             ),
-            fc1_sum,
+            fc1_bias_sum,
         ],
         axis=1,
     )
-    vector_grads = jnp.pad(vector_grads, ((0, 0), (0, 128 - count)))
-
-    fc_grad = lax.psum_scatter(outer["fc"], FSDP, scatter_dimension=0, tiled=True)
-    a1, dq = outer["q"]
-    dkv = outer["kv"][1]
-    o, e1 = outer["proj"]
-    a_parts = [
-        jnp.concatenate([t_mm(a1, dq[i]), t_mm(o, e1[i]), vector_grads], axis=1) for i in range(2)
+    step = 256
+    vector_grads = jnp.pad(vector_grads, ((0, 0), (0, step - count))).astype(bf16)
+
+    rows = [
+        lax.psum_scatter(g, RING_Z, scatter_dimension=0, tiled=True) for g in outer_parts["fc"]
     ]
-    b_parts = [t_mm(a1, dkv[i]) for i in range(2)]
-    b_sum = ring_sum(core_sum(*b_parts).reshape(4, 4, own, width), RING_Z)
-    b_grad = ring_sum(b_sum, RING_Y)
-    a_blocks = core_sum(*a_parts).reshape(4, 4, own, width + 128)
-    a_sum = ring_sum(jnp.swapaxes(a_blocks, 0, 1), RING_Y)
-    a_grad = ring_sum(a_sum, RING_Z)
-
-    parts = [a_grad, b_grad, fc_grad]
+    fc_grad = lax.psum_scatter(
+        jnp.concatenate(rows, axis=1), RING_Y, scatter_dimension=0, tiled=True
+    )
+    a1, dq = outer_parts["q"]
+    dkv = outer_parts["kv"][1]
+    o, e1 = outer_parts["proj"]
+    make = lambda i, **more: outer(
+        [((a1, 0), dq[i], width), ((o, 0), e1[i], width), ((a1, 0), dkv[i], width)], step, **more
+    )
+    ab = make(0, add=swap(make(1), "core"), tail=vector_grads)
+    ab = ring_sum(ab.reshape(4, 4, own, 2 * width + step), RING_Y, 1)
+    ab_grad = ring_sum(ab, RING_Z, 0, direct=True)
+
+    parts = [ab_grad, fc_grad]
     parts = [(a.astype(f32) + swap(a, "xhi").astype(f32)).astype(bf16) for a in parts]
-    vec_grad = parts[0][:, width : width + count].T.astype(f32)
     others = [swap(a, "core") for a in parts]
-    a_pair, b_pair, fc_pair = (
+    vec_grad = sum(p[0][:, 2 * width : 2 * width + count].astype(f32) for p in (parts, others)).T
+    ab_pair, fc_pair = (
         ordered(core, a.astype(f32), b.astype(f32)) for a, b in zip(parts, others)
     )
-    q_grad = jnp.concatenate([p[:, :half] for p in a_pair], axis=1)
-    proj_out = jnp.concatenate([p[:, half:width] for p in a_pair], axis=1)
-    kv_grads = [p.reshape(own, groups, 2, PAIR) for p in b_pair]
+    q_grad = jnp.concatenate([p[:, :half] for p in ab_pair], axis=1)
+    proj_out = jnp.concatenate([p[:, half:width] for p in ab_pair], axis=1)
+    kv_grads = [p[:, width : 2 * width].reshape(own, groups, 2, PAIR) for p in ab_pair]
     k_grad, v_grad = (
         jnp.concatenate([p[:, :, i].reshape(own, half) for p in kv_grads], axis=1)
         for i in range(2)

time: 689 us -> 657 us (0.954)
  the two profiles are of different devices: /device:TPU:1 before, /device:TPU:25 now
where the time goes in v4:
time: 657 us; the launch traced here: 646 us
  waiting for transfers between devices  177 us (27%)
  starting transfers between devices  134 us (20%)
  Pallas kernels  94.2 us (14%)
  matrix products  89.9 us (14%)
  local copies, waits for them, and re-layouts  87.7 us (13%)
  other arithmetic  46.5 us (7%)
  between operations  17.1 us (3%)
    dot_general x48, matrix products, dot(): return lax.dot_general(a, b, (dims, ((), ())), preferred_element_type=f32)  89.9 us
    ppermute x35, starting transfers between devices, swap(): return lax.ppermute(value, axis, [(0, 1), (1, 0)])  83.4 us
    ppermute x35, waiting for transfers between devices, swap(): return lax.ppermute(value, axis, [(0, 1), (1, 0)])  74.4 us
    pallas_call x4, Pallas kernels, attend_back(): pl.pallas_call(attend_back_kernel, grid=(pairs,), in_specs=[q_spec] + kv_...  36.9 us
    pallas_call x4, Pallas kernels, attend(): pl.pallas_call(attend_kernel, grid=(pairs,), in_specs=[q_spec] + kv_specs...  30 us
    pallas_call x6, Pallas kernels, outer(): pl.pallas_call(kernel, grid=(grid,), in_specs=in_specs, out_specs=pl.Bloc...  25.5 us
    unnamed x247, local copies, waits for them, and re-layouts  23.8 us
    ppermute x1, waiting for transfers between devices, ring_sum(): before = lax.ppermute(before, axis, BACK)  23.7 us
  transfers between devices with their start and end apart: 69, of which 27 were waited for; matrix products, arithmetic and copies ran while one was open for 21% of the time, Pallas kernels for 10%

profile of v4, /device:TPU:25, one launch (start us, length us, event | category | flops | bytes accessed | tf_op | source)
XLA Modules:
  0.0 646.2 jit_solution(2589325030610979651)
XLA Ops:
  44.4 5.4 collective-permute-start
  60.3 12.3 %collective-permute-start.16 = (bf16[1024,1024]{1,0:T(8,128)(2,1)S(1)}, bf16[1024,1024]{1,0:T(8,128)(2,1)}, u32[]{:S(2)}, u32[]{:S(2)}) collective-permute-start(bf16[1024,1024]{1,0:T(8,128)(2,1)S(1)} %bitcast.204), channel_id=1, source_target_pairs={{0,1},{1,0},{2,3},{3,2},{4,5},{5,4},{6,7},{7,6},{8,9},{9,8},{10,11... | collective-permute-start | bytes 6291464 | tf_op jit(solution)/shard_map/ppermute | solution.py:36
  80.2 8.9 %collective-permute-done.9.refs_3_ = bf16[128,1152]{1,0:T(8,128)(2,1)S(1)} collective-permute-done((bf16[128,1152]{1,0:T(8,128)(2,1)S(1)}, bf16[128,1152]{1,0:T(8,128)(2,1)S(1)}, u32[]{:S(2)}, u32[]{:S(2)}) %collective-permute-start.9) | collective-permute-done | bytes 294944 | tf_op jit(solution)/shard_map/ppermute | solution.py:254
  102.1 16.1 %all-gather.2.cloned.1.call-done = bf16[1024,4096]{1,0:T(8,128)(2,1)} async-done(((bf16[64,4096]{1,0:T(8,128)(2,1)}), bf16[1024,4096]{1,0:T(8,128)(2,1)}) %all-gather.2.cloned.1.call-update) | async-done | bytes 8388624 | tf_op jit(solution)/shard_map/all_gather | solution.py:518
  127.0 10.6 %collective-permute-done.18.near_ref = bf16[256,1024]{1,0:T(8,128)(2,1)} collective-permute-done((bf16[256,1024]{1,0:T(8,128)(2,1)}, bf16[256,1024]{1,0:T(8,128)(2,1)}, u32[]{:S(2)}, u32[]{:S(2)}) %collective-permute-start.18) | collective-permute-done | bytes 524320 | tf_op jit(solution)/shard_map/ppermute | solution.py:36
  141.2 8.5 %collective-permute-done.21.near_ref = bf16[256,1024]{1,0:T(8,128)(2,1)S(1)} collective-permute-done((bf16[256,1024]{1,0:T(8,128)(2,1)S(1)}, bf16[256,1024]{1,0:T(8,128)(2,1)S(1)}, u32[]{:S(2)}, u32[]{:S(2)}) %collective-permute-start.21) | collective-permute-done | bytes 524320 | tf_op jit(solution)/shard_map/ppermute | solution.py:36
  152.5 8.4 %attend.4 = (bf16[256,512]{1,0:T(8,128)(2,1)S(1)}, f32[4,2,256]{2,1,0:T(2,128)}) custom-call(bf16[256,512]{1,0:T(8,128)(2,1)S(1)} %pad_maximum_fusion.12.q_ref, bf16[256,1024]{1,0:T(8,128)(2,1)S(1)} %copy-done.29, bf16[256,1024]{1,0:T(8,128)(2,1)S(1)} %collective-permute-done.17.mate_ref, bf16[256,1024]{1,0:T(8,128)(2,1)} %collective-permute-done.18.near_ref, ...), custom_call_target="tpu_custom_call" | custom-call | flops 2147483648 | bytes 4194304 | tf_op jit(solution)/shard_map/attend/pallas_call | solution.py:118
  160.9 7.6 %attend.5 = (bf16[256,512]{1,0:T(8,128)(2,1)S(1)}, f32[4,2,256]{2,1,0:T(2,128)}) custom-call(bf16[256,512]{1,0:T(8,128)(2,1)S(1)} %pad_maximum_fusion.13.q_ref, bf16[256,1024]{1,0:T(8,128)(2,1)S(1)} %copy-done.28, bf16[256,1024]{1,0:T(8,128)(2,1)S(1)} %collective-permute-done.20.mate_ref, bf16[256,1024]{1,0:T(8,128)(2,1)S(1)} %collective-permute-done.21.near_ref, ...), custom_call_target="tpu_custom_call" | custom-call | flops 2147483648 | bytes 4194304 | tf_op jit(solution)/shard_map/attend/pallas_call | solution.py:118
  191.7 8.7 %all-to-all-done.1 = bf16[4,64,1024]{2,1,0:T(8,128)(2,1)S(1)} async-done(((bf16[4,64,1024]{2,1,0:T(8,128)(2,1)}), bf16[4,64,1024]{2,1,0:T(8,128)(2,1)S(1)}, u32[]{:S(2)}, u32[]{:S(2)}) %all-to-all-start.1) | async-done | bytes 524320 | tf_op jit(solution)/shard_map/all_to_all | solution.py:226
  214.5 4.9 collective-permute-done.27.near_ref
  236.7 7.0 %attend.6 = (bf16[256,512]{1,0:T(8,128)(2,1)S(1)}, f32[4,2,256]{2,1,0:T(2,128)S(1)}) custom-call(bf16[256,512]{1,0:T(8,128)(2,1)S(1)} %pad_maximum_fusion.14.q_ref, bf16[256,1024]{1,0:T(8,128)(2,1)S(1)} %pad_maximum_fusion.8.own_ref, bf16[256,1024]{1,0:T(8,128)(2,1)S(1)} %collective-permute-done.26.mate_ref, ...), custom_call_target="tpu_custom_call" | custom-call | flops 2147483648 | bytes 4194304 | tf_op jit(solution)/shard_map/attend/pallas_call | solution.py:118
  243.9 7.0 %attend.7 = (bf16[256,512]{1,0:T(8,128)(2,1)S(1)}, f32[4,2,256]{2,1,0:T(2,128)S(1)}) custom-call(bf16[256,512]{1,0:T(8,128)(2,1)S(1)} %pad_maximum_fusion.15.q_ref, bf16[256,1024]{1,0:T(8,128)(2,1)S(1)} %pad_maximum_fusion.9.own_ref, bf16[256,1024]{1,0:T(8,128)(2,1)S(1)} %collective-permute-done.29.mate_ref, ...), custom_call_target="tpu_custom_call" | custom-call | flops 2147483648 | bytes 4194304 | tf_op jit(solution)/shard_map/attend/pallas_call | solution.py:118
  258.3 5.3 fusion.43
  263.6 4.2 fusion.205
  271.5 10.0 %attend_back.4 = (bf16[256,512]{1,0:T(8,128)(2,1)S(1)}, bf16[256,1024]{1,0:T(8,128)(2,1)S(1)}, bf16[256,1024]{1,0:T(8,128)(2,1)S(1)}, bf16[256,1024]{1,0:T(8,128)(2,1)S(1)}, bf16[256,1024]{1,0:T(8,128)(2,1)}) custom-call(bf16[256,512]{1,0:T(8,128)(2,1)S(1)} %pad_maximum_fusion.14.q_ref, bf16[256,1024]{1,0:T(8,128)(2,1)S(1)} %pad_maximum_fusion.8.own_ref, ...), custom_call_target="tpu_custom_call" | custom-call | flops 5368709120 | bytes 4194304 | tf_op jit(solution)/shard_map/attend_back/pallas_call | solution.py:137
  288.1 9.0 %attend_back.5 = (bf16[256,512]{1,0:T(8,128)(2,1)S(1)}, bf16[256,1024]{1,0:T(8,128)(2,1)S(1)}, bf16[256,1024]{1,0:T(8,128)(2,1)S(1)}, bf16[256,1024]{1,0:T(8,128)(2,1)S(1)}, bf16[256,1024]{1,0:T(8,128)(2,1)S(1)}) custom-call(bf16[256,512]{1,0:T(8,128)(2,1)S(1)} %pad_maximum_fusion.15.q_ref, bf16[256,1024]{1,0:T(8,128)(2,1)S(1)} %copy-done.26, ...), custom_call_target="tpu_custom_call" | custom-call | flops 5368709120 | bytes 4194304 | tf_op jit(solution)/shard_map/attend_back/pallas_call | solution.py:137
  302.5 9.1 %collective-permute-done.35 = bf16[256,1024]{1,0:T(8,128)(2,1)S(1)} collective-permute-done((bf16[256,1024]{1,0:T(8,128)(2,1)S(1)}, bf16[256,1024]{1,0:T(8,128)(2,1)S(1)}, u32[]{:S(2)}, u32[]{:S(2)}) %collective-permute-start.35) | collective-permute-done | bytes 524320 | tf_op jit(solution)/shard_map/ppermute | solution.py:36
  312.0 10.9 %collective-permute-done.38 = bf16[256,1024]{1,0:T(8,128)(2,1)S(1)} collective-permute-done((bf16[256,1024]{1,0:T(8,128)(2,1)S(1)}, bf16[256,1024]{1,0:T(8,128)(2,1)S(1)}, u32[]{:S(2)}, u32[]{:S(2)}) %collective-permute-start.38) | collective-permute-done | bytes 524320 | tf_op jit(solution)/shard_map/ppermute | solution.py:36
  332.5 9.7 %collective-permute-done.39 = bf16[256,1024]{1,0:T(8,128)(2,1)S(1)} collective-permute-done((bf16[256,1024]{1,0:T(8,128)(2,1)S(1)}, bf16[256,1024]{1,0:T(8,128)(2,1)S(1)}, u32[]{:S(2)}, u32[]{:S(2)}) %collective-permute-start.39) | collective-permute-done | bytes 524320 | tf_op jit(solution)/shard_map/ppermute | solution.py:588
  370.6 4.3 multiply_reduce_fusion.1
  385.8 4.4 outer.9
  397.6 8.9 %attend_back.6 = (bf16[256,512]{1,0:T(8,128)(2,1)S(1)}, bf16[256,1024]{1,0:T(8,128)(2,1)S(1)}, bf16[256,1024]{1,0:T(8,128)(2,1)S(1)}, bf16[256,1024]{1,0:T(8,128)(2,1)S(1)}, bf16[256,1024]{1,0:T(8,128)(2,1)S(1)}) custom-call(bf16[256,512]{1,0:T(8,128)(2,1)S(1)} %copy-done.35, bf16[256,1024]{1,0:T(8,128)(2,1)S(1)} %copy-done.24, ...), custom_call_target="tpu_custom_call" | custom-call | flops 5368709120 | bytes 4194304 | tf_op jit(solution)/shard_map/attend_back/pallas_call | solution.py:137
  408.8 9.0 %attend_back.7 = (bf16[256,512]{1,0:T(8,128)(2,1)S(1)}, bf16[256,1024]{1,0:T(8,128)(2,1)S(1)}, bf16[256,1024]{1,0:T(8,128)(2,1)S(1)}, bf16[256,1024]{1,0:T(8,128)(2,1)S(1)}, bf16[256,1024]{1,0:T(8,128)(2,1)S(1)}) custom-call(bf16[256,512]{1,0:T(8,128)(2,1)S(1)} %pad_maximum_fusion.15.q_ref, bf16[256,1024]{1,0:T(8,128)(2,1)S(1)} %copy-done.27, ...), custom_call_target="tpu_custom_call" | custom-call | flops 5368709120 | bytes 4194304 | tf_op jit(solution)/shard_map/attend_back/pallas_call | solution.py:137
  421.7 11.7 %collective-permute-done.44 = bf16[256,1024]{1,0:T(8,128)(2,1)S(1)} collective-permute-done((bf16[256,1024]{1,0:T(8,128)(2,1)S(1)}, bf16[256,1024]{1,0:T(8,128)(2,1)S(1)}, u32[]{:S(2)}, u32[]{:S(2)}) %collective-permute-start.44) | collective-permute-done | bytes 524320 | tf_op jit(solution)/shard_map/ppermute | solution.py:36
  434.4 10.1 %collective-permute-done.47 = bf16[256,1024]{1,0:T(8,128)(2,1)S(1)} collective-permute-done((bf16[256,1024]{1,0:T(8,128)(2,1)S(1)}, bf16[256,1024]{1,0:T(8,128)(2,1)S(1)}, u32[]{:S(2)}, u32[]{:S(2)}) %collective-permute-start.47) | collective-permute-done | bytes 524320 | tf_op jit(solution)/shard_map/ppermute | solution.py:36
  446.3 5.5 outer.10
  487.6 6.9 %outer.11 = bf16[1024,2304]{1,0:T(8,128)(2,1)S(1)} custom-call(bf16[256,1024]{1,0:T(8,128)(2,1)S(1)} %fusion.118.refs_0_.refs_4_, bf16[256,512]{1,0:T(8,128)(2,1)S(1)} %pad_maximum_fusion.20.refs_1_, bf16[256,1024]{1,0:T(8,128)(2,1)S(1)} %copy-done.4, bf16[256,512]{1,0:T(8,128)(2,1)S(1)} %copy-done.22, bf16[256,1024]{1,0:T(8,128)(2,1)S(1)} %fusion.118.refs_0_.refs_4_, ...), custom_call_target="tpu_custom_call" | custom-call | flops 1073741824 | bytes 9437184 | tf_op jit(solution)/shard_map/outer/pallas_call | solution.py:191
  498.1 12.7 %collective-permute-done.51 = bf16[2,64,2304]{2,1,0:T(8,128)(2,1)S(1)} collective-permute-done((bf16[2,64,2304]{2,1,0:T(8,128)(2,1)S(1)}, bf16[2,64,2304]{2,1,0:T(8,128)(2,1)S(1)}, u32[]{:S(2)}, u32[]{:S(2)}) %collective-permute-start.51) | collective-permute-done | bytes 589856 | tf_op jit(solution)/shard_map/ppermute | solution.py:291
  519.5 23.7 %collective-permute-done.54 = bf16[4,64,2304]{2,1,0:T(8,128)(2,1)S(1)} collective-permute-done((bf16[4,64,2304]{2,1,0:T(8,128)(2,1)}, bf16[4,64,2304]{2,1,0:T(8,128)(2,1)S(1)}, u32[]{:S(2)}, u32[]{:S(2)}) %collective-permute-start.54) | collective-permute-done | bytes 1179680 | tf_op jit(solution)/shard_map/ppermute | solution.py:296
  572.7 25.9 %collective-permute-start.59 = (bf16[64,2304]{1,0:T(8,128)(2,1)S(1)}, bf16[64,2304]{1,0:T(8,128)(2,1)S(1)}, u32[]{:S(2)}, u32[]{:S(2)}) collective-permute-start(bf16[64,2304]{1,0:T(8,128)(2,1)S(1)} %add_convert_fusion.12), channel_id=1, source_target_pairs={{0,1},{1,0},{2,3},{3,2},{4,5},{5,4},{6,7},{7,6},{8,9},{9,8},{10,11... | collective-permute-start | bytes 884744 | tf_op jit(solution)/shard_map/ppermute | solution.py:36
  612.0 11.8 %collective-permute-start.61 = (bf16[64,4096]{1,0:T(8,128)(2,1)S(1)}, bf16[64,4096]{1,0:T(8,128)(2,1)S(1)}, u32[]{:S(2)}, u32[]{:S(2)}) collective-permute-start(bf16[64,4096]{1,0:T(8,128)(2,1)S(1)} %add_convert_fusion), channel_id=1, source_target_pairs={{0,1},{1,0},{2,3},{3,2},{4,5},{5,4},{6,7},{7,6},{8,9},{9,8},{10,11... | collective-permute-start | bytes 1572872 | tf_op jit(solution)/shard_map/ppermute | solution.py:36
  634.0 4.2 broadcast_in_dim_reshape.2
  (633 shorter events, 326.4 us)
Async XLA Ops:
  7.2 110.9 %all-gather.2.cloned.1.call-start = ((), (), s32[]{:S(2)}) async-start(), calls=%async_computation.6 | async-start | bytes 8912896 | tf_op jit(solution)/shard_map/all_gather | solution.py:518
  14.5 15.9 %collective-permute-start.1 = (bf16[64,1152]{1,0:T(8,128)(2,1)S(1)}, bf16[64,1152]{1,0:T(8,128)(2,1)S(1)}, u32[]{:S(2)}, u32[]{:S(2)}) collective-permute-start(bf16[64,1152]{1,0:T(8,128)(2,1)S(1)} %fusion.177.refs_0_), channel_id=1, source_target_pairs={{0,4},{4,8},{8,12},{12,0},{1,5},{5,9},{9,13},{13,1},{2,6},{6,10},{... | collective-permute-start | bytes 442376 | tf_op jit(solution)/shard_map/ppermute | solution.py:248
  14.6 15.8 %collective-permute-start.2 = (bf16[64,1152]{1,0:T(8,128)(2,1)S(1)}, bf16[64,1152]{1,0:T(8,128)(2,1)S(1)}, u32[]{:S(2)}, u32[]{:S(2)}) collective-permute-start(bf16[64,1152]{1,0:T(8,128)(2,1)S(1)} %fusion.177.refs_0_), channel_id=1, source_target_pairs={{0,12},{4,0},{8,4},{12,8},{1,13},{5,1},{9,5},{13,9},{2,14},{6,2},{... | collective-permute-start | bytes 442376 | tf_op jit(solution)/shard_map/ppermute | solution.py:249
  36.6 36.0 %collective-permute-start.7 = (bf16[256,1152]{1,0:T(8,128)(2,1)S(1)}, bf16[256,1152]{1,0:T(8,128)(2,1)}, u32[]{:S(2)}, u32[]{:S(2)}) collective-permute-start(bf16[256,1152]{1,0:T(8,128)(2,1)S(1)} %bitcast.222), channel_id=1, source_target_pairs={{0,16},{16,32},{32,48},{48,0},{1,17},{17,33},{33,49},{49,1},{2,18}... | collective-permute-start | bytes 1769480 | tf_op jit(solution)/shard_map/ppermute | solution.py:248
  38.1 35.7 %collective-permute-start.8 = (bf16[256,1152]{1,0:T(8,128)(2,1)S(1)}, bf16[256,1152]{1,0:T(8,128)(2,1)}, u32[]{:S(2)}, u32[]{:S(2)}) collective-permute-start(bf16[256,1152]{1,0:T(8,128)(2,1)S(1)} %bitcast.223), channel_id=1, source_target_pairs={{0,48},{16,0},{32,16},{48,32},{1,49},{17,1},{33,17},{49,33},{2,50}... | collective-permute-start | bytes 1769480 | tf_op jit(solution)/shard_map/ppermute | solution.py:249
  44.4 33.3 %collective-permute-start = (bf16[256,1024]{1,0:T(8,128)(2,1)}, bf16[256,1024]{1,0:T(8,128)(2,1)}, u32[]{:S(2)}, u32[]{:S(2)}) collective-permute-start(bf16[256,1024]{1,0:T(8,128)(2,1)} %bitcast), channel_id=1, source_target_pairs={{0,0},{1,8},{8,1},{9,9},{2,2},{3,10},{10,3},{11,11},{4,4},{5,12},{... | collective-permute-start | bytes 1572872 | tf_op jit(solution)/shard_map/ppermute | solution.py:227
  60.3 37.4 %collective-permute-start.16 = (bf16[1024,1024]{1,0:T(8,128)(2,1)S(1)}, bf16[1024,1024]{1,0:T(8,128)(2,1)}, u32[]{:S(2)}, u32[]{:S(2)}) collective-permute-start(bf16[1024,1024]{1,0:T(8,128)(2,1)S(1)} %bitcast.204), channel_id=1, source_target_pairs={{0,1},{1,0},{2,3},{3,2},{4,5},{5,4},{6,7},{7,6},{8,9},{9,8},{10,11... | collective-permute-start | bytes 6291464 | tf_op jit(solution)/shard_map/ppermute | solution.py:36
  73.7 15.5 %collective-permute-start.9 = (bf16[128,1152]{1,0:T(8,128)(2,1)S(1)}, bf16[128,1152]{1,0:T(8,128)(2,1)S(1)}, u32[]{:S(2)}, u32[]{:S(2)}) collective-permute-start(bf16[128,1152]{1,0:T(8,128)(2,1)S(1)} %slice.579), channel_id=1, source_target_pairs={{0,16},{16,32},{32,48},{48,0},{1,17},{17,33},{33,49},{49,1},{2,18}... | collective-permute-start | bytes 884744 | tf_op jit(solution)/shard_map/ppermute | solution.py:254
  74.7 15.8 %collective-permute-start.10 = (bf16[128,1152]{1,0:T(8,128)(2,1)S(1)}, bf16[128,1152]{1,0:T(8,128)(2,1)S(1)}, u32[]{:S(2)}, u32[]{:S(2)}) collective-permute-start(bf16[128,1152]{1,0:T(8,128)(2,1)S(1)} %slice.580), channel_id=1, source_target_pairs={{0,48},{16,0},{32,16},{48,32},{1,49},{17,1},{33,17},{49,33},{2,50}... | collective-permute-start | bytes 884744 | tf_op jit(solution)/shard_map/ppermute | solution.py:255
  118.1 57.6 %collective-permute-start.24 = (bf16[1024,4096]{1,0:T(8,128)(2,1)}, bf16[1024,4096]{1,0:T(8,128)(2,1)}, u32[]{:S(2)}, u32[]{:S(2)}) collective-permute-start(bf16[1024,4096]{1,0:T(8,128)(2,1)} %all-gather.2.cloned.1.call-done), channel_id=1, source_target_pairs={{0,1},{1,0},{2,3},{3,2},{4,5},{5,4},{6,7},{7,6},{8,9},{9,8},{10,11... | collective-permute-start | bytes 25165832 | tf_op jit(solution)/shard_map/ppermute | solution.py:36
  118.7 20.4 %collective-permute-start.11 = (bf16[1024,512]{1,0:T(8,128)(2,1)}, bf16[1024,512]{1,0:T(8,128)(2,1)}, u32[]{:S(2)}, u32[]{:S(2)}) collective-permute-start(bf16[1024,512]{1,0:T(8,128)(2,1)} %bitcast.217), channel_id=1, source_target_pairs={{0,1},{1,0},{2,3},{3,2},{4,5},{5,4},{6,7},{7,6},{8,9},{9,8},{10,11... | collective-permute-start | bytes 3145736 | tf_op jit(solution)/shard_map/ppermute | solution.py:36
  126.4 25.5 %collective-permute-start.17 = (bf16[256,1024]{1,0:T(8,128)(2,1)S(1)}, bf16[256,1024]{1,0:T(8,128)(2,1)S(1)}, u32[]{:S(2)}, u32[]{:S(2)}) collective-permute-start(bf16[256,1024]{1,0:T(8,128)(2,1)S(1)} %copy-done.29), channel_id=1, source_target_pairs={{0,1},{1,0},{2,3},{3,2},{4,5},{5,4},{6,7},{7,6},{8,9},{9,8},{10,11... | collective-permute-start | bytes 1572872 | tf_op jit(solution)/shard_map/ppermute | solution.py:36
  141.1 19.8 %collective-permute-start.20 = (bf16[256,1024]{1,0:T(8,128)(2,1)S(1)}, bf16[256,1024]{1,0:T(8,128)(2,1)S(1)}, u32[]{:S(2)}, u32[]{:S(2)}) collective-permute-start(bf16[256,1024]{1,0:T(8,128)(2,1)S(1)} %copy-done.28), channel_id=1, source_target_pairs={{0,1},{1,0},{2,3},{3,2},{4,5},{5,4},{6,7},{7,6},{8,9},{9,8},{10,11... | collective-permute-start | bytes 1572872 | tf_op jit(solution)/shard_map/ppermute | solution.py:36
  151.9 17.0 %collective-permute-start.23 = (bf16[1024,512]{1,0:T(8,128)(2,1)S(1)}, bf16[1024,512]{1,0:T(8,128)(2,1)S(1)}, u32[]{:S(2)}, u32[]{:S(2)}) collective-permute-start(bf16[1024,512]{1,0:T(8,128)(2,1)S(1)} %bitcast.212), channel_id=1, source_target_pairs={{0,1},{1,0},{2,3},{3,2},{4,5},{5,4},{6,7},{7,6},{8,9},{9,8},{10,11... | collective-permute-start | bytes 3145736 | tf_op jit(solution)/shard_map/ppermute | solution.py:36
  185.1 16.0 %collective-permute-start.25 = (bf16[256,1024]{1,0:T(8,128)(2,1)}, bf16[256,1024]{1,0:T(8,128)(2,1)S(1)}, u32[]{:S(2)}, u32[]{:S(2)}) collective-permute-start(bf16[256,1024]{1,0:T(8,128)(2,1)} %fusion.92), channel_id=1, source_target_pairs={{0,64},{1,65},{2,66},{3,67},{4,68},{5,69},{6,70},{7,71},{8,72},{9,... | collective-permute-start | bytes 1572872 | tf_op jit(solution)/shard_map/ppermute | solution.py:582
  191.6 358.3 %reduce-scatter.6.cloned.1.call-start = ((), (), s32[]{:S(2)}) async-start(), calls=%async_computation.8 | async-start | bytes 5242880 | tf_op jit(solution)/shard_map/reduce_scatter | solution.py:625
  208.7 28.0 %collective-permute-start.26 = (bf16[256,1024]{1,0:T(8,128)(2,1)S(1)}, bf16[256,1024]{1,0:T(8,128)(2,1)S(1)}, u32[]{:S(2)}, u32[]{:S(2)}) collective-permute-start(bf16[256,1024]{1,0:T(8,128)(2,1)S(1)} %pad_maximum_fusion.8.own_ref), channel_id=1, source_target_pairs={{0,1},{1,0},{2,3},{3,2},{4,5},{5,4},{6,7},{7,6},{8,9},{9,8},{10,11... | collective-permute-start | bytes 1572872 | tf_op jit(solution)/shard_map/ppermute | solution.py:36
  227.5 16.3 %collective-permute-start.29 = (bf16[256,1024]{1,0:T(8,128)(2,1)S(1)}, bf16[256,1024]{1,0:T(8,128)(2,1)S(1)}, u32[]{:S(2)}, u32[]{:S(2)}) collective-permute-start(bf16[256,1024]{1,0:T(8,128)(2,1)S(1)} %pad_maximum_fusion.9.own_ref), channel_id=1, source_target_pairs={{0,1},{1,0},{2,3},{3,2},{4,5},{5,4},{6,7},{7,6},{8,9},{9,8},{10,11... | collective-permute-start | bytes 1572872 | tf_op jit(solution)/shard_map/ppermute | solution.py:36
  283.9 18.6 %collective-permute-start.34 = (bf16[256,1024]{1,0:T(8,128)(2,1)}, bf16[256,1024]{1,0:T(8,128)(2,1)S(1)}, u32[]{:S(2)}, u32[]{:S(2)}) collective-permute-start(bf16[256,1024]{1,0:T(8,128)(2,1)} %copy-done.52), channel_id=1, source_target_pairs={{0,1},{1,0},{2,3},{3,2},{4,5},{5,4},{6,7},{7,6},{8,9},{9,8},{10,11... | collective-permute-start | bytes 1572872 | tf_op jit(solution)/shard_map/ppermute | solution.py:36
  300.2 22.7 %collective-permute-start.38 = (bf16[256,1024]{1,0:T(8,128)(2,1)S(1)}, bf16[256,1024]{1,0:T(8,128)(2,1)S(1)}, u32[]{:S(2)}, u32[]{:S(2)}) collective-permute-start(bf16[256,1024]{1,0:T(8,128)(2,1)S(1)} %add_convert_fusion.6), channel_id=1, source_target_pairs={{0,4},{4,0},{1,5},{5,1},{2,6},{6,2},{3,7},{7,3},{8,12},{12,8},{9,1... | collective-permute-start | bytes 1572872 | tf_op jit(solution)/shard_map/ppermute | solution.py:36
  361.2 18.5 %collective-permute-start.40 = (bf16[1024,2048]{1,0:T(8,128)(2,1)S(1)}, bf16[1024,2048]{1,0:T(8,128)(2,1)S(1)}, u32[]{:S(2)}, u32[]{:S(2)}) collective-permute-start(bf16[1024,2048]{1,0:T(8,128)(2,1)S(1)} %outer.6), channel_id=1, source_target_pairs={{0,1},{1,0},{2,3},{3,2},{4,5},{5,4},{6,7},{7,6},{8,9},{9,8},{10,11... | collective-permute-start | bytes 12582920 | tf_op jit(solution)/shard_map/ppermute | solution.py:36
  363.4 21.1 %collective-permute-start.41 = (bf16[1024,2048]{1,0:T(8,128)(2,1)}, bf16[1024,2048]{1,0:T(8,128)(2,1)}, u32[]{:S(2)}, u32[]{:S(2)}) collective-permute-start(bf16[1024,2048]{1,0:T(8,128)(2,1)} %outer.8), channel_id=1, source_target_pairs={{0,1},{1,0},{2,3},{3,2},{4,5},{5,4},{6,7},{7,6},{8,9},{9,8},{10,11... | collective-permute-start | bytes 12582920 | tf_op jit(solution)/shard_map/ppermute | solution.py:36
  392.2 157.8 %reduce-scatter.4.cloned.1.call-start = ((), (), s32[]{:S(2)}) async-start(), calls=%async_computation.7 | async-start | bytes 5242880 | tf_op jit(solution)/shard_map/reduce_scatter | solution.py:625
  421.5 22.9 %collective-permute-start.47 = (bf16[256,1024]{1,0:T(8,128)(2,1)S(1)}, bf16[256,1024]{1,0:T(8,128)(2,1)S(1)}, u32[]{:S(2)}, u32[]{:S(2)}) collective-permute-start(bf16[256,1024]{1,0:T(8,128)(2,1)S(1)} %add_convert_fusion.2), channel_id=1, source_target_pairs={{0,4},{4,0},{1,5},{5,1},{2,6},{6,2},{3,7},{7,3},{8,12},{12,8},{9,1... | collective-permute-start | bytes 1572872 | tf_op jit(solution)/shard_map/ppermute | solution.py:36
  451.7 35.8 %collective-permute-start.50 = (bf16[1024,2048]{1,0:T(8,128)(2,1)}, bf16[1024,2048]{1,0:T(8,128)(2,1)}, u32[]{:S(2)}, u32[]{:S(2)}) collective-permute-start(bf16[1024,2048]{1,0:T(8,128)(2,1)} %outer.10), channel_id=1, source_target_pairs={{0,1},{1,0},{2,3},{3,2},{4,5},{5,4},{6,7},{7,6},{8,9},{9,8},{10,11... | collective-permute-start | bytes 12582920 | tf_op jit(solution)/shard_map/ppermute | solution.py:36
  452.7 148.3 %reduce-scatter.8.cloned.1.call-start = ((), (), s32[]{:S(2)}) async-start(), calls=%async_computation.9 | async-start | bytes 2621440 | tf_op jit(solution)/shard_map/reduce_scatter | solution.py:627
  494.6 16.2 %collective-permute-start.51 = (bf16[2,64,2304]{2,1,0:T(8,128)(2,1)S(1)}, bf16[2,64,2304]{2,1,0:T(8,128)(2,1)S(1)}, u32[]{:S(2)}, u32[]{:S(2)}) collective-permute-start(bf16[2,64,2304]{2,1,0:T(8,128)(2,1)S(1)} %get-tuple-element.160), channel_id=1, source_target_pairs={{0,4},{4,8},{8,12},{12,0},{1,5},{5,9},{9,13},{13,1},{2,6},{6,10},{... | collective-permute-start | bytes 1769480 | tf_op jit(solution)/shard_map/ppermute | solution.py:291
  498.1 15.8 %collective-permute-start.53 = (bf16[2,64,2304]{2,1,0:T(8,128)(2,1)S(1)}, bf16[2,64,2304]{2,1,0:T(8,128)(2,1)S(1)}, u32[]{:S(2)}, u32[]{:S(2)}) collective-permute-start(bf16[2,64,2304]{2,1,0:T(8,128)(2,1)S(1)} %get-tuple-element.162), channel_id=1, source_target_pairs={{0,12},{4,0},{8,4},{12,8},{1,13},{5,1},{9,5},{13,9},{2,14},{6,2},{... | collective-permute-start | bytes 1769480 | tf_op jit(solution)/shard_map/ppermute | solution.py:292
  515.5 27.8 %collective-permute-start.54 = (bf16[4,64,2304]{2,1,0:T(8,128)(2,1)}, bf16[4,64,2304]{2,1,0:T(8,128)(2,1)S(1)}, u32[]{:S(2)}, u32[]{:S(2)}) collective-permute-start(bf16[4,64,2304]{2,1,0:T(8,128)(2,1)} %pad_maximum_fusion.3), channel_id=1, source_target_pairs={{0,12},{4,0},{8,4},{12,8},{1,13},{5,1},{9,5},{13,9},{2,14},{6,2},{... | collective-permute-start | bytes 3538952 | tf_op jit(solution)/shard_map/ppermute | solution.py:296
  516.6 27.7 %collective-permute-start.52 = (bf16[4,64,2304]{2,1,0:T(8,128)(2,1)}, bf16[4,64,2304]{2,1,0:T(8,128)(2,1)S(1)}, u32[]{:S(2)}, u32[]{:S(2)}) collective-permute-start(bf16[4,64,2304]{2,1,0:T(8,128)(2,1)} %pad_maximum_fusion.2), channel_id=1, source_target_pairs={{0,4},{4,8},{8,12},{12,0},{1,5},{5,9},{9,13},{13,1},{2,6},{6,10},{... | collective-permute-start | bytes 3538952 | tf_op jit(solution)/shard_map/ppermute | solution.py:295
  568.4 30.3 %all-to-all-start.2 = ((bf16[4,2,64,1024]{3,2,1,0:T(8,128)(2,1)}), bf16[4,2,64,1024]{3,2,1,0:T(8,128)(2,1)S(1)}, u32[]{:S(2)}, u32[]{:S(2)}) async-start(bf16[4,2,64,1024]{3,2,1,0:T(8,128)(2,1)} %pad_maximum_fusion.4), calls=%async_computation.2 | async-start | bytes 2097152 | tf_op jit(solution)/shard_map/all_to_all | solution.py:234
  572.7 27.2 %collective-permute-start.59 = (bf16[64,2304]{1,0:T(8,128)(2,1)S(1)}, bf16[64,2304]{1,0:T(8,128)(2,1)S(1)}, u32[]{:S(2)}, u32[]{:S(2)}) collective-permute-start(bf16[64,2304]{1,0:T(8,128)(2,1)S(1)} %add_convert_fusion.12), channel_id=1, source_target_pairs={{0,1},{1,0},{2,3},{3,2},{4,5},{5,4},{6,7},{7,6},{8,9},{9,8},{10,11... | collective-permute-start | bytes 884744 | tf_op jit(solution)/shard_map/ppermute | solution.py:36
  (158 other events, 2291.7 us)
Sparse Core Ops, SparseCore 0:
  30.6 87.4 all-gather.1
  392.3 47.6 reduce-scatter.5
  452.8 47.3 reduce-scatter.3
  553.2 40.3 reduce-scatter.7

commit v5 on v4

--- a/solution.py
+++ b/solution.py
@@ -204,18 +204,72 @@
     )(*operands)
 
 
-def fc1_sum(normed, grad_before):
-    width = normed.shape[1]
-    make = lambda g, add=None: outer([((normed, 0), g, width)], 512, add=add)
-    return make(grad_before[0], swap(make(grad_before[1]), "core"))
-
-
-def fc2_sum(activated, grad_branch):
+def fc1_part(normed, grad_before, add=None):
+    return outer([((normed, 0), grad_before, normed.shape[1])], 512, add=add)
+
+
+def fc2_part(activated, grad_branch, add=None):
     width = grad_branch.shape[1]
-    make = lambda z, add=None: outer(
-        [((z, i), grad_branch, width) for i in range(z.shape[1] // width)], 512, add=add
-    )
-    return make(activated[0], swap(make(activated[1]), "core"))
+    count = activated.shape[1] // width
+    return outer([((activated, i), grad_branch, width) for i in range(count)], 512, add=add)
+
+
+def join(kernel, core, inputs, shapes):
+    vmem = pl.BlockSpec(memory_space=pltpu.VMEM)
+    return pl.pallas_call(
+        kernel,
+        in_specs=[pl.BlockSpec(memory_space=pltpu.SMEM)] + [vmem] * len(inputs),
+        out_specs=[vmem] * len(shapes),
+        out_shape=[jax.ShapeDtypeStruct(shape, f32) for shape in shapes],
+        compiler_params=pltpu.CompilerParams(vmem_limit_bytes=24 * 2**20),
+        cost_estimate=pl.CostEstimate(
+            flops=0, bytes_accessed=6 * sum(a.size for a in inputs), transcendentals=0
+        ),
+        name="join",
+    )(core.reshape(1), *inputs)
+
+
+def join_qkv(core, mine, other, width):
+    rows, half = mine.shape[0], width // 2
+
+    def kernel(core_ref, mine_ref, other_ref, qkv_ref, proj_ref):
+        for ref, place in ((mine_ref, core_ref[0]), (other_ref, 1 - core_ref[0])):
+            at = place * half
+            columns = lambda start, size: pl.ds(pl.multiple_of(at + start, PAIR), size)
+            qkv_ref[:, columns(0, half)] = ref[:, :half].astype(f32)
+            proj_ref[:, columns(0, half)] = ref[:, half:width].astype(f32)
+            for g in range(half // PAIR):
+                k = width + 2 * g * PAIR
+                for i in range(2):
+                    qkv_ref[:, columns((i + 1) * width + g * PAIR, PAIR)] = ref[
+                        :, k + i * PAIR : k + (i + 1) * PAIR
+                    ].astype(f32)
+
+    return join(kernel, core, [mine, other], [(rows, 3 * width), (rows, width)])
+
+
+def join_fc(core, mine, other, width, shards):
+    rows = mine.shape[0]
+    wide = mine.shape[1] - 2 * width
+    part = wide // (2 * shards)
+    pair = 2 * part
+
+    def kernel(core_ref, mine_ref, other_ref, fc1_ref, fc2_ref):
+        for ref, place in ((mine_ref, core_ref[0]), (other_ref, 1 - core_ref[0])):
+            for f in range(shards):
+                at = pl.multiple_of(2 * pair * f + place * pair, pair)
+                value = [
+                    ref[:, i * shards * part + f * part : i * shards * part + (f + 1) * part]
+                    for i in range(2)
+                ]
+                fc1_ref[:, pl.ds(at, pair)] = jnp.concatenate(value, axis=1).astype(f32)
+            for i in range(2):
+                at = pl.multiple_of(place * 2 * rows + i * rows, rows)
+                fc2_ref[pl.ds(at, rows)] = ref[
+                    :, wide + i * width : wide + (i + 1) * width
+                ].astype(f32)
+
+    return join(kernel, core, [mine, other], [(rows, 2 * wide), (4 * rows, width)])
 
 
 FLIP = [(0, 0), (1, 2), (2, 1), (3, 3)]
@@ -224,12 +278,16 @@
 def to_images(tokens):
     count, rows, width = tokens.shape
     mixed = lax.all_to_all(tokens, "z", split_axis=0, concat_axis=0, tiled=True)
-    return lax.ppermute(mixed.reshape(count * rows, width), ("yh", "core"), FLIP)
+    return mixed.reshape(count * rows, width)
+
+
+def flip(tokens):
+    return lax.ppermute(tokens, ("yh", "core"), FLIP)
 
 
 def from_images(arrays, count):
     rows, width = arrays[0].shape
-    mixed = [lax.ppermute(a, ("yh", "core"), FLIP) for a in arrays]
+    mixed = [flip(a) for a in arrays]
     mixed = jnp.stack([m.reshape(count, rows // count, width) for m in mixed], axis=1)
     mixed = lax.all_to_all(mixed, "z", split_axis=0, concat_axis=0, tiled=True)
     return [mixed[:, i] for i in range(len(arrays))]
@@ -297,21 +355,10 @@
     return add(block(0), after, before)
 
 
-def group_blocks(key_value):
-    mate = swap(key_value, "core")
-    near = swap(key_value, "yl")
-    far = swap(near, "core")
-    return (key_value, mate, near, far)
-
-
 def group_parts(own, mate, near, far):
     mate, far = swap(mate, "core"), swap(far, "core")
     sent = (near.astype(f32) + far.astype(f32)).astype(bf16)
     return own.astype(f32) + mate.astype(f32), sent
-
-
-def group_add(kept, sent):
-    return (kept + swap(sent, "yl").astype(f32)).astype(bf16)
 
 
 def normal_part(values):
@@ -357,16 +404,24 @@
         (mm(normed_one, part) + bias).astype(bf16) for part, bias in zip(w[name], w[name + "_bias"])
     ]
     key_value = chunked(project("kv"))
-    if late is not None:
-        key_value, gathered = lax.optimization_barrier((key_value, late[0]))
-        w.update(late[1](gathered))
-    blocks = [group_blocks(key_value[0])]
-    for c in key_value[1:]:
-        c, near = lax.optimization_barrier((c, blocks[-1][2]))
-        blocks[-1] = (*blocks[-1][:2], near, blocks[-1][3])
-        blocks.append(group_blocks(c))
     queries = chunked(project("q"))
-    attended, log_total = zip(*(attend(q, b) for q, b in zip(queries, blocks)))
+    mate, near = swap(key_value[0], "core"), swap(key_value[0], "yl")
+    blocks, results = [], []
+    for i, own in enumerate(key_value):
+        blocks.append((own, mate, near, swap(near, "core")))
+        if i + 1 < CHUNKS:
+            following, near = lax.optimization_barrier((key_value[i + 1], near))
+            mate, near = swap(following, "core"), swap(following, "yl")
+            result = attend(queries[i], blocks[i])
+            result, near = lax.optimization_barrier((result, near))
+        else:
+            if late is not None:
+                (own, near), gathered = lax.optimization_barrier(((own, near), late[0]))
+                w.update(late[1](gathered))
+                blocks[i] = (own, mate, near, blocks[i][3])
+            result = attend(queries[i], blocks[i])
+        results.append(result)
+    attended, log_total = zip(*results)
     attended = jnp.concatenate(unchunked(attended), axis=1)
     attended = flip_halves(w["core"], attended)
     branch = flip_halves(w["core"], jnp.concatenate([mm(attended, p) for p in w["proj"]], axis=1))
@@ -407,12 +462,16 @@
     grad_before = []
     grad_normed_two = 0.0
     if last:
-        fc2 = fc2_sum(kept["activated"], grad_branch_two)
+        fc2_sent = swap(fc2_part(kept["activated"][1], grad_branch_two), "core")
     for up, down, slope in zip(w["fc1"], w["fc2"], kept["slope"]):
         part = jnp.concatenate([mm_t(grad_branch_two, d) for d in down], axis=1)
         part = (part * slope.astype(f32)).astype(bf16)
         grad_before.append(part)
         grad_normed_two = grad_normed_two + mm_t(part, up)
+    if last:
+        fc2 = fc2_part(kept["activated"][0], grad_branch_two, fc2_sent)
+        fc2, grad_normed_two = lax.optimization_barrier((fc2, grad_normed_two))
+        fc2 = lax.psum_scatter(fc2, RING_Z, scatter_dimension=0, tiled=True)
     normal_two, factor_two = normal_part(kept["middle"])
     grad_middle = grad_out + norm_back(grad_normed_two, normal_two, factor_two, w["gain"][1])
     grad_branch = (w["scale"][0] * grad_middle).astype(bf16)
@@ -424,19 +483,31 @@
     grad_attended = flip_halves(w["core"], grad_attended)
     fc_grad = None
     if last:
-        fc_grad = [fc1_sum(kept["normed_two"], grad_before), fc2]
-        fc_grad, grad_attended = lax.optimization_barrier((fc_grad, grad_attended))
+        fc1_sent = fc1_part(kept["normed_two"], grad_before[1])
+        fc1_sent, grad_attended = lax.optimization_barrier((fc1_sent, grad_attended))
+        fc1_sent = swap(fc1_sent, "core")
     grad_chunks = chunked([grad_attended[:, :half], grad_attended[:, half:]])
     q_chunks, kv_chunks = [], []
     ready = None
-    for q, b, g, t in zip(kept["queries"], kept["blocks"], grad_chunks, kept["log_total"]):
+    for i in range(CHUNKS):
+        g = grad_chunks[i]
         if ready is not None:
-            sent, g = lax.optimization_barrier((ready[1], g))
-            kv_chunks.append(group_add(ready[0], sent))
-        parts = attend_back(q, b, g, t)
+            own, sent = ready
+            if last and fc_grad is None:
+                fc1 = fc1_part(kept["normed_two"], grad_before[0], fc1_sent)
+                sent, g, fc1 = lax.optimization_barrier((sent, g, fc1))
+                fc1 = lax.psum_scatter(fc1, RING_Z, scatter_dimension=0, tiled=True)
+                fc_grad = [fc1, fc2]
+            else:
+                sent, g = lax.optimization_barrier((sent, g))
+            came = swap(sent, "yl")
+        parts = attend_back(kept["queries"][i], kept["blocks"][i], g, kept["log_total"][i])
+        if ready is not None:
+            parts, came = lax.optimization_barrier((parts, came))
+            kv_chunks.append((own + came.astype(f32)).astype(bf16))
         q_chunks.append(parts[0])
         ready = group_parts(*parts[1:])
-    kv_chunks.append(group_add(*ready))
+    kv_chunks.append((ready[0] + swap(ready[1], "yl").astype(f32)).astype(bf16))
     grad_q, grad_kv = unchunked(q_chunks), unchunked(kv_chunks)
     grad_normed_one = sum(
         mm_t(g, part) for g, part in zip(grad_q + grad_kv, w["q"] + w["kv"])
@@ -514,7 +585,10 @@
     first_tokens = to_images(patch_tokens)
     a_row = ring_place(a_mine, RING_Y, [(4, own, a_mine.shape[1])], in_order, direct=True)[0]
     b_row = ring_place(kv_mine, RING_Z, [(4, own, width)], in_order, direct=True)[0]
-    a_row, b_row, fc_mine = lax.optimization_barrier((a_row, b_row, fc_mine))
+    a_row, b_row, fc_mine, first_tokens = lax.optimization_barrier(
+        (a_row, b_row, fc_mine, first_tokens)
+    )
+    first_tokens = flip(first_tokens)
     fc_half = lax.all_gather(fc_mine, FSDP, axis=0, tiled=True)
     a_row = a_row.reshape(4 * own, a_mine.shape[1])
 
@@ -580,14 +654,14 @@
     live_grad = out_grad * live[:, None, None]
     sent, live_grad = lax.optimization_barrier((sent, live_grad))
     passed = lax.ppermute(sent, "section", [(0, 1)])
-    last_grad = to_images(live_grad)
+    last_grad = flip(to_images(live_grad))
     tokens = jnp.where(section == 0, first_tokens, passed)
     result, kept = forward(tokens, w)
 
     sent, _, _ = backward(last_grad.astype(f32), kept, w)
     passed = lax.ppermute(sent, "section", [(1, 0)])
     grad_out = jnp.where(section == 1, last_grad, passed).astype(f32)
-    grad_inputs, sums, outer_parts = backward(grad_out, kept, w, last=True)
+    grad_inputs, sums, products = backward(grad_out, kept, w, last=True)
     result, grad_inputs = lax.optimization_barrier((result, grad_inputs))
     block_out, in_grad = from_images([result, grad_inputs], images)
 
@@ -601,63 +675,43 @@
         ),
         axis=1,
     ).reshape(width, hidden // own)
-    vector_grads = jnp.concatenate(
+    vector_grads = jnp.stack(
         [
-            jnp.stack(
-                [
-                    *sums["gain"],
-                    *sums["shift"],
-                    natural(sums["q"]),
-                    natural([v_sum(g) for g in sums["kv"]]),
-                    *sums["out_bias"],
-                    *sums["scale"],
-                ],
-                axis=1,
-            ),
-            fc1_bias_sum,
-        ],
-        axis=1,
-    )
-    step = 256
-    vector_grads = jnp.pad(vector_grads, ((0, 0), (0, step - count))).astype(bf16)
-
-    rows = [
-        lax.psum_scatter(g, RING_Z, scatter_dimension=0, tiled=True) for g in outer_parts["fc"]
-    ]
+            *sums["gain"],
+            *sums["shift"],
+            natural(sums["q"]),
+            natural([v_sum(g) for g in sums["kv"]]),
+            *sums["out_bias"],
+            *sums["scale"],
+            *fc1_bias_sum.T,
+        ]
+    )
+    vector_grads = jnp.pad(vector_grads, ((0, PAIR - count), (0, 0))).astype(bf16).T
+
+    a1, dq = products["q"]
+    dkv = products["kv"][1]
+    o, e1 = products["proj"]
+    make = lambda i, add=None: outer(
+        [((a1, 0), dq[i], width), ((o, 0), e1[i], width), ((a1, 0), dkv[i], width)], 256, add=add
+    )
+    ab = make(0, swap(make(1), "core")).reshape(4, 4, own, 2 * width)
+    ab = ring_sum(ab, RING_Y, 1)
+    vector_grads = ring_sum(vector_grads.reshape(4, 4, own, PAIR), RING_Y, 1, direct=True)
+    ab, vector_grads, rows = lax.optimization_barrier((ab, vector_grads, products["fc"]))
     fc_grad = lax.psum_scatter(
         jnp.concatenate(rows, axis=1), RING_Y, scatter_dimension=0, tiled=True
     )
-    a1, dq = outer_parts["q"]
-    dkv = outer_parts["kv"][1]
-    o, e1 = outer_parts["proj"]
-    make = lambda i, **more: outer(
-        [((a1, 0), dq[i], width), ((o, 0), e1[i], width), ((a1, 0), dkv[i], width)], step, **more
-    )
-    ab = make(0, add=swap(make(1), "core"), tail=vector_grads)
-    ab = ring_sum(ab.reshape(4, 4, own, 2 * width + step), RING_Y, 1)
-    ab_grad = ring_sum(ab, RING_Z, 0, direct=True)
-
-    parts = [ab_grad, fc_grad]
-    parts = [(a.astype(f32) + swap(a, "xhi").astype(f32)).astype(bf16) for a in parts]
-    others = [swap(a, "core") for a in parts]
-    vec_grad = sum(p[0][:, 2 * width : 2 * width + count].astype(f32) for p in (parts, others)).T
-    ab_pair, fc_pair = (
-        ordered(core, a.astype(f32), b.astype(f32)) for a, b in zip(parts, others)
-    )
-    q_grad = jnp.concatenate([p[:, :half] for p in ab_pair], axis=1)
-    proj_out = jnp.concatenate([p[:, half:width] for p in ab_pair], axis=1)
-    kv_grads = [p[:, width : 2 * width].reshape(own, groups, 2, PAIR) for p in ab_pair]
-    k_grad, v_grad = (
-        jnp.concatenate([p[:, :, i].reshape(own, half) for p in kv_grads], axis=1)
-        for i in range(2)
-    )
-    qkv_out = jnp.concatenate([q_grad, k_grad, v_grad], axis=1)
-    fc1_out = jnp.stack(
-        [jnp.swapaxes(p[:, :wide].reshape(own, 2, shards, part), 1, 2) for p in fc_pair], axis=2
-    ).reshape(own, 2 * wide)
-    fc2_out = jnp.concatenate(
-        [p[:, wide + i * width : wide + (i + 1) * width] for p in fc_pair for i in range(2)], axis=0
-    )
+    ab = ring_sum(jnp.concatenate([ab, vector_grads], axis=2), RING_Z, 0, direct=True)
+
+    def chips_sum(a):
+        return (a.astype(f32) + swap(a, "xhi").astype(f32)).astype(bf16)
+
+    ab = chips_sum(ab)
+    ab_other = swap(ab, "core")
+    qkv_out, proj_out = join_qkv(core, ab, ab_other, width)
+    vec_grad = sum(p[:, 2 * width : 2 * width + count].astype(f32) for p in (ab, ab_other)).T
+    fc_grad = chips_sum(fc_grad)
+    fc1_out, fc2_out = join_fc(core, fc_grad, swap(fc_grad, "core"), width, shards)
     return (
         block_out[None],
         in_grad[None],

time: 657 us -> 624 us (0.950)
  the two profiles are of different devices: /device:TPU:25 before, /device:TPU:1 now
where the time goes in v5:
time: 624 us; the launch traced here: 612 us
  waiting for transfers between devices  186 us (30%)
  starting transfers between devices  101 us (16%)
  Pallas kernels  93.9 us (15%)
  matrix products  85.3 us (14%)
  local copies, waits for them, and re-layouts  83.7 us (13%)
  other arithmetic  45.7 us (7%)
  between operations  17.2 us (3%)
    dot_general x48, matrix products, dot(): return lax.dot_general(a, b, (dims, ((), ())), preferred_element_type=f32)  85.3 us
    ppermute x35, waiting for transfers between devices, swap(): return lax.ppermute(value, axis, [(0, 1), (1, 0)])  49 us
    pallas_call x4, Pallas kernels, attend_back(): pl.pallas_call(attend_back_kernel, grid=(pairs,), in_specs=[q_spec] + kv_...  37.1 us
    ppermute x35, starting transfers between devices, swap(): return lax.ppermute(value, axis, [(0, 1), (1, 0)])  35.5 us
    unnamed x311, local copies, waits for them, and re-layouts  32.1 us
    ppermute x4, waiting for transfers between devices, flip(): return lax.ppermute(tokens, ('yh', 'core'), FLIP)  30.5 us
    pallas_call x4, Pallas kernels, attend(): pl.pallas_call(attend_kernel, grid=(pairs,), in_specs=[q_spec] + kv_specs...  30 us
    ppermute x4, waiting for transfers between devices, ring_place(): back = lax.ppermute(value, axis, BACK)  29.7 us
  transfers between devices with their start and end apart: 72, of which 25 were waited for; matrix products, arithmetic and copies ran while one was open for 23% of the time, Pallas kernels for 12%

profile of v5, /device:TPU:1, one launch (start us, length us, event | category | flops | bytes accessed | tf_op | source)
XLA Modules:
  0.0 612.3 jit_solution(9695763252397011547)
XLA Ops:
  34.1 9.1 %collective-permute-done.13.refs_2_ = bf16[4,64,1024]{2,1,0:T(8,128)(2,1)S(1)} collective-permute-done((bf16[4,64,1024]{2,1,0:T(8,128)(2,1)S(1)}, bf16[4,64,1024]{2,1,0:T(8,128)(2,1)S(1)}, u32[]{:S(2)}, u32[]{:S(2)}) %collective-permute-start.13) | collective-permute-done | bytes 524320 | tf_op jit(solution)/shard_map/ppermute | solution.py:307
  45.0 7.0 %collective-permute-start.6 = (bf16[256,1024]{1,0:T(8,128)(2,1)}, bf16[256,1024]{1,0:T(8,128)(2,1)}, u32[]{:S(2)}, u32[]{:S(2)}) collective-permute-start(bf16[256,1024]{1,0:T(8,128)(2,1)} %bitcast.17), channel_id=1, source_target_pairs={{0,0},{1,8},{8,1},{9,9},{2,2},{3,10},{10,3},{11,11},{4,4},{5,12},{... | collective-permute-start | bytes 1572872 | tf_op jit(solution)/shard_map/ppermute | solution.py:285
  58.5 10.2 %collective-permute-start.16 = (bf16[1024,1024]{1,0:T(8,128)(2,1)S(1)}, bf16[1024,1024]{1,0:T(8,128)(2,1)}, u32[]{:S(2)}, u32[]{:S(2)}) collective-permute-start(bf16[1024,1024]{1,0:T(8,128)(2,1)S(1)} %bitcast.195), channel_id=1, source_target_pairs={{0,1},{1,0},{2,3},{3,2},{4,5},{5,4},{6,7},{7,6},{8,9},{9,8},{10,11... | collective-permute-start | bytes 6291464 | tf_op jit(solution)/shard_map/ppermute | solution.py:36
  72.6 20.6 %collective-permute-done.8.refs_2_ = bf16[256,1152]{1,0:T(8,128)(2,1)S(1)} collective-permute-done((bf16[256,1152]{1,0:T(8,128)(2,1)S(1)}, bf16[256,1152]{1,0:T(8,128)(2,1)S(1)}, u32[]{:S(2)}, u32[]{:S(2)}) %collective-permute-start.8) | collective-permute-done | bytes 589856 | tf_op jit(solution)/shard_map/ppermute | solution.py:307
  99.4 9.8 %collective-permute-done.10.refs_4_ = bf16[128,1152]{1,0:T(8,128)(2,1)S(1)} collective-permute-done((bf16[128,1152]{1,0:T(8,128)(2,1)S(1)}, bf16[128,1152]{1,0:T(8,128)(2,1)S(1)}, u32[]{:S(2)}, u32[]{:S(2)}) %collective-permute-start.10) | collective-permute-done | bytes 294944 | tf_op jit(solution)/shard_map/ppermute | solution.py:313
  109.2 4.7 collective-permute-done.9.refs_3_
  130.4 10.8 %collective-permute-done.18.near_ref = bf16[256,1024]{1,0:T(8,128)(2,1)S(1)} collective-permute-done((bf16[256,1024]{1,0:T(8,128)(2,1)S(1)}, bf16[256,1024]{1,0:T(8,128)(2,1)S(1)}, u32[]{:S(2)}, u32[]{:S(2)}) %collective-permute-start.18) | collective-permute-done | bytes 524320 | tf_op jit(solution)/shard_map/ppermute | solution.py:36
  144.9 7.6 %attend.4 = (bf16[256,512]{1,0:T(8,128)(2,1)S(1)}, f32[4,2,256]{2,1,0:T(2,128)}) custom-call(bf16[256,512]{1,0:T(8,128)(2,1)S(1)} %pad_maximum_fusion.11.q_ref, bf16[256,1024]{1,0:T(8,128)(2,1)S(1)} %pad_maximum_fusion.5.own_ref, bf16[256,1024]{1,0:T(8,128)(2,1)S(1)} %collective-permute-done.17.mate_ref, ...), custom_call_target="tpu_custom_call" | custom-call | flops 2147483648 | bytes 4194304 | tf_op jit(solution)/shard_map/attend/pallas_call | solution.py:118
  152.5 5.1 collective-permute-done.20.near_ref
  178.5 8.4 %attend.5 = (bf16[256,512]{1,0:T(8,128)(2,1)S(1)}, f32[4,2,256]{2,1,0:T(2,128)}) custom-call(bf16[256,512]{1,0:T(8,128)(2,1)S(1)} %pad_maximum_fusion.12.q_ref, bf16[256,1024]{1,0:T(8,128)(2,1)S(1)} %copy-done.31, bf16[256,1024]{1,0:T(8,128)(2,1)} %collective-permute-done.21.mate_ref, bf16[256,1024]{1,0:T(8,128)(2,1)S(1)} %copy-done.63, ...), custom_call_target="tpu_custom_call" | custom-call | flops 2147483648 | bytes 4194304 | tf_op jit(solution)/shard_map/attend/pallas_call | solution.py:118
  209.8 8.8 %all-to-all-done.1 = bf16[4,64,1024]{2,1,0:T(8,128)(2,1)} async-done(((bf16[4,64,1024]{2,1,0:T(8,128)(2,1)}), bf16[4,64,1024]{2,1,0:T(8,128)(2,1)}, u32[]{:S(2)}, u32[]{:S(2)}) %all-to-all-start.1) | async-done | bytes 524320 | tf_op jit(solution)/shard_map/all_to_all | solution.py:280
  229.8 6.5 %collective-permute-done.32 = bf16[256,1024]{1,0:T(8,128)(2,1)S(1)} collective-permute-done((bf16[256,1024]{1,0:T(8,128)(2,1)}, bf16[256,1024]{1,0:T(8,128)(2,1)S(1)}, u32[]{:S(2)}, u32[]{:S(2)}) %collective-permute-start.32) | collective-permute-done | bytes 524320 | tf_op jit(solution)/shard_map/ppermute | solution.py:285
  247.4 7.0 %attend.6 = (bf16[256,512]{1,0:T(8,128)(2,1)S(1)}, f32[4,2,256]{2,1,0:T(2,128)S(1)}) custom-call(bf16[256,512]{1,0:T(8,128)(2,1)S(1)} %pad_maximum_fusion.13.q_ref, bf16[256,1024]{1,0:T(8,128)(2,1)S(1)} %pad_maximum_fusion.7.own_ref, bf16[256,1024]{1,0:T(8,128)(2,1)S(1)} %collective-permute-done.26.mate_ref, ...), custom_call_target="tpu_custom_call" | custom-call | flops 2147483648 | bytes 4194304 | tf_op jit(solution)/shard_map/attend/pallas_call | solution.py:118
  256.5 7.0 %attend.7 = (bf16[256,512]{1,0:T(8,128)(2,1)S(1)}, f32[4,2,256]{2,1,0:T(2,128)S(1)}) custom-call(bf16[256,512]{1,0:T(8,128)(2,1)S(1)} %pad_maximum_fusion.14.q_ref, bf16[256,1024]{1,0:T(8,128)(2,1)S(1)} %pad_maximum_fusion.8.own_ref, bf16[256,1024]{1,0:T(8,128)(2,1)S(1)} %collective-permute-done.30.mate_ref, ...), custom_call_target="tpu_custom_call" | custom-call | flops 2147483648 | bytes 4194304 | tf_op jit(solution)/shard_map/attend/pallas_call | solution.py:118
  270.8 5.2 fusion.41
  283.1 9.0 %attend_back.4 = (bf16[256,512]{1,0:T(8,128)(2,1)S(1)}, bf16[256,1024]{1,0:T(8,128)(2,1)S(1)}, bf16[256,1024]{1,0:T(8,128)(2,1)S(1)}, bf16[256,1024]{1,0:T(8,128)(2,1)S(1)}, bf16[256,1024]{1,0:T(8,128)(2,1)S(1)}) custom-call(bf16[256,512]{1,0:T(8,128)(2,1)S(1)} %pad_maximum_fusion.13.q_ref, bf16[256,1024]{1,0:T(8,128)(2,1)S(1)} %pad_maximum_fusion.7.own_ref, ...), custom_call_target="tpu_custom_call" | custom-call | flops 5368709120 | bytes 4194304 | tf_op jit(solution)/shard_map/attend_back/pallas_call | solution.py:137
  302.8 8.9 %attend_back.5 = (bf16[256,512]{1,0:T(8,128)(2,1)S(1)}, bf16[256,1024]{1,0:T(8,128)(2,1)S(1)}, bf16[256,1024]{1,0:T(8,128)(2,1)S(1)}, bf16[256,1024]{1,0:T(8,128)(2,1)S(1)}, bf16[256,1024]{1,0:T(8,128)(2,1)S(1)}) custom-call(bf16[256,512]{1,0:T(8,128)(2,1)S(1)} %pad_maximum_fusion.14.q_ref, bf16[256,1024]{1,0:T(8,128)(2,1)S(1)} %copy-done.26, ...), custom_call_target="tpu_custom_call" | custom-call | flops 5368709120 | bytes 4194304 | tf_op jit(solution)/shard_map/attend_back/pallas_call | solution.py:137
  317.9 12.1 %collective-permute-done.38 = bf16[256,1024]{1,0:T(8,128)(2,1)S(1)} collective-permute-done((bf16[256,1024]{1,0:T(8,128)(2,1)S(1)}, bf16[256,1024]{1,0:T(8,128)(2,1)S(1)}, u32[]{:S(2)}, u32[]{:S(2)}) %collective-permute-start.38) | collective-permute-done | bytes 524320 | tf_op jit(solution)/shard_map/ppermute | solution.py:36
  341.4 8.4 %collective-permute-done.39 = bf16[256,1024]{1,0:T(8,128)(2,1)S(1)} collective-permute-done((bf16[256,1024]{1,0:T(8,128)(2,1)S(1)}, bf16[256,1024]{1,0:T(8,128)(2,1)S(1)}, u32[]{:S(2)}, u32[]{:S(2)}) %collective-permute-start.39) | collective-permute-done | bytes 524320 | tf_op jit(solution)/shard_map/ppermute | solution.py:662
  371.6 4.5 fusion.86
  392.6 9.6 %attend_back.6 = (bf16[256,512]{1,0:T(8,128)(2,1)S(1)}, bf16[256,1024]{1,0:T(8,128)(2,1)S(1)}, bf16[256,1024]{1,0:T(8,128)(2,1)}, bf16[256,1024]{1,0:T(8,128)(2,1)S(1)}, bf16[256,1024]{1,0:T(8,128)(2,1)S(1)}) custom-call(bf16[256,512]{1,0:T(8,128)(2,1)S(1)} %copy-done.39, bf16[256,1024]{1,0:T(8,128)(2,1)S(1)} %copy-done.29, ...), custom_call_target="tpu_custom_call" | custom-call | flops 5368709120 | bytes 4194304 | tf_op jit(solution)/shard_map/attend_back/pallas_call | solution.py:137
  415.7 9.6 %attend_back.7 = (bf16[256,512]{1,0:T(8,128)(2,1)S(1)}, bf16[256,1024]{1,0:T(8,128)(2,1)S(1)}, bf16[256,1024]{1,0:T(8,128)(2,1)S(1)}, bf16[256,1024]{1,0:T(8,128)(2,1)S(1)}, bf16[256,1024]{1,0:T(8,128)(2,1)}) custom-call(bf16[256,512]{1,0:T(8,128)(2,1)S(1)} %pad_maximum_fusion.14.q_ref, bf16[256,1024]{1,0:T(8,128)(2,1)S(1)} %copy-done.27, ...), custom_call_target="tpu_custom_call" | custom-call | flops 5368709120 | bytes 4194304 | tf_op jit(solution)/shard_map/attend_back/pallas_call | solution.py:137
  436.6 10.1 %collective-permute-done.47 = bf16[256,1024]{1,0:T(8,128)(2,1)S(1)} collective-permute-done((bf16[256,1024]{1,0:T(8,128)(2,1)S(1)}, bf16[256,1024]{1,0:T(8,128)(2,1)S(1)}, u32[]{:S(2)}, u32[]{:S(2)}) %collective-permute-start.47) | collective-permute-done | bytes 524320 | tf_op jit(solution)/shard_map/ppermute | solution.py:36
  447.8 5.4 outer.10
  473.0 6.8 %outer.11 = bf16[1024,2048]{1,0:T(8,128)(2,1)S(1)} custom-call(bf16[256,1024]{1,0:T(8,128)(2,1)S(1)} %fusion.116.refs_0_.refs_4_, bf16[256,512]{1,0:T(8,128)(2,1)S(1)} %pad_maximum_fusion.19.refs_1_, bf16[256,1024]{1,0:T(8,128)(2,1)S(1)} %maximum_select_fusion.3.refs_2_, bf16[256,512]{1,0:T(8,128)(2,1)S(1)} %get-tuple-element.225.refs_3_, ...), custom_call_target="tpu_custom_call" | custom-call | flops 1073741824 | bytes 8388608 | tf_op jit(solution)/shard_map/outer/pallas_call | solution.py:191
  486.0 10.3 %collective-permute-done.51 = bf16[2,64,2048]{2,1,0:T(8,128)(2,1)S(1)} collective-permute-done((bf16[2,64,2048]{2,1,0:T(8,128)(2,1)S(1)}, bf16[2,64,2048]{2,1,0:T(8,128)(2,1)S(1)}, u32[]{:S(2)}, u32[]{:S(2)}) %collective-permute-start.51) | collective-permute-done | bytes 524320 | tf_op jit(solution)/shard_map/ppermute | solution.py:349
  512.9 16.1 %collective-permute-done.55 = bf16[4,64,128]{2,1,0:T(8,128)(2,1)S(1)} collective-permute-done((bf16[4,64,128]{2,1,0:T(8,128)(2,1)S(1)}, bf16[4,64,128]{2,1,0:T(8,128)(2,1)S(1)}, u32[]{:S(2)}, u32[]{:S(2)}) %collective-permute-start.55) | collective-permute-done | bytes 65568 | tf_op jit(solution)/shard_map/ppermute | solution.py:346
  537.2 4.7 collective-permute-start.48
  547.9 10.9 %collective-permute-done.48 = bf16[256,1024]{1,0:T(8,128)(2,1)S(1)} collective-permute-done((bf16[256,1024]{1,0:T(8,128)(2,1)}, bf16[256,1024]{1,0:T(8,128)(2,1)S(1)}, u32[]{:S(2)}, u32[]{:S(2)}) %collective-permute-start.48) | collective-permute-done | bytes 524320 | tf_op jit(solution)/shard_map/ppermute | solution.py:285
  558.8 13.1 %collective-permute-done.49 = bf16[256,1024]{1,0:T(8,128)(2,1)S(1)} collective-permute-done((bf16[256,1024]{1,0:T(8,128)(2,1)S(1)}, bf16[256,1024]{1,0:T(8,128)(2,1)S(1)}, u32[]{:S(2)}, u32[]{:S(2)}) %collective-permute-start.49) | collective-permute-done | bytes 524320 | tf_op jit(solution)/shard_map/ppermute | solution.py:285
  579.2 7.3 %all-to-all-done.2 = bf16[4,2,64,1024]{3,2,1,0:T(8,128)(2,1)S(1)} async-done(((bf16[4,2,64,1024]{3,2,1,0:T(8,128)(2,1)}), bf16[4,2,64,1024]{3,2,1,0:T(8,128)(2,1)S(1)}, u32[]{:S(2)}, u32[]{:S(2)}) %all-to-all-start.2) | async-done | bytes 1048608 | tf_op jit(solution)/shard_map/all_to_all | solution.py:292
  589.9 7.5 %collective-permute-done.63 = bf16[64,4096]{1,0:T(8,128)(2,1)S(1)} collective-permute-done((bf16[64,4096]{1,0:T(8,128)(2,1)}, bf16[64,4096]{1,0:T(8,128)(2,1)S(1)}, u32[]{:S(2)}, u32[]{:S(2)}) %collective-permute-start.63) | collective-permute-done | bytes 524320 | tf_op jit(solution)/shard_map/ppermute | solution.py:36
  (687 shorter events, 313.0 us)
Async XLA Ops:
  9.4 17.5 %collective-permute-start.5 = (bf16[64,1024]{1,0:T(8,128)(2,1)S(1)}, bf16[64,1024]{1,0:T(8,128)(2,1)S(1)}, u32[]{:S(2)}, u32[]{:S(2)}) collective-permute-start(bf16[64,1024]{1,0:T(8,128)(2,1)S(1)} %reshape.236.refs_0_), channel_id=1, source_target_pairs={{0,32},{16,48},{32,0},{48,16},{1,33},{17,49},{33,1},{49,17},{2,34}... | collective-permute-start | bytes 393224 | tf_op jit(solution)/shard_map/ppermute | solution.py:310
  24.6 133.8 %all-gather.2.cloned.1.call-start = ((), (), s32[]{:S(2)}) async-start(), calls=%async_computation.6 | async-start | bytes 8912896 | tf_op jit(solution)/shard_map/all_gather | solution.py:592
  45.0 26.3 %collective-permute-start.6 = (bf16[256,1024]{1,0:T(8,128)(2,1)}, bf16[256,1024]{1,0:T(8,128)(2,1)}, u32[]{:S(2)}, u32[]{:S(2)}) collective-permute-start(bf16[256,1024]{1,0:T(8,128)(2,1)} %bitcast.17), channel_id=1, source_target_pairs={{0,0},{1,8},{8,1},{9,9},{2,2},{3,10},{10,3},{11,11},{4,4},{5,12},{... | collective-permute-start | bytes 1572872 | tf_op jit(solution)/shard_map/ppermute | solution.py:285
  58.5 66.5 %collective-permute-start.16 = (bf16[1024,1024]{1,0:T(8,128)(2,1)S(1)}, bf16[1024,1024]{1,0:T(8,128)(2,1)}, u32[]{:S(2)}, u32[]{:S(2)}) collective-permute-start(bf16[1024,1024]{1,0:T(8,128)(2,1)S(1)} %bitcast.195), channel_id=1, source_target_pairs={{0,1},{1,0},{2,3},{3,2},{4,5},{5,4},{6,7},{7,6},{8,9},{9,8},{10,11... | collective-permute-start | bytes 6291464 | tf_op jit(solution)/shard_map/ppermute | solution.py:36
  68.7 24.5 %collective-permute-start.8 = (bf16[256,1152]{1,0:T(8,128)(2,1)S(1)}, bf16[256,1152]{1,0:T(8,128)(2,1)S(1)}, u32[]{:S(2)}, u32[]{:S(2)}) collective-permute-start(bf16[256,1152]{1,0:T(8,128)(2,1)S(1)} %bitcast.213), channel_id=1, source_target_pairs={{0,48},{16,0},{32,16},{48,32},{1,49},{17,1},{33,17},{49,33},{2,50}... | collective-permute-start | bytes 1769480 | tf_op jit(solution)/shard_map/ppermute | solution.py:307
  71.3 25.5 %collective-permute-start.7 = (bf16[256,1152]{1,0:T(8,128)(2,1)S(1)}, bf16[256,1152]{1,0:T(8,128)(2,1)}, u32[]{:S(2)}, u32[]{:S(2)}) collective-permute-start(bf16[256,1152]{1,0:T(8,128)(2,1)S(1)} %bitcast.214), channel_id=1, source_target_pairs={{0,16},{16,32},{32,48},{48,0},{1,17},{17,33},{33,49},{49,1},{2,18}... | collective-permute-start | bytes 1769480 | tf_op jit(solution)/shard_map/ppermute | solution.py:306
  93.2 16.0 %collective-permute-start.10 = (bf16[128,1152]{1,0:T(8,128)(2,1)S(1)}, bf16[128,1152]{1,0:T(8,128)(2,1)S(1)}, u32[]{:S(2)}, u32[]{:S(2)}) collective-permute-start(bf16[128,1152]{1,0:T(8,128)(2,1)S(1)} %slice.517), channel_id=1, source_target_pairs={{0,48},{16,0},{32,16},{48,32},{1,49},{17,1},{33,17},{49,33},{2,50}... | collective-permute-start | bytes 884744 | tf_op jit(solution)/shard_map/ppermute | solution.py:313
  97.8 16.1 %collective-permute-start.9 = (bf16[128,1152]{1,0:T(8,128)(2,1)S(1)}, bf16[128,1152]{1,0:T(8,128)(2,1)S(1)}, u32[]{:S(2)}, u32[]{:S(2)}) collective-permute-start(bf16[128,1152]{1,0:T(8,128)(2,1)S(1)} %slice.516), channel_id=1, source_target_pairs={{0,16},{16,32},{32,48},{48,0},{1,17},{17,33},{33,49},{49,1},{2,18}... | collective-permute-start | bytes 884744 | tf_op jit(solution)/shard_map/ppermute | solution.py:312
  120.3 21.7 %collective-permute-start.11 = (bf16[1024,512]{1,0:T(8,128)(2,1)}, bf16[1024,512]{1,0:T(8,128)(2,1)S(1)}, u32[]{:S(2)}, u32[]{:S(2)}) collective-permute-start(bf16[1024,512]{1,0:T(8,128)(2,1)} %bitcast.208), channel_id=1, source_target_pairs={{0,1},{1,0},{2,3},{3,2},{4,5},{5,4},{6,7},{7,6},{8,9},{9,8},{10,11... | collective-permute-start | bytes 3145736 | tf_op jit(solution)/shard_map/ppermute | solution.py:36
  158.4 35.7 %collective-permute-start.24 = (bf16[1024,4096]{1,0:T(8,128)(2,1)}, bf16[1024,4096]{1,0:T(8,128)(2,1)}, u32[]{:S(2)}, u32[]{:S(2)}) collective-permute-start(bf16[1024,4096]{1,0:T(8,128)(2,1)} %all-gather.2.cloned.1.call-done), channel_id=1, source_target_pairs={{0,1},{1,0},{2,3},{3,2},{4,5},{5,4},{6,7},{7,6},{8,9},{9,8},{10,11... | collective-permute-start | bytes 25165832 | tf_op jit(solution)/shard_map/ppermute | solution.py:36
  202.7 17.8 %collective-permute-start.25 = (bf16[256,1024]{1,0:T(8,128)(2,1)S(1)}, bf16[256,1024]{1,0:T(8,128)(2,1)S(1)}, u32[]{:S(2)}, u32[]{:S(2)}) collective-permute-start(bf16[256,1024]{1,0:T(8,128)(2,1)S(1)} %fusion.92), channel_id=1, source_target_pairs={{0,64},{1,65},{2,66},{3,67},{4,68},{5,69},{6,70},{7,71},{8,72},{9,... | collective-permute-start | bytes 1572872 | tf_op jit(solution)/shard_map/ppermute | solution.py:656
  209.8 322.7 %reduce-scatter.6.cloned.1.call-start = ((), (), s32[]{:S(2)}) async-start(), calls=%async_computation.8 | async-start | bytes 5242880 | tf_op jit(solution)/shard_map/reduce_scatter | solution.py:474
  218.6 17.7 %collective-permute-start.32 = (bf16[256,1024]{1,0:T(8,128)(2,1)}, bf16[256,1024]{1,0:T(8,128)(2,1)S(1)}, u32[]{:S(2)}, u32[]{:S(2)}) collective-permute-start(bf16[256,1024]{1,0:T(8,128)(2,1)} %bitcast.36), channel_id=1, source_target_pairs={{0,0},{1,8},{8,1},{9,9},{2,2},{3,10},{10,3},{11,11},{4,4},{5,12},{... | collective-permute-start | bytes 1572872 | tf_op jit(solution)/shard_map/ppermute | solution.py:285
  227.5 19.9 %collective-permute-start.26 = (bf16[256,1024]{1,0:T(8,128)(2,1)S(1)}, bf16[256,1024]{1,0:T(8,128)(2,1)S(1)}, u32[]{:S(2)}, u32[]{:S(2)}) collective-permute-start(bf16[256,1024]{1,0:T(8,128)(2,1)S(1)} %pad_maximum_fusion.7.own_ref), channel_id=1, source_target_pairs={{0,1},{1,0},{2,3},{3,2},{4,5},{5,4},{6,7},{7,6},{8,9},{9,8},{10,11... | collective-permute-start | bytes 1572872 | tf_op jit(solution)/shard_map/ppermute | solution.py:36
  295.5 16.3 %collective-permute-start.34 = (bf16[256,1024]{1,0:T(8,128)(2,1)}, bf16[256,1024]{1,0:T(8,128)(2,1)}, u32[]{:S(2)}, u32[]{:S(2)}) collective-permute-start(bf16[256,1024]{1,0:T(8,128)(2,1)} %add_convert_fusion.8), channel_id=1, source_target_pairs={{0,4},{4,0},{1,5},{5,1},{2,6},{6,2},{3,7},{7,3},{8,12},{12,8},{9,1... | collective-permute-start | bytes 1572872 | tf_op jit(solution)/shard_map/ppermute | solution.py:36
  297.1 17.8 %collective-permute-start.35 = (bf16[256,1024]{1,0:T(8,128)(2,1)}, bf16[256,1024]{1,0:T(8,128)(2,1)S(1)}, u32[]{:S(2)}, u32[]{:S(2)}) collective-permute-start(bf16[256,1024]{1,0:T(8,128)(2,1)} %copy-done.65), channel_id=1, source_target_pairs={{0,1},{1,0},{2,3},{3,2},{4,5},{5,4},{6,7},{7,6},{8,9},{9,8},{10,11... | collective-permute-start | bytes 1572872 | tf_op jit(solution)/shard_map/ppermute | solution.py:36
  357.2 18.9 %collective-permute-start.40 = (bf16[1024,2048]{1,0:T(8,128)(2,1)S(1)}, bf16[1024,2048]{1,0:T(8,128)(2,1)S(1)}, u32[]{:S(2)}, u32[]{:S(2)}) collective-permute-start(bf16[1024,2048]{1,0:T(8,128)(2,1)S(1)} %outer.6), channel_id=1, source_target_pairs={{0,1},{1,0},{2,3},{3,2},{4,5},{5,4},{6,7},{7,6},{8,9},{9,8},{10,11... | collective-permute-start | bytes 12582920 | tf_op jit(solution)/shard_map/ppermute | solution.py:36
  381.1 151.4 %reduce-scatter.4.cloned.1.call-start = ((), (), s32[]{:S(2)}) async-start(), calls=%async_computation.7 | async-start | bytes 5242880 | tf_op jit(solution)/shard_map/reduce_scatter | solution.py:499
  410.2 17.4 %collective-permute-start.43 = (bf16[256,1024]{1,0:T(8,128)(2,1)}, bf16[256,1024]{1,0:T(8,128)(2,1)S(1)}, u32[]{:S(2)}, u32[]{:S(2)}) collective-permute-start(bf16[256,1024]{1,0:T(8,128)(2,1)} %add_convert_fusion.4), channel_id=1, source_target_pairs={{0,4},{4,0},{1,5},{5,1},{2,6},{6,2},{3,7},{7,3},{8,12},{12,8},{9,1... | collective-permute-start | bytes 1572872 | tf_op jit(solution)/shard_map/ppermute | solution.py:36
  429.7 157.9 %reduce-scatter.8.cloned.1.call-start = ((), (), s32[]{:S(2)}) async-start(), calls=%async_computation.9 | async-start | bytes 2621440 | tf_op jit(solution)/shard_map/reduce_scatter | solution.py:701
  453.2 19.8 %collective-permute-start.50 = (bf16[1024,2048]{1,0:T(8,128)(2,1)}, bf16[1024,2048]{1,0:T(8,128)(2,1)}, u32[]{:S(2)}, u32[]{:S(2)}) collective-permute-start(bf16[1024,2048]{1,0:T(8,128)(2,1)} %outer.10), channel_id=1, source_target_pairs={{0,1},{1,0},{2,3},{3,2},{4,5},{5,4},{6,7},{7,6},{8,9},{9,8},{10,11... | collective-permute-start | bytes 12582920 | tf_op jit(solution)/shard_map/ppermute | solution.py:36
  480.0 16.2 %collective-permute-start.51 = (bf16[2,64,2048]{2,1,0:T(8,128)(2,1)S(1)}, bf16[2,64,2048]{2,1,0:T(8,128)(2,1)S(1)}, u32[]{:S(2)}, u32[]{:S(2)}) collective-permute-start(bf16[2,64,2048]{2,1,0:T(8,128)(2,1)S(1)} %get-tuple-element.210), channel_id=1, source_target_pairs={{0,4},{4,8},{8,12},{12,0},{1,5},{5,9},{9,13},{13,1},{2,6},{6,10},{... | collective-permute-start | bytes 1572872 | tf_op jit(solution)/shard_map/ppermute | solution.py:349
  498.3 30.7 %collective-permute-start.54 = (bf16[4,64,2048]{2,1,0:T(8,128)(2,1)}, bf16[4,64,2048]{2,1,0:T(8,128)(2,1)}, u32[]{:S(2)}, u32[]{:S(2)}) collective-permute-start(bf16[4,64,2048]{2,1,0:T(8,128)(2,1)} %pad_maximum_fusion.3), channel_id=1, source_target_pairs={{0,12},{4,0},{8,4},{12,8},{1,13},{5,1},{9,5},{13,9},{2,14},{6,2},{... | collective-permute-start | bytes 3145736 | tf_op jit(solution)/shard_map/ppermute | solution.py:354
  501.7 27.4 %collective-permute-start.52 = (bf16[4,64,2048]{2,1,0:T(8,128)(2,1)}, bf16[4,64,2048]{2,1,0:T(8,128)(2,1)}, u32[]{:S(2)}, u32[]{:S(2)}) collective-permute-start(bf16[4,64,2048]{2,1,0:T(8,128)(2,1)} %pad_maximum_fusion.2), channel_id=1, source_target_pairs={{0,4},{4,8},{8,12},{12,0},{1,5},{5,9},{9,13},{13,1},{2,6},{6,10},{... | collective-permute-start | bytes 3145736 | tf_op jit(solution)/shard_map/ppermute | solution.py:353
  509.1 19.9 %collective-permute-start.55 = (bf16[4,64,128]{2,1,0:T(8,128)(2,1)S(1)}, bf16[4,64,128]{2,1,0:T(8,128)(2,1)S(1)}, u32[]{:S(2)}, u32[]{:S(2)}) collective-permute-start(bf16[4,64,128]{2,1,0:T(8,128)(2,1)S(1)} %get-tuple-element.263), channel_id=1, source_target_pairs={{0,4},{4,8},{8,12},{12,0},{1,5},{5,9},{9,13},{13,1},{2,6},{6,10},{... | collective-permute-start | bytes 196616 | tf_op jit(solution)/shard_map/ppermute | solution.py:346
  509.4 19.6 %collective-permute-start.57 = (bf16[4,64,128]{2,1,0:T(8,128)(2,1)S(1)}, bf16[4,64,128]{2,1,0:T(8,128)(2,1)S(1)}, u32[]{:S(2)}, u32[]{:S(2)}) collective-permute-start(bf16[4,64,128]{2,1,0:T(8,128)(2,1)S(1)} %get-tuple-element.264), channel_id=1, source_target_pairs={{0,8},{4,12},{8,0},{12,4},{1,9},{5,13},{9,1},{13,5},{2,10},{6,14},... | collective-permute-start | bytes 196616 | tf_op jit(solution)/shard_map/ppermute | solution.py:346
  512.9 16.1 %collective-permute-start.56 = (bf16[4,64,128]{2,1,0:T(8,128)(2,1)S(1)}, bf16[4,64,128]{2,1,0:T(8,128)(2,1)S(1)}, u32[]{:S(2)}, u32[]{:S(2)}) collective-permute-start(bf16[4,64,128]{2,1,0:T(8,128)(2,1)S(1)} %get-tuple-element.265), channel_id=1, source_target_pairs={{0,12},{4,0},{8,4},{12,8},{1,13},{5,1},{9,5},{13,9},{2,14},{6,2},{... | collective-permute-start | bytes 196616 | tf_op jit(solution)/shard_map/ppermute | solution.py:346
  537.2 21.5 %collective-permute-start.48 = (bf16[256,1024]{1,0:T(8,128)(2,1)}, bf16[256,1024]{1,0:T(8,128)(2,1)S(1)}, u32[]{:S(2)}, u32[]{:S(2)}) collective-permute-start(bf16[256,1024]{1,0:T(8,128)(2,1)} %get-tuple-element.152), channel_id=1, source_target_pairs={{0,0},{1,8},{8,1},{9,9},{2,2},{3,10},{10,3},{11,11},{4,4},{5,12},{... | collective-permute-start | bytes 1572872 | tf_op jit(solution)/shard_map/ppermute | solution.py:285
  541.9 30.0 %collective-permute-start.49 = (bf16[256,1024]{1,0:T(8,128)(2,1)S(1)}, bf16[256,1024]{1,0:T(8,128)(2,1)S(1)}, u32[]{:S(2)}, u32[]{:S(2)}) collective-permute-start(bf16[256,1024]{1,0:T(8,128)(2,1)S(1)} %fusion.126), channel_id=1, source_target_pairs={{0,0},{1,8},{8,1},{9,9},{2,2},{3,10},{10,3},{11,11},{4,4},{5,12},{... | collective-permute-start | bytes 1572872 | tf_op jit(solution)/shard_map/ppermute | solution.py:285
  545.2 31.3 %collective-permute-start.58 = (bf16[64,2176]{1,0:T(8,128)(2,1)}, bf16[64,2176]{1,0:T(8,128)(2,1)S(1)}, u32[]{:S(2)}, u32[]{:S(2)}) collective-permute-start(bf16[64,2176]{1,0:T(8,128)(2,1)} %get-tuple-element.218), channel_id=1, source_target_pairs={{0,16},{16,32},{32,48},{48,0},{1,17},{17,33},{33,49},{49,1},{2,18}... | collective-permute-start | bytes 835592 | tf_op jit(solution)/shard_map/ppermute | solution.py:346
  545.5 31.1 %collective-permute-start.60 = (bf16[64,2176]{1,0:T(8,128)(2,1)S(1)}, bf16[64,2176]{1,0:T(8,128)(2,1)S(1)}, u32[]{:S(2)}, u32[]{:S(2)}) collective-permute-start(bf16[64,2176]{1,0:T(8,128)(2,1)S(1)} %get-tuple-element.219), channel_id=1, source_target_pairs={{0,32},{16,48},{32,0},{48,16},{1,33},{17,49},{33,1},{49,17},{2,34}... | collective-permute-start | bytes 835592 | tf_op jit(solution)/shard_map/ppermute | solution.py:346
  547.3 29.2 %collective-permute-start.59 = (bf16[64,2176]{1,0:T(8,128)(2,1)S(1)}, bf16[64,2176]{1,0:T(8,128)(2,1)S(1)}, u32[]{:S(2)}, u32[]{:S(2)}) collective-permute-start(bf16[64,2176]{1,0:T(8,128)(2,1)S(1)} %get-tuple-element.220), channel_id=1, source_target_pairs={{0,48},{16,0},{32,16},{48,32},{1,49},{17,1},{33,17},{49,33},{2,50}... | collective-permute-start | bytes 835592 | tf_op jit(solution)/shard_map/ppermute | solution.py:346
  (194 other events, 1781.0 us)
Sparse Core Ops, SparseCore 0:
  32.7 95.5 all-gather.1
  381.2 46.7 reduce-scatter.5
  430.6 46.9 reduce-scatter.3
  535.7 37.3 reduce-scatter.7

commit v6 on v5

--- a/solution.py
+++ b/solution.py
@@ -301,16 +301,22 @@
 ACROSS = [(i, (i + 2) % 4) for i in range(4)]
 
 
-def ring_place(value, axis, out_shapes, views, direct=False):
-    half = value.shape[0] // 2
-    ahead = lax.ppermute(value, axis, AHEAD)
-    back = lax.ppermute(value, axis, BACK)
-    pieces = [(value, 0, 0), (ahead, 3, 0), (back, 1, 0)]
-    if direct:
-        pieces.append((lax.ppermute(value, axis, ACROSS), 2, 0))
-    else:
-        pieces.append((lax.ppermute(ahead[:half], axis, AHEAD), 2, 0))
-        pieces.append((lax.ppermute(back[half:], axis, BACK), 2, half))
+def first_hop(value, axis):
+    return lax.ppermute(value, axis, AHEAD), lax.ppermute(value, axis, BACK)
+
+
+def second_hop(ahead, back, axis):
+    half = ahead.shape[0] // 2
+    return (
+        lax.ppermute(ahead[:half], axis, AHEAD),
+        lax.ppermute(back[half:], axis, BACK),
+    )
+
+
+def ring_place(value, axis, hops, out_shapes, views):
+    pieces = [(value, 0, 0), (hops[0], 3, 0), (hops[1], 1, 0), (hops[2], 2, 0)]
+    if len(hops) > 3:
+        pieces.append((hops[3], 2, hops[2].shape[0]))
     n_outs = len(out_shapes)
 
     def kernel(index_ref, *refs):
@@ -337,22 +343,43 @@
     outs[0][place, pl.ds(start, piece.shape[0])] = piece[...]
 
 
-def ring_sum(blocks, axis, dim, direct=False):
+def add(*parts):
+    return sum(p.astype(f32) for p in parts).astype(bf16)
+
+
+def ring_blocks(blocks, axis, dim):
     index = lax.axis_index(axis)
-    block = lambda k: lax.dynamic_index_in_dim(blocks, (index + k) % 4, dim, keepdims=False)
-    add = lambda *parts: sum(p.astype(f32) for p in parts).astype(bf16)
-    if direct:
-        ways = [(1, AHEAD), (3, BACK), (2, ACROSS)]
-        return add(block(0), *(lax.ppermute(block(k), axis, way) for k, way in ways))
-    far, after, before = block(2), block(1), block(3)
-    half = far.shape[0] // 2
-    low = lax.ppermute(far[:half], axis, AHEAD)
-    high = lax.ppermute(far[half:], axis, BACK)
-    after = jnp.concatenate([add(after[:half], low), after[half:]])
-    before = jnp.concatenate([before[:half], add(before[half:], high)])
-    after = lax.ppermute(after, axis, AHEAD)
-    before = lax.ppermute(before, axis, BACK)
-    return add(block(0), after, before)
+    return [
+        lax.dynamic_index_in_dim(blocks, (index + k) % 4, dim, keepdims=False) for k in range(4)
+    ]
+
+
+def ring_sums(items, beside):
+    blocks = [ring_blocks(*item) for item in items]
+    hops = []
+    for (_, axis, _), (_, _, far, _) in zip(items, blocks):
+        half = far.shape[0] // 2
+        hops.append(
+            (lax.ppermute(far[:half], axis, AHEAD), lax.ppermute(far[half:], axis, BACK))
+        )
+    hops, beside = lax.optimization_barrier((hops, beside))
+    ends = []
+    for (_, axis, _), (own, after, _, before), (low, high) in zip(items, blocks, hops):
+        half = low.shape[0]
+        after = jnp.concatenate([add(after[:half], low), after[half:]])
+        before = jnp.concatenate([before[:half], add(before[half:], high)])
+        ends.append((own, lax.ppermute(after, axis, AHEAD), lax.ppermute(before, axis, BACK)))
+    ends = lax.optimization_barrier(ends)
+    return [add(*e) for e in ends], beside
+
+
+def direct_sums(items):
+    ways = [(1, AHEAD), (3, BACK), (2, ACROSS)]
+    parts = []
+    for blocks, axis, dim in items:
+        block = ring_blocks(blocks, axis, dim)
+        parts.append([block[0]] + [lax.ppermute(block[k], axis, way) for k, way in ways])
+    return [add(*p) for p in lax.optimization_barrier(parts)]
 
 
 def group_parts(own, mate, near, far):
@@ -514,7 +541,7 @@
     )
     normal_one, factor_one = normal_part(kept["inputs"])
     grad_inputs = grad_middle + norm_back(grad_normed_one, normal_one, factor_one, w["gain"][0])
-    total = lambda a: jnp.sum(a.astype(f32), axis=0)
+    total = lambda a: jnp.sum(a.astype(f32), axis=0, keepdims=True)
     vectors = dict(
         gain=(total(grad_normed_one * normal_one), total(grad_normed_two * normal_two)),
         shift=(total(grad_normed_one), total(grad_normed_two)),
@@ -571,7 +598,7 @@
     proj_mine = pick(proj_weight[0].reshape(own, 2, half), core, 1)
     vectors = jnp.concatenate(
         [a[0] for a in (norm_gain, norm_bias, qv_bias, out_bias, layer_scale)]
-        + [fc1_bias[0].reshape(own, hidden // own).T],
+        + [fc1_bias[0].reshape(hidden // own, own)],
         axis=0,
     ).T
     count = vectors.shape[1]
@@ -582,15 +609,23 @@
     fc_mine = jnp.concatenate([fc1_mine, fc2_mine[0], fc2_mine[1]], axis=1)
 
     a_mine = jnp.concatenate([q_mine, proj_mine, vectors], axis=1)
-    first_tokens = to_images(patch_tokens)
-    a_row = ring_place(a_mine, RING_Y, [(4, own, a_mine.shape[1])], in_order, direct=True)[0]
-    b_row = ring_place(kv_mine, RING_Z, [(4, own, width)], in_order, direct=True)[0]
-    a_row, b_row, fc_mine, first_tokens = lax.optimization_barrier(
-        (a_row, b_row, fc_mine, first_tokens)
-    )
-    first_tokens = flip(first_tokens)
+    live = (
+        jnp.arange(images) % IMG_MB < jnp.repeat(batch_counts[0], IMG_MB)
+    ).astype(bf16)
+    live_grad = out_grad * live[:, None, None]
+    direct = lambda value, axis: (*first_hop(value, axis), lax.ppermute(value, axis, ACROSS))
+    first = (direct(a_mine, RING_Y), direct(kv_mine, RING_Z))
+    first, fc_mine, live_grad, first_tokens = lax.optimization_barrier(
+        (first, fc_mine, live_grad, to_images(patch_tokens))
+    )
     fc_half = lax.all_gather(fc_mine, FSDP, axis=0, tiled=True)
-    a_row = a_row.reshape(4 * own, a_mine.shape[1])
+    a_wide = a_mine.shape[1]
+    a_row = ring_place(a_mine, RING_Y, first[0], [(4, own, a_wide)], in_order)[0]
+    a_row = a_row.reshape(4 * own, a_wide)
+    b_row = ring_place(kv_mine, RING_Z, first[1], [(4, own, width)], in_order)[0]
+    hops = lax.optimization_barrier((first_hop(a_row, RING_Z), first_hop(b_row, RING_Y)))
+    more = (second_hop(*hops[0], RING_Z), second_hop(*hops[1], RING_Y))
+    more, first_tokens = lax.optimization_barrier((more, flip(first_tokens)))
 
     def a_views(outs, piece, place, start):
         at = 0
@@ -606,36 +641,38 @@
     q_half, proj_half, vectors = (
         o.reshape(width, -1)
         for o in ring_place(
-            a_row, RING_Z, [(4, 4 * own, half), (4, 4 * own, half), (4, 4 * own, 128)], a_views
+            a_row, RING_Z, hops[0] + more[0], [(4, 4 * own, half), (4, 4 * own, half), (4, 4 * own, 128)], a_views
         )
     )
-    kv_half = ring_place(b_row, RING_Y, [(4, 4, own, width)], b_views)[0].reshape(width, width)
-    vectors = vectors[:, :count].T.astype(f32)
-    fc1_b = vectors[10:].T.reshape(shards, 2, 2, part)
-
-    def halves(vector):
-        pair = vector.reshape(2, half)
-        return pick(pair, core, 0), pick(pair, 1 - core, 0)
+    kv_half = ring_place(b_row, RING_Y, hops[1] + more[1], [(4, 4, own, width)], b_views)[0]
+    kv_half = kv_half.reshape(width, width)
+    vectors = vectors[:, :16].T.astype(f32)
+
+    def halves(row):
+        return ordered(core, row[:, :half], row[:, half:])
+
+    def fc1_bias_of(which):
+        rows = jnp.where(which == 0, vectors[10:12], vectors[12:14])
+        return jnp.concatenate([rows[0:1], rows[1:2]], axis=1)
 
     def kv_bias(v_half):
-        v_part = v_half.reshape(groups, 1, PAIR)
-        return jnp.concatenate([jnp.zeros_like(v_part), v_part], axis=1).reshape(width)
+        zeros = jnp.zeros((1, PAIR), f32)
+        cuts = [v_half[:, i * PAIR : (i + 1) * PAIR] for i in range(groups)]
+        return jnp.concatenate([x for c in cuts for x in (zeros, c)], axis=1)
 
     wide = shards * mid
     w = dict(
         core=core,
-        gain=vectors[0:2],
-        shift=vectors[2:4],
-        out_bias=vectors[6:8],
-        scale=vectors[8:10],
+        gain=(vectors[0:1], vectors[1:2]),
+        shift=(vectors[2:3], vectors[3:4]),
+        out_bias=(vectors[6:7], vectors[7:8]),
+        scale=(vectors[8:9], vectors[9:10]),
         q=[q_half, swap(q_half, "core")],
-        q_bias=halves(vectors[4]),
+        q_bias=halves(vectors[4:5]),
         kv=[kv_half, swap(kv_half, "core")],
-        kv_bias=[kv_bias(b) for b in halves(vectors[5])],
+        kv_bias=[kv_bias(b) for b in halves(vectors[5:6])],
         proj=(proj_half, swap(proj_half, "core")),
-        fc1_bias=[
-            jnp.swapaxes(pick(fc1_b, c, 1), 0, 1).reshape(-1) for c in (core, 1 - core)
-        ],
+        fc1_bias=[fc1_bias_of(c) for c in (core, 1 - core)],
     )
 
     def fc_weights(gathered):
@@ -646,12 +683,7 @@
         )
 
 
-    live = (
-        jnp.arange(images) % IMG_MB < jnp.repeat(batch_counts[0], IMG_MB)
-    ).astype(bf16)
-
     sent, _ = forward(first_tokens, w, late=(fc_half, fc_weights))
-    live_grad = out_grad * live[:, None, None]
     sent, live_grad = lax.optimization_barrier((sent, live_grad))
     passed = lax.ppermute(sent, "section", [(0, 1)])
     last_grad = flip(to_images(live_grad))
@@ -666,16 +698,17 @@
     block_out, in_grad = from_images([result, grad_inputs], images)
 
     def natural(pair):
-        return jnp.concatenate(ordered(core, *pair))
-
-    v_sum = lambda a: a.reshape(groups, 2, PAIR)[:, 1].reshape(half)
-    fc1_bias_sum = jnp.stack(
-        ordered(
-            core, *(jnp.swapaxes(s.reshape(2, shards, part), 0, 1) for s in sums["fc1_bias"])
-        ),
-        axis=1,
-    ).reshape(width, hidden // own)
-    vector_grads = jnp.stack(
+        return jnp.concatenate(ordered(core, *pair), axis=1)
+
+    def v_sum(a):
+        cuts = [a[:, (2 * i + 1) * PAIR : (2 * i + 2) * PAIR] for i in range(groups)]
+        return jnp.concatenate(cuts, axis=1)
+
+    fc1_rows = [
+        jnp.concatenate([b[:, :width], b[:, width:]], axis=0)
+        for b in ordered(core, *sums["fc1_bias"])
+    ]
+    vector_grads = jnp.concatenate(
         [
             *sums["gain"],
             *sums["shift"],
@@ -683,10 +716,12 @@
             natural([v_sum(g) for g in sums["kv"]]),
             *sums["out_bias"],
             *sums["scale"],
-            *fc1_bias_sum.T,
-        ]
-    )
-    vector_grads = jnp.pad(vector_grads, ((0, PAIR - count), (0, 0))).astype(bf16).T
+            *fc1_rows,
+            jnp.zeros((PAIR - count, width), f32),
+        ],
+        axis=0,
+    )
+    vector_grads = vector_grads.astype(bf16).T
 
     a1, dq = products["q"]
     dkv = products["kv"][1]
@@ -695,13 +730,19 @@
         [((a1, 0), dq[i], width), ((o, 0), e1[i], width), ((a1, 0), dkv[i], width)], 256, add=add
     )
     ab = make(0, swap(make(1), "core")).reshape(4, 4, own, 2 * width)
-    ab = ring_sum(ab, RING_Y, 1)
-    vector_grads = ring_sum(vector_grads.reshape(4, 4, own, PAIR), RING_Y, 1, direct=True)
-    ab, vector_grads, rows = lax.optimization_barrier((ab, vector_grads, products["fc"]))
+    (a_sum, b_sum), (rows, vector_grads) = ring_sums(
+        [(ab[..., :width], RING_Y, 1), (ab[..., width:], RING_Z, 0)],
+        (products["fc"], vector_grads),
+    )
     fc_grad = lax.psum_scatter(
         jnp.concatenate(rows, axis=1), RING_Y, scatter_dimension=0, tiled=True
     )
-    ab = ring_sum(jnp.concatenate([ab, vector_grads], axis=2), RING_Z, 0, direct=True)
+    vector_grads = vector_grads.reshape(4, 4, own, PAIR)
+    (vector_sum,) = direct_sums([(vector_grads, RING_Y, 1)])
+    ab = direct_sums(
+        [(jnp.concatenate([a_sum, vector_sum], axis=2), RING_Z, 0), (b_sum, RING_Y, 0)]
+    )
+    ab = jnp.concatenate([ab[0][:, :width], ab[1], ab[0][:, width:]], axis=1)
 
     def chips_sum(a):
         return (a.astype(f32) + swap(a, "xhi").astype(f32)).astype(bf16)
@@ -721,7 +762,7 @@
         vec_grad[4:6][None],
         proj_out[None],
         fc1_out[None],
-        vec_grad[10:].T.reshape(1, hidden),
+        vec_grad[10:].reshape(1, hidden),
         fc2_out[None],
         vec_grad[6:8][None],
         vec_grad[8:10][None],

time: 624 us -> 590 us (0.946)
  waiting for transfers between devices: 186 us -> 151 us
  other arithmetic: 45.7 us -> 39 us
    ppermute x24 -> x31, waiting for transfers between devices: 81.4 us -> 35.8 us  [the longest x9 26.7 us: direct_sums(): lax.ppermute(block[k], axis, way)]
    ppermute x35, waiting for transfers between devices: 49 us -> 77.4 us  [swap(): return lax.ppermute(value, axis, [(0, 1), (1, 0)])]
    another operation x15 -> x3, local copies, waits for them, and re-layouts: 14.7 us -> 0.1 us  [the longest x1 0.09 us: per_device(): fc1_bias[0].reshape(hidden // own, own)]
    broadcast_in_dim x0 -> x9, local copies, waits for them, and re-layouts: none -> 11.3 us  [the longest x8 10.5 us: backward(): total = lambda a: jnp.sum(a.astype(f32), axis=0, keepdims=True)]
    ppermute x4, waiting for transfers between devices: 30.5 us -> 20.6 us  [flip(): return lax.ppermute(tokens, ('yh', 'core'), FLIP)]
    unnamed x311 -> x369, local copies, waits for them, and re-layouts: 32.1 us -> 41.1 us
    slice x6 -> x22, local copies, waits for them, and re-layouts: 4.24 us -> 13.1 us  [the longest x4 4.32 us: per_device(): b[:, width:]]
    ppermute x4, starting transfers between devices: 16 us -> 24.8 us  [flip(): return lax.ppermute(tokens, ('yh', 'core'), FLIP)]
  transfers between devices with their start and end apart: 72 -> 79, of which waited for: 25 -> 25; matrix products, arithmetic and copies ran while one was open for 23% -> 23% of each run, Pallas kernels for 12% -> 12%
where the time goes in v6:
time: 590 us; the launch traced here: 578 us
  waiting for transfers between devices  151 us (26%)
  starting transfers between devices  107 us (18%)
  Pallas kernels  92.9 us (16%)
  local copies, waits for them, and re-layouts  89.2 us (15%)
  matrix products  82.1 us (14%)
  other arithmetic  39 us (7%)
  between operations  17.2 us (3%)
    dot_general x48, matrix products, dot(): return lax.dot_general(a, b, (dims, ((), ())), preferred_element_type=f32)  82.1 us
    ppermute x35, waiting for transfers between devices, swap(): return lax.ppermute(value, axis, [(0, 1), (1, 0)])  77.4 us
    unnamed x369, local copies, waits for them, and re-layouts  41.1 us
    pallas_call x4, Pallas kernels, attend_back(): pl.pallas_call(attend_back_kernel, grid=(pairs,), in_specs=[q_spec] + kv_...  35.8 us
    ppermute x35, starting transfers between devices, swap(): return lax.ppermute(value, axis, [(0, 1), (1, 0)])  30 us
    pallas_call x4, Pallas kernels, attend(): pl.pallas_call(attend_kernel, grid=(pairs,), in_specs=[q_spec] + kv_specs...  29.2 us
    ppermute x9, waiting for transfers between devices, direct_sums(): lax.ppermute(block[k], axis, way)  26.7 us
    ppermute x4, starting transfers between devices, flip(): return lax.ppermute(tokens, ('yh', 'core'), FLIP)  24.8 us
  transfers between devices with their start and end apart: 79, of which 25 were waited for; matrix products, arithmetic and copies ran while one was open for 23% of the time, Pallas kernels for 12%

profile of v6, /device:TPU:1, one launch (start us, length us, event | category | flops | bytes accessed | tf_op | source)
XLA Modules:
  0.0 578.2 jit_solution(4083040410528683205)
XLA Ops:
  9.4 4.5 collective-permute-start.5
  37.9 6.3 %collective-permute-start.14 = (bf16[256,1024]{1,0:T(8,128)(2,1)}, bf16[256,1024]{1,0:T(8,128)(2,1)}, u32[]{:S(2)}, u32[]{:S(2)}) collective-permute-start(bf16[256,1024]{1,0:T(8,128)(2,1)} %bitcast.16), channel_id=1, source_target_pairs={{0,0},{1,8},{8,1},{9,9},{2,2},{3,10},{10,3},{11,11},{4,4},{5,12},{... | collective-permute-start | bytes 1572872 | tf_op jit(solution)/shard_map/ppermute | solution.py:285
  55.2 12.3 %collective-permute-done.14 = bf16[256,1024]{1,0:T(8,128)(2,1)} collective-permute-done((bf16[256,1024]{1,0:T(8,128)(2,1)}, bf16[256,1024]{1,0:T(8,128)(2,1)}, u32[]{:S(2)}, u32[]{:S(2)}) %collective-permute-start.14) | collective-permute-done | bytes 524320 | tf_op jit(solution)/shard_map/ppermute | solution.py:285
  78.8 8.1 %collective-permute-start.16 = (bf16[1024,1024]{1,0:T(8,128)(2,1)S(1)}, bf16[1024,1024]{1,0:T(8,128)(2,1)S(1)}, u32[]{:S(2)}, u32[]{:S(2)}) collective-permute-start(bf16[1024,1024]{1,0:T(8,128)(2,1)S(1)} %bitcast.200), channel_id=1, source_target_pairs={{0,1},{1,0},{2,3},{3,2},{4,5},{5,4},{6,7},{7,6},{8,9},{9,8},{10,11... | collective-permute-start | bytes 6291464 | tf_op jit(solution)/shard_map/ppermute | solution.py:36
  100.0 21.4 %collective-permute-done.18.near_ref = bf16[256,1024]{1,0:T(8,128)(2,1)S(1)} collective-permute-done((bf16[256,1024]{1,0:T(8,128)(2,1)S(1)}, bf16[256,1024]{1,0:T(8,128)(2,1)S(1)}, u32[]{:S(2)}, u32[]{:S(2)}) %collective-permute-start.18) | collective-permute-done | bytes 524320 | tf_op jit(solution)/shard_map/ppermute | solution.py:36
  126.1 7.6 %attend.4 = (bf16[256,512]{1,0:T(8,128)(2,1)S(1)}, f32[4,2,256]{2,1,0:T(2,128)}) custom-call(bf16[256,512]{1,0:T(8,128)(2,1)S(1)} %pad_maximum_fusion.14.q_ref, bf16[256,1024]{1,0:T(8,128)(2,1)S(1)} %pad_maximum_fusion.3.own_ref, bf16[256,1024]{1,0:T(8,128)(2,1)S(1)} %collective-permute-done.17.mate_ref, ...), custom_call_target="tpu_custom_call" | custom-call | flops 2147483648 | bytes 4194304 | tf_op jit(solution)/shard_map/attend/pallas_call | solution.py:118
  133.7 5.1 collective-permute-done.20.near_ref
  143.0 7.9 %collective-permute-done.21.mate_ref = bf16[256,1024]{1,0:T(8,128)(2,1)S(1)} collective-permute-done((bf16[256,1024]{1,0:T(8,128)(2,1)}, bf16[256,1024]{1,0:T(8,128)(2,1)S(1)}, u32[]{:S(2)}, u32[]{:S(2)}) %collective-permute-start.21) | collective-permute-done | bytes 524320 | tf_op jit(solution)/shard_map/ppermute | solution.py:36
  154.4 7.6 %attend.5 = (bf16[256,512]{1,0:T(8,128)(2,1)S(1)}, f32[4,2,256]{2,1,0:T(2,128)}) custom-call(bf16[256,512]{1,0:T(8,128)(2,1)S(1)} %pad_maximum_fusion.15.q_ref, bf16[256,1024]{1,0:T(8,128)(2,1)S(1)} %copy-done.33, bf16[256,1024]{1,0:T(8,128)(2,1)S(1)} %collective-permute-done.21.mate_ref, bf16[256,1024]{1,0:T(8,128)(2,1)S(1)} %copy-done.65, ...), custom_call_target="tpu_custom_call" | custom-call | flops 2147483648 | bytes 4194304 | tf_op jit(solution)/shard_map/attend/pallas_call | solution.py:118
  185.3 9.0 %all-to-all-done.1 = bf16[4,64,1024]{2,1,0:T(8,128)(2,1)} async-done(((bf16[4,64,1024]{2,1,0:T(8,128)(2,1)}), bf16[4,64,1024]{2,1,0:T(8,128)(2,1)}, u32[]{:S(2)}, u32[]{:S(2)}) %all-to-all-start.1) | async-done | bytes 524320 | tf_op jit(solution)/shard_map/all_to_all | solution.py:280
  194.2 5.7 collective-permute-start.32
  210.7 7.1 %collective-permute-done.27.near_ref = bf16[256,1024]{1,0:T(8,128)(2,1)S(1)} collective-permute-done((bf16[256,1024]{1,0:T(8,128)(2,1)S(1)}, bf16[256,1024]{1,0:T(8,128)(2,1)S(1)}, u32[]{:S(2)}, u32[]{:S(2)}) %collective-permute-start.27) | collective-permute-done | bytes 524320 | tf_op jit(solution)/shard_map/ppermute | solution.py:36
  225.2 7.0 %attend.6 = (bf16[256,512]{1,0:T(8,128)(2,1)S(1)}, f32[4,2,256]{2,1,0:T(2,128)S(1)}) custom-call(bf16[256,512]{1,0:T(8,128)(2,1)S(1)} %pad_maximum_fusion.16.q_ref, bf16[256,1024]{1,0:T(8,128)(2,1)S(1)} %pad_maximum_fusion.5.own_ref, bf16[256,1024]{1,0:T(8,128)(2,1)S(1)} %collective-permute-done.26.mate_ref, ...), custom_call_target="tpu_custom_call" | custom-call | flops 2147483648 | bytes 4194304 | tf_op jit(solution)/shard_map/attend/pallas_call | solution.py:118
  234.2 7.0 %attend.7 = (bf16[256,512]{1,0:T(8,128)(2,1)S(1)}, f32[4,2,256]{2,1,0:T(2,128)S(1)}) custom-call(bf16[256,512]{1,0:T(8,128)(2,1)S(1)} %pad_maximum_fusion.17.q_ref, bf16[256,1024]{1,0:T(8,128)(2,1)S(1)} %pad_maximum_fusion.6.own_ref, bf16[256,1024]{1,0:T(8,128)(2,1)S(1)} %collective-permute-done.30.mate_ref, ...), custom_call_target="tpu_custom_call" | custom-call | flops 2147483648 | bytes 4194304 | tf_op jit(solution)/shard_map/attend/pallas_call | solution.py:118
  248.5 5.2 fusion.41
  253.8 4.2 fusion.206
  260.9 9.0 %attend_back.4 = (bf16[256,512]{1,0:T(8,128)(2,1)S(1)}, bf16[256,1024]{1,0:T(8,128)(2,1)S(1)}, bf16[256,1024]{1,0:T(8,128)(2,1)S(1)}, bf16[256,1024]{1,0:T(8,128)(2,1)S(1)}, bf16[256,1024]{1,0:T(8,128)(2,1)S(1)}) custom-call(bf16[256,512]{1,0:T(8,128)(2,1)S(1)} %pad_maximum_fusion.16.q_ref, bf16[256,1024]{1,0:T(8,128)(2,1)S(1)} %pad_maximum_fusion.5.own_ref, ...), custom_call_target="tpu_custom_call" | custom-call | flops 5368709120 | bytes 4194304 | tf_op jit(solution)/shard_map/attend_back/pallas_call | solution.py:137
  279.8 9.0 %attend_back.5 = (bf16[256,512]{1,0:T(8,128)(2,1)S(1)}, bf16[256,1024]{1,0:T(8,128)(2,1)S(1)}, bf16[256,1024]{1,0:T(8,128)(2,1)S(1)}, bf16[256,1024]{1,0:T(8,128)(2,1)S(1)}, bf16[256,1024]{1,0:T(8,128)(2,1)S(1)}) custom-call(bf16[256,512]{1,0:T(8,128)(2,1)S(1)} %pad_maximum_fusion.17.q_ref, bf16[256,1024]{1,0:T(8,128)(2,1)S(1)} %copy-done.28, ...), custom_call_target="tpu_custom_call" | custom-call | flops 5368709120 | bytes 4194304 | tf_op jit(solution)/shard_map/attend_back/pallas_call | solution.py:137
  294.9 12.1 %collective-permute-done.38 = bf16[256,1024]{1,0:T(8,128)(2,1)S(1)} collective-permute-done((bf16[256,1024]{1,0:T(8,128)(2,1)S(1)}, bf16[256,1024]{1,0:T(8,128)(2,1)S(1)}, u32[]{:S(2)}, u32[]{:S(2)}) %collective-permute-start.38) | collective-permute-done | bytes 524320 | tf_op jit(solution)/shard_map/ppermute | solution.py:36
  317.3 8.4 %collective-permute-done.39 = bf16[256,1024]{1,0:T(8,128)(2,1)S(1)} collective-permute-done((bf16[256,1024]{1,0:T(8,128)(2,1)S(1)}, bf16[256,1024]{1,0:T(8,128)(2,1)S(1)}, u32[]{:S(2)}, u32[]{:S(2)}) %collective-permute-start.39) | collective-permute-done | bytes 524320 | tf_op jit(solution)/shard_map/ppermute | solution.py:694
  347.5 4.4 fusion.84
  368.5 9.0 %attend_back.6 = (bf16[256,512]{1,0:T(8,128)(2,1)S(1)}, bf16[256,1024]{1,0:T(8,128)(2,1)S(1)}, bf16[256,1024]{1,0:T(8,128)(2,1)S(1)}, bf16[256,1024]{1,0:T(8,128)(2,1)S(1)}, bf16[256,1024]{1,0:T(8,128)(2,1)S(1)}) custom-call(bf16[256,512]{1,0:T(8,128)(2,1)S(1)} %copy-done.40, bf16[256,1024]{1,0:T(8,128)(2,1)S(1)} %copy-done.31, ...), custom_call_target="tpu_custom_call" | custom-call | flops 5368709120 | bytes 4194304 | tf_op jit(solution)/shard_map/attend_back/pallas_call | solution.py:137
  391.0 8.9 %attend_back.7 = (bf16[256,512]{1,0:T(8,128)(2,1)S(1)}, bf16[256,1024]{1,0:T(8,128)(2,1)S(1)}, bf16[256,1024]{1,0:T(8,128)(2,1)S(1)}, bf16[256,1024]{1,0:T(8,128)(2,1)S(1)}, bf16[256,1024]{1,0:T(8,128)(2,1)S(1)}) custom-call(bf16[256,512]{1,0:T(8,128)(2,1)S(1)} %pad_maximum_fusion.17.q_ref, bf16[256,1024]{1,0:T(8,128)(2,1)S(1)} %copy-done.29, ...), custom_call_target="tpu_custom_call" | custom-call | flops 5368709120 | bytes 4194304 | tf_op jit(solution)/shard_map/attend_back/pallas_call | solution.py:137
  405.1 11.2 %collective-permute-done.47 = bf16[256,1024]{1,0:T(8,128)(2,1)S(1)} collective-permute-done((bf16[256,1024]{1,0:T(8,128)(2,1)S(1)}, bf16[256,1024]{1,0:T(8,128)(2,1)S(1)}, u32[]{:S(2)}, u32[]{:S(2)}) %collective-permute-start.47) | collective-permute-done | bytes 524320 | tf_op jit(solution)/shard_map/ppermute | solution.py:36
  418.1 5.5 outer.10
  451.8 6.7 %outer.11 = bf16[1024,2048]{1,0:T(8,128)(2,1)S(1)} custom-call(bf16[256,1024]{1,0:T(8,128)(2,1)S(1)} %fusion.114.refs_0_.refs_4_, bf16[256,512]{1,0:T(8,128)(2,1)S(1)} %pad_maximum_fusion.22.refs_1_, bf16[256,1024]{1,0:T(8,128)(2,1)S(1)} %maximum_select_fusion.3.refs_2_, bf16[256,512]{1,0:T(8,128)(2,1)S(1)} %get-tuple-element.296.refs_3_, ...), custom_call_target="tpu_custom_call" | custom-call | flops 1073741824 | bytes 8388608 | tf_op jit(solution)/shard_map/outer/pallas_call | solution.py:191
  488.3 18.4 %collective-permute-done.60 = bf16[4,64,128]{2,1,0:T(8,128)(2,1)S(1)} collective-permute-done((bf16[4,64,128]{2,1,0:T(8,128)(2,1)S(1)}, bf16[4,64,128]{2,1,0:T(8,128)(2,1)S(1)}, u32[]{:S(2)}, u32[]{:S(2)}) %collective-permute-start.60) | collective-permute-done | bytes 65568 | tf_op jit(solution)/shard_map/ppermute | solution.py:381
  508.0 5.4 collective-permute-done.59
  522.5 10.8 %collective-permute-start.48 = (bf16[256,1024]{1,0:T(8,128)(2,1)S(1)}, bf16[256,1024]{1,0:T(8,128)(2,1)S(1)}, u32[]{:S(2)}, u32[]{:S(2)}) collective-permute-start(bf16[256,1024]{1,0:T(8,128)(2,1)S(1)} %copy-done.163), channel_id=1, source_target_pairs={{0,0},{1,8},{8,1},{9,9},{2,2},{3,10},{10,3},{11,11},{4,4},{5,12},{... | collective-permute-start | bytes 1572872 | tf_op jit(solution)/shard_map/ppermute | solution.py:285
  540.2 5.9 %collective-permute-done.49 = bf16[256,1024]{1,0:T(8,128)(2,1)S(1)} collective-permute-done((bf16[256,1024]{1,0:T(8,128)(2,1)S(1)}, bf16[256,1024]{1,0:T(8,128)(2,1)S(1)}, u32[]{:S(2)}, u32[]{:S(2)}) %collective-permute-start.49) | collective-permute-done | bytes 524320 | tf_op jit(solution)/shard_map/ppermute | solution.py:285
  547.1 4.2 all-to-all-start.2
  553.6 7.6 %collective-permute-done.70 = bf16[64,4096]{1,0:T(8,128)(2,1)S(1)} collective-permute-done((bf16[64,4096]{1,0:T(8,128)(2,1)}, bf16[64,4096]{1,0:T(8,128)(2,1)S(1)}, u32[]{:S(2)}, u32[]{:S(2)}) %collective-permute-start.70) | collective-permute-done | bytes 524320 | tf_op jit(solution)/shard_map/ppermute | solution.py:36
  (770 shorter events, 298.1 us)
Async XLA Ops:
  9.4 18.9 %collective-permute-start.5 = (bf16[64,1024]{1,0:T(8,128)(2,1)S(1)}, bf16[64,1024]{1,0:T(8,128)(2,1)S(1)}, u32[]{:S(2)}, u32[]{:S(2)}) collective-permute-start(bf16[64,1024]{1,0:T(8,128)(2,1)S(1)} %reshape.458.refs_0_), channel_id=1, source_target_pairs={{0,32},{16,48},{32,0},{48,16},{1,33},{17,49},{33,1},{49,17},{2,34}... | collective-permute-start | bytes 393224 | tf_op jit(solution)/shard_map/ppermute | solution.py:616
  13.9 16.1 %collective-permute-start.4 = (bf16[64,1024]{1,0:T(8,128)(2,1)S(1)}, bf16[64,1024]{1,0:T(8,128)(2,1)S(1)}, u32[]{:S(2)}, u32[]{:S(2)}) collective-permute-start(bf16[64,1024]{1,0:T(8,128)(2,1)S(1)} %reshape.458.refs_0_), channel_id=1, source_target_pairs={{0,48},{16,0},{32,16},{48,32},{1,49},{17,1},{33,17},{49,33},{2,50}... | collective-permute-start | bytes 393224 | tf_op jit(solution)/shard_map/ppermute | solution.py:305
  14.3 15.6 %collective-permute-start.3 = (bf16[64,1024]{1,0:T(8,128)(2,1)S(1)}, bf16[64,1024]{1,0:T(8,128)(2,1)S(1)}, u32[]{:S(2)}, u32[]{:S(2)}) collective-permute-start(bf16[64,1024]{1,0:T(8,128)(2,1)S(1)} %reshape.458.refs_0_), channel_id=1, source_target_pairs={{0,16},{16,32},{32,48},{48,0},{1,17},{17,33},{33,49},{49,1},{2,18}... | collective-permute-start | bytes 393224 | tf_op jit(solution)/shard_map/ppermute | solution.py:305
  24.1 115.5 %all-gather.2.cloned.1.call-start = ((), (), s32[]{:S(2)}) async-start(), calls=%async_computation.6 | async-start | bytes 8912896 | tf_op jit(solution)/shard_map/all_gather | solution.py:621
  37.9 29.6 %collective-permute-start.14 = (bf16[256,1024]{1,0:T(8,128)(2,1)}, bf16[256,1024]{1,0:T(8,128)(2,1)}, u32[]{:S(2)}, u32[]{:S(2)}) collective-permute-start(bf16[256,1024]{1,0:T(8,128)(2,1)} %bitcast.16), channel_id=1, source_target_pairs={{0,0},{1,8},{8,1},{9,9},{2,2},{3,10},{10,3},{11,11},{4,4},{5,12},{... | collective-permute-start | bytes 1572872 | tf_op jit(solution)/shard_map/ppermute | solution.py:285
  50.0 18.3 %collective-permute-start.11 = (bf16[128,1152]{1,0:T(8,128)(2,1)}, bf16[128,1152]{1,0:T(8,128)(2,1)S(1)}, u32[]{:S(2)}, u32[]{:S(2)}) collective-permute-start(bf16[128,1152]{1,0:T(8,128)(2,1)} %slice.504), channel_id=1, source_target_pairs={{0,48},{16,0},{32,16},{48,32},{1,49},{17,1},{33,17},{49,33},{2,50}... | collective-permute-start | bytes 884744 | tf_op jit(solution)/shard_map/ppermute | solution.py:312
  51.3 17.0 %collective-permute-start.10 = (bf16[128,1152]{1,0:T(8,128)(2,1)}, bf16[128,1152]{1,0:T(8,128)(2,1)}, u32[]{:S(2)}, u32[]{:S(2)}) collective-permute-start(bf16[128,1152]{1,0:T(8,128)(2,1)} %slice.503), channel_id=1, source_target_pairs={{0,16},{16,32},{32,48},{48,0},{1,17},{17,33},{33,49},{49,1},{2,18}... | collective-permute-start | bytes 884744 | tf_op jit(solution)/shard_map/ppermute | solution.py:311
  87.1 35.3 %collective-permute-start.15 = (bf16[1024,512]{1,0:T(8,128)(2,1)S(1)}, bf16[1024,512]{1,0:T(8,128)(2,1)S(1)}, u32[]{:S(2)}, u32[]{:S(2)}) collective-permute-start(bf16[1024,512]{1,0:T(8,128)(2,1)S(1)} %bitcast.213), channel_id=1, source_target_pairs={{0,1},{1,0},{2,3},{3,2},{4,5},{5,4},{6,7},{7,6},{8,9},{9,8},{10,11... | collective-permute-start | bytes 3145736 | tf_op jit(solution)/shard_map/ppermute | solution.py:36
  96.3 25.0 %collective-permute-start.18 = (bf16[256,1024]{1,0:T(8,128)(2,1)S(1)}, bf16[256,1024]{1,0:T(8,128)(2,1)S(1)}, u32[]{:S(2)}, u32[]{:S(2)}) collective-permute-start(bf16[256,1024]{1,0:T(8,128)(2,1)S(1)} %pad_maximum_fusion.3.own_ref), channel_id=1, source_target_pairs={{0,4},{4,0},{1,5},{5,1},{2,6},{6,2},{3,7},{7,3},{8,12},{12,8},{9,1... | collective-permute-start | bytes 1572872 | tf_op jit(solution)/shard_map/ppermute | solution.py:36
  99.1 27.0 %collective-permute-start.17 = (bf16[256,1024]{1,0:T(8,128)(2,1)S(1)}, bf16[256,1024]{1,0:T(8,128)(2,1)S(1)}, u32[]{:S(2)}, u32[]{:S(2)}) collective-permute-start(bf16[256,1024]{1,0:T(8,128)(2,1)S(1)} %pad_maximum_fusion.3.own_ref), channel_id=1, source_target_pairs={{0,1},{1,0},{2,3},{3,2},{4,5},{5,4},{6,7},{7,6},{8,9},{9,8},{10,11... | collective-permute-start | bytes 1572872 | tf_op jit(solution)/shard_map/ppermute | solution.py:36
  139.6 29.7 %collective-permute-start.24 = (bf16[1024,4096]{1,0:T(8,128)(2,1)}, bf16[1024,4096]{1,0:T(8,128)(2,1)}, u32[]{:S(2)}, u32[]{:S(2)}) collective-permute-start(bf16[1024,4096]{1,0:T(8,128)(2,1)} %all-gather.2.cloned.1.call-done), channel_id=1, source_target_pairs={{0,1},{1,0},{2,3},{3,2},{4,5},{5,4},{6,7},{7,6},{8,9},{9,8},{10,11... | collective-permute-start | bytes 25165832 | tf_op jit(solution)/shard_map/ppermute | solution.py:36
  140.4 22.1 %collective-permute-start.23 = (bf16[1024,512]{1,0:T(8,128)(2,1)S(1)}, bf16[1024,512]{1,0:T(8,128)(2,1)S(1)}, u32[]{:S(2)}, u32[]{:S(2)}) collective-permute-start(bf16[1024,512]{1,0:T(8,128)(2,1)S(1)} %bitcast.206), channel_id=1, source_target_pairs={{0,1},{1,0},{2,3},{3,2},{4,5},{5,4},{6,7},{7,6},{8,9},{9,8},{10,11... | collective-permute-start | bytes 3145736 | tf_op jit(solution)/shard_map/ppermute | solution.py:36
  177.9 22.1 %collective-permute-start.25 = (bf16[256,1024]{1,0:T(8,128)(2,1)S(1)}, bf16[256,1024]{1,0:T(8,128)(2,1)S(1)}, u32[]{:S(2)}, u32[]{:S(2)}) collective-permute-start(bf16[256,1024]{1,0:T(8,128)(2,1)S(1)} %fusion.90), channel_id=1, source_target_pairs={{0,64},{1,65},{2,66},{3,67},{4,68},{5,69},{6,70},{7,71},{8,72},{9,... | collective-permute-start | bytes 1572872 | tf_op jit(solution)/shard_map/ppermute | solution.py:688
  185.2 288.8 %reduce-scatter.6.cloned.1.call-start = ((), (), s32[]{:S(2)}) async-start(), calls=%async_computation.8 | async-start | bytes 5242880 | tf_op jit(solution)/shard_map/reduce_scatter | solution.py:501
  206.2 19.0 %collective-permute-start.26 = (bf16[256,1024]{1,0:T(8,128)(2,1)S(1)}, bf16[256,1024]{1,0:T(8,128)(2,1)S(1)}, u32[]{:S(2)}, u32[]{:S(2)}) collective-permute-start(bf16[256,1024]{1,0:T(8,128)(2,1)S(1)} %pad_maximum_fusion.5.own_ref), channel_id=1, source_target_pairs={{0,1},{1,0},{2,3},{3,2},{4,5},{5,4},{6,7},{7,6},{8,9},{9,8},{10,11... | collective-permute-start | bytes 1572872 | tf_op jit(solution)/shard_map/ppermute | solution.py:36
  273.3 15.4 %collective-permute-start.34 = (bf16[256,1024]{1,0:T(8,128)(2,1)}, bf16[256,1024]{1,0:T(8,128)(2,1)}, u32[]{:S(2)}, u32[]{:S(2)}) collective-permute-start(bf16[256,1024]{1,0:T(8,128)(2,1)} %add_convert_fusion.10), channel_id=1, source_target_pairs={{0,4},{4,0},{1,5},{5,1},{2,6},{6,2},{3,7},{7,3},{8,12},{12,8},{9,1... | collective-permute-start | bytes 1572872 | tf_op jit(solution)/shard_map/ppermute | solution.py:36
  274.0 17.8 %collective-permute-start.35 = (bf16[256,1024]{1,0:T(8,128)(2,1)}, bf16[256,1024]{1,0:T(8,128)(2,1)S(1)}, u32[]{:S(2)}, u32[]{:S(2)}) collective-permute-start(bf16[256,1024]{1,0:T(8,128)(2,1)} %copy-done.66), channel_id=1, source_target_pairs={{0,1},{1,0},{2,3},{3,2},{4,5},{5,4},{6,7},{7,6},{8,9},{9,8},{10,11... | collective-permute-start | bytes 1572872 | tf_op jit(solution)/shard_map/ppermute | solution.py:36
  333.1 18.8 %collective-permute-start.40 = (bf16[1024,2048]{1,0:T(8,128)(2,1)S(1)}, bf16[1024,2048]{1,0:T(8,128)(2,1)S(1)}, u32[]{:S(2)}, u32[]{:S(2)}) collective-permute-start(bf16[1024,2048]{1,0:T(8,128)(2,1)S(1)} %outer.6), channel_id=1, source_target_pairs={{0,1},{1,0},{2,3},{3,2},{4,5},{5,4},{6,7},{7,6},{8,9},{9,8},{10,11... | collective-permute-start | bytes 12582920 | tf_op jit(solution)/shard_map/ppermute | solution.py:36
  356.8 117.3 %reduce-scatter.4.cloned.1.call-start = ((), (), s32[]{:S(2)}) async-start(), calls=%async_computation.7 | async-start | bytes 5242880 | tf_op jit(solution)/shard_map/reduce_scatter | solution.py:526
  385.5 165.9 %reduce-scatter.8.cloned.1.call-start = ((), (), s32[]{:S(2)}) async-start(), calls=%async_computation.9 | async-start | bytes 2621440 | tf_op jit(solution)/shard_map/reduce_scatter | solution.py:737
  423.6 28.2 %collective-permute-start.50 = (bf16[1024,2048]{1,0:T(8,128)(2,1)}, bf16[1024,2048]{1,0:T(8,128)(2,1)}, u32[]{:S(2)}, u32[]{:S(2)}) collective-permute-start(bf16[1024,2048]{1,0:T(8,128)(2,1)} %outer.10), channel_id=1, source_target_pairs={{0,1},{1,0},{2,3},{3,2},{4,5},{5,4},{6,7},{7,6},{8,9},{9,8},{10,11... | collective-permute-start | bytes 12582920 | tf_op jit(solution)/shard_map/ppermute | solution.py:36
  480.4 33.1 %collective-permute-start.57 = (bf16[4,64,1024]{2,1,0:T(8,128)(2,1)S(1)}, bf16[4,64,1024]{2,1,0:T(8,128)(2,1)S(1)}, u32[]{:S(2)}, u32[]{:S(2)}) collective-permute-start(bf16[4,64,1024]{2,1,0:T(8,128)(2,1)S(1)} %pad_maximum_fusion.11), channel_id=1, source_target_pairs={{0,16},{16,32},{32,48},{48,0},{1,17},{17,33},{33,49},{49,1},{2,18}... | collective-permute-start | bytes 1572872 | tf_op jit(solution)/shard_map/ppermute | solution.py:371
  482.0 31.5 %collective-permute-start.55 = (bf16[4,64,1024]{2,1,0:T(8,128)(2,1)S(1)}, bf16[4,64,1024]{2,1,0:T(8,128)(2,1)S(1)}, u32[]{:S(2)}, u32[]{:S(2)}) collective-permute-start(bf16[4,64,1024]{2,1,0:T(8,128)(2,1)S(1)} %pad_maximum_fusion.9), channel_id=1, source_target_pairs={{0,4},{4,8},{8,12},{12,0},{1,5},{5,9},{9,13},{13,1},{2,6},{6,10},{... | collective-permute-start | bytes 1572872 | tf_op jit(solution)/shard_map/ppermute | solution.py:371
  483.1 30.4 %collective-permute-start.56 = (bf16[4,64,1024]{2,1,0:T(8,128)(2,1)S(1)}, bf16[4,64,1024]{2,1,0:T(8,128)(2,1)S(1)}, u32[]{:S(2)}, u32[]{:S(2)}) collective-permute-start(bf16[4,64,1024]{2,1,0:T(8,128)(2,1)S(1)} %pad_maximum_fusion.10), channel_id=1, source_target_pairs={{0,12},{4,0},{8,4},{12,8},{1,13},{5,1},{9,5},{13,9},{2,14},{6,2},{... | collective-permute-start | bytes 1572872 | tf_op jit(solution)/shard_map/ppermute | solution.py:371
  484.9 28.6 %collective-permute-start.58 = (bf16[4,64,1024]{2,1,0:T(8,128)(2,1)S(1)}, bf16[4,64,1024]{2,1,0:T(8,128)(2,1)S(1)}, u32[]{:S(2)}, u32[]{:S(2)}) collective-permute-start(bf16[4,64,1024]{2,1,0:T(8,128)(2,1)S(1)} %pad_maximum_fusion.12), channel_id=1, source_target_pairs={{0,48},{16,0},{32,16},{48,32},{1,49},{17,1},{33,17},{49,33},{2,50}... | collective-permute-start | bytes 1572872 | tf_op jit(solution)/shard_map/ppermute | solution.py:371
  487.4 19.3 %collective-permute-start.60 = (bf16[4,64,128]{2,1,0:T(8,128)(2,1)S(1)}, bf16[4,64,128]{2,1,0:T(8,128)(2,1)S(1)}, u32[]{:S(2)}, u32[]{:S(2)}) collective-permute-start(bf16[4,64,128]{2,1,0:T(8,128)(2,1)S(1)} %get-tuple-element.335), channel_id=1, source_target_pairs={{0,12},{4,0},{8,4},{12,8},{1,13},{5,1},{9,5},{13,9},{2,14},{6,2},{... | collective-permute-start | bytes 196616 | tf_op jit(solution)/shard_map/ppermute | solution.py:381
  515.1 20.2 %collective-permute-start.64 = (bf16[64,1152]{1,0:T(8,128)(2,1)S(1)}, bf16[64,1152]{1,0:T(8,128)(2,1)S(1)}, u32[]{:S(2)}, u32[]{:S(2)}) collective-permute-start(bf16[64,1152]{1,0:T(8,128)(2,1)S(1)} %get-tuple-element.287), channel_id=1, source_target_pairs={{0,32},{16,48},{32,0},{48,16},{1,33},{17,49},{33,1},{49,17},{2,34}... | collective-permute-start | bytes 442376 | tf_op jit(solution)/shard_map/ppermute | solution.py:381
  515.1 20.1 %collective-permute-start.62 = (bf16[64,1152]{1,0:T(8,128)(2,1)S(1)}, bf16[64,1152]{1,0:T(8,128)(2,1)S(1)}, u32[]{:S(2)}, u32[]{:S(2)}) collective-permute-start(bf16[64,1152]{1,0:T(8,128)(2,1)S(1)} %get-tuple-element.289), channel_id=1, source_target_pairs={{0,16},{16,32},{32,48},{48,0},{1,17},{17,33},{33,49},{49,1},{2,18}... | collective-permute-start | bytes 442376 | tf_op jit(solution)/shard_map/ppermute | solution.py:381
  517.0 18.3 %collective-permute-start.63 = (bf16[64,1152]{1,0:T(8,128)(2,1)S(1)}, bf16[64,1152]{1,0:T(8,128)(2,1)S(1)}, u32[]{:S(2)}, u32[]{:S(2)}) collective-permute-start(bf16[64,1152]{1,0:T(8,128)(2,1)S(1)} %get-tuple-element.290), channel_id=1, source_target_pairs={{0,48},{16,0},{32,16},{48,32},{1,49},{17,1},{33,17},{49,33},{2,50}... | collective-permute-start | bytes 442376 | tf_op jit(solution)/shard_map/ppermute | solution.py:381
  522.5 17.7 %collective-permute-start.48 = (bf16[256,1024]{1,0:T(8,128)(2,1)S(1)}, bf16[256,1024]{1,0:T(8,128)(2,1)S(1)}, u32[]{:S(2)}, u32[]{:S(2)}) collective-permute-start(bf16[256,1024]{1,0:T(8,128)(2,1)S(1)} %copy-done.163), channel_id=1, source_target_pairs={{0,0},{1,8},{8,1},{9,9},{2,2},{3,10},{10,3},{11,11},{4,4},{5,12},{... | collective-permute-start | bytes 1572872 | tf_op jit(solution)/shard_map/ppermute | solution.py:285
  535.5 17.9 %collective-permute-start.68 = (bf16[64,2176]{1,0:T(8,128)(2,1)S(1)}, bf16[64,2176]{1,0:T(8,128)(2,1)S(1)}, u32[]{:S(2)}, u32[]{:S(2)}) collective-permute-start(bf16[64,2176]{1,0:T(8,128)(2,1)S(1)} %pad_maximum_fusion.13), channel_id=1, source_target_pairs={{0,2},{2,0},{1,3},{3,1},{4,6},{6,4},{5,7},{7,5},{8,10},{10,8},{9,1... | collective-permute-start | bytes 835592 | tf_op jit(solution)/shard_map/ppermute | solution.py:36
  547.1 15.4 %all-to-all-start.2 = ((bf16[4,2,64,1024]{3,2,1,0:T(8,128)(2,1)}), bf16[4,2,64,1024]{3,2,1,0:T(8,128)(2,1)}, u32[]{:S(2)}, u32[]{:S(2)}) async-start(bf16[4,2,64,1024]{3,2,1,0:T(8,128)(2,1)} %pad_maximum_fusion.1), calls=%async_computation.2 | async-start | bytes 2097152 | tf_op jit(solution)/shard_map/all_to_all | solution.py:292
  (223 other events, 2025.0 us)
Sparse Core Ops, SparseCore 0:
  34.1 88.0 all-gather.1
  356.9 43.6 reduce-scatter.5
  403.2 46.5 reduce-scatter.3
  478.8 37.5 reduce-scatter.7

commit v7 on v6

--- a/solution.py
+++ b/solution.py
@@ -229,6 +229,44 @@
     )(core.reshape(1), *inputs)
 
 
+def vector_block(core, sums, width, columns):
+    half = width // 2
+    whole = [*sums["gain"], *sums["shift"], *sums["out_bias"], *sums["scale"]]
+    halves = [*sums["q"], *sums["kv"], *sums["fc1_bias"]]
+
+    def kernel(core_ref, *refs):
+        out_ref, rows_ref = refs[-2:]
+        flag = core_ref[0]
+        order = lambda a, b: (jnp.where(flag == 0, a, b), jnp.where(flag == 0, b, a))
+        rows_ref[...] = jnp.zeros(rows_ref.shape, f32)
+        for ref, row in zip(refs, (0, 1, 2, 3, 6, 7, 8, 9)):
+            rows_ref[row : row + 1, :] = ref[...]
+        q_mine, q_other, kv_mine, kv_other, fc_mine, fc_other = (
+            r[...] for r in refs[len(whole) : len(whole) + len(halves)]
+        )
+        for i, value in enumerate(order(q_mine, q_other)):
+            rows_ref[4:5, i * half : (i + 1) * half] = value
+        for i, value in enumerate(order(kv_mine, kv_other)):
+            for g in range(half // PAIR):
+                at = i * half + g * PAIR
+                rows_ref[5:6, at : at + PAIR] = value[:, (2 * g + 1) * PAIR : (2 * g + 2) * PAIR]
+        for i, value in enumerate(order(fc_mine, fc_other)):
+            for k in range(2):
+                row = 10 + 2 * i + k
+                rows_ref[row : row + 1, :] = value[:, k * width : (k + 1) * width]
+        out_ref[...] = rows_ref[...].T.astype(bf16)
+
+    vmem = pl.BlockSpec(memory_space=pltpu.VMEM)
+    return pl.pallas_call(
+        kernel,
+        in_specs=[pl.BlockSpec(memory_space=pltpu.SMEM)] + [vmem] * len(whole + halves),
+        out_specs=vmem,
+        out_shape=jax.ShapeDtypeStruct((width, columns), bf16),
+        scratch_shapes=[pltpu.VMEM((columns, width), f32)],
+        name="vector_block",
+    )(core.reshape(1), *whole, *halves)
+
+
 def join_qkv(core, mine, other, width):
     rows, half = mine.shape[0], width // 2
 
@@ -285,12 +323,10 @@
     return lax.ppermute(tokens, ("yh", "core"), FLIP)
 
 
-def from_images(arrays, count):
-    rows, width = arrays[0].shape
-    mixed = [flip(a) for a in arrays]
-    mixed = jnp.stack([m.reshape(count, rows // count, width) for m in mixed], axis=1)
-    mixed = lax.all_to_all(mixed, "z", split_axis=0, concat_axis=0, tiled=True)
-    return [mixed[:, i] for i in range(len(arrays))]
+def from_images(tokens, count):
+    rows, width = tokens.shape
+    mixed = flip(tokens).reshape(count, rows // count, width)
+    return lax.all_to_all(mixed, "z", split_axis=0, concat_axis=0, tiled=True)
 
 
 RING_Z, RING_Y = "z", ("yh", "yl")
@@ -373,13 +409,14 @@
     return [add(*e) for e in ends], beside
 
 
-def direct_sums(items):
+def direct_sums(items, beside=None):
     ways = [(1, AHEAD), (3, BACK), (2, ACROSS)]
     parts = []
     for blocks, axis, dim in items:
         block = ring_blocks(blocks, axis, dim)
         parts.append([block[0]] + [lax.ppermute(block[k], axis, way) for k, way in ways])
-    return [add(*p) for p in lax.optimization_barrier(parts)]
+    parts, beside = lax.optimization_barrier((parts, beside))
+    return [add(*p) for p in parts], beside
 
 
 def group_parts(own, mate, near, far):
@@ -440,12 +477,11 @@
             following, near = lax.optimization_barrier((key_value[i + 1], near))
             mate, near = swap(following, "core"), swap(following, "yl")
             result = attend(queries[i], blocks[i])
-            result, near = lax.optimization_barrier((result, near))
+            result, near, mate = lax.optimization_barrier((result, near, mate))
         else:
             if late is not None:
-                (own, near), gathered = lax.optimization_barrier(((own, near), late[0]))
+                blocks[i], gathered = lax.optimization_barrier((blocks[i], late[0]))
                 w.update(late[1](gathered))
-                blocks[i] = (own, mate, near, blocks[i][3])
             result = attend(queries[i], blocks[i])
         results.append(result)
     attended, log_total = zip(*results)
@@ -484,7 +520,7 @@
     return result, kept
 
 
-def backward(grad_out, kept, w, last=False):
+def backward(grad_out, kept, w, last=False, beside=None):
     grad_branch_two = (w["scale"][1] * grad_out).astype(bf16)
     grad_before = []
     grad_normed_two = 0.0
@@ -530,7 +566,7 @@
             came = swap(sent, "yl")
         parts = attend_back(kept["queries"][i], kept["blocks"][i], g, kept["log_total"][i])
         if ready is not None:
-            parts, came = lax.optimization_barrier((parts, came))
+            parts, came, beside = lax.optimization_barrier((parts, came, beside))
             kv_chunks.append((own + came.astype(f32)).astype(bf16))
         q_chunks.append(parts[0])
         ready = group_parts(*parts[1:])
@@ -556,6 +592,7 @@
         kv=(kept["normed_one"], grad_kv),
         proj=(kept["attended"], grad_halves),
         fc=fc_grad,
+        beside=beside,
     )
     return grad_inputs.astype(bf16), vectors, products
 
@@ -607,45 +644,39 @@
     fc1_mine = jnp.swapaxes(fc1_mine, 1, 2).reshape(own, shards * mid)
     fc2_mine = pick(fc2_weight[0].reshape(2, 2, part, width), core, 0)
     fc_mine = jnp.concatenate([fc1_mine, fc2_mine[0], fc2_mine[1]], axis=1)
-
-    a_mine = jnp.concatenate([q_mine, proj_mine, vectors], axis=1)
+    fc_row = lax.all_gather(fc_mine, RING_Y, axis=0, tiled=True)
+
+    mine = jnp.concatenate([kv_mine, q_mine, proj_mine, vectors], axis=1)
     live = (
         jnp.arange(images) % IMG_MB < jnp.repeat(batch_counts[0], IMG_MB)
     ).astype(bf16)
     live_grad = out_grad * live[:, None, None]
-    direct = lambda value, axis: (*first_hop(value, axis), lax.ppermute(value, axis, ACROSS))
-    first = (direct(a_mine, RING_Y), direct(kv_mine, RING_Z))
-    first, fc_mine, live_grad, first_tokens = lax.optimization_barrier(
-        (first, fc_mine, live_grad, to_images(patch_tokens))
-    )
-    fc_half = lax.all_gather(fc_mine, FSDP, axis=0, tiled=True)
-    a_wide = a_mine.shape[1]
-    a_row = ring_place(a_mine, RING_Y, first[0], [(4, own, a_wide)], in_order)[0]
-    a_row = a_row.reshape(4 * own, a_wide)
-    b_row = ring_place(kv_mine, RING_Z, first[1], [(4, own, width)], in_order)[0]
-    hops = lax.optimization_barrier((first_hop(a_row, RING_Z), first_hop(b_row, RING_Y)))
-    more = (second_hop(*hops[0], RING_Z), second_hop(*hops[1], RING_Y))
-    more, first_tokens = lax.optimization_barrier((more, flip(first_tokens)))
-
-    def a_views(outs, piece, place, start):
-        at = 0
-        for out in outs:
-            size = out.shape[-1]
-            out[place, pl.ds(start, piece.shape[0])] = piece[:, pl.ds(at, size)]
-            at += size
-
-    def b_views(outs, piece, place, start):
+    hops = (*first_hop(mine, RING_Z), lax.ppermute(mine, RING_Z, ACROSS))
+    hops, fc_row, live_grad, first_tokens = lax.optimization_barrier(
+        (hops, fc_row, live_grad, to_images(patch_tokens))
+    )
+    fc_half = lax.all_gather(fc_row, RING_Z, axis=0, tiled=True)
+    row = ring_place(mine, RING_Z, hops, [(4, *mine.shape)], in_order)[0]
+    hops = lax.optimization_barrier(first_hop(row, RING_Y))
+    more, first_tokens = lax.optimization_barrier(
+        (second_hop(*hops, RING_Y), flip(first_tokens))
+    )
+
+    def views(outs, piece, place, start):
         for i in range(piece.shape[0]):
-            outs[0][start + i, place] = piece[i]
-
-    q_half, proj_half, vectors = (
+            at = 0
+            for out in outs:
+                size = out.shape[-1]
+                out[start + i, place] = piece[i, :, at : at + size]
+                at += size
+
+    sizes = (width, half, half, 128)
+    kv_half, q_half, proj_half, vectors = (
         o.reshape(width, -1)
         for o in ring_place(
-            a_row, RING_Z, hops[0] + more[0], [(4, 4 * own, half), (4, 4 * own, half), (4, 4 * own, 128)], a_views
+            row, RING_Y, hops + more, [(4, 4, own, size) for size in sizes], views
         )
     )
-    kv_half = ring_place(b_row, RING_Y, hops[1] + more[1], [(4, 4, own, width)], b_views)[0]
-    kv_half = kv_half.reshape(width, width)
     vectors = vectors[:, :16].T.astype(f32)
 
     def halves(row):
@@ -691,56 +722,38 @@
     result, kept = forward(tokens, w)
 
     sent, _, _ = backward(last_grad.astype(f32), kept, w)
+    sent, result = lax.optimization_barrier((sent, result))
     passed = lax.ppermute(sent, "section", [(1, 0)])
+    block_out = from_images(result, images)
     grad_out = jnp.where(section == 1, last_grad, passed).astype(f32)
-    grad_inputs, sums, products = backward(grad_out, kept, w, last=True)
-    result, grad_inputs = lax.optimization_barrier((result, grad_inputs))
-    block_out, in_grad = from_images([result, grad_inputs], images)
-
-    def natural(pair):
-        return jnp.concatenate(ordered(core, *pair), axis=1)
-
-    def v_sum(a):
-        cuts = [a[:, (2 * i + 1) * PAIR : (2 * i + 2) * PAIR] for i in range(groups)]
-        return jnp.concatenate(cuts, axis=1)
-
-    fc1_rows = [
-        jnp.concatenate([b[:, :width], b[:, width:]], axis=0)
-        for b in ordered(core, *sums["fc1_bias"])
-    ]
-    vector_grads = jnp.concatenate(
-        [
-            *sums["gain"],
-            *sums["shift"],
-            natural(sums["q"]),
-            natural([v_sum(g) for g in sums["kv"]]),
-            *sums["out_bias"],
-            *sums["scale"],
-            *fc1_rows,
-            jnp.zeros((PAIR - count, width), f32),
-        ],
-        axis=0,
-    )
-    vector_grads = vector_grads.astype(bf16).T
+    grad_inputs, sums, products = backward(grad_out, kept, w, True, block_out)
+
+    vector_grads = vector_block(core, sums, width, PAIR)
 
     a1, dq = products["q"]
     dkv = products["kv"][1]
     o, e1 = products["proj"]
-    make = lambda i, add=None: outer(
-        [((a1, 0), dq[i], width), ((o, 0), e1[i], width), ((a1, 0), dkv[i], width)], 256, add=add
-    )
-    ab = make(0, swap(make(1), "core")).reshape(4, 4, own, 2 * width)
-    (a_sum, b_sum), (rows, vector_grads) = ring_sums(
-        [(ab[..., :width], RING_Y, 1), (ab[..., width:], RING_Z, 0)],
-        (products["fc"], vector_grads),
-    )
+    make_a = lambda i, add=None: outer(
+        [((a1, 0), dq[i], width), ((o, 0), e1[i], width)], half // 2, add=add
+    )
+    make_b = lambda i, add=None: outer([((a1, 0), dkv[i], width)], half // 2, add=add)
+    a_full, b_full = (
+        make(0, swap(make(1), "core")).reshape(4, 4, own, width) for make in (make_a, make_b)
+    )
+    (a_sum, b_sum), (rows, vector_grads, grad_inputs) = ring_sums(
+        [(a_full, RING_Y, 1), (b_full, RING_Z, 0)],
+        (products["fc"], vector_grads, grad_inputs),
+    )
+    in_grad = from_images(grad_inputs, images)
+    block_out = products["beside"]
     fc_grad = lax.psum_scatter(
         jnp.concatenate(rows, axis=1), RING_Y, scatter_dimension=0, tiled=True
     )
     vector_grads = vector_grads.reshape(4, 4, own, PAIR)
-    (vector_sum,) = direct_sums([(vector_grads, RING_Y, 1)])
-    ab = direct_sums(
-        [(jnp.concatenate([a_sum, vector_sum], axis=2), RING_Z, 0), (b_sum, RING_Y, 0)]
+    (vector_sum,), _ = direct_sums([(vector_grads, RING_Y, 1)])
+    ab, in_grad = direct_sums(
+        [(jnp.concatenate([a_sum, vector_sum], axis=2), RING_Z, 0), (b_sum, RING_Y, 0)],
+        in_grad,
     )
     ab = jnp.concatenate([ab[0][:, :width], ab[1], ab[0][:, width:]], axis=1)
 

time: 590 us -> 587 us (level)
  local copies, waits for them, and re-layouts: 89.2 us -> 46.7 us
  waiting for transfers between devices: 151 us -> 187 us
    ppermute x35 -> x36, waiting for transfers between devices: 77.4 us -> 51.9 us  [swap(): return lax.ppermute(value, axis, [(0, 1), (1, 0)])]
    ppermute x8 -> x4, waiting for transfers between devices: 8.29 us -> 24.5 us  [first_hop(): return (lax.ppermute(value, axis, AHEAD), lax.ppermute(value, axis, BACK))]
    broadcast_in_dim x9 -> x0, local copies, waits for them, and re-layouts: 11.3 us -> none  [the longest x8 10.5 us: backward(): total = lambda a: jnp.sum(a.astype(f32), axis=0, keepdims=True)]
    ppermute x4, waiting for transfers between devices: 20.6 us -> 30.2 us  [flip(): return lax.ppermute(tokens, ('yh', 'core'), FLIP)]
    unnamed x369 -> x235, local copies, waits for them, and re-layouts: 41.1 us -> 32 us
    all_gather x1 -> x2, waiting for transfers between devices: 0.01 us -> 8.72 us  [the longest x1 8.72 us: per_device(): fc_row = lax.all_gather(fc_mine, RING_Y, axis=0, tiled=True)]
    ppermute x35 -> x36, starting transfers between devices: 30 us -> 38.5 us  [swap(): return lax.ppermute(value, axis, [(0, 1), (1, 0)])]
    slice x9 -> x0, local copies, waits for them, and re-layouts: 7.25 us -> none  [the longest x4 4.32 us: per_device(): b[:, width:]]
  transfers between devices with their start and end apart: 79 -> 75, of which waited for: 25 -> 30; matrix products, arithmetic and copies ran while one was open for 23% -> 16% of each run, Pallas kernels for 12% -> 12%
where the time goes in v7:
time: 587 us; the launch traced here: 576 us
  waiting for transfers between devices  187 us (32%)
  starting transfers between devices  111 us (19%)
  Pallas kernels  93.1 us (16%)
  matrix products  82 us (14%)
  local copies, waits for them, and re-layouts  46.7 us (8%)
  other arithmetic  39.1 us (7%)
  between operations  16.9 us (3%)
    dot_general x48, matrix products, dot(): return lax.dot_general(a, b, (dims, ((), ())), preferred_element_type=f32)  82 us
    ppermute x36, waiting for transfers between devices, swap(): return lax.ppermute(value, axis, [(0, 1), (1, 0)])  51.9 us
    ppermute x36, starting transfers between devices, swap(): return lax.ppermute(value, axis, [(0, 1), (1, 0)])  38.5 us
    pallas_call x4, Pallas kernels, attend_back(): pl.pallas_call(attend_back_kernel, grid=(pairs,), in_specs=[q_spec] + kv_...  36.7 us
    ppermute x9, waiting for transfers between devices, direct_sums(): lax.ppermute(block[k], axis, way)  33.1 us
    unnamed x235, local copies, waits for them, and re-layouts  32 us
    ppermute x4, waiting for transfers between devices, flip(): return lax.ppermute(tokens, ('yh', 'core'), FLIP)  30.2 us
    pallas_call x4, Pallas kernels, attend(): pl.pallas_call(attend_kernel, grid=(pairs,), in_specs=[q_spec] + kv_specs...  29.2 us
  transfers between devices with their start and end apart: 75, of which 30 were waited for; matrix products, arithmetic and copies ran while one was open for 16% of the time, Pallas kernels for 12%

profile of v7, /device:TPU:1, one launch (start us, length us, event | category | flops | bytes accessed | tf_op | source)
XLA Modules:
  0.0 575.7 jit_solution(10398320284262339637)
XLA Ops:
  24.9 6.9 %collective-permute-done.2.refs_3_ = bf16[64,2176]{1,0:T(8,128)(2,1)S(1)} collective-permute-done((bf16[64,2176]{1,0:T(8,128)(2,1)S(1)}, bf16[64,2176]{1,0:T(8,128)(2,1)S(1)}, u32[]{:S(2)}, u32[]{:S(2)}) %collective-permute-start.2) | collective-permute-done | bytes 278560 | tf_op jit(solution)/shard_map/ppermute | solution.py:654
  31.8 5.6 all-to-all-done
  37.4 8.7 %all-gather.3.cloned.1.call-done = bf16[256,4096]{1,0:T(8,128)(2,1)} async-done(((bf16[64,4096]{1,0:T(8,128)(2,1)}), bf16[256,4096]{1,0:T(8,128)(2,1)}) %all-gather.3.cloned.1.call-update) | async-done | bytes 2097168 | tf_op jit(solution)/shard_map/all_gather | solution.py:647
  49.0 24.1 %collective-permute-done.3.refs_1_ = bf16[4,64,2176]{2,1,0:T(8,128)(2,1)S(1)} collective-permute-done((bf16[4,64,2176]{2,1,0:T(8,128)(2,1)S(1)}, bf16[4,64,2176]{2,1,0:T(8,128)(2,1)S(1)}, u32[]{:S(2)}, u32[]{:S(2)}) %collective-permute-start.3) | collective-permute-done | bytes 1114144 | tf_op jit(solution)/shard_map/ppermute | solution.py:341
  78.5 4.7 collective-permute-start.7
  83.2 14.1 %collective-permute-done.7 = bf16[256,1024]{1,0:T(8,128)(2,1)S(1)} collective-permute-done((bf16[256,1024]{1,0:T(8,128)(2,1)}, bf16[256,1024]{1,0:T(8,128)(2,1)S(1)}, u32[]{:S(2)}, u32[]{:S(2)}) %collective-permute-start.7) | collective-permute-done | bytes 524320 | tf_op jit(solution)/shard_map/ppermute | solution.py:323
  116.1 11.5 %collective-permute-done.11.near_ref = bf16[256,1024]{1,0:T(8,128)(2,1)S(1)} collective-permute-done((bf16[256,1024]{1,0:T(8,128)(2,1)S(1)}, bf16[256,1024]{1,0:T(8,128)(2,1)S(1)}, u32[]{:S(2)}, u32[]{:S(2)}) %collective-permute-start.11) | collective-permute-done | bytes 524320 | tf_op jit(solution)/shard_map/ppermute | solution.py:36
  130.8 7.6 %attend.4 = (bf16[256,512]{1,0:T(8,128)(2,1)S(1)}, f32[4,2,256]{2,1,0:T(2,128)}) custom-call(bf16[256,512]{1,0:T(8,128)(2,1)S(1)} %pad_maximum_fusion.13.q_ref, bf16[256,1024]{1,0:T(8,128)(2,1)S(1)} %pad_maximum_fusion.2.own_ref, bf16[256,1024]{1,0:T(8,128)(2,1)S(1)} %collective-permute-done.10.mate_ref, ...), custom_call_target="tpu_custom_call" | custom-call | flops 2147483648 | bytes 4194304 | tf_op jit(solution)/shard_map/attend/pallas_call | solution.py:118
  147.3 7.6 %attend.5 = (bf16[256,512]{1,0:T(8,128)(2,1)S(1)}, f32[4,2,256]{2,1,0:T(2,128)}) custom-call(bf16[256,512]{1,0:T(8,128)(2,1)S(1)} %pad_maximum_fusion.14.q_ref, bf16[256,1024]{1,0:T(8,128)(2,1)S(1)} %pad_maximum_fusion.3.own_ref, bf16[256,1024]{1,0:T(8,128)(2,1)S(1)} %collective-permute-done.14.mate_ref, ...), custom_call_target="tpu_custom_call" | custom-call | flops 2147483648 | bytes 4194304 | tf_op jit(solution)/shard_map/attend/pallas_call | solution.py:118
  176.2 8.3 %all-to-all-done.1 = bf16[4,64,1024]{2,1,0:T(8,128)(2,1)S(1)} async-done(((bf16[4,64,1024]{2,1,0:T(8,128)(2,1)}), bf16[4,64,1024]{2,1,0:T(8,128)(2,1)S(1)}, u32[]{:S(2)}, u32[]{:S(2)}) %all-to-all-start.1) | async-done | bytes 524320 | tf_op jit(solution)/shard_map/all_to_all | solution.py:318
  184.5 5.4 collective-permute-start.25
  202.1 6.1 %collective-permute-done.20.near_ref = bf16[256,1024]{1,0:T(8,128)(2,1)S(1)} collective-permute-done((bf16[256,1024]{1,0:T(8,128)(2,1)S(1)}, bf16[256,1024]{1,0:T(8,128)(2,1)S(1)}, u32[]{:S(2)}, u32[]{:S(2)}) %collective-permute-start.20) | collective-permute-done | bytes 524320 | tf_op jit(solution)/shard_map/ppermute | solution.py:36
  214.0 7.0 %attend.6 = (bf16[256,512]{1,0:T(8,128)(2,1)S(1)}, f32[4,2,256]{2,1,0:T(2,128)S(1)}) custom-call(bf16[256,512]{1,0:T(8,128)(2,1)S(1)} %pad_maximum_fusion.16.q_ref, bf16[256,1024]{1,0:T(8,128)(2,1)S(1)} %pad_maximum_fusion.5.own_ref, bf16[256,1024]{1,0:T(8,128)(2,1)S(1)} %collective-permute-done.19.mate_ref, ...), custom_call_target="tpu_custom_call" | custom-call | flops 2147483648 | bytes 4194304 | tf_op jit(solution)/shard_map/attend/pallas_call | solution.py:118
  223.8 7.0 %attend.7 = (bf16[256,512]{1,0:T(8,128)(2,1)S(1)}, f32[4,2,256]{2,1,0:T(2,128)S(1)}) custom-call(bf16[256,512]{1,0:T(8,128)(2,1)S(1)} %pad_maximum_fusion.15.q_ref, bf16[256,1024]{1,0:T(8,128)(2,1)S(1)} %pad_maximum_fusion.4.own_ref, bf16[256,1024]{1,0:T(8,128)(2,1)S(1)} %collective-permute-done.23.mate_ref, ...), custom_call_target="tpu_custom_call" | custom-call | flops 2147483648 | bytes 4194304 | tf_op jit(solution)/shard_map/attend/pallas_call | solution.py:118
  233.7 4.9 fusion.36
  238.6 5.0 multiply_convert_fusion
  251.1 9.2 %attend_back.4 = (bf16[256,512]{1,0:T(8,128)(2,1)S(1)}, bf16[256,1024]{1,0:T(8,128)(2,1)S(1)}, bf16[256,1024]{1,0:T(8,128)(2,1)S(1)}, bf16[256,1024]{1,0:T(8,128)(2,1)S(1)}, bf16[256,1024]{1,0:T(8,128)(2,1)S(1)}) custom-call(bf16[256,512]{1,0:T(8,128)(2,1)S(1)} %pad_maximum_fusion.16.q_ref, bf16[256,1024]{1,0:T(8,128)(2,1)S(1)} %pad_maximum_fusion.5.own_ref, ...), custom_call_target="tpu_custom_call" | custom-call | flops 5368709120 | bytes 4194304 | tf_op jit(solution)/shard_map/attend_back/pallas_call | solution.py:137
  270.2 9.0 %attend_back.5 = (bf16[256,512]{1,0:T(8,128)(2,1)S(1)}, bf16[256,1024]{1,0:T(8,128)(2,1)S(1)}, bf16[256,1024]{1,0:T(8,128)(2,1)S(1)}, bf16[256,1024]{1,0:T(8,128)(2,1)S(1)}, bf16[256,1024]{1,0:T(8,128)(2,1)S(1)}) custom-call(bf16[256,512]{1,0:T(8,128)(2,1)S(1)} %pad_maximum_fusion.15.q_ref, bf16[256,1024]{1,0:T(8,128)(2,1)S(1)} %pad_maximum_fusion.4.own_ref, ...), custom_call_target="tpu_custom_call" | custom-call | flops 5368709120 | bytes 4194304 | tf_op jit(solution)/shard_map/attend_back/pallas_call | solution.py:137
  285.8 11.0 %collective-permute-done.31 = bf16[256,1024]{1,0:T(8,128)(2,1)S(1)} collective-permute-done((bf16[256,1024]{1,0:T(8,128)(2,1)S(1)}, bf16[256,1024]{1,0:T(8,128)(2,1)S(1)}, u32[]{:S(2)}, u32[]{:S(2)}) %collective-permute-start.31) | collective-permute-done | bytes 524320 | tf_op jit(solution)/shard_map/ppermute | solution.py:36
  303.3 12.6 %collective-permute-done.32 = bf16[256,1024]{1,0:T(8,128)(2,1)} collective-permute-done((bf16[256,1024]{1,0:T(8,128)(2,1)}, bf16[256,1024]{1,0:T(8,128)(2,1)}, u32[]{:S(2)}, u32[]{:S(2)}) %collective-permute-start.32) | collective-permute-done | bytes 524320 | tf_op jit(solution)/shard_map/ppermute | solution.py:726
  358.5 9.6 %attend_back.6 = (bf16[256,512]{1,0:T(8,128)(2,1)S(1)}, bf16[256,1024]{1,0:T(8,128)(2,1)S(1)}, bf16[256,1024]{1,0:T(8,128)(2,1)}, bf16[256,1024]{1,0:T(8,128)(2,1)S(1)}, bf16[256,1024]{1,0:T(8,128)(2,1)S(1)}) custom-call(bf16[256,512]{1,0:T(8,128)(2,1)S(1)} %pad_maximum_fusion.16.q_ref, bf16[256,1024]{1,0:T(8,128)(2,1)S(1)} %copy-done.29, ...), custom_call_target="tpu_custom_call" | custom-call | flops 5368709120 | bytes 4194304 | tf_op jit(solution)/shard_map/attend_back/pallas_call | solution.py:137
  375.9 5.8 %collective-permute-start.37 = (bf16[256,1024]{1,0:T(8,128)(2,1)}, bf16[256,1024]{1,0:T(8,128)(2,1)}, u32[]{:S(2)}, u32[]{:S(2)}) collective-permute-start(bf16[256,1024]{1,0:T(8,128)(2,1)} %get-tuple-element.192), channel_id=1, source_target_pairs={{0,0},{1,8},{8,1},{9,9},{2,2},{3,10},{10,3},{11,11},{4,4},{5,12},{... | collective-permute-start | bytes 1572872 | tf_op jit(solution)/shard_map/ppermute | solution.py:323
  381.7 7.1 %collective-permute-done.37 = bf16[256,1024]{1,0:T(8,128)(2,1)} collective-permute-done((bf16[256,1024]{1,0:T(8,128)(2,1)}, bf16[256,1024]{1,0:T(8,128)(2,1)}, u32[]{:S(2)}, u32[]{:S(2)}) %collective-permute-start.37) | collective-permute-done | bytes 524320 | tf_op jit(solution)/shard_map/ppermute | solution.py:323
  398.2 9.0 %attend_back.7 = (bf16[256,512]{1,0:T(8,128)(2,1)S(1)}, bf16[256,1024]{1,0:T(8,128)(2,1)S(1)}, bf16[256,1024]{1,0:T(8,128)(2,1)S(1)}, bf16[256,1024]{1,0:T(8,128)(2,1)S(1)}, bf16[256,1024]{1,0:T(8,128)(2,1)S(1)}) custom-call(bf16[256,512]{1,0:T(8,128)(2,1)S(1)} %copy-done.35, bf16[256,1024]{1,0:T(8,128)(2,1)S(1)} %copy-done.27, ...), custom_call_target="tpu_custom_call" | custom-call | flops 5368709120 | bytes 4194304 | tf_op jit(solution)/shard_map/attend_back/pallas_call | solution.py:137
  416.5 8.8 %collective-permute-done.44 = bf16[256,1024]{1,0:T(8,128)(2,1)S(1)} collective-permute-done((bf16[256,1024]{1,0:T(8,128)(2,1)S(1)}, bf16[256,1024]{1,0:T(8,128)(2,1)S(1)}, u32[]{:S(2)}, u32[]{:S(2)}) %collective-permute-start.44) | collective-permute-done | bytes 524320 | tf_op jit(solution)/shard_map/ppermute | solution.py:36
  474.7 4.9 collective-permute-done.52
  480.7 16.4 %collective-permute-done.53 = bf16[4,64,128]{2,1,0:T(8,128)(2,1)S(1)} collective-permute-done((bf16[4,64,128]{2,1,0:T(8,128)(2,1)}, bf16[4,64,128]{2,1,0:T(8,128)(2,1)S(1)}, u32[]{:S(2)}, u32[]{:S(2)}) %collective-permute-start.53) | collective-permute-done | bytes 65568 | tf_op jit(solution)/shard_map/ppermute | solution.py:417
  497.1 7.1 %collective-permute-done.54 = bf16[4,64,128]{2,1,0:T(8,128)(2,1)S(1)} collective-permute-done((bf16[4,64,128]{2,1,0:T(8,128)(2,1)}, bf16[4,64,128]{2,1,0:T(8,128)(2,1)S(1)}, u32[]{:S(2)}, u32[]{:S(2)}) %collective-permute-start.54) | collective-permute-done | bytes 65568 | tf_op jit(solution)/shard_map/ppermute | solution.py:417
  504.2 6.6 %collective-permute-start.61 = (bf16[256,1024]{1,0:T(8,128)(2,1)}, bf16[256,1024]{1,0:T(8,128)(2,1)}, u32[]{:S(2)}, u32[]{:S(2)}) collective-permute-start(bf16[256,1024]{1,0:T(8,128)(2,1)} %fusion.125), channel_id=1, source_target_pairs={{0,0},{1,8},{8,1},{9,9},{2,2},{3,10},{10,3},{11,11},{4,4},{5,12},{... | collective-permute-start | bytes 1572872 | tf_op jit(solution)/shard_map/ppermute | solution.py:323
  513.7 5.8 %collective-permute-done.61 = bf16[256,1024]{1,0:T(8,128)(2,1)} collective-permute-done((bf16[256,1024]{1,0:T(8,128)(2,1)}, bf16[256,1024]{1,0:T(8,128)(2,1)}, u32[]{:S(2)}, u32[]{:S(2)}) %collective-permute-start.61) | collective-permute-done | bytes 524320 | tf_op jit(solution)/shard_map/ppermute | solution.py:323
  543.2 8.8 %collective-permute-start.63 = (bf16[64,2176]{1,0:T(8,128)(2,1)S(1)}, bf16[64,2176]{1,0:T(8,128)(2,1)S(1)}, u32[]{:S(2)}, u32[]{:S(2)}) collective-permute-start(bf16[64,2176]{1,0:T(8,128)(2,1)S(1)} %add_convert_fusion.14.mine_ref), channel_id=1, source_target_pairs={{0,1},{1,0},{2,3},{3,2},{4,5},{5,4},{6,7},{7,6},{8,9},{9,8},{10,11... | collective-permute-start | bytes 835592 | tf_op jit(solution)/shard_map/ppermute | solution.py:36
  553.8 5.5 collective-permute-start.65
  (597 shorter events, 287.3 us)
Async XLA Ops:
  7.2 39.0 %all-gather.3.cloned.1.call-start = ((), (), s32[]{:S(2)}) async-start(), calls=%async_computation.7 | async-start | bytes 2621440 | tf_op jit(solution)/shard_map/all_gather | solution.py:647
  19.8 17.6 %all-to-all-start = ((bf16[4,64,1024]{2,1,0:T(8,128)(2,1)}), bf16[4,64,1024]{2,1,0:T(8,128)(2,1)S(1)}, u32[]{:S(2)}, u32[]{:S(2)}) async-start(bf16[4,64,1024]{2,1,0:T(8,128)(2,1)} %param.13), calls=%async_computation | async-start | bytes 1048576 | tf_op jit(solution)/shard_map/all_to_all | solution.py:318
  23.3 122.3 %all-gather.5.cloned.1.call-start = ((), (), s32[]{:S(2)}) async-start(), calls=%async_computation.8 | async-start | bytes 10485760 | tf_op jit(solution)/shard_map/all_gather | solution.py:658
  46.3 26.8 %collective-permute-start.3 = (bf16[4,64,2176]{2,1,0:T(8,128)(2,1)S(1)}, bf16[4,64,2176]{2,1,0:T(8,128)(2,1)S(1)}, u32[]{:S(2)}, u32[]{:S(2)}) collective-permute-start(bf16[4,64,2176]{2,1,0:T(8,128)(2,1)S(1)} %ring_place.2.refs_0_), channel_id=1, source_target_pairs={{0,4},{4,8},{8,12},{12,0},{1,5},{5,9},{9,13},{13,1},{2,6},{6,10},{... | collective-permute-start | bytes 3342344 | tf_op jit(solution)/shard_map/ppermute | solution.py:341
  46.6 26.5 %collective-permute-start.4 = (bf16[4,64,2176]{2,1,0:T(8,128)(2,1)S(1)}, bf16[4,64,2176]{2,1,0:T(8,128)(2,1)S(1)}, u32[]{:S(2)}, u32[]{:S(2)}) collective-permute-start(bf16[4,64,2176]{2,1,0:T(8,128)(2,1)S(1)} %ring_place.2.refs_0_), channel_id=1, source_target_pairs={{0,12},{4,0},{8,4},{12,8},{1,13},{5,1},{9,5},{13,9},{2,14},{6,2},{... | collective-permute-start | bytes 3342344 | tf_op jit(solution)/shard_map/ppermute | solution.py:341
  75.0 22.3 %collective-permute-start.5 = (bf16[2,64,2176]{2,1,0:T(8,128)(2,1)}, bf16[2,64,2176]{2,1,0:T(8,128)(2,1)S(1)}, u32[]{:S(2)}, u32[]{:S(2)}) collective-permute-start(bf16[2,64,2176]{2,1,0:T(8,128)(2,1)} %slice.445), channel_id=1, source_target_pairs={{0,4},{4,8},{8,12},{12,0},{1,5},{5,9},{9,13},{13,1},{2,6},{6,10},{... | collective-permute-start | bytes 1671176 | tf_op jit(solution)/shard_map/ppermute | solution.py:347
  75.8 22.3 %collective-permute-start.6 = (bf16[2,64,2176]{2,1,0:T(8,128)(2,1)}, bf16[2,64,2176]{2,1,0:T(8,128)(2,1)S(1)}, u32[]{:S(2)}, u32[]{:S(2)}) collective-permute-start(bf16[2,64,2176]{2,1,0:T(8,128)(2,1)} %slice.446), channel_id=1, source_target_pairs={{0,12},{4,0},{8,4},{12,8},{1,13},{5,1},{9,5},{13,9},{2,14},{6,2},{... | collective-permute-start | bytes 1671176 | tf_op jit(solution)/shard_map/ppermute | solution.py:348
  78.5 18.8 %collective-permute-start.7 = (bf16[256,1024]{1,0:T(8,128)(2,1)}, bf16[256,1024]{1,0:T(8,128)(2,1)S(1)}, u32[]{:S(2)}, u32[]{:S(2)}) collective-permute-start(bf16[256,1024]{1,0:T(8,128)(2,1)} %bitcast.234), channel_id=1, source_target_pairs={{0,0},{1,8},{8,1},{9,9},{2,2},{3,10},{10,3},{11,11},{4,4},{5,12},{... | collective-permute-start | bytes 1572872 | tf_op jit(solution)/shard_map/ppermute | solution.py:323
  105.7 22.6 %collective-permute-start.8 = (bf16[1024,512]{1,0:T(8,128)(2,1)S(1)}, bf16[1024,512]{1,0:T(8,128)(2,1)S(1)}, u32[]{:S(2)}, u32[]{:S(2)}) collective-permute-start(bf16[1024,512]{1,0:T(8,128)(2,1)S(1)} %bitcast.219), channel_id=1, source_target_pairs={{0,1},{1,0},{2,3},{3,2},{4,5},{5,4},{6,7},{7,6},{8,9},{9,8},{10,11... | collective-permute-start | bytes 3145736 | tf_op jit(solution)/shard_map/ppermute | solution.py:36
  115.7 15.0 %collective-permute-start.10 = (bf16[256,1024]{1,0:T(8,128)(2,1)S(1)}, bf16[256,1024]{1,0:T(8,128)(2,1)S(1)}, u32[]{:S(2)}, u32[]{:S(2)}) collective-permute-start(bf16[256,1024]{1,0:T(8,128)(2,1)S(1)} %pad_maximum_fusion.2.own_ref), channel_id=1, source_target_pairs={{0,1},{1,0},{2,3},{3,2},{4,5},{5,4},{6,7},{7,6},{8,9},{9,8},{10,11... | collective-permute-start | bytes 1572872 | tf_op jit(solution)/shard_map/ppermute | solution.py:36
  145.6 15.1 %collective-permute-start.17 = (bf16[1024,4096]{1,0:T(8,128)(2,1)}, bf16[1024,4096]{1,0:T(8,128)(2,1)}, u32[]{:S(2)}, u32[]{:S(2)}) collective-permute-start(bf16[1024,4096]{1,0:T(8,128)(2,1)} %all-gather.5.cloned.1.call-done), channel_id=1, source_target_pairs={{0,1},{1,0},{2,3},{3,2},{4,5},{5,4},{6,7},{7,6},{8,9},{9,8},{10,11... | collective-permute-start | bytes 25165832 | tf_op jit(solution)/shard_map/ppermute | solution.py:36
  169.2 20.7 %collective-permute-start.18 = (bf16[256,1024]{1,0:T(8,128)(2,1)S(1)}, bf16[256,1024]{1,0:T(8,128)(2,1)S(1)}, u32[]{:S(2)}, u32[]{:S(2)}) collective-permute-start(bf16[256,1024]{1,0:T(8,128)(2,1)S(1)} %fusion.90), channel_id=1, source_target_pairs={{0,64},{1,65},{2,66},{3,67},{4,68},{5,69},{6,70},{7,71},{8,72},{9,... | collective-permute-start | bytes 1572872 | tf_op jit(solution)/shard_map/ppermute | solution.py:719
  176.2 284.4 %reduce-scatter.6.cloned.1.call-start = ((), (), s32[]{:S(2)}) async-start(), calls=%async_computation.10 | async-start | bytes 5242880 | tf_op jit(solution)/shard_map/reduce_scatter | solution.py:537
  195.1 18.9 %collective-permute-start.19 = (bf16[256,1024]{1,0:T(8,128)(2,1)S(1)}, bf16[256,1024]{1,0:T(8,128)(2,1)S(1)}, u32[]{:S(2)}, u32[]{:S(2)}) collective-permute-start(bf16[256,1024]{1,0:T(8,128)(2,1)S(1)} %pad_maximum_fusion.5.own_ref), channel_id=1, source_target_pairs={{0,1},{1,0},{2,3},{3,2},{4,5},{5,4},{6,7},{7,6},{8,9},{9,8},{10,11... | collective-permute-start | bytes 1572872 | tf_op jit(solution)/shard_map/ppermute | solution.py:36
  260.8 22.3 %collective-permute-start.28 = (bf16[256,1024]{1,0:T(8,128)(2,1)S(1)}, bf16[256,1024]{1,0:T(8,128)(2,1)S(1)}, u32[]{:S(2)}, u32[]{:S(2)}) collective-permute-start(bf16[256,1024]{1,0:T(8,128)(2,1)S(1)} %get-tuple-element.173), channel_id=1, source_target_pairs={{0,1},{1,0},{2,3},{3,2},{4,5},{5,4},{6,7},{7,6},{8,9},{9,8},{10,11... | collective-permute-start | bytes 1572872 | tf_op jit(solution)/shard_map/ppermute | solution.py:36
  321.4 20.5 %collective-permute-start.33 = (bf16[1024,2048]{1,0:T(8,128)(2,1)S(1)}, bf16[1024,2048]{1,0:T(8,128)(2,1)S(1)}, u32[]{:S(2)}, u32[]{:S(2)}) collective-permute-start(bf16[1024,2048]{1,0:T(8,128)(2,1)S(1)} %outer.9), channel_id=1, source_target_pairs={{0,1},{1,0},{2,3},{3,2},{4,5},{5,4},{6,7},{7,6},{8,9},{9,8},{10,11... | collective-permute-start | bytes 12582920 | tf_op jit(solution)/shard_map/ppermute | solution.py:36
  346.8 113.8 %reduce-scatter.4.cloned.1.call-start = ((), (), s32[]{:S(2)}) async-start(), calls=%async_computation.9 | async-start | bytes 5242880 | tf_op jit(solution)/shard_map/reduce_scatter | solution.py:562
  388.8 20.8 %all-to-all-start.2 = ((bf16[4,64,1024]{2,1,0:T(8,128)(2,1)}), bf16[4,64,1024]{2,1,0:T(8,128)(2,1)}, u32[]{:S(2)}, u32[]{:S(2)}) async-start(bf16[4,64,1024]{2,1,0:T(8,128)(2,1)} %bitcast.38), calls=%async_computation.2 | async-start | bytes 1048576 | tf_op jit(solution)/shard_map/all_to_all | solution.py:329
  392.9 145.9 %reduce-scatter.8.cloned.1.call-start = ((), (), s32[]{:S(2)}) async-start(), calls=%async_computation.11 | async-start | bytes 2621440 | tf_op jit(solution)/shard_map/reduce_scatter | solution.py:749
  393.0 16.6 %collective-permute-start.36 = (bf16[256,1024]{1,0:T(8,128)(2,1)}, bf16[256,1024]{1,0:T(8,128)(2,1)}, u32[]{:S(2)}, u32[]{:S(2)}) collective-permute-start(bf16[256,1024]{1,0:T(8,128)(2,1)} %add_convert_fusion.6), channel_id=1, source_target_pairs={{0,4},{4,0},{1,5},{5,1},{2,6},{6,2},{3,7},{7,3},{8,12},{12,8},{9,1... | collective-permute-start | bytes 1572872 | tf_op jit(solution)/shard_map/ppermute | solution.py:36
  395.1 19.9 %collective-permute-start.41 = (bf16[256,1024]{1,0:T(8,128)(2,1)}, bf16[256,1024]{1,0:T(8,128)(2,1)}, u32[]{:S(2)}, u32[]{:S(2)}) collective-permute-start(bf16[256,1024]{1,0:T(8,128)(2,1)} %get-tuple-element.197), channel_id=1, source_target_pairs={{0,1},{1,0},{2,3},{3,2},{4,5},{5,4},{6,7},{7,6},{8,9},{9,8},{10,11... | collective-permute-start | bytes 1572872 | tf_op jit(solution)/shard_map/ppermute | solution.py:36
  414.2 26.3 %collective-permute-start.38 = (bf16[1024,1024]{1,0:T(8,128)(2,1)S(1)}, bf16[1024,1024]{1,0:T(8,128)(2,1)}, u32[]{:S(2)}, u32[]{:S(2)}) collective-permute-start(bf16[1024,1024]{1,0:T(8,128)(2,1)S(1)} %outer.12), channel_id=1, source_target_pairs={{0,1},{1,0},{2,3},{3,2},{4,5},{5,4},{6,7},{7,6},{8,9},{9,8},{10,11... | collective-permute-start | bytes 6291464 | tf_op jit(solution)/shard_map/ppermute | solution.py:36
  428.7 19.3 %collective-permute-start.45 = (bf16[1024,1024]{1,0:T(8,128)(2,1)}, bf16[1024,1024]{1,0:T(8,128)(2,1)}, u32[]{:S(2)}, u32[]{:S(2)}) collective-permute-start(bf16[1024,1024]{1,0:T(8,128)(2,1)} %outer.14), channel_id=1, source_target_pairs={{0,1},{1,0},{2,3},{3,2},{4,5},{5,4},{6,7},{7,6},{8,9},{9,8},{10,11... | collective-permute-start | bytes 6291464 | tf_op jit(solution)/shard_map/ppermute | solution.py:36
  465.9 45.0 %collective-permute-start.51 = (bf16[4,64,1024]{2,1,0:T(8,128)(2,1)}, bf16[4,64,1024]{2,1,0:T(8,128)(2,1)}, u32[]{:S(2)}, u32[]{:S(2)}) collective-permute-start(bf16[4,64,1024]{2,1,0:T(8,128)(2,1)} %pad_maximum_fusion.11), channel_id=1, source_target_pairs={{0,48},{16,0},{32,16},{48,32},{1,49},{17,1},{33,17},{49,33},{2,50}... | collective-permute-start | bytes 1572872 | tf_op jit(solution)/shard_map/ppermute | solution.py:407
  469.2 41.7 %collective-permute-start.50 = (bf16[4,64,1024]{2,1,0:T(8,128)(2,1)}, bf16[4,64,1024]{2,1,0:T(8,128)(2,1)}, u32[]{:S(2)}, u32[]{:S(2)}) collective-permute-start(bf16[4,64,1024]{2,1,0:T(8,128)(2,1)} %pad_maximum_fusion.10), channel_id=1, source_target_pairs={{0,16},{16,32},{32,48},{48,0},{1,17},{17,33},{33,49},{49,1},{2,18}... | collective-permute-start | bytes 1572872 | tf_op jit(solution)/shard_map/ppermute | solution.py:407
  471.3 39.6 %collective-permute-start.49 = (bf16[4,64,1024]{2,1,0:T(8,128)(2,1)}, bf16[4,64,1024]{2,1,0:T(8,128)(2,1)}, u32[]{:S(2)}, u32[]{:S(2)}) collective-permute-start(bf16[4,64,1024]{2,1,0:T(8,128)(2,1)} %pad_maximum_fusion.9), channel_id=1, source_target_pairs={{0,12},{4,0},{8,4},{12,8},{1,13},{5,1},{9,5},{13,9},{2,14},{6,2},{... | collective-permute-start | bytes 1572872 | tf_op jit(solution)/shard_map/ppermute | solution.py:407
  473.6 37.3 %collective-permute-start.48 = (bf16[4,64,1024]{2,1,0:T(8,128)(2,1)S(1)}, bf16[4,64,1024]{2,1,0:T(8,128)(2,1)}, u32[]{:S(2)}, u32[]{:S(2)}) collective-permute-start(bf16[4,64,1024]{2,1,0:T(8,128)(2,1)S(1)} %pad_maximum_fusion.8), channel_id=1, source_target_pairs={{0,4},{4,8},{8,12},{12,0},{1,5},{5,9},{9,13},{13,1},{2,6},{6,10},{... | collective-permute-start | bytes 1572872 | tf_op jit(solution)/shard_map/ppermute | solution.py:407
  479.6 17.5 %collective-permute-start.53 = (bf16[4,64,128]{2,1,0:T(8,128)(2,1)}, bf16[4,64,128]{2,1,0:T(8,128)(2,1)S(1)}, u32[]{:S(2)}, u32[]{:S(2)}) collective-permute-start(bf16[4,64,128]{2,1,0:T(8,128)(2,1)} %get-tuple-element.333), channel_id=1, source_target_pairs={{0,12},{4,0},{8,4},{12,8},{1,13},{5,1},{9,5},{13,9},{2,14},{6,2},{... | collective-permute-start | bytes 196616 | tf_op jit(solution)/shard_map/ppermute | solution.py:417
  504.2 15.3 %collective-permute-start.61 = (bf16[256,1024]{1,0:T(8,128)(2,1)}, bf16[256,1024]{1,0:T(8,128)(2,1)}, u32[]{:S(2)}, u32[]{:S(2)}) collective-permute-start(bf16[256,1024]{1,0:T(8,128)(2,1)} %fusion.125), channel_id=1, source_target_pairs={{0,0},{1,8},{8,1},{9,9},{2,2},{3,10},{10,3},{11,11},{4,4},{5,12},{... | collective-permute-start | bytes 1572872 | tf_op jit(solution)/shard_map/ppermute | solution.py:323
  512.4 17.3 %collective-permute-start.58 = (bf16[64,1024]{1,0:T(8,128)(2,1)S(1)}, bf16[64,1024]{1,0:T(8,128)(2,1)S(1)}, u32[]{:S(2)}, u32[]{:S(2)}) collective-permute-start(bf16[64,1024]{1,0:T(8,128)(2,1)S(1)} %get-tuple-element.290), channel_id=1, source_target_pairs={{0,4},{4,8},{8,12},{12,0},{1,5},{5,9},{9,13},{13,1},{2,6},{6,10},{... | collective-permute-start | bytes 393224 | tf_op jit(solution)/shard_map/ppermute | solution.py:417
  519.5 16.4 %all-to-all-start.3 = ((bf16[4,64,1024]{2,1,0:T(8,128)(2,1)}), bf16[4,64,1024]{2,1,0:T(8,128)(2,1)S(1)}, u32[]{:S(2)}, u32[]{:S(2)}) async-start(bf16[4,64,1024]{2,1,0:T(8,128)(2,1)} %bitcast.84), calls=%async_computation.5 | async-start | bytes 1048576 | tf_op jit(solution)/shard_map/all_to_all | solution.py:329
  543.2 16.1 %collective-permute-start.63 = (bf16[64,2176]{1,0:T(8,128)(2,1)S(1)}, bf16[64,2176]{1,0:T(8,128)(2,1)S(1)}, u32[]{:S(2)}, u32[]{:S(2)}) collective-permute-start(bf16[64,2176]{1,0:T(8,128)(2,1)S(1)} %add_convert_fusion.14.mine_ref), channel_id=1, source_target_pairs={{0,1},{1,0},{2,3},{3,2},{4,5},{5,4},{6,7},{7,6},{8,9},{9,8},{10,11... | collective-permute-start | bytes 835592 | tf_op jit(solution)/shard_map/ppermute | solution.py:36
  (151 other events, 1588.8 us)
Sparse Core Ops, SparseCore 0:
  12.0 34.0 all-gather.2
  47.8 83.3 all-gather.4
  347.0 47.8 reduce-scatter.5
  397.3 47.2 reduce-scatter.3
  463.9 45.4 reduce-scatter.7

commit v8 on v7

--- a/solution.py
+++ b/solution.py
@@ -313,20 +313,16 @@
 FLIP = [(0, 0), (1, 2), (2, 1), (3, 3)]
 
 
-def to_images(tokens):
-    count, rows, width = tokens.shape
-    mixed = lax.all_to_all(tokens, "z", split_axis=0, concat_axis=0, tiled=True)
-    return mixed.reshape(count * rows, width)
-
-
 def flip(tokens):
     return lax.ppermute(tokens, ("yh", "core"), FLIP)
 
 
-def from_images(tokens, count):
-    rows, width = tokens.shape
-    mixed = flip(tokens).reshape(count, rows // count, width)
-    return lax.all_to_all(mixed, "z", split_axis=0, concat_axis=0, tiled=True)
+def trade(tokens):
+    return lax.all_to_all(tokens, "z", split_axis=0, concat_axis=0, tiled=True)
+
+
+def as_image(tokens):
+    return tokens.reshape(-1, tokens.shape[-1])
 
 
 RING_Z, RING_Y = "z", ("yh", "yl")
@@ -390,7 +386,7 @@
     ]
 
 
-def ring_sums(items, beside):
+def ring_sums(items, beside, tokens):
     blocks = [ring_blocks(*item) for item in items]
     hops = []
     for (_, axis, _), (_, _, far, _) in zip(items, blocks):
@@ -398,15 +394,15 @@
         hops.append(
             (lax.ppermute(far[:half], axis, AHEAD), lax.ppermute(far[half:], axis, BACK))
         )
-    hops, beside = lax.optimization_barrier((hops, beside))
+    hops, beside, tokens = lax.optimization_barrier((hops, beside, tokens))
     ends = []
     for (_, axis, _), (own, after, _, before), (low, high) in zip(items, blocks, hops):
         half = low.shape[0]
         after = jnp.concatenate([add(after[:half], low), after[half:]])
         before = jnp.concatenate([before[:half], add(before[half:], high)])
         ends.append((own, lax.ppermute(after, axis, AHEAD), lax.ppermute(before, axis, BACK)))
-    ends = lax.optimization_barrier(ends)
-    return [add(*e) for e in ends], beside
+    ends, traded = lax.optimization_barrier((ends, trade(tokens)))
+    return [add(*e) for e in ends], beside, traded
 
 
 def direct_sums(items, beside=None):
@@ -520,7 +516,7 @@
     return result, kept
 
 
-def backward(grad_out, kept, w, last=False, beside=None):
+def backward(grad_out, kept, w, last=False, result=None):
     grad_branch_two = (w["scale"][1] * grad_out).astype(bf16)
     grad_before = []
     grad_normed_two = 0.0
@@ -566,11 +562,17 @@
             came = swap(sent, "yl")
         parts = attend_back(kept["queries"][i], kept["blocks"][i], g, kept["log_total"][i])
         if ready is not None:
-            parts, came, beside = lax.optimization_barrier((parts, came, beside))
+            parts, came = lax.optimization_barrier((parts, came))
             kv_chunks.append((own + came.astype(f32)).astype(bf16))
         q_chunks.append(parts[0])
         ready = group_parts(*parts[1:])
-    kv_chunks.append((ready[0] + swap(ready[1], "yl").astype(f32)).astype(bf16))
+    own, sent = ready
+    traded = None
+    if result is not None:
+        sent, result = lax.optimization_barrier((sent, result))
+        traded = trade(result)
+    came, traded = lax.optimization_barrier((swap(sent, "yl"), traded))
+    kv_chunks.append((own + came.astype(f32)).astype(bf16))
     grad_q, grad_kv = unchunked(q_chunks), unchunked(kv_chunks)
     grad_normed_one = sum(
         mm_t(g, part) for g, part in zip(grad_q + grad_kv, w["q"] + w["kv"])
@@ -592,7 +594,7 @@
         kv=(kept["normed_one"], grad_kv),
         proj=(kept["attended"], grad_halves),
         fc=fc_grad,
-        beside=beside,
+        traded=traded,
     )
     return grad_inputs.astype(bf16), vectors, products
 
@@ -653,14 +655,12 @@
     live_grad = out_grad * live[:, None, None]
     hops = (*first_hop(mine, RING_Z), lax.ppermute(mine, RING_Z, ACROSS))
     hops, fc_row, live_grad, first_tokens = lax.optimization_barrier(
-        (hops, fc_row, live_grad, to_images(patch_tokens))
+        (hops, fc_row, live_grad, as_image(trade(flip(patch_tokens))))
     )
     fc_half = lax.all_gather(fc_row, RING_Z, axis=0, tiled=True)
     row = ring_place(mine, RING_Z, hops, [(4, *mine.shape)], in_order)[0]
     hops = lax.optimization_barrier(first_hop(row, RING_Y))
-    more, first_tokens = lax.optimization_barrier(
-        (second_hop(*hops, RING_Y), flip(first_tokens))
-    )
+    more = lax.optimization_barrier(second_hop(*hops, RING_Y))
 
     def views(outs, piece, place, start):
         for i in range(piece.shape[0]):
@@ -717,16 +717,18 @@
     sent, _ = forward(first_tokens, w, late=(fc_half, fc_weights))
     sent, live_grad = lax.optimization_barrier((sent, live_grad))
     passed = lax.ppermute(sent, "section", [(0, 1)])
-    last_grad = flip(to_images(live_grad))
+    last_grad = as_image(flip(trade(live_grad)))
     tokens = jnp.where(section == 0, first_tokens, passed)
     result, kept = forward(tokens, w)
 
-    sent, _, _ = backward(last_grad.astype(f32), kept, w)
-    sent, result = lax.optimization_barrier((sent, result))
-    passed = lax.ppermute(sent, "section", [(1, 0)])
-    block_out = from_images(result, images)
+    slots = (images, result.shape[0] // images, width)
+    sent, _, early = backward(last_grad.astype(f32), kept, w, result=result.reshape(slots))
+    sent, traded = lax.optimization_barrier((sent, early["traded"]))
+    passed, block_out = lax.optimization_barrier(
+        (lax.ppermute(sent, "section", [(1, 0)]), flip(traded))
+    )
     grad_out = jnp.where(section == 1, last_grad, passed).astype(f32)
-    grad_inputs, sums, products = backward(grad_out, kept, w, True, block_out)
+    grad_inputs, sums, products = backward(grad_out, kept, w, last=True)
 
     vector_grads = vector_block(core, sums, width, PAIR)
 
@@ -737,24 +739,17 @@
         [((a1, 0), dq[i], width), ((o, 0), e1[i], width)], half // 2, add=add
     )
     make_b = lambda i, add=None: outer([((a1, 0), dkv[i], width)], half // 2, add=add)
-    a_full, b_full = (
-        make(0, swap(make(1), "core")).reshape(4, 4, own, width) for make in (make_a, make_b)
-    )
-    (a_sum, b_sum), (rows, vector_grads, grad_inputs) = ring_sums(
-        [(a_full, RING_Y, 1), (b_full, RING_Z, 0)],
-        (products["fc"], vector_grads, grad_inputs),
-    )
-    in_grad = from_images(grad_inputs, images)
-    block_out = products["beside"]
+    a_full, b_full = (make(0, swap(make(1), "core")) for make in (make_a, make_b))
+    a_full = jnp.concatenate([a_full, vector_grads], axis=1).reshape(4, 4, own, width + PAIR)
+    (a_sum, b_sum), rows, traded = ring_sums(
+        [(a_full, RING_Y, 1), (b_full.reshape(4, 4, own, width), RING_Z, 0)],
+        products["fc"],
+        grad_inputs.reshape(slots),
+    )
     fc_grad = lax.psum_scatter(
         jnp.concatenate(rows, axis=1), RING_Y, scatter_dimension=0, tiled=True
     )
-    vector_grads = vector_grads.reshape(4, 4, own, PAIR)
-    (vector_sum,), _ = direct_sums([(vector_grads, RING_Y, 1)])
-    ab, in_grad = direct_sums(
-        [(jnp.concatenate([a_sum, vector_sum], axis=2), RING_Z, 0), (b_sum, RING_Y, 0)],
-        in_grad,
-    )
+    ab, in_grad = direct_sums([(a_sum, RING_Z, 0), (b_sum, RING_Y, 0)], flip(traded))
     ab = jnp.concatenate([ab[0][:, :width], ab[1], ab[0][:, width:]], axis=1)
 
     def chips_sum(a):

time: 587 us -> 548 us (0.934)
  waiting for transfers between devices: 187 us -> 158 us
    ppermute x9 -> x6, waiting for transfers between devices: 33.1 us -> 5.88 us  [direct_sums(): lax.ppermute(block[k], axis, way)]
    ppermute x4, waiting for transfers between devices: 30.2 us -> 5.89 us  [flip(): return lax.ppermute(tokens, ('yh', 'core'), FLIP)]
    ppermute x1, waiting for transfers between devices: 0.01 us -> 10.6 us  [second_hop(): lax.ppermute(back[half:], axis, BACK)]
    all_to_all x4, waiting for transfers between devices: 13.9 us -> 23.8 us  [trade(): return lax.all_to_all(tokens, 'z', split_axis=0, concat_axis=0, tiled=True)]
    ppermute x4, waiting for transfers between devices: 24.5 us -> 32.1 us  [first_hop(): return (lax.ppermute(value, axis, AHEAD), lax.ppermute(value, axis, BACK))]
    ppermute x1, waiting for transfers between devices: 6.87 us -> 0.01 us  [per_device(): hops = (*first_hop(mine, RING_Z), lax.ppermute(mine, RING_Z, ACROSS))]
    unnamed x235 -> x279, local copies, waits for them, and re-layouts: 32 us -> 25.5 us
  transfers between devices with their start and end apart: 75 -> 72, of which waited for: 30 -> 32; matrix products, arithmetic and copies ran while one was open for 16% -> 16% of each run, Pallas kernels for 12% -> 13%
where the time goes in v8:
time: 548 us; the launch traced here: 538 us
  waiting for transfers between devices  158 us (29%)
  starting transfers between devices  110 us (20%)
  Pallas kernels  94.9 us (17%)
  matrix products  77.5 us (14%)
  local copies, waits for them, and re-layouts  43.2 us (8%)
  other arithmetic  37.6 us (7%)
  between operations  17 us (3%)
    dot_general x48, matrix products, dot(): return lax.dot_general(a, b, (dims, ((), ())), preferred_element_type=f32)  77.5 us
    ppermute x36, waiting for transfers between devices, swap(): return lax.ppermute(value, axis, [(0, 1), (1, 0)])  54.7 us
    pallas_call x4, Pallas kernels, attend_back(): pl.pallas_call(attend_back_kernel, grid=(pairs,), in_specs=[q_spec] + kv_...  36.9 us
    ppermute x36, starting transfers between devices, swap(): return lax.ppermute(value, axis, [(0, 1), (1, 0)])  36.3 us
    ppermute x4, waiting for transfers between devices, first_hop(): return (lax.ppermute(value, axis, AHEAD), lax.ppermute(value, axis, BACK))  32.1 us
    pallas_call x4, Pallas kernels, attend(): pl.pallas_call(attend_kernel, grid=(pairs,), in_specs=[q_spec] + kv_specs...  29.4 us
    ppermute x4, starting transfers between devices, flip(): return lax.ppermute(tokens, ('yh', 'core'), FLIP)  25.6 us
    unnamed x279, local copies, waits for them, and re-layouts  25.5 us
  transfers between devices with their start and end apart: 72, of which 32 were waited for; matrix products, arithmetic and copies ran while one was open for 16% of the time, Pallas kernels for 13%

profile of v8, /device:TPU:1, one launch (start us, length us, event | category | flops | bytes accessed | tf_op | source)
XLA Modules:
  0.0 537.6 jit_solution(6032324527658069565)
XLA Ops:
  12.0 6.2 %collective-permute-start.3 = (bf16[4,64,1024]{2,1,0:T(8,128)(2,1)S(1)}, bf16[4,64,1024]{2,1,0:T(8,128)(2,1)}, u32[]{:S(2)}, u32[]{:S(2)}) collective-permute-start(bf16[4,64,1024]{2,1,0:T(8,128)(2,1)S(1)} %copy-done.121), channel_id=1, source_target_pairs={{0,0},{1,8},{8,1},{9,9},{2,2},{3,10},{10,3},{11,11},{4,4},{5,12},{... | collective-permute-start | bytes 1572872 | tf_op jit(solution)/shard_map/ppermute | solution.py:317
  25.4 4.8 all-to-all-start
  31.1 6.7 %collective-permute-done.1.refs_2_ = bf16[64,2176]{1,0:T(8,128)(2,1)S(1)} collective-permute-done((bf16[64,2176]{1,0:T(8,128)(2,1)S(1)}, bf16[64,2176]{1,0:T(8,128)(2,1)S(1)}, u32[]{:S(2)}, u32[]{:S(2)}) %collective-permute-start.1) | collective-permute-done | bytes 278560 | tf_op jit(solution)/shard_map/ppermute | solution.py:337
  40.2 6.1 %all-gather.3.cloned.1.call-done = bf16[256,4096]{1,0:T(8,128)(2,1)} async-done(((bf16[64,4096]{1,0:T(8,128)(2,1)}), bf16[256,4096]{1,0:T(8,128)(2,1)}) %all-gather.3.cloned.1.call-update) | async-done | bytes 2097168 | tf_op jit(solution)/shard_map/all_gather | solution.py:649
  48.0 23.9 %collective-permute-done.5.refs_2_ = bf16[4,64,2176]{2,1,0:T(8,128)(2,1)S(1)} collective-permute-done((bf16[4,64,2176]{2,1,0:T(8,128)(2,1)S(1)}, bf16[4,64,2176]{2,1,0:T(8,128)(2,1)S(1)}, u32[]{:S(2)}, u32[]{:S(2)}) %collective-permute-start.5) | collective-permute-done | bytes 1114144 | tf_op jit(solution)/shard_map/ppermute | solution.py:337
  76.4 10.6 %collective-permute-done.7.refs_4_ = bf16[2,64,2176]{2,1,0:T(8,128)(2,1)S(1)} collective-permute-done((bf16[2,64,2176]{2,1,0:T(8,128)(2,1)S(1)}, bf16[2,64,2176]{2,1,0:T(8,128)(2,1)S(1)}, u32[]{:S(2)}, u32[]{:S(2)}) %collective-permute-start.7) | collective-permute-done | bytes 557088 | tf_op jit(solution)/shard_map/ppermute | solution.py:344
  104.0 12.2 %collective-permute-done.11.near_ref = bf16[256,1024]{1,0:T(8,128)(2,1)S(1)} collective-permute-done((bf16[256,1024]{1,0:T(8,128)(2,1)S(1)}, bf16[256,1024]{1,0:T(8,128)(2,1)S(1)}, u32[]{:S(2)}, u32[]{:S(2)}) %collective-permute-start.11) | collective-permute-done | bytes 524320 | tf_op jit(solution)/shard_map/ppermute | solution.py:36
  119.3 7.6 %attend.4 = (bf16[256,512]{1,0:T(8,128)(2,1)S(1)}, f32[4,2,256]{2,1,0:T(2,128)}) custom-call(bf16[256,512]{1,0:T(8,128)(2,1)S(1)} %pad_maximum_fusion.14.q_ref, bf16[256,1024]{1,0:T(8,128)(2,1)S(1)} %pad_maximum_fusion.5.own_ref, bf16[256,1024]{1,0:T(8,128)(2,1)S(1)} %collective-permute-done.10.mate_ref, ...), custom_call_target="tpu_custom_call" | custom-call | flops 2147483648 | bytes 4194304 | tf_op jit(solution)/shard_map/attend/pallas_call | solution.py:118
  126.9 4.7 collective-permute-done.13.near_ref
  136.9 7.6 %attend.5 = (bf16[256,512]{1,0:T(8,128)(2,1)S(1)}, f32[4,2,256]{2,1,0:T(2,128)}) custom-call(bf16[256,512]{1,0:T(8,128)(2,1)S(1)} %pad_maximum_fusion.15.q_ref, bf16[256,1024]{1,0:T(8,128)(2,1)S(1)} %pad_maximum_fusion.6.own_ref, bf16[256,1024]{1,0:T(8,128)(2,1)S(1)} %collective-permute-done.14.mate_ref, ...), custom_call_target="tpu_custom_call" | custom-call | flops 2147483648 | bytes 4194304 | tf_op jit(solution)/shard_map/attend/pallas_call | solution.py:118
  162.9 4.1 all-to-all-start.1
  167.0 8.7 %all-to-all-done.1 = bf16[4,64,1024]{2,1,0:T(8,128)(2,1)} async-done(((bf16[4,64,1024]{2,1,0:T(8,128)(2,1)}), bf16[4,64,1024]{2,1,0:T(8,128)(2,1)}, u32[]{:S(2)}, u32[]{:S(2)}) %all-to-all-start.1) | async-done | bytes 524320 | tf_op jit(solution)/shard_map/all_to_all | solution.py:321
  185.8 5.7 %collective-permute-done.18 = bf16[4,64,1024]{2,1,0:T(8,128)(2,1)S(1)} collective-permute-done((bf16[4,64,1024]{2,1,0:T(8,128)(2,1)}, bf16[4,64,1024]{2,1,0:T(8,128)(2,1)S(1)}, u32[]{:S(2)}, u32[]{:S(2)}) %collective-permute-start.18) | collective-permute-done | bytes 524320 | tf_op jit(solution)/shard_map/ppermute | solution.py:317
  202.6 7.0 %attend.6 = (bf16[256,512]{1,0:T(8,128)(2,1)S(1)}, f32[4,2,256]{2,1,0:T(2,128)S(1)}) custom-call(bf16[256,512]{1,0:T(8,128)(2,1)S(1)} %pad_maximum_fusion.16.q_ref, bf16[256,1024]{1,0:T(8,128)(2,1)S(1)} %pad_maximum_fusion.7.own_ref, bf16[256,1024]{1,0:T(8,128)(2,1)S(1)} %collective-permute-done.20.mate_ref, ...), custom_call_target="tpu_custom_call" | custom-call | flops 2147483648 | bytes 4194304 | tf_op jit(solution)/shard_map/attend/pallas_call | solution.py:118
  216.3 7.2 %attend.7 = (bf16[256,512]{1,0:T(8,128)(2,1)S(1)}, f32[4,2,256]{2,1,0:T(2,128)S(1)}) custom-call(bf16[256,512]{1,0:T(8,128)(2,1)S(1)} %pad_maximum_fusion.17.q_ref, bf16[256,1024]{1,0:T(8,128)(2,1)S(1)} %pad_maximum_fusion.8.own_ref, bf16[256,1024]{1,0:T(8,128)(2,1)S(1)} %collective-permute-done.24.mate_ref, ...), custom_call_target="tpu_custom_call" | custom-call | flops 2147483648 | bytes 4194304 | tf_op jit(solution)/shard_map/attend/pallas_call | solution.py:118
  228.7 5.0 multiply_convert_fusion
  243.1 4.2 multiply_convert_fusion.5
  248.8 9.4 %attend_back.4 = (bf16[256,512]{1,0:T(8,128)(2,1)S(1)}, bf16[256,1024]{1,0:T(8,128)(2,1)S(1)}, bf16[256,1024]{1,0:T(8,128)(2,1)S(1)}, bf16[256,1024]{1,0:T(8,128)(2,1)S(1)}, bf16[256,1024]{1,0:T(8,128)(2,1)S(1)}) custom-call(bf16[256,512]{1,0:T(8,128)(2,1)S(1)} %pad_maximum_fusion.16.q_ref, bf16[256,1024]{1,0:T(8,128)(2,1)S(1)} %pad_maximum_fusion.7.own_ref, ...), custom_call_target="tpu_custom_call" | custom-call | flops 5368709120 | bytes 4194304 | tf_op jit(solution)/shard_map/attend_back/pallas_call | solution.py:137
  261.2 9.6 %attend_back.5 = (bf16[256,512]{1,0:T(8,128)(2,1)S(1)}, bf16[256,1024]{1,0:T(8,128)(2,1)S(1)}, bf16[256,1024]{1,0:T(8,128)(2,1)}, bf16[256,1024]{1,0:T(8,128)(2,1)S(1)}, bf16[256,1024]{1,0:T(8,128)(2,1)S(1)}) custom-call(bf16[256,512]{1,0:T(8,128)(2,1)S(1)} %pad_maximum_fusion.17.q_ref, bf16[256,1024]{1,0:T(8,128)(2,1)S(1)} %pad_maximum_fusion.8.own_ref, ...), custom_call_target="tpu_custom_call" | custom-call | flops 5368709120 | bytes 4194304 | tf_op jit(solution)/shard_map/attend_back/pallas_call | solution.py:137
  287.0 4.5 all-to-all-done.2
  300.1 5.8 %collective-permute-start.33 = (bf16[4,64,1024]{2,1,0:T(8,128)(2,1)}, bf16[4,64,1024]{2,1,0:T(8,128)(2,1)}, u32[]{:S(2)}, u32[]{:S(2)}) collective-permute-start(bf16[4,64,1024]{2,1,0:T(8,128)(2,1)} %all-to-all-done.2), channel_id=1, source_target_pairs={{0,0},{1,8},{8,1},{9,9},{2,2},{3,10},{10,3},{11,11},{4,4},{5,12},{... | collective-permute-start | bytes 1572872 | tf_op jit(solution)/shard_map/ppermute | solution.py:317
  305.9 7.0 %collective-permute-done.32 = bf16[256,1024]{1,0:T(8,128)(2,1)} collective-permute-done((bf16[256,1024]{1,0:T(8,128)(2,1)}, bf16[256,1024]{1,0:T(8,128)(2,1)}, u32[]{:S(2)}, u32[]{:S(2)}) %collective-permute-start.32) | collective-permute-done | bytes 524320 | tf_op jit(solution)/shard_map/ppermute | solution.py:728
  356.1 9.0 %attend_back.6 = (bf16[256,512]{1,0:T(8,128)(2,1)S(1)}, bf16[256,1024]{1,0:T(8,128)(2,1)S(1)}, bf16[256,1024]{1,0:T(8,128)(2,1)S(1)}, bf16[256,1024]{1,0:T(8,128)(2,1)S(1)}, bf16[256,1024]{1,0:T(8,128)(2,1)S(1)}) custom-call(bf16[256,512]{1,0:T(8,128)(2,1)S(1)} %copy-done.28, bf16[256,1024]{1,0:T(8,128)(2,1)S(1)} %copy-done.23, ...), custom_call_target="tpu_custom_call" | custom-call | flops 5368709120 | bytes 4194304 | tf_op jit(solution)/shard_map/attend_back/pallas_call | solution.py:137
  378.0 9.0 %attend_back.7 = (bf16[256,512]{1,0:T(8,128)(2,1)S(1)}, bf16[256,1024]{1,0:T(8,128)(2,1)S(1)}, bf16[256,1024]{1,0:T(8,128)(2,1)S(1)}, bf16[256,1024]{1,0:T(8,128)(2,1)S(1)}, bf16[256,1024]{1,0:T(8,128)(2,1)S(1)}) custom-call(bf16[256,512]{1,0:T(8,128)(2,1)S(1)} %pad_maximum_fusion.17.q_ref, bf16[256,1024]{1,0:T(8,128)(2,1)S(1)} %copy-done.21, ...), custom_call_target="tpu_custom_call" | custom-call | flops 5368709120 | bytes 4194304 | tf_op jit(solution)/shard_map/attend_back/pallas_call | solution.py:137
  395.9 11.6 %collective-permute-done.42 = bf16[256,1024]{1,0:T(8,128)(2,1)S(1)} collective-permute-done((bf16[256,1024]{1,0:T(8,128)(2,1)S(1)}, bf16[256,1024]{1,0:T(8,128)(2,1)S(1)}, u32[]{:S(2)}, u32[]{:S(2)}) %collective-permute-start.42) | collective-permute-done | bytes 524320 | tf_op jit(solution)/shard_map/ppermute | solution.py:36
  435.9 7.4 %collective-permute-done.46 = bf16[2,64,1024]{2,1,0:T(8,128)(2,1)} collective-permute-done((bf16[2,64,1024]{2,1,0:T(8,128)(2,1)S(1)}, bf16[2,64,1024]{2,1,0:T(8,128)(2,1)}, u32[]{:S(2)}, u32[]{:S(2)}) %collective-permute-start.46) | collective-permute-done | bytes 262176 | tf_op jit(solution)/shard_map/ppermute | solution.py:395
  456.6 4.2 all-to-all-start.3
  462.0 8.3 %all-to-all-done.3 = bf16[4,64,1024]{2,1,0:T(8,128)(2,1)} async-done(((bf16[4,64,1024]{2,1,0:T(8,128)(2,1)}), bf16[4,64,1024]{2,1,0:T(8,128)(2,1)}, u32[]{:S(2)}, u32[]{:S(2)}) %all-to-all-start.3) | async-done | bytes 524320 | tf_op jit(solution)/shard_map/all_to_all | solution.py:321
  477.3 9.9 %collective-permute-start.58 = (bf16[4,64,1024]{2,1,0:T(8,128)(2,1)}, bf16[4,64,1024]{2,1,0:T(8,128)(2,1)S(1)}, u32[]{:S(2)}, u32[]{:S(2)}) collective-permute-start(bf16[4,64,1024]{2,1,0:T(8,128)(2,1)} %all-to-all-done.3), channel_id=1, source_target_pairs={{0,0},{1,8},{8,1},{9,9},{2,2},{3,10},{10,3},{11,11},{4,4},{5,12},{... | collective-permute-start | bytes 1572872 | tf_op jit(solution)/shard_map/ppermute | solution.py:317
  492.0 5.3 collective-permute-done.55
  505.2 8.0 %collective-permute-start.60 = (bf16[64,2176]{1,0:T(8,128)(2,1)S(1)}, bf16[64,2176]{1,0:T(8,128)(2,1)S(1)}, u32[]{:S(2)}, u32[]{:S(2)}) collective-permute-start(bf16[64,2176]{1,0:T(8,128)(2,1)S(1)} %add_convert_fusion.14.mine_ref), channel_id=1, source_target_pairs={{0,1},{1,0},{2,3},{3,2},{4,5},{5,4},{6,7},{7,6},{8,9},{9,8},{10,11... | collective-permute-start | bytes 835592 | tf_op jit(solution)/shard_map/ppermute | solution.py:36
  516.6 4.7 collective-permute-start.62
  (634 shorter events, 274.6 us)
Async XLA Ops:
  7.2 39.0 %all-gather.3.cloned.1.call-start = ((), (), s32[]{:S(2)}) async-start(), calls=%async_computation.7 | async-start | bytes 2621440 | tf_op jit(solution)/shard_map/all_gather | solution.py:649
  25.4 14.7 %all-to-all-start = ((bf16[4,64,1024]{2,1,0:T(8,128)(2,1)}), bf16[4,64,1024]{2,1,0:T(8,128)(2,1)S(1)}, u32[]{:S(2)}, u32[]{:S(2)}) async-start(bf16[4,64,1024]{2,1,0:T(8,128)(2,1)} %collective-permute-done.3), calls=%async_computation | async-start | bytes 1048576 | tf_op jit(solution)/shard_map/all_to_all | solution.py:321
  30.2 105.0 %all-gather.5.cloned.1.call-start = ((), (), s32[]{:S(2)}) async-start(), calls=%async_computation.8 | async-start | bytes 10485760 | tf_op jit(solution)/shard_map/all_gather | solution.py:660
  46.3 25.6 %collective-permute-start.5 = (bf16[4,64,2176]{2,1,0:T(8,128)(2,1)S(1)}, bf16[4,64,2176]{2,1,0:T(8,128)(2,1)S(1)}, u32[]{:S(2)}, u32[]{:S(2)}) collective-permute-start(bf16[4,64,2176]{2,1,0:T(8,128)(2,1)S(1)} %ring_place.2.refs_0_), channel_id=1, source_target_pairs={{0,12},{4,0},{8,4},{12,8},{1,13},{5,1},{9,5},{13,9},{2,14},{6,2},{... | collective-permute-start | bytes 3342344 | tf_op jit(solution)/shard_map/ppermute | solution.py:337
  47.0 26.4 %collective-permute-start.4 = (bf16[4,64,2176]{2,1,0:T(8,128)(2,1)S(1)}, bf16[4,64,2176]{2,1,0:T(8,128)(2,1)}, u32[]{:S(2)}, u32[]{:S(2)}) collective-permute-start(bf16[4,64,2176]{2,1,0:T(8,128)(2,1)S(1)} %ring_place.2.refs_0_), channel_id=1, source_target_pairs={{0,4},{4,8},{8,12},{12,0},{1,5},{5,9},{9,13},{13,1},{2,6},{6,10},{... | collective-permute-start | bytes 3342344 | tf_op jit(solution)/shard_map/ppermute | solution.py:337
  93.3 24.5 %collective-permute-start.8 = (bf16[1024,512]{1,0:T(8,128)(2,1)S(1)}, bf16[1024,512]{1,0:T(8,128)(2,1)S(1)}, u32[]{:S(2)}, u32[]{:S(2)}) collective-permute-start(bf16[1024,512]{1,0:T(8,128)(2,1)S(1)} %bitcast.216), channel_id=1, source_target_pairs={{0,1},{1,0},{2,3},{3,2},{4,5},{5,4},{6,7},{7,6},{8,9},{9,8},{10,11... | collective-permute-start | bytes 3145736 | tf_op jit(solution)/shard_map/ppermute | solution.py:36
  103.6 15.2 %collective-permute-start.10 = (bf16[256,1024]{1,0:T(8,128)(2,1)S(1)}, bf16[256,1024]{1,0:T(8,128)(2,1)S(1)}, u32[]{:S(2)}, u32[]{:S(2)}) collective-permute-start(bf16[256,1024]{1,0:T(8,128)(2,1)S(1)} %pad_maximum_fusion.5.own_ref), channel_id=1, source_target_pairs={{0,1},{1,0},{2,3},{3,2},{4,5},{5,4},{6,7},{7,6},{8,9},{9,8},{10,11... | collective-permute-start | bytes 1572872 | tf_op jit(solution)/shard_map/ppermute | solution.py:36
  135.2 15.1 %collective-permute-start.17 = (bf16[1024,4096]{1,0:T(8,128)(2,1)}, bf16[1024,4096]{1,0:T(8,128)(2,1)}, u32[]{:S(2)}, u32[]{:S(2)}) collective-permute-start(bf16[1024,4096]{1,0:T(8,128)(2,1)} %all-gather.5.cloned.1.call-done), channel_id=1, source_target_pairs={{0,1},{1,0},{2,3},{3,2},{4,5},{5,4},{6,7},{7,6},{8,9},{9,8},{10,11... | collective-permute-start | bytes 25165832 | tf_op jit(solution)/shard_map/ppermute | solution.py:36
  159.6 19.7 %collective-permute-start.19 = (bf16[256,1024]{1,0:T(8,128)(2,1)}, bf16[256,1024]{1,0:T(8,128)(2,1)S(1)}, u32[]{:S(2)}, u32[]{:S(2)}) collective-permute-start(bf16[256,1024]{1,0:T(8,128)(2,1)} %fusion.90), channel_id=1, source_target_pairs={{0,64},{1,65},{2,66},{3,67},{4,68},{5,69},{6,70},{7,71},{8,72},{9,... | collective-permute-start | bytes 1572872 | tf_op jit(solution)/shard_map/ppermute | solution.py:719
  175.7 15.7 %collective-permute-start.18 = (bf16[4,64,1024]{2,1,0:T(8,128)(2,1)}, bf16[4,64,1024]{2,1,0:T(8,128)(2,1)S(1)}, u32[]{:S(2)}, u32[]{:S(2)}) collective-permute-start(bf16[4,64,1024]{2,1,0:T(8,128)(2,1)} %all-to-all-done.1), channel_id=1, source_target_pairs={{0,0},{1,8},{8,1},{9,9},{2,2},{3,10},{10,3},{11,11},{4,4},{5,12},{... | collective-permute-start | bytes 1572872 | tf_op jit(solution)/shard_map/ppermute | solution.py:317
  184.7 17.9 %collective-permute-start.20 = (bf16[256,1024]{1,0:T(8,128)(2,1)S(1)}, bf16[256,1024]{1,0:T(8,128)(2,1)S(1)}, u32[]{:S(2)}, u32[]{:S(2)}) collective-permute-start(bf16[256,1024]{1,0:T(8,128)(2,1)S(1)} %pad_maximum_fusion.7.own_ref), channel_id=1, source_target_pairs={{0,1},{1,0},{2,3},{3,2},{4,5},{5,4},{6,7},{7,6},{8,9},{9,8},{10,11... | collective-permute-start | bytes 1572872 | tf_op jit(solution)/shard_map/ppermute | solution.py:36
  260.7 14.7 %collective-permute-start.28 = (bf16[256,1024]{1,0:T(8,128)(2,1)S(1)}, bf16[256,1024]{1,0:T(8,128)(2,1)S(1)}, u32[]{:S(2)}, u32[]{:S(2)}) collective-permute-start(bf16[256,1024]{1,0:T(8,128)(2,1)S(1)} %get-tuple-element.172), channel_id=1, source_target_pairs={{0,1},{1,0},{2,3},{3,2},{4,5},{5,4},{6,7},{7,6},{8,9},{9,8},{10,11... | collective-permute-start | bytes 1572872 | tf_op jit(solution)/shard_map/ppermute | solution.py:36
  275.5 16.1 %collective-permute-start.29 = (bf16[256,1024]{1,0:T(8,128)(2,1)}, bf16[256,1024]{1,0:T(8,128)(2,1)}, u32[]{:S(2)}, u32[]{:S(2)}) collective-permute-start(bf16[256,1024]{1,0:T(8,128)(2,1)} %get-tuple-element.175), channel_id=1, source_target_pairs={{0,1},{1,0},{2,3},{3,2},{4,5},{5,4},{6,7},{7,6},{8,9},{9,8},{10,11... | collective-permute-start | bytes 1572872 | tf_op jit(solution)/shard_map/ppermute | solution.py:36
  277.3 14.2 %collective-permute-start.31 = (bf16[256,1024]{1,0:T(8,128)(2,1)}, bf16[256,1024]{1,0:T(8,128)(2,1)}, u32[]{:S(2)}, u32[]{:S(2)}) collective-permute-start(bf16[256,1024]{1,0:T(8,128)(2,1)} %add_convert_fusion.9), channel_id=1, source_target_pairs={{0,4},{4,0},{1,5},{5,1},{2,6},{6,2},{3,7},{7,3},{8,12},{12,8},{9,1... | collective-permute-start | bytes 1572872 | tf_op jit(solution)/shard_map/ppermute | solution.py:36
  282.6 160.8 %reduce-scatter.6.cloned.1.call-start = ((), (), s32[]{:S(2)}) async-start(), calls=%async_computation.10 | async-start | bytes 5242880 | tf_op jit(solution)/shard_map/reduce_scatter | solution.py:533
  298.7 14.2 %collective-permute-start.32 = (bf16[256,1024]{1,0:T(8,128)(2,1)}, bf16[256,1024]{1,0:T(8,128)(2,1)}, u32[]{:S(2)}, u32[]{:S(2)}) collective-permute-start(bf16[256,1024]{1,0:T(8,128)(2,1)} %fusion.119), channel_id=1, source_target_pairs={{64,0},{65,1},{66,2},{67,3},{68,4},{69,5},{70,6},{71,7},{72,8},{73... | collective-permute-start | bytes 1572872 | tf_op jit(solution)/shard_map/ppermute | solution.py:728
  318.7 20.9 %collective-permute-start.34 = (bf16[1024,2048]{1,0:T(8,128)(2,1)S(1)}, bf16[1024,2048]{1,0:T(8,128)(2,1)S(1)}, u32[]{:S(2)}, u32[]{:S(2)}) collective-permute-start(bf16[1024,2048]{1,0:T(8,128)(2,1)S(1)} %outer.9), channel_id=1, source_target_pairs={{0,1},{1,0},{2,3},{3,2},{4,5},{5,4},{6,7},{7,6},{8,9},{9,8},{10,11... | collective-permute-start | bytes 12582920 | tf_op jit(solution)/shard_map/ppermute | solution.py:36
  344.6 98.8 %reduce-scatter.4.cloned.1.call-start = ((), (), s32[]{:S(2)}) async-start(), calls=%async_computation.9 | async-start | bytes 5242880 | tf_op jit(solution)/shard_map/reduce_scatter | solution.py:558
  373.2 127.5 %reduce-scatter.8.cloned.1.call-start = ((), (), s32[]{:S(2)}) async-start(), calls=%async_computation.11 | async-start | bytes 2621440 | tf_op jit(solution)/shard_map/reduce_scatter | solution.py:749
  376.4 18.7 %collective-permute-start.39 = (bf16[256,1024]{1,0:T(8,128)(2,1)}, bf16[256,1024]{1,0:T(8,128)(2,1)S(1)}, u32[]{:S(2)}, u32[]{:S(2)}) collective-permute-start(bf16[256,1024]{1,0:T(8,128)(2,1)} %copy-done.42), channel_id=1, source_target_pairs={{0,1},{1,0},{2,3},{3,2},{4,5},{5,4},{6,7},{7,6},{8,9},{9,8},{10,11... | collective-permute-start | bytes 1572872 | tf_op jit(solution)/shard_map/ppermute | solution.py:36
  388.8 18.6 %collective-permute-start.40 = (bf16[256,1024]{1,0:T(8,128)(2,1)S(1)}, bf16[256,1024]{1,0:T(8,128)(2,1)S(1)}, u32[]{:S(2)}, u32[]{:S(2)}) collective-permute-start(bf16[256,1024]{1,0:T(8,128)(2,1)S(1)} %get-tuple-element.204), channel_id=1, source_target_pairs={{0,1},{1,0},{2,3},{3,2},{4,5},{5,4},{6,7},{7,6},{8,9},{9,8},{10,11... | collective-permute-start | bytes 1572872 | tf_op jit(solution)/shard_map/ppermute | solution.py:36
  391.7 28.6 %collective-permute-start.38 = (bf16[1024,1024]{1,0:T(8,128)(2,1)S(1)}, bf16[1024,1024]{1,0:T(8,128)(2,1)}, u32[]{:S(2)}, u32[]{:S(2)}) collective-permute-start(bf16[1024,1024]{1,0:T(8,128)(2,1)S(1)} %outer.12), channel_id=1, source_target_pairs={{0,1},{1,0},{2,3},{3,2},{4,5},{5,4},{6,7},{7,6},{8,9},{9,8},{10,11... | collective-permute-start | bytes 6291464 | tf_op jit(solution)/shard_map/ppermute | solution.py:36
  410.8 17.4 %collective-permute-start.45 = (bf16[1024,1024]{1,0:T(8,128)(2,1)}, bf16[1024,1024]{1,0:T(8,128)(2,1)}, u32[]{:S(2)}, u32[]{:S(2)}) collective-permute-start(bf16[1024,1024]{1,0:T(8,128)(2,1)} %outer.14), channel_id=1, source_target_pairs={{0,1},{1,0},{2,3},{3,2},{4,5},{5,4},{6,7},{7,6},{8,9},{9,8},{10,11... | collective-permute-start | bytes 6291464 | tf_op jit(solution)/shard_map/ppermute | solution.py:36
  445.6 24.6 %collective-permute-start.50 = (bf16[4,64,1024]{2,1,0:T(8,128)(2,1)}, bf16[4,64,1024]{2,1,0:T(8,128)(2,1)}, u32[]{:S(2)}, u32[]{:S(2)}) collective-permute-start(bf16[4,64,1024]{2,1,0:T(8,128)(2,1)} %pad_maximum_fusion.11), channel_id=1, source_target_pairs={{0,16},{16,32},{32,48},{48,0},{1,17},{17,33},{33,49},{49,1},{2,18}... | collective-permute-start | bytes 1572872 | tf_op jit(solution)/shard_map/ppermute | solution.py:403
  449.5 20.8 %collective-permute-start.48 = (bf16[4,64,1152]{2,1,0:T(8,128)(2,1)}, bf16[4,64,1152]{2,1,0:T(8,128)(2,1)}, u32[]{:S(2)}, u32[]{:S(2)}) collective-permute-start(bf16[4,64,1152]{2,1,0:T(8,128)(2,1)} %pad_maximum_fusion.2), channel_id=1, source_target_pairs={{0,4},{4,8},{8,12},{12,0},{1,5},{5,9},{9,13},{13,1},{2,6},{6,10},{... | collective-permute-start | bytes 1769480 | tf_op jit(solution)/shard_map/ppermute | solution.py:403
  451.6 20.6 %collective-permute-start.49 = (bf16[4,64,1152]{2,1,0:T(8,128)(2,1)}, bf16[4,64,1152]{2,1,0:T(8,128)(2,1)}, u32[]{:S(2)}, u32[]{:S(2)}) collective-permute-start(bf16[4,64,1152]{2,1,0:T(8,128)(2,1)} %pad_maximum_fusion.3), channel_id=1, source_target_pairs={{0,12},{4,0},{8,4},{12,8},{1,13},{5,1},{9,5},{13,9},{2,14},{6,2},{... | collective-permute-start | bytes 1769480 | tf_op jit(solution)/shard_map/ppermute | solution.py:403
  453.9 16.4 %collective-permute-start.51 = (bf16[4,64,1024]{2,1,0:T(8,128)(2,1)}, bf16[4,64,1024]{2,1,0:T(8,128)(2,1)}, u32[]{:S(2)}, u32[]{:S(2)}) collective-permute-start(bf16[4,64,1024]{2,1,0:T(8,128)(2,1)} %pad_maximum_fusion.12), channel_id=1, source_target_pairs={{0,48},{16,0},{32,16},{48,32},{1,49},{17,1},{33,17},{49,33},{2,50}... | collective-permute-start | bytes 1572872 | tf_op jit(solution)/shard_map/ppermute | solution.py:403
  473.8 17.8 %collective-permute-start.57 = (bf16[64,1024]{1,0:T(8,128)(2,1)S(1)}, bf16[64,1024]{1,0:T(8,128)(2,1)S(1)}, u32[]{:S(2)}, u32[]{:S(2)}) collective-permute-start(bf16[64,1024]{1,0:T(8,128)(2,1)S(1)} %get-tuple-element.288), channel_id=1, source_target_pairs={{0,8},{4,12},{8,0},{12,4},{1,9},{5,13},{9,1},{13,5},{2,10},{6,14},... | collective-permute-start | bytes 393224 | tf_op jit(solution)/shard_map/ppermute | solution.py:413
  475.6 16.4 %collective-permute-start.56 = (bf16[64,1024]{1,0:T(8,128)(2,1)S(1)}, bf16[64,1024]{1,0:T(8,128)(2,1)S(1)}, u32[]{:S(2)}, u32[]{:S(2)}) collective-permute-start(bf16[64,1024]{1,0:T(8,128)(2,1)S(1)} %get-tuple-element.289), channel_id=1, source_target_pairs={{0,12},{4,0},{8,4},{12,8},{1,13},{5,1},{9,5},{13,9},{2,14},{6,2},{... | collective-permute-start | bytes 393224 | tf_op jit(solution)/shard_map/ppermute | solution.py:413
  477.3 20.6 %collective-permute-start.58 = (bf16[4,64,1024]{2,1,0:T(8,128)(2,1)}, bf16[4,64,1024]{2,1,0:T(8,128)(2,1)S(1)}, u32[]{:S(2)}, u32[]{:S(2)}) collective-permute-start(bf16[4,64,1024]{2,1,0:T(8,128)(2,1)} %all-to-all-done.3), channel_id=1, source_target_pairs={{0,0},{1,8},{8,1},{9,9},{2,2},{3,10},{10,3},{11,11},{4,4},{5,12},{... | collective-permute-start | bytes 1572872 | tf_op jit(solution)/shard_map/ppermute | solution.py:317
  500.7 14.7 %collective-permute-start.61 = (bf16[64,4096]{1,0:T(8,128)(2,1)}, bf16[64,4096]{1,0:T(8,128)(2,1)S(1)}, u32[]{:S(2)}, u32[]{:S(2)}) collective-permute-start(bf16[64,4096]{1,0:T(8,128)(2,1)} %reduce-scatter.8.cloned.1.call-done), channel_id=1, source_target_pairs={{0,2},{2,0},{1,3},{3,1},{4,6},{6,4},{5,7},{7,5},{8,10},{10,8},{9,1... | collective-permute-start | bytes 1572872 | tf_op jit(solution)/shard_map/ppermute | solution.py:36
  505.2 16.1 %collective-permute-start.60 = (bf16[64,2176]{1,0:T(8,128)(2,1)S(1)}, bf16[64,2176]{1,0:T(8,128)(2,1)S(1)}, u32[]{:S(2)}, u32[]{:S(2)}) collective-permute-start(bf16[64,2176]{1,0:T(8,128)(2,1)S(1)} %add_convert_fusion.14.mine_ref), channel_id=1, source_target_pairs={{0,1},{1,0},{2,3},{3,2},{4,5},{5,4},{6,7},{7,6},{8,9},{9,8},{10,11... | collective-permute-start | bytes 835592 | tf_op jit(solution)/shard_map/ppermute | solution.py:36
  (170 other events, 2211.9 us)
Sparse Core Ops, SparseCore 0:
  12.1 34.0 all-gather.2
  47.9 83.3 all-gather.4
  344.7 45.3 reduce-scatter.5
  392.4 47.9 reduce-scatter.3
  447.4 43.5 reduce-scatter.7

commit v9 on v8

--- a/solution.py
+++ b/solution.py
@@ -405,14 +405,13 @@
     return [add(*e) for e in ends], beside, traded
 
 
-def direct_sums(items, beside=None):
+def direct_sums(items):
     ways = [(1, AHEAD), (3, BACK), (2, ACROSS)]
     parts = []
     for blocks, axis, dim in items:
         block = ring_blocks(blocks, axis, dim)
         parts.append([block[0]] + [lax.ppermute(block[k], axis, way) for k, way in ways])
-    parts, beside = lax.optimization_barrier((parts, beside))
-    return [add(*p) for p in parts], beside
+    return [add(*p) for p in lax.optimization_barrier(parts)]
 
 
 def group_parts(own, mate, near, far):
@@ -466,14 +465,16 @@
     key_value = chunked(project("kv"))
     queries = chunked(project("q"))
     mate, near = swap(key_value[0], "core"), swap(key_value[0], "yl")
-    blocks, results = [], []
+    blocks, results, traded = [], [], None
     for i, own in enumerate(key_value):
         blocks.append((own, mate, near, swap(near, "core")))
         if i + 1 < CHUNKS:
             following, near = lax.optimization_barrier((key_value[i + 1], near))
+            if late is not None:
+                traded = trade(late[2])
             mate, near = swap(following, "core"), swap(following, "yl")
             result = attend(queries[i], blocks[i])
-            result, near, mate = lax.optimization_barrier((result, near, mate))
+            result, near, mate, traded = lax.optimization_barrier((result, near, mate, traded))
         else:
             if late is not None:
                 blocks[i], gathered = lax.optimization_barrier((blocks[i], late[0]))
@@ -504,6 +505,7 @@
         normed_one=normed_one,
         queries=queries,
         blocks=blocks,
+        traded=traded,
         attended=attended,
         log_total=log_total,
         branch=branch,
@@ -571,7 +573,19 @@
     if result is not None:
         sent, result = lax.optimization_barrier((sent, result))
         traded = trade(result)
-    came, traded = lax.optimization_barrier((swap(sent, "yl"), traded))
+    a_full = None
+    if last:
+        grad_q = unchunked(q_chunks)
+        make = lambda i, add=None: outer(
+            [
+                ((kept["normed_one"], 0), grad_q[i], width),
+                ((kept["attended"], 0), grad_halves[i], width),
+            ],
+            half // 2,
+            add=add,
+        )
+        a_full = make(0, swap(make(1), "core"))
+    came, traded, a_full = lax.optimization_barrier((swap(sent, "yl"), traded, a_full))
     kv_chunks.append((own + came.astype(f32)).astype(bf16))
     grad_q, grad_kv = unchunked(q_chunks), unchunked(kv_chunks)
     grad_normed_one = sum(
@@ -590,9 +604,8 @@
         fc1_bias=[total(g) for g in grad_before],
     )
     products = dict(
-        q=(kept["normed_one"], grad_q),
+        a=a_full,
         kv=(kept["normed_one"], grad_kv),
-        proj=(kept["attended"], grad_halves),
         fc=fc_grad,
         traded=traded,
     )
@@ -648,19 +661,30 @@
     fc_mine = jnp.concatenate([fc1_mine, fc2_mine[0], fc2_mine[1]], axis=1)
     fc_row = lax.all_gather(fc_mine, RING_Y, axis=0, tiled=True)
 
-    mine = jnp.concatenate([kv_mine, q_mine, proj_mine, vectors], axis=1)
+    mine = jnp.concatenate([kv_mine, vectors, q_mine, proj_mine], axis=1)
     live = (
         jnp.arange(images) % IMG_MB < jnp.repeat(batch_counts[0], IMG_MB)
     ).astype(bf16)
     live_grad = out_grad * live[:, None, None]
     hops = (*first_hop(mine, RING_Z), lax.ppermute(mine, RING_Z, ACROSS))
-    hops, fc_row, live_grad, first_tokens = lax.optimization_barrier(
-        (hops, fc_row, live_grad, as_image(trade(flip(patch_tokens))))
-    )
+    hops, live_grad, first_tokens = lax.optimization_barrier(
+        (hops, live_grad, as_image(trade(flip(patch_tokens))))
+    )
+
+    def row_views(outs, piece, place, start):
+        at = 0
+        for out in outs:
+            size = out.shape[-1]
+            out[place] = piece[:, at : at + size]
+            at += size
+
+    early, later = ring_place(
+        mine, RING_Z, hops, [(4, own, width + 128), (4, own, width)], row_views
+    )
+    early_hops = first_hop(early, RING_Y)
+    later, fc_row = lax.optimization_barrier((later, fc_row))
     fc_half = lax.all_gather(fc_row, RING_Z, axis=0, tiled=True)
-    row = ring_place(mine, RING_Z, hops, [(4, *mine.shape)], in_order)[0]
-    hops = lax.optimization_barrier(first_hop(row, RING_Y))
-    more = lax.optimization_barrier(second_hop(*hops, RING_Y))
+    later_hops = first_hop(later, RING_Y)
 
     def views(outs, piece, place, start):
         for i in range(piece.shape[0]):
@@ -670,13 +694,14 @@
                 out[start + i, place] = piece[i, :, at : at + size]
                 at += size
 
-    sizes = (width, half, half, 128)
-    kv_half, q_half, proj_half, vectors = (
-        o.reshape(width, -1)
-        for o in ring_place(
-            row, RING_Y, hops + more, [(4, 4, own, size) for size in sizes], views
-        )
-    )
+    def spread(row, hops, sizes):
+        hops = lax.optimization_barrier(hops)
+        more = lax.optimization_barrier(second_hop(*hops, RING_Y))
+        shapes = [(4, 4, own, size) for size in sizes]
+        return [o.reshape(width, -1) for o in ring_place(row, RING_Y, hops + more, shapes, views)]
+
+    kv_half, vectors = spread(early, early_hops, (width, 128))
+    q_half, proj_half = spread(later, later_hops, (half, half))
     vectors = vectors[:, :16].T.astype(f32)
 
     def halves(row):
@@ -714,10 +739,10 @@
         )
 
 
-    sent, _ = forward(first_tokens, w, late=(fc_half, fc_weights))
-    sent, live_grad = lax.optimization_barrier((sent, live_grad))
+    sent, first = forward(first_tokens, w, late=(fc_half, fc_weights, live_grad))
+    sent, traded = lax.optimization_barrier((sent, first["traded"]))
     passed = lax.ppermute(sent, "section", [(0, 1)])
-    last_grad = as_image(flip(trade(live_grad)))
+    last_grad = as_image(flip(traded))
     tokens = jnp.where(section == 0, first_tokens, passed)
     result, kept = forward(tokens, w)
 
@@ -732,14 +757,10 @@
 
     vector_grads = vector_block(core, sums, width, PAIR)
 
-    a1, dq = products["q"]
-    dkv = products["kv"][1]
-    o, e1 = products["proj"]
-    make_a = lambda i, add=None: outer(
-        [((a1, 0), dq[i], width), ((o, 0), e1[i], width)], half // 2, add=add
-    )
-    make_b = lambda i, add=None: outer([((a1, 0), dkv[i], width)], half // 2, add=add)
-    a_full, b_full = (make(0, swap(make(1), "core")) for make in (make_a, make_b))
+    a1, dkv = products["kv"]
+    make = lambda i, add=None: outer([((a1, 0), dkv[i], width)], half // 2, add=add)
+    b_full = make(0, swap(make(1), "core"))
+    a_full = products["a"]
     a_full = jnp.concatenate([a_full, vector_grads], axis=1).reshape(4, 4, own, width + PAIR)
     (a_sum, b_sum), rows, traded = ring_sums(
         [(a_full, RING_Y, 1), (b_full.reshape(4, 4, own, width), RING_Z, 0)],
@@ -749,7 +770,8 @@
     fc_grad = lax.psum_scatter(
         jnp.concatenate(rows, axis=1), RING_Y, scatter_dimension=0, tiled=True
     )
-    ab, in_grad = direct_sums([(a_sum, RING_Z, 0), (b_sum, RING_Y, 0)], flip(traded))
+    ab = direct_sums([(a_sum, RING_Z, 0), (b_sum, RING_Y, 0)])
+    in_grad = flip(traded)
     ab = jnp.concatenate([ab[0][:, :width], ab[1], ab[0][:, width:]], axis=1)
 
     def chips_sum(a):

time: 548 us -> 560 us (1.022)
  starting transfers between devices: 110 us -> 123 us
  waiting for transfers between devices: 158 us -> 148 us
  other arithmetic: 37.6 us -> 44.7 us
  matrix products: 77.5 us -> 83.7 us
    all_to_all x4, waiting for transfers between devices: 23.8 us -> 14.1 us  [trade(): return lax.all_to_all(tokens, 'z', split_axis=0, concat_axis=0, tiled=True)]
    ppermute x1, waiting for transfers between devices: 0.01 us -> 8.25 us  [per_device(): passed = lax.ppermute(sent, 'section', [(0, 1)])]
    unnamed x279 -> x325, local copies, waits for them, and re-layouts: 25.5 us -> 19.2 us
    dot_general x48, matrix products: 77.5 us -> 83.7 us  [dot(): return lax.dot_general(a, b, (dims, ((), ())), preferred_element_type=f32)]
    ppermute x4, waiting for transfers between devices: 5.89 us -> 0.01 us  [flip(): return lax.ppermute(tokens, ('yh', 'core'), FLIP)]
    ppermute x4 -> x6, waiting for transfers between devices: 32.1 us -> 31.4 us  [first_hop(): return (lax.ppermute(value, axis, AHEAD), lax.ppermute(value, axis, BACK))]
  transfers between devices with their start and end apart: 72 -> 76, of which waited for: 32 -> 32; matrix products, arithmetic and copies ran while one was open for 16% -> 18% of each run, Pallas kernels for 13% -> 13%
where the time goes in v9:
time: 560 us; the launch traced here: 555 us
  waiting for transfers between devices  148 us (26%)
  starting transfers between devices  123 us (22%)
  Pallas kernels  97.2 us (17%)
  matrix products  83.7 us (15%)
  other arithmetic  44.7 us (8%)
  local copies, waits for them, and re-layouts  40.7 us (7%)
  between operations  17 us (3%)
    dot_general x48, matrix products, dot(): return lax.dot_general(a, b, (dims, ((), ())), preferred_element_type=f32)  83.7 us
    ppermute x36, waiting for transfers between devices, swap(): return lax.ppermute(value, axis, [(0, 1), (1, 0)])  60.2 us
    ppermute x36, starting transfers between devices, swap(): return lax.ppermute(value, axis, [(0, 1), (1, 0)])  39.6 us
    pallas_call x4, Pallas kernels, attend_back(): pl.pallas_call(attend_back_kernel, grid=(pairs,), in_specs=[q_spec] + kv_...  37.9 us
    ppermute x6, waiting for transfers between devices, first_hop(): return (lax.ppermute(value, axis, AHEAD), lax.ppermute(value, axis, BACK))  31.4 us
    pallas_call x4, Pallas kernels, attend(): pl.pallas_call(attend_kernel, grid=(pairs,), in_specs=[q_spec] + kv_specs...  30.6 us
    ppermute x4, starting transfers between devices, flip(): return lax.ppermute(tokens, ('yh', 'core'), FLIP)  29.4 us
    pallas_call x8, Pallas kernels, outer(): pl.pallas_call(kernel, grid=(grid,), in_specs=in_specs, out_specs=pl.Bloc...  22.6 us
  transfers between devices with their start and end apart: 76, of which 32 were waited for; matrix products, arithmetic and copies ran while one was open for 18% of the time, Pallas kernels for 13%

profile of v9, /device:TPU:1, one launch (start us, length us, event | category | flops | bytes accessed | tf_op | source)
XLA Modules:
  0.0 554.8 jit_solution(10508318123411185069)
XLA Ops:
  12.0 6.2 %collective-permute-start.3 = (bf16[4,64,1024]{2,1,0:T(8,128)(2,1)S(1)}, bf16[4,64,1024]{2,1,0:T(8,128)(2,1)}, u32[]{:S(2)}, u32[]{:S(2)}) collective-permute-start(bf16[4,64,1024]{2,1,0:T(8,128)(2,1)S(1)} %copy-done.140), channel_id=1, source_target_pairs={{0,0},{1,8},{8,1},{9,9},{2,2},{3,10},{10,3},{11,11},{4,4},{5,12},{... | collective-permute-start | bytes 1572872 | tf_op jit(solution)/shard_map/ppermute | solution.py:317
  25.4 4.8 all-to-all-start
  31.1 6.7 %collective-permute-done.1.refs_2_ = bf16[64,2176]{1,0:T(8,128)(2,1)S(1)} collective-permute-done((bf16[64,2176]{1,0:T(8,128)(2,1)S(1)}, bf16[64,2176]{1,0:T(8,128)(2,1)S(1)}, u32[]{:S(2)}, u32[]{:S(2)}) %collective-permute-start.1) | collective-permute-done | bytes 278560 | tf_op jit(solution)/shard_map/ppermute | solution.py:337
  40.3 6.0 %all-gather.3.cloned.1.call-done = bf16[256,4096]{1,0:T(8,128)(2,1)} async-done(((bf16[64,4096]{1,0:T(8,128)(2,1)}), bf16[256,4096]{1,0:T(8,128)(2,1)}) %all-gather.3.cloned.1.call-update) | async-done | bytes 2097168 | tf_op jit(solution)/shard_map/all_gather | solution.py:662
  48.0 12.6 %collective-permute-done.5.refs_2_ = bf16[4,64,1152]{2,1,0:T(8,128)(2,1)S(1)} collective-permute-done((bf16[4,64,1152]{2,1,0:T(8,128)(2,1)S(1)}, bf16[4,64,1152]{2,1,0:T(8,128)(2,1)S(1)}, u32[]{:S(2)}, u32[]{:S(2)}) %collective-permute-start.5) | collective-permute-done | bytes 589856 | tf_op jit(solution)/shard_map/ppermute | solution.py:337
  65.2 4.2 all-to-all-start.1
  81.3 9.6 %collective-permute-done.9.refs_2_ = bf16[4,64,1024]{2,1,0:T(8,128)(2,1)S(1)} collective-permute-done((bf16[4,64,1024]{2,1,0:T(8,128)(2,1)S(1)}, bf16[4,64,1024]{2,1,0:T(8,128)(2,1)S(1)}, u32[]{:S(2)}, u32[]{:S(2)}) %collective-permute-start.9) | collective-permute-done | bytes 524320 | tf_op jit(solution)/shard_map/ppermute | solution.py:337
  93.6 5.5 collective-permute-done.11.refs_4_
  100.5 16.4 %collective-permute-start.12 = (bf16[1024,512]{1,0:T(8,128)(2,1)S(1)}, bf16[1024,512]{1,0:T(8,128)(2,1)S(1)}, u32[]{:S(2)}, u32[]{:S(2)}) collective-permute-start(bf16[1024,512]{1,0:T(8,128)(2,1)S(1)} %bitcast.211), channel_id=1, source_target_pairs={{0,1},{1,0},{2,3},{3,2},{4,5},{5,4},{6,7},{7,6},{8,9},{9,8},{10,11... | collective-permute-start | bytes 3145736 | tf_op jit(solution)/shard_map/ppermute | solution.py:36
  119.5 12.6 %collective-permute-done.15.near_ref = bf16[256,1024]{1,0:T(8,128)(2,1)S(1)} collective-permute-done((bf16[256,1024]{1,0:T(8,128)(2,1)S(1)}, bf16[256,1024]{1,0:T(8,128)(2,1)S(1)}, u32[]{:S(2)}, u32[]{:S(2)}) %collective-permute-start.15) | collective-permute-done | bytes 524320 | tf_op jit(solution)/shard_map/ppermute | solution.py:36
  135.2 7.6 %attend.4 = (bf16[256,512]{1,0:T(8,128)(2,1)S(1)}, f32[4,2,256]{2,1,0:T(2,128)}) custom-call(bf16[256,512]{1,0:T(8,128)(2,1)S(1)} %pad_maximum_fusion.14.q_ref, bf16[256,1024]{1,0:T(8,128)(2,1)S(1)} %pad_maximum_fusion.5.own_ref, bf16[256,1024]{1,0:T(8,128)(2,1)S(1)} %collective-permute-done.14.mate_ref, ...), custom_call_target="tpu_custom_call" | custom-call | flops 2147483648 | bytes 4194304 | tf_op jit(solution)/shard_map/attend/pallas_call | solution.py:118
  151.5 8.6 %attend.5 = (bf16[256,512]{1,0:T(8,128)(2,1)S(1)}, f32[4,2,256]{2,1,0:T(2,128)}) custom-call(bf16[256,512]{1,0:T(8,128)(2,1)S(1)} %pad_maximum_fusion.15.q_ref, bf16[256,1024]{1,0:T(8,128)(2,1)S(1)} %pad_maximum_fusion.6.own_ref, bf16[256,1024]{1,0:T(8,128)(2,1)} %collective-permute-done.18.mate_ref, bf16[256,1024]{1,0:T(8,128)(2,1)} %collective-permute-done.17.near_ref, ...), custom_call_target="tpu_custom_call" | custom-call | flops 2147483648 | bytes 4194304 | tf_op jit(solution)/shard_map/attend/pallas_call | solution.py:118
  184.0 8.2 %collective-permute-done.23 = bf16[256,1024]{1,0:T(8,128)(2,1)S(1)} collective-permute-done((bf16[256,1024]{1,0:T(8,128)(2,1)}, bf16[256,1024]{1,0:T(8,128)(2,1)S(1)}, u32[]{:S(2)}, u32[]{:S(2)}) %collective-permute-start.23) | collective-permute-done | bytes 524320 | tf_op jit(solution)/shard_map/ppermute | solution.py:744
  202.6 6.3 %collective-permute-done.25.near_ref = bf16[256,1024]{1,0:T(8,128)(2,1)S(1)} collective-permute-done((bf16[256,1024]{1,0:T(8,128)(2,1)S(1)}, bf16[256,1024]{1,0:T(8,128)(2,1)S(1)}, u32[]{:S(2)}, u32[]{:S(2)}) %collective-permute-start.25) | collective-permute-done | bytes 524320 | tf_op jit(solution)/shard_map/ppermute | solution.py:36
  213.8 7.0 %attend.6 = (bf16[256,512]{1,0:T(8,128)(2,1)S(1)}, f32[4,2,256]{2,1,0:T(2,128)S(1)}) custom-call(bf16[256,512]{1,0:T(8,128)(2,1)S(1)} %pad_maximum_fusion.16.q_ref, bf16[256,1024]{1,0:T(8,128)(2,1)S(1)} %pad_maximum_fusion.7.own_ref, bf16[256,1024]{1,0:T(8,128)(2,1)S(1)} %collective-permute-done.24.mate_ref, ...), custom_call_target="tpu_custom_call" | custom-call | flops 2147483648 | bytes 4194304 | tf_op jit(solution)/shard_map/attend/pallas_call | solution.py:118
  228.9 7.4 %attend.7 = (bf16[256,512]{1,0:T(8,128)(2,1)S(1)}, f32[4,2,256]{2,1,0:T(2,128)S(1)}) custom-call(bf16[256,512]{1,0:T(8,128)(2,1)S(1)} %pad_maximum_fusion.17.q_ref, bf16[256,1024]{1,0:T(8,128)(2,1)S(1)} %pad_maximum_fusion.8.own_ref, bf16[256,1024]{1,0:T(8,128)(2,1)S(1)} %collective-permute-done.28.mate_ref, ...), custom_call_target="tpu_custom_call" | custom-call | flops 2147483648 | bytes 4194304 | tf_op jit(solution)/shard_map/attend/pallas_call | solution.py:118
  241.5 5.0 multiply_convert_fusion
  255.9 4.2 multiply_convert_fusion.5
  261.6 9.1 %attend_back.4 = (bf16[256,512]{1,0:T(8,128)(2,1)S(1)}, bf16[256,1024]{1,0:T(8,128)(2,1)S(1)}, bf16[256,1024]{1,0:T(8,128)(2,1)S(1)}, bf16[256,1024]{1,0:T(8,128)(2,1)S(1)}, bf16[256,1024]{1,0:T(8,128)(2,1)S(1)}) custom-call(bf16[256,512]{1,0:T(8,128)(2,1)S(1)} %pad_maximum_fusion.16.q_ref, bf16[256,1024]{1,0:T(8,128)(2,1)S(1)} %pad_maximum_fusion.7.own_ref, ...), custom_call_target="tpu_custom_call" | custom-call | flops 5368709120 | bytes 4194304 | tf_op jit(solution)/shard_map/attend_back/pallas_call | solution.py:137
  273.6 9.6 %attend_back.5 = (bf16[256,512]{1,0:T(8,128)(2,1)S(1)}, bf16[256,1024]{1,0:T(8,128)(2,1)S(1)}, bf16[256,1024]{1,0:T(8,128)(2,1)}, bf16[256,1024]{1,0:T(8,128)(2,1)S(1)}, bf16[256,1024]{1,0:T(8,128)(2,1)S(1)}) custom-call(bf16[256,512]{1,0:T(8,128)(2,1)S(1)} %pad_maximum_fusion.17.q_ref, bf16[256,1024]{1,0:T(8,128)(2,1)S(1)} %pad_maximum_fusion.8.own_ref, ...), custom_call_target="tpu_custom_call" | custom-call | flops 5368709120 | bytes 4194304 | tf_op jit(solution)/shard_map/attend_back/pallas_call | solution.py:137
  290.9 4.1 all-to-all-start.2
  313.3 4.9 collective-permute-start.37
  318.2 7.9 %collective-permute-done.36 = bf16[256,1024]{1,0:T(8,128)(2,1)} collective-permute-done((bf16[256,1024]{1,0:T(8,128)(2,1)}, bf16[256,1024]{1,0:T(8,128)(2,1)}, u32[]{:S(2)}, u32[]{:S(2)}) %collective-permute-start.36) | collective-permute-done | bytes 524320 | tf_op jit(solution)/shard_map/ppermute | solution.py:753
  369.4 9.6 %attend_back.6 = (bf16[256,512]{1,0:T(8,128)(2,1)S(1)}, bf16[256,1024]{1,0:T(8,128)(2,1)S(1)}, bf16[256,1024]{1,0:T(8,128)(2,1)}, bf16[256,1024]{1,0:T(8,128)(2,1)S(1)}, bf16[256,1024]{1,0:T(8,128)(2,1)S(1)}) custom-call(bf16[256,512]{1,0:T(8,128)(2,1)S(1)} %pad_maximum_fusion.16.q_ref, bf16[256,1024]{1,0:T(8,128)(2,1)S(1)} %copy-done.19, ...), custom_call_target="tpu_custom_call" | custom-call | flops 5368709120 | bytes 4194304 | tf_op jit(solution)/shard_map/attend_back/pallas_call | solution.py:137
  392.5 9.6 %attend_back.7 = (bf16[256,512]{1,0:T(8,128)(2,1)S(1)}, bf16[256,1024]{1,0:T(8,128)(2,1)S(1)}, bf16[256,1024]{1,0:T(8,128)(2,1)S(1)}, bf16[256,1024]{1,0:T(8,128)(2,1)S(1)}, bf16[256,1024]{1,0:T(8,128)(2,1)}) custom-call(bf16[256,512]{1,0:T(8,128)(2,1)S(1)} %copy-done.25, bf16[256,1024]{1,0:T(8,128)(2,1)S(1)} %copy-done.17, ...), custom_call_target="tpu_custom_call" | custom-call | flops 5368709120 | bytes 4194304 | tf_op jit(solution)/shard_map/attend_back/pallas_call | solution.py:137
  420.0 8.5 %collective-permute-done.43 = bf16[256,1024]{1,0:T(8,128)(2,1)S(1)} collective-permute-done((bf16[256,1024]{1,0:T(8,128)(2,1)S(1)}, bf16[256,1024]{1,0:T(8,128)(2,1)S(1)}, u32[]{:S(2)}, u32[]{:S(2)}) %collective-permute-start.43) | collective-permute-done | bytes 524320 | tf_op jit(solution)/shard_map/ppermute | solution.py:36
  455.2 4.8 collective-permute-done.50
  474.1 4.1 all-to-all-start.3
  479.4 7.9 %all-to-all-done.3 = bf16[4,64,1024]{2,1,0:T(8,128)(2,1)} async-done(((bf16[4,64,1024]{2,1,0:T(8,128)(2,1)}), bf16[4,64,1024]{2,1,0:T(8,128)(2,1)}, u32[]{:S(2)}, u32[]{:S(2)}) %all-to-all-start.3) | async-done | bytes 524320 | tf_op jit(solution)/shard_map/all_to_all | solution.py:321
  492.2 4.5 collective-permute-start.59
  507.8 15.3 %collective-permute-start.56 = (bf16[4,64,1024]{2,1,0:T(8,128)(2,1)}, bf16[4,64,1024]{2,1,0:T(8,128)(2,1)S(1)}, u32[]{:S(2)}, u32[]{:S(2)}) collective-permute-start(bf16[4,64,1024]{2,1,0:T(8,128)(2,1)} %all-to-all-done.3), channel_id=1, source_target_pairs={{0,0},{1,8},{8,1},{9,9},{2,2},{3,10},{10,3},{11,11},{4,4},{5,12},{... | collective-permute-start | bytes 1572872 | tf_op jit(solution)/shard_map/ppermute | solution.py:317
  524.7 12.7 %collective-permute-done.65 = bf16[64,4096]{1,0:T(8,128)(2,1)S(1)} collective-permute-done((bf16[64,4096]{1,0:T(8,128)(2,1)}, bf16[64,4096]{1,0:T(8,128)(2,1)S(1)}, u32[]{:S(2)}, u32[]{:S(2)}) %collective-permute-start.65) | collective-permute-done | bytes 524320 | tf_op jit(solution)/shard_map/ppermute | solution.py:36
  (691 shorter events, 286.2 us)
Async XLA Ops:
  7.2 39.0 %all-gather.3.cloned.1.call-start = ((), (), s32[]{:S(2)}) async-start(), calls=%async_computation.7 | async-start | bytes 2621440 | tf_op jit(solution)/shard_map/all_gather | solution.py:662
  25.4 14.7 %all-to-all-start = ((bf16[4,64,1024]{2,1,0:T(8,128)(2,1)}), bf16[4,64,1024]{2,1,0:T(8,128)(2,1)S(1)}, u32[]{:S(2)}, u32[]{:S(2)}) async-start(bf16[4,64,1024]{2,1,0:T(8,128)(2,1)} %collective-permute-done.3), calls=%async_computation | async-start | bytes 1048576 | tf_op jit(solution)/shard_map/all_to_all | solution.py:321
  30.2 118.7 %all-gather.5.cloned.1.call-start = ((), (), s32[]{:S(2)}) async-start(), calls=%async_computation.8 | async-start | bytes 10485760 | tf_op jit(solution)/shard_map/all_gather | solution.py:686
  46.9 15.1 %collective-permute-start.4 = (bf16[4,64,1152]{2,1,0:T(8,128)(2,1)S(1)}, bf16[4,64,1152]{2,1,0:T(8,128)(2,1)S(1)}, u32[]{:S(2)}, u32[]{:S(2)}) collective-permute-start(bf16[4,64,1152]{2,1,0:T(8,128)(2,1)S(1)} %get-tuple-element.137.refs_0_), channel_id=1, source_target_pairs={{0,4},{4,8},{8,12},{12,0},{1,5},{5,9},{9,13},{13,1},{2,6},{6,10},{... | collective-permute-start | bytes 1769480 | tf_op jit(solution)/shard_map/ppermute | solution.py:337
  65.2 77.6 %all-to-all-start.1 = ((bf16[4,64,1024]{2,1,0:T(8,128)(2,1)}), bf16[4,64,1024]{2,1,0:T(8,128)(2,1)}, u32[]{:S(2)}, u32[]{:S(2)}) async-start(bf16[4,64,1024]{2,1,0:T(8,128)(2,1)} %broadcast_multiply_fusion), calls=%async_computation.1 | async-start | bytes 1048576 | tf_op jit(solution)/shard_map/all_to_all | solution.py:321
  73.6 43.3 %collective-permute-start.13 = (bf16[1024,1024]{1,0:T(8,128)(2,1)}, bf16[1024,1024]{1,0:T(8,128)(2,1)S(1)}, u32[]{:S(2)}, u32[]{:S(2)}) collective-permute-start(bf16[1024,1024]{1,0:T(8,128)(2,1)} %bitcast.26), channel_id=1, source_target_pairs={{0,1},{1,0},{2,3},{3,2},{4,5},{5,4},{6,7},{7,6},{8,9},{9,8},{10,11... | collective-permute-start | bytes 6291464 | tf_op jit(solution)/shard_map/ppermute | solution.py:36
  77.3 14.7 %collective-permute-start.8 = (bf16[4,64,1024]{2,1,0:T(8,128)(2,1)S(1)}, bf16[4,64,1024]{2,1,0:T(8,128)(2,1)S(1)}, u32[]{:S(2)}, u32[]{:S(2)}) collective-permute-start(bf16[4,64,1024]{2,1,0:T(8,128)(2,1)S(1)} %get-tuple-element.144.refs_0_), channel_id=1, source_target_pairs={{0,4},{4,8},{8,12},{12,0},{1,5},{5,9},{9,13},{13,1},{2,6},{6,10},{... | collective-permute-start | bytes 1572872 | tf_op jit(solution)/shard_map/ppermute | solution.py:337
  100.5 32.7 %collective-permute-start.12 = (bf16[1024,512]{1,0:T(8,128)(2,1)S(1)}, bf16[1024,512]{1,0:T(8,128)(2,1)S(1)}, u32[]{:S(2)}, u32[]{:S(2)}) collective-permute-start(bf16[1024,512]{1,0:T(8,128)(2,1)S(1)} %bitcast.211), channel_id=1, source_target_pairs={{0,1},{1,0},{2,3},{3,2},{4,5},{5,4},{6,7},{7,6},{8,9},{9,8},{10,11... | collective-permute-start | bytes 3145736 | tf_op jit(solution)/shard_map/ppermute | solution.py:36
  118.5 16.6 %collective-permute-start.14 = (bf16[256,1024]{1,0:T(8,128)(2,1)S(1)}, bf16[256,1024]{1,0:T(8,128)(2,1)S(1)}, u32[]{:S(2)}, u32[]{:S(2)}) collective-permute-start(bf16[256,1024]{1,0:T(8,128)(2,1)S(1)} %pad_maximum_fusion.5.own_ref), channel_id=1, source_target_pairs={{0,1},{1,0},{2,3},{3,2},{4,5},{5,4},{6,7},{7,6},{8,9},{9,8},{10,11... | collective-permute-start | bytes 1572872 | tf_op jit(solution)/shard_map/ppermute | solution.py:36
  149.0 19.4 %collective-permute-start.21 = (bf16[1024,4096]{1,0:T(8,128)(2,1)}, bf16[1024,4096]{1,0:T(8,128)(2,1)}, u32[]{:S(2)}, u32[]{:S(2)}) collective-permute-start(bf16[1024,4096]{1,0:T(8,128)(2,1)} %all-gather.5.cloned.1.call-done), channel_id=1, source_target_pairs={{0,1},{1,0},{2,3},{3,2},{4,5},{5,4},{6,7},{7,6},{8,9},{9,8},{10,11... | collective-permute-start | bytes 25165832 | tf_op jit(solution)/shard_map/ppermute | solution.py:36
  177.7 14.5 %collective-permute-start.23 = (bf16[256,1024]{1,0:T(8,128)(2,1)}, bf16[256,1024]{1,0:T(8,128)(2,1)S(1)}, u32[]{:S(2)}, u32[]{:S(2)}) collective-permute-start(bf16[256,1024]{1,0:T(8,128)(2,1)} %fusion.90), channel_id=1, source_target_pairs={{0,64},{1,65},{2,66},{3,67},{4,68},{5,69},{6,70},{7,71},{8,72},{9,... | collective-permute-start | bytes 1572872 | tf_op jit(solution)/shard_map/ppermute | solution.py:744
  181.0 18.1 %collective-permute-start.22 = (bf16[4,64,1024]{2,1,0:T(8,128)(2,1)}, bf16[4,64,1024]{2,1,0:T(8,128)(2,1)S(1)}, u32[]{:S(2)}, u32[]{:S(2)}) collective-permute-start(bf16[4,64,1024]{2,1,0:T(8,128)(2,1)} %all-to-all-done.1), channel_id=1, source_target_pairs={{0,0},{1,8},{8,1},{9,9},{2,2},{3,10},{10,3},{11,11},{4,4},{5,12},{... | collective-permute-start | bytes 1572872 | tf_op jit(solution)/shard_map/ppermute | solution.py:317
  196.7 17.0 %collective-permute-start.24 = (bf16[256,1024]{1,0:T(8,128)(2,1)S(1)}, bf16[256,1024]{1,0:T(8,128)(2,1)S(1)}, u32[]{:S(2)}, u32[]{:S(2)}) collective-permute-start(bf16[256,1024]{1,0:T(8,128)(2,1)S(1)} %pad_maximum_fusion.7.own_ref), channel_id=1, source_target_pairs={{0,1},{1,0},{2,3},{3,2},{4,5},{5,4},{6,7},{7,6},{8,9},{9,8},{10,11... | collective-permute-start | bytes 1572872 | tf_op jit(solution)/shard_map/ppermute | solution.py:36
  273.1 14.9 %collective-permute-start.32 = (bf16[256,1024]{1,0:T(8,128)(2,1)S(1)}, bf16[256,1024]{1,0:T(8,128)(2,1)S(1)}, u32[]{:S(2)}, u32[]{:S(2)}) collective-permute-start(bf16[256,1024]{1,0:T(8,128)(2,1)S(1)} %get-tuple-element.189), channel_id=1, source_target_pairs={{0,1},{1,0},{2,3},{3,2},{4,5},{5,4},{6,7},{7,6},{8,9},{9,8},{10,11... | collective-permute-start | bytes 1572872 | tf_op jit(solution)/shard_map/ppermute | solution.py:36
  288.1 15.4 %collective-permute-start.33 = (bf16[256,1024]{1,0:T(8,128)(2,1)}, bf16[256,1024]{1,0:T(8,128)(2,1)}, u32[]{:S(2)}, u32[]{:S(2)}) collective-permute-start(bf16[256,1024]{1,0:T(8,128)(2,1)} %get-tuple-element.192), channel_id=1, source_target_pairs={{0,1},{1,0},{2,3},{3,2},{4,5},{5,4},{6,7},{7,6},{8,9},{9,8},{10,11... | collective-permute-start | bytes 1572872 | tf_op jit(solution)/shard_map/ppermute | solution.py:36
  295.0 160.2 %reduce-scatter.6.cloned.1.call-start = ((), (), s32[]{:S(2)}) async-start(), calls=%async_computation.10 | async-start | bytes 5242880 | tf_op jit(solution)/shard_map/reduce_scatter | solution.py:535
  311.8 14.3 %collective-permute-start.36 = (bf16[256,1024]{1,0:T(8,128)(2,1)}, bf16[256,1024]{1,0:T(8,128)(2,1)}, u32[]{:S(2)}, u32[]{:S(2)}) collective-permute-start(bf16[256,1024]{1,0:T(8,128)(2,1)} %fusion.119), channel_id=1, source_target_pairs={{64,0},{65,1},{66,2},{67,3},{68,4},{69,5},{70,6},{71,7},{72,8},{73... | collective-permute-start | bytes 1572872 | tf_op jit(solution)/shard_map/ppermute | solution.py:753
  331.8 21.2 %collective-permute-start.38 = (bf16[1024,2048]{1,0:T(8,128)(2,1)S(1)}, bf16[1024,2048]{1,0:T(8,128)(2,1)S(1)}, u32[]{:S(2)}, u32[]{:S(2)}) collective-permute-start(bf16[1024,2048]{1,0:T(8,128)(2,1)S(1)} %outer.9), channel_id=1, source_target_pairs={{0,1},{1,0},{2,3},{3,2},{4,5},{5,4},{6,7},{7,6},{8,9},{9,8},{10,11... | collective-permute-start | bytes 12582920 | tf_op jit(solution)/shard_map/ppermute | solution.py:36
  358.0 102.1 %reduce-scatter.4.cloned.1.call-start = ((), (), s32[]{:S(2)}) async-start(), calls=%async_computation.9 | async-start | bytes 5242880 | tf_op jit(solution)/shard_map/reduce_scatter | solution.py:560
  387.1 136.0 %reduce-scatter.8.cloned.1.call-start = ((), (), s32[]{:S(2)}) async-start(), calls=%async_computation.11 | async-start | bytes 2621440 | tf_op jit(solution)/shard_map/reduce_scatter | solution.py:770
  388.3 14.6 %collective-permute-start.41 = (bf16[256,1024]{1,0:T(8,128)(2,1)}, bf16[256,1024]{1,0:T(8,128)(2,1)S(1)}, u32[]{:S(2)}, u32[]{:S(2)}) collective-permute-start(bf16[256,1024]{1,0:T(8,128)(2,1)} %add_convert_fusion.6), channel_id=1, source_target_pairs={{0,4},{4,0},{1,5},{5,1},{2,6},{6,2},{3,7},{7,3},{8,12},{12,8},{9,1... | collective-permute-start | bytes 1572872 | tf_op jit(solution)/shard_map/ppermute | solution.py:36
  406.7 21.8 %collective-permute-start.46 = (bf16[256,1024]{1,0:T(8,128)(2,1)}, bf16[256,1024]{1,0:T(8,128)(2,1)S(1)}, u32[]{:S(2)}, u32[]{:S(2)}) collective-permute-start(bf16[256,1024]{1,0:T(8,128)(2,1)} %copy-done.39), channel_id=1, source_target_pairs={{0,1},{1,0},{2,3},{3,2},{4,5},{5,4},{6,7},{7,6},{8,9},{9,8},{10,11... | collective-permute-start | bytes 1572872 | tf_op jit(solution)/shard_map/ppermute | solution.py:36
  431.8 14.9 %collective-permute-start.49 = (bf16[1024,1024]{1,0:T(8,128)(2,1)}, bf16[1024,1024]{1,0:T(8,128)(2,1)}, u32[]{:S(2)}, u32[]{:S(2)}) collective-permute-start(bf16[1024,1024]{1,0:T(8,128)(2,1)} %outer.14), channel_id=1, source_target_pairs={{0,1},{1,0},{2,3},{3,2},{4,5},{5,4},{6,7},{7,6},{8,9},{9,8},{10,11... | collective-permute-start | bytes 6291464 | tf_op jit(solution)/shard_map/ppermute | solution.py:36
  463.1 24.3 %collective-permute-start.54 = (bf16[4,64,1024]{2,1,0:T(8,128)(2,1)}, bf16[4,64,1024]{2,1,0:T(8,128)(2,1)}, u32[]{:S(2)}, u32[]{:S(2)}) collective-permute-start(bf16[4,64,1024]{2,1,0:T(8,128)(2,1)} %pad_maximum_fusion.11), channel_id=1, source_target_pairs={{0,16},{16,32},{32,48},{48,0},{1,17},{17,33},{33,49},{49,1},{2,18}... | collective-permute-start | bytes 1572872 | tf_op jit(solution)/shard_map/ppermute | solution.py:403
  467.0 20.4 %collective-permute-start.52 = (bf16[4,64,1152]{2,1,0:T(8,128)(2,1)}, bf16[4,64,1152]{2,1,0:T(8,128)(2,1)}, u32[]{:S(2)}, u32[]{:S(2)}) collective-permute-start(bf16[4,64,1152]{2,1,0:T(8,128)(2,1)} %pad_maximum_fusion.2), channel_id=1, source_target_pairs={{0,4},{4,8},{8,12},{12,0},{1,5},{5,9},{9,13},{13,1},{2,6},{6,10},{... | collective-permute-start | bytes 1769480 | tf_op jit(solution)/shard_map/ppermute | solution.py:403
  467.9 21.1 %collective-permute-start.53 = (bf16[4,64,1152]{2,1,0:T(8,128)(2,1)}, bf16[4,64,1152]{2,1,0:T(8,128)(2,1)}, u32[]{:S(2)}, u32[]{:S(2)}) collective-permute-start(bf16[4,64,1152]{2,1,0:T(8,128)(2,1)} %pad_maximum_fusion.3), channel_id=1, source_target_pairs={{0,12},{4,0},{8,4},{12,8},{1,13},{5,1},{9,5},{13,9},{2,14},{6,2},{... | collective-permute-start | bytes 1769480 | tf_op jit(solution)/shard_map/ppermute | solution.py:403
  471.4 16.0 %collective-permute-start.55 = (bf16[4,64,1024]{2,1,0:T(8,128)(2,1)}, bf16[4,64,1024]{2,1,0:T(8,128)(2,1)}, u32[]{:S(2)}, u32[]{:S(2)}) collective-permute-start(bf16[4,64,1024]{2,1,0:T(8,128)(2,1)} %pad_maximum_fusion.12), channel_id=1, source_target_pairs={{0,48},{16,0},{32,16},{48,32},{1,49},{17,1},{33,17},{49,33},{2,50}... | collective-permute-start | bytes 1572872 | tf_op jit(solution)/shard_map/ppermute | solution.py:403
  492.2 14.6 %collective-permute-start.59 = (bf16[64,1152]{1,0:T(8,128)(2,1)S(1)}, bf16[64,1152]{1,0:T(8,128)(2,1)S(1)}, u32[]{:S(2)}, u32[]{:S(2)}) collective-permute-start(bf16[64,1152]{1,0:T(8,128)(2,1)S(1)} %get-tuple-element.302), channel_id=1, source_target_pairs={{0,32},{16,48},{32,0},{48,16},{1,33},{17,49},{33,1},{49,17},{2,34}... | collective-permute-start | bytes 442376 | tf_op jit(solution)/shard_map/ppermute | solution.py:413
  507.0 16.3 %collective-permute-start.63 = (bf16[64,2176]{1,0:T(8,128)(2,1)S(1)}, bf16[64,2176]{1,0:T(8,128)(2,1)S(1)}, u32[]{:S(2)}, u32[]{:S(2)}) collective-permute-start(bf16[64,2176]{1,0:T(8,128)(2,1)S(1)} %pad_maximum_fusion.13), channel_id=1, source_target_pairs={{0,2},{2,0},{1,3},{3,1},{4,6},{6,4},{5,7},{7,5},{8,10},{10,8},{9,1... | collective-permute-start | bytes 835592 | tf_op jit(solution)/shard_map/ppermute | solution.py:36
  507.8 30.9 %collective-permute-start.56 = (bf16[4,64,1024]{2,1,0:T(8,128)(2,1)}, bf16[4,64,1024]{2,1,0:T(8,128)(2,1)S(1)}, u32[]{:S(2)}, u32[]{:S(2)}) collective-permute-start(bf16[4,64,1024]{2,1,0:T(8,128)(2,1)} %all-to-all-done.3), channel_id=1, source_target_pairs={{0,0},{1,8},{8,1},{9,9},{2,2},{3,10},{10,3},{11,11},{4,4},{5,12},{... | collective-permute-start | bytes 1572872 | tf_op jit(solution)/shard_map/ppermute | solution.py:317
  523.2 14.3 %collective-permute-start.65 = (bf16[64,4096]{1,0:T(8,128)(2,1)}, bf16[64,4096]{1,0:T(8,128)(2,1)S(1)}, u32[]{:S(2)}, u32[]{:S(2)}) collective-permute-start(bf16[64,4096]{1,0:T(8,128)(2,1)} %reduce-scatter.8.cloned.1.call-done), channel_id=1, source_target_pairs={{0,2},{2,0},{1,3},{3,1},{4,6},{6,4},{5,7},{7,5},{8,10},{10,8},{9,1... | collective-permute-start | bytes 1572872 | tf_op jit(solution)/shard_map/ppermute | solution.py:36
  523.3 15.4 %collective-permute-start.64 = (bf16[64,2176]{1,0:T(8,128)(2,1)S(1)}, bf16[64,2176]{1,0:T(8,128)(2,1)S(1)}, u32[]{:S(2)}, u32[]{:S(2)}) collective-permute-start(bf16[64,2176]{1,0:T(8,128)(2,1)S(1)} %add_convert_fusion.14.mine_ref), channel_id=1, source_target_pairs={{0,1},{1,0},{2,3},{3,2},{4,5},{5,4},{6,7},{7,6},{8,9},{9,8},{10,11... | collective-permute-start | bytes 835592 | tf_op jit(solution)/shard_map/ppermute | solution.py:36
  (197 other events, 2768.3 us)
Sparse Core Ops, SparseCore 0:
  12.1 34.0 all-gather.2
  47.9 88.9 all-gather.4
  358.1 45.0 reduce-scatter.5
  405.5 46.5 reduce-scatter.3
  464.8 38.5 reduce-scatter.7

commit v10 on v8

--- a/solution.py
+++ b/solution.py
@@ -405,14 +405,13 @@
     return [add(*e) for e in ends], beside, traded
 
 
-def direct_sums(items, beside=None):
+def direct_sums(items):
     ways = [(1, AHEAD), (3, BACK), (2, ACROSS)]
     parts = []
     for blocks, axis, dim in items:
         block = ring_blocks(blocks, axis, dim)
         parts.append([block[0]] + [lax.ppermute(block[k], axis, way) for k, way in ways])
-    parts, beside = lax.optimization_barrier((parts, beside))
-    return [add(*p) for p in parts], beside
+    return [add(*p) for p in lax.optimization_barrier(parts)]
 
 
 def group_parts(own, mate, near, far):
@@ -466,14 +465,16 @@
     key_value = chunked(project("kv"))
     queries = chunked(project("q"))
     mate, near = swap(key_value[0], "core"), swap(key_value[0], "yl")
-    blocks, results = [], []
+    blocks, results, traded = [], [], None
     for i, own in enumerate(key_value):
         blocks.append((own, mate, near, swap(near, "core")))
         if i + 1 < CHUNKS:
             following, near = lax.optimization_barrier((key_value[i + 1], near))
+            if late is not None:
+                traded = trade(late[2])
             mate, near = swap(following, "core"), swap(following, "yl")
             result = attend(queries[i], blocks[i])
-            result, near, mate = lax.optimization_barrier((result, near, mate))
+            result, near, mate, traded = lax.optimization_barrier((result, near, mate, traded))
         else:
             if late is not None:
                 blocks[i], gathered = lax.optimization_barrier((blocks[i], late[0]))
@@ -504,6 +505,7 @@
         normed_one=normed_one,
         queries=queries,
         blocks=blocks,
+        traded=traded,
         attended=attended,
         log_total=log_total,
         branch=branch,
@@ -714,10 +716,10 @@
         )
 
 
-    sent, _ = forward(first_tokens, w, late=(fc_half, fc_weights))
-    sent, live_grad = lax.optimization_barrier((sent, live_grad))
+    sent, first = forward(first_tokens, w, late=(fc_half, fc_weights, live_grad))
+    sent, traded = lax.optimization_barrier((sent, first["traded"]))
     passed = lax.ppermute(sent, "section", [(0, 1)])
-    last_grad = as_image(flip(trade(live_grad)))
+    last_grad = as_image(flip(traded))
     tokens = jnp.where(section == 0, first_tokens, passed)
     result, kept = forward(tokens, w)
 
@@ -749,7 +751,8 @@
     fc_grad = lax.psum_scatter(
         jnp.concatenate(rows, axis=1), RING_Y, scatter_dimension=0, tiled=True
     )
-    ab, in_grad = direct_sums([(a_sum, RING_Z, 0), (b_sum, RING_Y, 0)], flip(traded))
+    ab = direct_sums([(a_sum, RING_Z, 0), (b_sum, RING_Y, 0)])
+    in_grad = flip(traded)
     ab = jnp.concatenate([ab[0][:, :width], ab[1], ab[0][:, width:]], axis=1)
 
     def chips_sum(a):

time: 548 us -> 542 us (0.989)
  waiting for transfers between devices: 158 us -> 147 us
  matrix products: 77.5 us -> 84.1 us
    all_to_all x4, waiting for transfers between devices: 23.8 us -> 15.1 us  [trade(): return lax.all_to_all(tokens, 'z', split_axis=0, concat_axis=0, tiled=True)]
    dot_general x48, matrix products: 77.5 us -> 84.1 us  [dot(): return lax.dot_general(a, b, (dims, ((), ())), preferred_element_type=f32)]
    ppermute x4, waiting for transfers between devices: 5.89 us -> 0.01 us  [flip(): return lax.ppermute(tokens, ('yh', 'core'), FLIP)]
    unnamed x279 -> x303, local copies, waits for them, and re-layouts: 25.5 us -> 20.7 us
  transfers between devices with their start and end apart: 72 -> 72, of which waited for: 32 -> 30; matrix products, arithmetic and copies ran while one was open for 16% -> 18% of each run, Pallas kernels for 13% -> 14%
where the time goes in v10:
time: 542 us; the launch traced here: 531 us
  waiting for transfers between devices  147 us (27%)
  starting transfers between devices  107 us (20%)
  Pallas kernels  96.5 us (18%)
  matrix products  84.1 us (16%)
  local copies, waits for them, and re-layouts  39.7 us (7%)
  other arithmetic  39 us (7%)
  between operations  17.2 us (3%)
    dot_general x48, matrix products, dot(): return lax.dot_general(a, b, (dims, ((), ())), preferred_element_type=f32)  84.1 us
    ppermute x36, waiting for transfers between devices, swap(): return lax.ppermute(value, axis, [(0, 1), (1, 0)])  54.4 us
    pallas_call x4, Pallas kernels, attend_back(): pl.pallas_call(attend_back_kernel, grid=(pairs,), in_specs=[q_spec] + kv_...  36.9 us
    ppermute x4, waiting for transfers between devices, first_hop(): return (lax.ppermute(value, axis, AHEAD), lax.ppermute(value, axis, BACK))  32.1 us
    pallas_call x4, Pallas kernels, attend(): pl.pallas_call(attend_kernel, grid=(pairs,), in_specs=[q_spec] + kv_specs...  31.2 us
    ppermute x36, starting transfers between devices, swap(): return lax.ppermute(value, axis, [(0, 1), (1, 0)])  31 us
    ppermute x4, starting transfers between devices, flip(): return lax.ppermute(tokens, ('yh', 'core'), FLIP)  27.6 us
    pallas_call x8, Pallas kernels, outer(): pl.pallas_call(kernel, grid=(grid,), in_specs=in_specs, out_specs=pl.Bloc...  22.6 us
  transfers between devices with their start and end apart: 72, of which 30 were waited for; matrix products, arithmetic and copies ran while one was open for 18% of the time, Pallas kernels for 14%

profile of v10, /device:TPU:1, one launch (start us, length us, event | category | flops | bytes accessed | tf_op | source)
XLA Modules:
  0.0 531.0 jit_solution(10279515918217521177)
XLA Ops:
  12.0 6.2 %collective-permute-start.3 = (bf16[4,64,1024]{2,1,0:T(8,128)(2,1)S(1)}, bf16[4,64,1024]{2,1,0:T(8,128)(2,1)}, u32[]{:S(2)}, u32[]{:S(2)}) collective-permute-start(bf16[4,64,1024]{2,1,0:T(8,128)(2,1)S(1)} %copy-done.129), channel_id=1, source_target_pairs={{0,0},{1,8},{8,1},{9,9},{2,2},{3,10},{10,3},{11,11},{4,4},{5,12},{... | collective-permute-start | bytes 1572872 | tf_op jit(solution)/shard_map/ppermute | solution.py:317
  25.4 4.8 all-to-all-start
  31.1 6.7 %collective-permute-done.1.refs_2_ = bf16[64,2176]{1,0:T(8,128)(2,1)S(1)} collective-permute-done((bf16[64,2176]{1,0:T(8,128)(2,1)S(1)}, bf16[64,2176]{1,0:T(8,128)(2,1)S(1)}, u32[]{:S(2)}, u32[]{:S(2)}) %collective-permute-start.1) | collective-permute-done | bytes 278560 | tf_op jit(solution)/shard_map/ppermute | solution.py:337
  40.2 6.1 %all-gather.3.cloned.1.call-done = bf16[256,4096]{1,0:T(8,128)(2,1)} async-done(((bf16[64,4096]{1,0:T(8,128)(2,1)}), bf16[256,4096]{1,0:T(8,128)(2,1)}) %all-gather.3.cloned.1.call-update) | async-done | bytes 2097168 | tf_op jit(solution)/shard_map/all_gather | solution.py:651
  48.0 23.9 %collective-permute-done.5.refs_2_ = bf16[4,64,2176]{2,1,0:T(8,128)(2,1)S(1)} collective-permute-done((bf16[4,64,2176]{2,1,0:T(8,128)(2,1)S(1)}, bf16[4,64,2176]{2,1,0:T(8,128)(2,1)S(1)}, u32[]{:S(2)}, u32[]{:S(2)}) %collective-permute-start.5) | collective-permute-done | bytes 1114144 | tf_op jit(solution)/shard_map/ppermute | solution.py:337
  76.4 10.6 %collective-permute-done.7.refs_4_ = bf16[2,64,2176]{2,1,0:T(8,128)(2,1)S(1)} collective-permute-done((bf16[2,64,2176]{2,1,0:T(8,128)(2,1)S(1)}, bf16[2,64,2176]{2,1,0:T(8,128)(2,1)S(1)}, u32[]{:S(2)}, u32[]{:S(2)}) %collective-permute-start.7) | collective-permute-done | bytes 557088 | tf_op jit(solution)/shard_map/ppermute | solution.py:344
  103.7 4.2 all-to-all-start.1
  109.0 7.9 %collective-permute-done.11.near_ref = bf16[256,1024]{1,0:T(8,128)(2,1)} collective-permute-done((bf16[256,1024]{1,0:T(8,128)(2,1)S(1)}, bf16[256,1024]{1,0:T(8,128)(2,1)}, u32[]{:S(2)}, u32[]{:S(2)}) %collective-permute-start.11) | collective-permute-done | bytes 524320 | tf_op jit(solution)/shard_map/ppermute | solution.py:36
  120.7 8.4 %attend.4 = (bf16[256,512]{1,0:T(8,128)(2,1)S(1)}, f32[4,2,256]{2,1,0:T(2,128)}) custom-call(bf16[256,512]{1,0:T(8,128)(2,1)S(1)} %pad_maximum_fusion.14.q_ref, bf16[256,1024]{1,0:T(8,128)(2,1)S(1)} %pad_maximum_fusion.5.own_ref, bf16[256,1024]{1,0:T(8,128)(2,1)S(1)} %collective-permute-done.10.mate_ref, bf16[256,1024]{1,0:T(8,128)(2,1)} %collective-permute-done.11.near_ref, ...), custom_call_target="tpu_custom_call" | custom-call | flops 2147483648 | bytes 4194304 | tf_op jit(solution)/shard_map/attend/pallas_call | solution.py:118
  129.0 4.7 collective-permute-done.13.near_ref
  138.6 8.5 %attend.5 = (bf16[256,512]{1,0:T(8,128)(2,1)S(1)}, f32[4,2,256]{2,1,0:T(2,128)}) custom-call(bf16[256,512]{1,0:T(8,128)(2,1)S(1)} %pad_maximum_fusion.15.q_ref, bf16[256,1024]{1,0:T(8,128)(2,1)S(1)} %pad_maximum_fusion.6.own_ref, bf16[256,1024]{1,0:T(8,128)(2,1)S(1)} %collective-permute-done.14.mate_ref, bf16[256,1024]{1,0:T(8,128)(2,1)} %collective-permute-done.13.near_ref, ...), custom_call_target="tpu_custom_call" | custom-call | flops 2147483648 | bytes 4194304 | tf_op jit(solution)/shard_map/attend/pallas_call | solution.py:118
  164.7 5.5 %collective-permute-start.18 = (bf16[4,64,1024]{2,1,0:T(8,128)(2,1)}, bf16[4,64,1024]{2,1,0:T(8,128)(2,1)S(1)}, u32[]{:S(2)}, u32[]{:S(2)}) collective-permute-start(bf16[4,64,1024]{2,1,0:T(8,128)(2,1)} %all-to-all-done.1), channel_id=1, source_target_pairs={{0,0},{1,8},{8,1},{9,9},{2,2},{3,10},{10,3},{11,11},{4,4},{5,12},{... | collective-permute-start | bytes 1572872 | tf_op jit(solution)/shard_map/ppermute | solution.py:317
  170.2 5.2 collective-permute-done.19
  197.9 7.0 %attend.6 = (bf16[256,512]{1,0:T(8,128)(2,1)S(1)}, f32[4,2,256]{2,1,0:T(2,128)S(1)}) custom-call(bf16[256,512]{1,0:T(8,128)(2,1)S(1)} %pad_maximum_fusion.16.q_ref, bf16[256,1024]{1,0:T(8,128)(2,1)S(1)} %pad_maximum_fusion.7.own_ref, bf16[256,1024]{1,0:T(8,128)(2,1)S(1)} %collective-permute-done.20.mate_ref, ...), custom_call_target="tpu_custom_call" | custom-call | flops 2147483648 | bytes 4194304 | tf_op jit(solution)/shard_map/attend/pallas_call | solution.py:118
  212.1 7.2 %attend.7 = (bf16[256,512]{1,0:T(8,128)(2,1)S(1)}, f32[4,2,256]{2,1,0:T(2,128)S(1)}) custom-call(bf16[256,512]{1,0:T(8,128)(2,1)S(1)} %pad_maximum_fusion.17.q_ref, bf16[256,1024]{1,0:T(8,128)(2,1)S(1)} %pad_maximum_fusion.8.own_ref, bf16[256,1024]{1,0:T(8,128)(2,1)S(1)} %collective-permute-done.24.mate_ref, ...), custom_call_target="tpu_custom_call" | custom-call | flops 2147483648 | bytes 4194304 | tf_op jit(solution)/shard_map/attend/pallas_call | solution.py:118
  224.5 5.0 multiply_convert_fusion
  238.9 4.2 multiply_convert_fusion.5
  244.6 9.4 %attend_back.4 = (bf16[256,512]{1,0:T(8,128)(2,1)S(1)}, bf16[256,1024]{1,0:T(8,128)(2,1)S(1)}, bf16[256,1024]{1,0:T(8,128)(2,1)S(1)}, bf16[256,1024]{1,0:T(8,128)(2,1)S(1)}, bf16[256,1024]{1,0:T(8,128)(2,1)S(1)}) custom-call(bf16[256,512]{1,0:T(8,128)(2,1)S(1)} %pad_maximum_fusion.16.q_ref, bf16[256,1024]{1,0:T(8,128)(2,1)S(1)} %pad_maximum_fusion.7.own_ref, ...), custom_call_target="tpu_custom_call" | custom-call | flops 5368709120 | bytes 4194304 | tf_op jit(solution)/shard_map/attend_back/pallas_call | solution.py:137
  257.9 9.6 %attend_back.5 = (bf16[256,512]{1,0:T(8,128)(2,1)S(1)}, bf16[256,1024]{1,0:T(8,128)(2,1)S(1)}, bf16[256,1024]{1,0:T(8,128)(2,1)}, bf16[256,1024]{1,0:T(8,128)(2,1)S(1)}, bf16[256,1024]{1,0:T(8,128)(2,1)S(1)}) custom-call(bf16[256,512]{1,0:T(8,128)(2,1)S(1)} %pad_maximum_fusion.17.q_ref, bf16[256,1024]{1,0:T(8,128)(2,1)S(1)} %pad_maximum_fusion.8.own_ref, ...), custom_call_target="tpu_custom_call" | custom-call | flops 5368709120 | bytes 4194304 | tf_op jit(solution)/shard_map/attend_back/pallas_call | solution.py:137
  275.2 4.1 all-to-all-start.2
  283.7 4.5 all-to-all-done.2
  297.4 5.8 %collective-permute-start.33 = (bf16[4,64,1024]{2,1,0:T(8,128)(2,1)}, bf16[4,64,1024]{2,1,0:T(8,128)(2,1)}, u32[]{:S(2)}, u32[]{:S(2)}) collective-permute-start(bf16[4,64,1024]{2,1,0:T(8,128)(2,1)} %all-to-all-done.2), channel_id=1, source_target_pairs={{0,0},{1,8},{8,1},{9,9},{2,2},{3,10},{10,3},{11,11},{4,4},{5,12},{... | collective-permute-start | bytes 1572872 | tf_op jit(solution)/shard_map/ppermute | solution.py:317
  303.2 7.2 %collective-permute-done.32 = bf16[256,1024]{1,0:T(8,128)(2,1)} collective-permute-done((bf16[256,1024]{1,0:T(8,128)(2,1)}, bf16[256,1024]{1,0:T(8,128)(2,1)}, u32[]{:S(2)}, u32[]{:S(2)}) %collective-permute-start.32) | collective-permute-done | bytes 524320 | tf_op jit(solution)/shard_map/ppermute | solution.py:730
  353.6 9.0 %attend_back.6 = (bf16[256,512]{1,0:T(8,128)(2,1)S(1)}, bf16[256,1024]{1,0:T(8,128)(2,1)S(1)}, bf16[256,1024]{1,0:T(8,128)(2,1)S(1)}, bf16[256,1024]{1,0:T(8,128)(2,1)S(1)}, bf16[256,1024]{1,0:T(8,128)(2,1)S(1)}) custom-call(bf16[256,512]{1,0:T(8,128)(2,1)S(1)} %copy-done.27, bf16[256,1024]{1,0:T(8,128)(2,1)S(1)} %copy-done.22, ...), custom_call_target="tpu_custom_call" | custom-call | flops 5368709120 | bytes 4194304 | tf_op jit(solution)/shard_map/attend_back/pallas_call | solution.py:137
  374.6 9.0 %attend_back.7 = (bf16[256,512]{1,0:T(8,128)(2,1)S(1)}, bf16[256,1024]{1,0:T(8,128)(2,1)S(1)}, bf16[256,1024]{1,0:T(8,128)(2,1)S(1)}, bf16[256,1024]{1,0:T(8,128)(2,1)S(1)}, bf16[256,1024]{1,0:T(8,128)(2,1)S(1)}) custom-call(bf16[256,512]{1,0:T(8,128)(2,1)S(1)} %pad_maximum_fusion.17.q_ref, bf16[256,1024]{1,0:T(8,128)(2,1)S(1)} %copy-done.20, ...), custom_call_target="tpu_custom_call" | custom-call | flops 5368709120 | bytes 4194304 | tf_op jit(solution)/shard_map/attend_back/pallas_call | solution.py:137
  392.8 12.2 %collective-permute-done.42 = bf16[256,1024]{1,0:T(8,128)(2,1)S(1)} collective-permute-done((bf16[256,1024]{1,0:T(8,128)(2,1)S(1)}, bf16[256,1024]{1,0:T(8,128)(2,1)S(1)}, u32[]{:S(2)}, u32[]{:S(2)}) %collective-permute-start.42) | collective-permute-done | bytes 524320 | tf_op jit(solution)/shard_map/ppermute | solution.py:36
  434.3 6.7 %collective-permute-done.46 = bf16[2,64,1024]{2,1,0:T(8,128)(2,1)} collective-permute-done((bf16[2,64,1024]{2,1,0:T(8,128)(2,1)S(1)}, bf16[2,64,1024]{2,1,0:T(8,128)(2,1)}, u32[]{:S(2)}, u32[]{:S(2)}) %collective-permute-start.46) | collective-permute-done | bytes 262176 | tf_op jit(solution)/shard_map/ppermute | solution.py:395
  454.2 4.1 all-to-all-start.3
  459.5 8.3 %all-to-all-done.3 = bf16[4,64,1024]{2,1,0:T(8,128)(2,1)} async-done(((bf16[4,64,1024]{2,1,0:T(8,128)(2,1)}), bf16[4,64,1024]{2,1,0:T(8,128)(2,1)}, u32[]{:S(2)}, u32[]{:S(2)}) %all-to-all-start.3) | async-done | bytes 524320 | tf_op jit(solution)/shard_map/all_to_all | solution.py:321
  480.7 4.7 collective-permute-done.57
  488.9 10.1 %collective-permute-start.52 = (bf16[4,64,1024]{2,1,0:T(8,128)(2,1)}, bf16[4,64,1024]{2,1,0:T(8,128)(2,1)S(1)}, u32[]{:S(2)}, u32[]{:S(2)}) collective-permute-start(bf16[4,64,1024]{2,1,0:T(8,128)(2,1)} %all-to-all-done.3), channel_id=1, source_target_pairs={{0,0},{1,8},{8,1},{9,9},{2,2},{3,10},{10,3},{11,11},{4,4},{5,12},{... | collective-permute-start | bytes 1572872 | tf_op jit(solution)/shard_map/ppermute | solution.py:317
  501.4 11.9 %collective-permute-done.61 = bf16[64,4096]{1,0:T(8,128)(2,1)S(1)} collective-permute-done((bf16[64,4096]{1,0:T(8,128)(2,1)}, bf16[64,4096]{1,0:T(8,128)(2,1)S(1)}, u32[]{:S(2)}, u32[]{:S(2)}) %collective-permute-start.61) | collective-permute-done | bytes 524320 | tf_op jit(solution)/shard_map/ppermute | solution.py:36
  (658 shorter events, 270.9 us)
Async XLA Ops:
  7.2 39.0 %all-gather.3.cloned.1.call-start = ((), (), s32[]{:S(2)}) async-start(), calls=%async_computation.7 | async-start | bytes 2621440 | tf_op jit(solution)/shard_map/all_gather | solution.py:651
  23.8 14.1 %collective-permute-start.1 = (bf16[64,2176]{1,0:T(8,128)(2,1)S(1)}, bf16[64,2176]{1,0:T(8,128)(2,1)S(1)}, u32[]{:S(2)}, u32[]{:S(2)}) collective-permute-start(bf16[64,2176]{1,0:T(8,128)(2,1)S(1)} %fusion.160.refs_0_), channel_id=1, source_target_pairs={{0,48},{16,0},{32,16},{48,32},{1,49},{17,1},{33,17},{49,33},{2,50}... | collective-permute-start | bytes 835592 | tf_op jit(solution)/shard_map/ppermute | solution.py:337
  25.4 14.7 %all-to-all-start = ((bf16[4,64,1024]{2,1,0:T(8,128)(2,1)}), bf16[4,64,1024]{2,1,0:T(8,128)(2,1)S(1)}, u32[]{:S(2)}, u32[]{:S(2)}) async-start(bf16[4,64,1024]{2,1,0:T(8,128)(2,1)} %collective-permute-done.3), calls=%async_computation | async-start | bytes 1048576 | tf_op jit(solution)/shard_map/all_to_all | solution.py:321
  30.2 106.6 %all-gather.5.cloned.1.call-start = ((), (), s32[]{:S(2)}) async-start(), calls=%async_computation.8 | async-start | bytes 10485760 | tf_op jit(solution)/shard_map/all_gather | solution.py:662
  46.3 25.6 %collective-permute-start.5 = (bf16[4,64,2176]{2,1,0:T(8,128)(2,1)S(1)}, bf16[4,64,2176]{2,1,0:T(8,128)(2,1)S(1)}, u32[]{:S(2)}, u32[]{:S(2)}) collective-permute-start(bf16[4,64,2176]{2,1,0:T(8,128)(2,1)S(1)} %ring_place.2.refs_0_), channel_id=1, source_target_pairs={{0,12},{4,0},{8,4},{12,8},{1,13},{5,1},{9,5},{13,9},{2,14},{6,2},{... | collective-permute-start | bytes 3342344 | tf_op jit(solution)/shard_map/ppermute | solution.py:337
  47.0 26.4 %collective-permute-start.4 = (bf16[4,64,2176]{2,1,0:T(8,128)(2,1)S(1)}, bf16[4,64,2176]{2,1,0:T(8,128)(2,1)}, u32[]{:S(2)}, u32[]{:S(2)}) collective-permute-start(bf16[4,64,2176]{2,1,0:T(8,128)(2,1)S(1)} %ring_place.2.refs_0_), channel_id=1, source_target_pairs={{0,4},{4,8},{8,12},{12,0},{1,5},{5,9},{9,13},{13,1},{2,6},{6,10},{... | collective-permute-start | bytes 3342344 | tf_op jit(solution)/shard_map/ppermute | solution.py:337
  93.3 25.2 %collective-permute-start.8 = (bf16[1024,512]{1,0:T(8,128)(2,1)S(1)}, bf16[1024,512]{1,0:T(8,128)(2,1)}, u32[]{:S(2)}, u32[]{:S(2)}) collective-permute-start(bf16[1024,512]{1,0:T(8,128)(2,1)S(1)} %bitcast.216), channel_id=1, source_target_pairs={{0,1},{1,0},{2,3},{3,2},{4,5},{5,4},{6,7},{7,6},{8,9},{9,8},{10,11... | collective-permute-start | bytes 3145736 | tf_op jit(solution)/shard_map/ppermute | solution.py:36
  103.7 25.4 %all-to-all-start.1 = ((bf16[4,64,1024]{2,1,0:T(8,128)(2,1)}), bf16[4,64,1024]{2,1,0:T(8,128)(2,1)}, u32[]{:S(2)}, u32[]{:S(2)}) async-start(bf16[4,64,1024]{2,1,0:T(8,128)(2,1)} %broadcast_multiply_fusion), calls=%async_computation.1 | async-start | bytes 1048576 | tf_op jit(solution)/shard_map/all_to_all | solution.py:321
  136.9 16.1 %collective-permute-start.17 = (bf16[1024,4096]{1,0:T(8,128)(2,1)}, bf16[1024,4096]{1,0:T(8,128)(2,1)}, u32[]{:S(2)}, u32[]{:S(2)}) collective-permute-start(bf16[1024,4096]{1,0:T(8,128)(2,1)} %all-gather.5.cloned.1.call-done), channel_id=1, source_target_pairs={{0,1},{1,0},{2,3},{3,2},{4,5},{5,4},{6,7},{7,6},{8,9},{9,8},{10,11... | collective-permute-start | bytes 25165832 | tf_op jit(solution)/shard_map/ppermute | solution.py:36
  161.5 13.8 %collective-permute-start.19 = (bf16[256,1024]{1,0:T(8,128)(2,1)S(1)}, bf16[256,1024]{1,0:T(8,128)(2,1)S(1)}, u32[]{:S(2)}, u32[]{:S(2)}) collective-permute-start(bf16[256,1024]{1,0:T(8,128)(2,1)S(1)} %fusion.90), channel_id=1, source_target_pairs={{0,64},{1,65},{2,66},{3,67},{4,68},{5,69},{6,70},{7,71},{8,72},{9,... | collective-permute-start | bytes 1572872 | tf_op jit(solution)/shard_map/ppermute | solution.py:721
  164.7 20.1 %collective-permute-start.18 = (bf16[4,64,1024]{2,1,0:T(8,128)(2,1)}, bf16[4,64,1024]{2,1,0:T(8,128)(2,1)S(1)}, u32[]{:S(2)}, u32[]{:S(2)}) collective-permute-start(bf16[4,64,1024]{2,1,0:T(8,128)(2,1)} %all-to-all-done.1), channel_id=1, source_target_pairs={{0,0},{1,8},{8,1},{9,9},{2,2},{3,10},{10,3},{11,11},{4,4},{5,12},{... | collective-permute-start | bytes 1572872 | tf_op jit(solution)/shard_map/ppermute | solution.py:317
  181.0 16.9 %collective-permute-start.20 = (bf16[256,1024]{1,0:T(8,128)(2,1)S(1)}, bf16[256,1024]{1,0:T(8,128)(2,1)S(1)}, u32[]{:S(2)}, u32[]{:S(2)}) collective-permute-start(bf16[256,1024]{1,0:T(8,128)(2,1)S(1)} %pad_maximum_fusion.7.own_ref), channel_id=1, source_target_pairs={{0,1},{1,0},{2,3},{3,2},{4,5},{5,4},{6,7},{7,6},{8,9},{9,8},{10,11... | collective-permute-start | bytes 1572872 | tf_op jit(solution)/shard_map/ppermute | solution.py:36
  257.5 13.8 %collective-permute-start.28 = (bf16[256,1024]{1,0:T(8,128)(2,1)S(1)}, bf16[256,1024]{1,0:T(8,128)(2,1)S(1)}, u32[]{:S(2)}, u32[]{:S(2)}) collective-permute-start(bf16[256,1024]{1,0:T(8,128)(2,1)S(1)} %get-tuple-element.173), channel_id=1, source_target_pairs={{0,1},{1,0},{2,3},{3,2},{4,5},{5,4},{6,7},{7,6},{8,9},{9,8},{10,11... | collective-permute-start | bytes 1572872 | tf_op jit(solution)/shard_map/ppermute | solution.py:36
  271.3 17.0 %collective-permute-start.29 = (bf16[256,1024]{1,0:T(8,128)(2,1)}, bf16[256,1024]{1,0:T(8,128)(2,1)}, u32[]{:S(2)}, u32[]{:S(2)}) collective-permute-start(bf16[256,1024]{1,0:T(8,128)(2,1)} %get-tuple-element.176), channel_id=1, source_target_pairs={{0,1},{1,0},{2,3},{3,2},{4,5},{5,4},{6,7},{7,6},{8,9},{9,8},{10,11... | collective-permute-start | bytes 1572872 | tf_op jit(solution)/shard_map/ppermute | solution.py:36
  273.1 15.1 %collective-permute-start.31 = (bf16[256,1024]{1,0:T(8,128)(2,1)}, bf16[256,1024]{1,0:T(8,128)(2,1)}, u32[]{:S(2)}, u32[]{:S(2)}) collective-permute-start(bf16[256,1024]{1,0:T(8,128)(2,1)} %add_convert_fusion.9), channel_id=1, source_target_pairs={{0,4},{4,0},{1,5},{5,1},{2,6},{6,2},{3,7},{7,3},{8,12},{12,8},{9,1... | collective-permute-start | bytes 1572872 | tf_op jit(solution)/shard_map/ppermute | solution.py:36
  279.3 161.7 %reduce-scatter.6.cloned.1.call-start = ((), (), s32[]{:S(2)}) async-start(), calls=%async_computation.10 | async-start | bytes 5242880 | tf_op jit(solution)/shard_map/reduce_scatter | solution.py:535
  296.0 14.5 %collective-permute-start.32 = (bf16[256,1024]{1,0:T(8,128)(2,1)}, bf16[256,1024]{1,0:T(8,128)(2,1)}, u32[]{:S(2)}, u32[]{:S(2)}) collective-permute-start(bf16[256,1024]{1,0:T(8,128)(2,1)} %fusion.119), channel_id=1, source_target_pairs={{64,0},{65,1},{66,2},{67,3},{68,4},{69,5},{70,6},{71,7},{72,8},{73... | collective-permute-start | bytes 1572872 | tf_op jit(solution)/shard_map/ppermute | solution.py:730
  316.1 21.0 %collective-permute-start.34 = (bf16[1024,2048]{1,0:T(8,128)(2,1)S(1)}, bf16[1024,2048]{1,0:T(8,128)(2,1)S(1)}, u32[]{:S(2)}, u32[]{:S(2)}) collective-permute-start(bf16[1024,2048]{1,0:T(8,128)(2,1)S(1)} %outer.9), channel_id=1, source_target_pairs={{0,1},{1,0},{2,3},{3,2},{4,5},{5,4},{6,7},{7,6},{8,9},{9,8},{10,11... | collective-permute-start | bytes 12582920 | tf_op jit(solution)/shard_map/ppermute | solution.py:36
  342.0 99.0 %reduce-scatter.4.cloned.1.call-start = ((), (), s32[]{:S(2)}) async-start(), calls=%async_computation.9 | async-start | bytes 5242880 | tf_op jit(solution)/shard_map/reduce_scatter | solution.py:560
  370.6 128.4 %reduce-scatter.8.cloned.1.call-start = ((), (), s32[]{:S(2)}) async-start(), calls=%async_computation.11 | async-start | bytes 2621440 | tf_op jit(solution)/shard_map/reduce_scatter | solution.py:751
  373.0 18.7 %collective-permute-start.39 = (bf16[256,1024]{1,0:T(8,128)(2,1)}, bf16[256,1024]{1,0:T(8,128)(2,1)S(1)}, u32[]{:S(2)}, u32[]{:S(2)}) collective-permute-start(bf16[256,1024]{1,0:T(8,128)(2,1)} %copy-done.41), channel_id=1, source_target_pairs={{0,1},{1,0},{2,3},{3,2},{4,5},{5,4},{6,7},{7,6},{8,9},{9,8},{10,11... | collective-permute-start | bytes 1572872 | tf_op jit(solution)/shard_map/ppermute | solution.py:36
  386.3 18.7 %collective-permute-start.40 = (bf16[256,1024]{1,0:T(8,128)(2,1)S(1)}, bf16[256,1024]{1,0:T(8,128)(2,1)S(1)}, u32[]{:S(2)}, u32[]{:S(2)}) collective-permute-start(bf16[256,1024]{1,0:T(8,128)(2,1)S(1)} %get-tuple-element.205), channel_id=1, source_target_pairs={{0,1},{1,0},{2,3},{3,2},{4,5},{5,4},{6,7},{7,6},{8,9},{9,8},{10,11... | collective-permute-start | bytes 1572872 | tf_op jit(solution)/shard_map/ppermute | solution.py:36
  389.2 29.5 %collective-permute-start.38 = (bf16[1024,1024]{1,0:T(8,128)(2,1)S(1)}, bf16[1024,1024]{1,0:T(8,128)(2,1)}, u32[]{:S(2)}, u32[]{:S(2)}) collective-permute-start(bf16[1024,1024]{1,0:T(8,128)(2,1)S(1)} %outer.12), channel_id=1, source_target_pairs={{0,1},{1,0},{2,3},{3,2},{4,5},{5,4},{6,7},{7,6},{8,9},{9,8},{10,11... | collective-permute-start | bytes 6291464 | tf_op jit(solution)/shard_map/ppermute | solution.py:36
  391.3 13.7 %collective-permute-start.42 = (bf16[256,1024]{1,0:T(8,128)(2,1)S(1)}, bf16[256,1024]{1,0:T(8,128)(2,1)S(1)}, u32[]{:S(2)}, u32[]{:S(2)}) collective-permute-start(bf16[256,1024]{1,0:T(8,128)(2,1)S(1)} %add_convert_fusion.4), channel_id=1, source_target_pairs={{0,4},{4,0},{1,5},{5,1},{2,6},{6,2},{3,7},{7,3},{8,12},{12,8},{9,1... | collective-permute-start | bytes 1572872 | tf_op jit(solution)/shard_map/ppermute | solution.py:36
  408.3 18.2 %collective-permute-start.45 = (bf16[1024,1024]{1,0:T(8,128)(2,1)}, bf16[1024,1024]{1,0:T(8,128)(2,1)}, u32[]{:S(2)}, u32[]{:S(2)}) collective-permute-start(bf16[1024,1024]{1,0:T(8,128)(2,1)} %outer.14), channel_id=1, source_target_pairs={{0,1},{1,0},{2,3},{3,2},{4,5},{5,4},{6,7},{7,6},{8,9},{9,8},{10,11... | collective-permute-start | bytes 6291464 | tf_op jit(solution)/shard_map/ppermute | solution.py:36
  443.2 24.6 %collective-permute-start.50 = (bf16[4,64,1024]{2,1,0:T(8,128)(2,1)}, bf16[4,64,1024]{2,1,0:T(8,128)(2,1)}, u32[]{:S(2)}, u32[]{:S(2)}) collective-permute-start(bf16[4,64,1024]{2,1,0:T(8,128)(2,1)} %pad_maximum_fusion.11), channel_id=1, source_target_pairs={{0,16},{16,32},{32,48},{48,0},{1,17},{17,33},{33,49},{49,1},{2,18}... | collective-permute-start | bytes 1572872 | tf_op jit(solution)/shard_map/ppermute | solution.py:403
  447.1 20.8 %collective-permute-start.48 = (bf16[4,64,1152]{2,1,0:T(8,128)(2,1)}, bf16[4,64,1152]{2,1,0:T(8,128)(2,1)}, u32[]{:S(2)}, u32[]{:S(2)}) collective-permute-start(bf16[4,64,1152]{2,1,0:T(8,128)(2,1)} %pad_maximum_fusion.2), channel_id=1, source_target_pairs={{0,4},{4,8},{8,12},{12,0},{1,5},{5,9},{9,13},{13,1},{2,6},{6,10},{... | collective-permute-start | bytes 1769480 | tf_op jit(solution)/shard_map/ppermute | solution.py:403
  449.3 20.5 %collective-permute-start.49 = (bf16[4,64,1152]{2,1,0:T(8,128)(2,1)}, bf16[4,64,1152]{2,1,0:T(8,128)(2,1)}, u32[]{:S(2)}, u32[]{:S(2)}) collective-permute-start(bf16[4,64,1152]{2,1,0:T(8,128)(2,1)} %pad_maximum_fusion.3), channel_id=1, source_target_pairs={{0,12},{4,0},{8,4},{12,8},{1,13},{5,1},{9,5},{13,9},{2,14},{6,2},{... | collective-permute-start | bytes 1769480 | tf_op jit(solution)/shard_map/ppermute | solution.py:403
  451.5 16.4 %collective-permute-start.51 = (bf16[4,64,1024]{2,1,0:T(8,128)(2,1)}, bf16[4,64,1024]{2,1,0:T(8,128)(2,1)}, u32[]{:S(2)}, u32[]{:S(2)}) collective-permute-start(bf16[4,64,1024]{2,1,0:T(8,128)(2,1)} %pad_maximum_fusion.12), channel_id=1, source_target_pairs={{0,48},{16,0},{32,16},{48,32},{1,49},{17,1},{33,17},{49,33},{2,50}... | collective-permute-start | bytes 1572872 | tf_op jit(solution)/shard_map/ppermute | solution.py:403
  488.9 25.7 %collective-permute-start.52 = (bf16[4,64,1024]{2,1,0:T(8,128)(2,1)}, bf16[4,64,1024]{2,1,0:T(8,128)(2,1)S(1)}, u32[]{:S(2)}, u32[]{:S(2)}) collective-permute-start(bf16[4,64,1024]{2,1,0:T(8,128)(2,1)} %all-to-all-done.3), channel_id=1, source_target_pairs={{0,0},{1,8},{8,1},{9,9},{2,2},{3,10},{10,3},{11,11},{4,4},{5,12},{... | collective-permute-start | bytes 1572872 | tf_op jit(solution)/shard_map/ppermute | solution.py:317
  499.1 14.3 %collective-permute-start.61 = (bf16[64,4096]{1,0:T(8,128)(2,1)}, bf16[64,4096]{1,0:T(8,128)(2,1)S(1)}, u32[]{:S(2)}, u32[]{:S(2)}) collective-permute-start(bf16[64,4096]{1,0:T(8,128)(2,1)} %reduce-scatter.8.cloned.1.call-done), channel_id=1, source_target_pairs={{0,2},{2,0},{1,3},{3,1},{4,6},{6,4},{5,7},{7,5},{8,10},{10,8},{9,1... | collective-permute-start | bytes 1572872 | tf_op jit(solution)/shard_map/ppermute | solution.py:36
  499.8 14.8 %collective-permute-start.60 = (bf16[64,2176]{1,0:T(8,128)(2,1)S(1)}, bf16[64,2176]{1,0:T(8,128)(2,1)S(1)}, u32[]{:S(2)}, u32[]{:S(2)}) collective-permute-start(bf16[64,2176]{1,0:T(8,128)(2,1)S(1)} %add_convert_fusion.14.mine_ref), channel_id=1, source_target_pairs={{0,1},{1,0},{2,3},{3,2},{4,5},{5,4},{6,7},{7,6},{8,9},{9,8},{10,11... | collective-permute-start | bytes 835592 | tf_op jit(solution)/shard_map/ppermute | solution.py:36
  (182 other events, 2171.2 us)
Sparse Core Ops, SparseCore 0:
  12.1 34.0 all-gather.2
  47.9 88.9 all-gather.4
  342.1 45.5 reduce-scatter.5
  390.1 47.1 reduce-scatter.3
  444.9 40.6 reduce-scatter.7
